TPU v7x, 32 devices: a whole 2x2x4 slice. The times are simulated.
32 devices in a mesh: dp: 4 (over y, x), expert: 8 (over z, core).
Axes of the slice: x: 2, y: 2, z: 4, core: 2. Of those that a mesh axis runs over, the one named last changes fastest.
Arguments:
- tokens: bfloat16 [8192, 1024], P(('dp', 'expert')), may hold values from -6 to 6
- cotangent: bfloat16 [8192, 1024], P(('dp', 'expert')), may hold values from -6 to 6
- gates: bfloat16 [8192, 2], P(('dp', 'expert')), may hold values from 0.099609375 to 1
- expert_ids: int32 [8192, 2], P(('dp', 'expert')), may hold values from 0 to 7, all different within a row; in each aligned block of 128 rows (0 to 127, 128 to 255, ...) at most 64 rows name the same one
- expert_weights: bfloat16 [8, 3, 1024, 768], P('expert'), may hold values from -0.1875 to 0.1875
Outputs:
- tokens_grad: bfloat16 [8192, 1024], P(('dp', 'expert'))
- gates_grad: bfloat16 [8192, 2], P(('dp', 'expert'))
- weights_grad: bfloat16 [8, 3, 1024, 768], P('expert', None, 'dp')
Inputs may be any that keep to these rules, and one draw needn't show every extreme that they name: `expert_ids`: within each micro-batch of 128 tokens of one device no expert is named by more than 64 routes, a bound that some block reaches; the two ids of a token differ.
All inputs are finite; a program needn't handle non-finite values.
Results may differ from a plain program's by a relative error of at most 0.017.
Values may be sent and summed in bfloat16 or wider, within the bound.
No kernel may reach another device: no remote copies, remote signals or barrier semaphores. Data moves between devices by JAX's collectives and lax.ppermute only.
A program may use at most 64 MiB of HBM per device.

v0:
```python
import jax
import jax.numpy as jnp
from jax import lax
from jax.sharding import PartitionSpec as P

MICRO = 2


def route_slots(ids_block, expert_count, capacity):
    flat_ids = ids_block.reshape(-1)
    one_hot = (flat_ids[:, None] == jnp.arange(expert_count, dtype=jnp.int32)[None, :]).astype(
        jnp.int32
    )
    earlier = jnp.cumsum(one_hot, axis=0) - one_hot
    rank_slot = jnp.sum(earlier * one_hot, axis=1)
    route_slot = flat_ids * capacity + rank_slot
    routes = jnp.arange(flat_ids.shape[0], dtype=jnp.int32)
    slot_route = jnp.zeros((expert_count * capacity,), jnp.int32).at[route_slot].set(routes)
    filled = jnp.zeros((expert_count * capacity,), jnp.int32).at[route_slot].set(1)
    return (route_slot, slot_route, filled)


def pack_rows(inputs, cotan, gate_vals, slot_route, filled, expert_count, capacity):
    token_index = slot_route // 2
    keeps = filled > 0
    feature_width = inputs.shape[1]
    rows_in = jnp.where(
        keeps[:, None], jnp.take(inputs, token_index, axis=0), jnp.zeros((), inputs.dtype)
    )
    rows_cot = jnp.where(
        keeps[:, None], jnp.take(cotan, token_index, axis=0), jnp.zeros((), cotan.dtype)
    )
    rows_gate = jnp.where(
        keeps, jnp.take(gate_vals.reshape(-1), slot_route), jnp.zeros((), gate_vals.dtype)
    )
    return (
        rows_in.reshape(expert_count, capacity, feature_width),
        rows_cot.reshape(expert_count, capacity, feature_width),
        rows_gate.reshape(expert_count, capacity),
    )


def expert_backward(rows_in, rows_cot, rows_gate, weights):
    w_gate = weights[0]
    w_up = weights[1]
    w_down = weights[2]
    contract_last = (((1,), (1,)), ((), ()))
    contract_first = (((0,), (0,)), ((), ()))
    pre_gate = jnp.dot(rows_in, w_gate, preferred_element_type=jnp.float32)
    pre_up = jnp.dot(rows_in, w_up, preferred_element_type=jnp.float32)
    sigmoid_gate = jax.nn.sigmoid(pre_gate)
    activated = pre_gate * sigmoid_gate
    hidden = (activated * pre_up).astype(jnp.bfloat16)
    output = lax.dot_general(hidden, w_down, contract_last, preferred_element_type=jnp.float32)
    gate_grad = jnp.sum(output * rows_cot.astype(jnp.float32), axis=1).astype(jnp.bfloat16)
    scaled = (rows_gate.astype(jnp.float32)[:, None] * rows_cot.astype(jnp.float32)).astype(
        jnp.bfloat16
    )
    hidden_grad = jnp.dot(scaled, w_down, preferred_element_type=jnp.float32)
    grad_pre_gate = (
        hidden_grad * pre_up * sigmoid_gate * (1.0 + pre_gate * (1.0 - sigmoid_gate))
    ).astype(jnp.bfloat16)
    grad_pre_up = (hidden_grad * activated).astype(jnp.bfloat16)
    input_grad = (
        lax.dot_general(grad_pre_gate, w_gate, contract_last, preferred_element_type=jnp.float32)
        + lax.dot_general(grad_pre_up, w_up, contract_last, preferred_element_type=jnp.float32)
    ).astype(jnp.bfloat16)
    weight_grad = jnp.stack(
        [
            lax.dot_general(
                rows_in, grad_pre_gate, contract_first, preferred_element_type=jnp.float32
            ),
            lax.dot_general(
                rows_in, grad_pre_up, contract_first, preferred_element_type=jnp.float32
            ),
            lax.dot_general(scaled, hidden, contract_first, preferred_element_type=jnp.float32),
        ]
    )
    return (input_grad, gate_grad, weight_grad)


def unpack(grad_flat, gate_flat, route_slot, batch_rows):
    feature_width = grad_flat.shape[1]
    routed = (
        jnp.take(grad_flat, route_slot, axis=0)
        .astype(jnp.float32)
        .reshape(batch_rows, 2, feature_width)
    )
    return (
        jnp.sum(routed, axis=1).astype(jnp.bfloat16),
        jnp.take(gate_flat, route_slot).reshape(batch_rows, 2),
    )


def on_device(tokens, cotangent, gates, expert_ids, expert_weights):
    local_experts = expert_weights.shape[0]
    expert_count = lax.axis_size("expert") * local_experts
    batch_rows = tokens.shape[0] // MICRO
    capacity = max(2, 4 * batch_rows // expert_count)
    feature_width = tokens.shape[1]
    slot_lists = []
    packed_list = []
    for micro_index in range(MICRO):
        lower = micro_index * batch_rows
        upper = lower + batch_rows
        route_slot, slot_route, filled = route_slots(
            expert_ids[lower:upper], expert_count, capacity
        )
        slot_lists.append(route_slot)
        packed_list.append(
            pack_rows(
                tokens[lower:upper],
                cotangent[lower:upper],
                gates[lower:upper],
                slot_route,
                filled,
                expert_count,
                capacity,
            )
        )
    joined = [
        jnp.concatenate([packed[member] for packed in packed_list], axis=1) for member in range(3)
    ]
    received = [
        (
            lax.all_to_all(joined[0], "expert", split_axis=0, concat_axis=1, tiled=True),
            lax.all_to_all(joined[1], "expert", split_axis=0, concat_axis=1, tiled=True),
            lax.all_to_all(joined[2], "expert", split_axis=0, concat_axis=1, tiled=True),
        )
    ]
    results = [[] for bundle in received]
    summed = None
    for number, bundle in enumerate(received):
        input_grad, gate_grad, weight_grad = expert_backward(
            bundle[0][0], bundle[1][0], bundle[2][0], expert_weights[0]
        )
        results[number].append((input_grad, gate_grad))
        summed = weight_grad
    rounded = lax.optimization_barrier(summed.astype(jnp.bfloat16)).astype(jnp.float32)
    grad_list = [rounded]
    weights_grad = lax.psum_scatter(
        jnp.stack(grad_list).astype(jnp.bfloat16), "dp", scatter_dimension=2, tiled=True
    )
    stacked = [
        (jnp.stack([pair[0] for pair in result]), jnp.stack([pair[1] for pair in result]))
        for result in results
    ]
    back_in, back_gate = (
        lax.all_to_all(stacked[0][0], "expert", split_axis=1, concat_axis=0, tiled=True),
        lax.all_to_all(stacked[0][1], "expert", split_axis=1, concat_axis=0, tiled=True),
    )
    returned = [
        (
            back_in[:, micro_index * capacity : (micro_index + 1) * capacity],
            back_gate[:, micro_index * capacity : (micro_index + 1) * capacity],
        )
        for micro_index in range(MICRO)
    ]
    token_parts = []
    gate_parts = []
    for micro_index in range(MICRO):
        grad_flat = returned[micro_index][0].reshape(expert_count * capacity, feature_width)
        gate_flat = returned[micro_index][1].reshape(expert_count * capacity)
        token_grad, gate_out = unpack(grad_flat, gate_flat, slot_lists[micro_index], batch_rows)
        token_parts.append(token_grad)
        gate_parts.append(gate_out)
    return (jnp.concatenate(token_parts, axis=0), jnp.concatenate(gate_parts, axis=0), weights_grad)


def solution(mesh):
    placed = (
        P(("dp", "expert"), None),
        P(("dp", "expert"), None),
        P(("dp", "expert"), None),
        P(("dp", "expert"), None),
        P("expert", None, None, None),
    )
    return jax.shard_map(
        on_device,
        mesh=mesh,
        in_specs=placed,
        out_specs=(
            P(("dp", "expert"), None),
            P(("dp", "expert"), None),
            P("expert", None, "dp", None),
        ),
        check_vma=False,
    )
```

profile of v0, /device:TPU:0, one launch (start us, length us, event | category | flops | bytes accessed | tf_op | source)
XLA Modules:
  0.0 311.4 jit_solution(5723615632908735291)
XLA Ops:
  18.2 3.4 %gather_fusion.1 = bf16[512]{0:T(512)(128)(2,1)S(1)} fusion(bf16[256]{0:T(256)(128)(2,1)S(1)} %reshape.245, s32[1024]{0:T(1024)S(1)} %pad_clamp_fusion.4), kind=kCustom, calls=%fused_computation.4.clone | custom fusion | bytes 4096 | tf_op jit(solution)/shard_map/jit(_take)/gather | solution.py:34
  21.6 3.4 %gather_fusion = bf16[512]{0:T(512)(128)(2,1)S(1)} fusion(bf16[256]{0:T(256)(128)(2,1)S(1)} %reshape.242, s32[1024]{0:T(1024)S(1)} %pad_clamp_fusion.5), kind=kCustom, calls=%fused_computation.clone | custom fusion | bytes 4096 | tf_op jit(solution)/shard_map/jit(_take)/gather | solution.py:34
  25.8 6.3 %all-to-all-start = ((bf16[8,1,128]{2,1,0:T(2,128)(2,1)}), bf16[8,1,128]{2,1,0:T(2,128)(2,1)S(1)}, u32[]{:S(2)}, u32[]{:S(2)}) async-start(bf16[8,1,128]{2,1,0:T(2,128)(2,1)} %copy.43), calls=%async_computation | async-start | bytes 8192 | tf_op jit(solution)/shard_map/all_to_all | solution.py:128
  32.2 2.8 gather_fusion.3
  35.0 2.8 gather_fusion.5
  37.8 2.1 gather_fusion.2
  39.9 2.8 gather_fusion.4
  47.5 15.8 %all-to-all-start.2 = ((bf16[8,128,1024]{2,1,0:T(8,128)(2,1)}), bf16[8,128,1024]{2,1,0:T(8,128)(2,1)}, u32[]{:S(2)}, u32[]{:S(2)}) async-start(bf16[8,128,1024]{2,1,0:T(8,128)(2,1)} %pad_maximum_fusion.2), calls=%async_computation.2 | async-start | bytes 4194304 | tf_op jit(solution)/shard_map/all_to_all | solution.py:126
  64.4 2.8 copy.44
  67.2 4.1 %pad_maximum_fusion.1 = bf16[8,128,1024]{1,2,0:T(8,128)(2,1)} fusion(bf16[8,64,1024]{1,2,0:T(8,128)(2,1)S(1)} %copy.45, bf16[8,64,1024]{1,2,0:T(8,128)(2,1)} %copy.44), kind=kLoop, calls=%fused_computation.26 | loop fusion | flops 4194304 | bytes 4194304 | tf_op jit(solution)/shard_map/concatenate | solution.py:122
  71.3 41.2 %all-to-all-done.2 = bf16[8,128,1024]{2,1,0:T(8,128)(2,1)} async-done(((bf16[8,128,1024]{2,1,0:T(8,128)(2,1)}), bf16[8,128,1024]{2,1,0:T(8,128)(2,1)}, u32[]{:S(2)}, u32[]{:S(2)}) %all-to-all-start.2) | async-done | bytes 2097184 | tf_op jit(solution)/shard_map/all_to_all | solution.py:126
  112.5 4.4 %all-to-all-start.1 = ((bf16[8,128,1024]{1,2,0:T(8,128)(2,1)}), bf16[8,128,1024]{1,2,0:T(8,128)(2,1)}, u32[]{:S(2)}, u32[]{:S(2)}) async-start(bf16[8,128,1024]{1,2,0:T(8,128)(2,1)} %pad_maximum_fusion.1), calls=%async_computation.1 | async-start | bytes 4194304 | tf_op jit(solution)/shard_map/all_to_all | solution.py:127
  116.9 5.5 %fusion.7 = f32[1024,768]{1,0:T(8,128)} fusion(bf16[1024,1024]{1,0:T(8,128)(2,1)} %bitcast.16, bf16[1,3,1024,768]{3,2,1,0:T(8,128)(2,1)} %param.17), kind=kOutput, calls=%fused_computation.34 | convolution fusion | flops 1610612736 | bytes 6815744 | tf_op jit(solution)/shard_map/dot_general | solution.py:49
  122.4 43.5 %all-to-all-done.1 = bf16[8,128,1024]{1,2,0:T(8,128)(2,1)} async-done(((bf16[8,128,1024]{1,2,0:T(8,128)(2,1)}), bf16[8,128,1024]{1,2,0:T(8,128)(2,1)}, u32[]{:S(2)}, u32[]{:S(2)}) %all-to-all-start.1) | async-done | bytes 2097184 | tf_op jit(solution)/shard_map/all_to_all | solution.py:127
  165.9 2.9 copy.46
  169.2 4.9 %fusion.13 = f32[1024,768]{1,0:T(8,128)} fusion(bf16[1024,1024]{1,0:T(8,128)(2,1)S(1)} %bitcast.93, bf16[1,3,1024,768]{3,2,1,0:T(8,128)(2,1)} %param.17), kind=kOutput, calls=%fused_computation.40 | convolution fusion | flops 1610612736 | bytes 6815744 | tf_op jit(solution)/shard_map/dot_general | solution.py:59
  174.0 3.1 copy.52
  177.2 6.6 %multiply_convert_fusion.2 = (bf16[1024,768]{1,0:T(8,128)(2,1)S(1)}, bf16[1024,768]{1,0:T(8,128)(2,1)S(1)}, bf16[1024,768]{1,0:T(8,128)(2,1)S(1)}) fusion(f32[1024,768]{1,0:T(8,128)} %fusion.7, f32[1024,768]{1,0:T(8,128)} %fusion.13, bf16[1024,1024]{1,0:T(8,128)(2,1)} %bitcast.16, bf16[1,3,1024,768]{3,2,1,0:T(8,128)(2,1)} %param.17), kind=kOutput, calls=%fused_computation.19 | convolution fusion | flops 1622409216 | bytes 14680064 | tf_op jit(solution)/shard_map/dot_general | solution.py:50
  183.8 4.6 %fusion.17 = bf16[1,1024,768]{2,1,0:T(8,128)(2,1)S(1)} fusion(bf16[1024,1024]{1,0:T(8,128)(2,1)} %bitcast.16, bf16[1024,768]{1,0:T(8,128)(2,1)S(1)} %get-tuple-element.24), kind=kOutput, calls=%fused_computation.44 | convolution fusion | flops 1611399168 | bytes 5242880 | tf_op jit(solution)/shard_map/dot_general | solution.py:73
  188.4 3.6 %fusion.16 = bf16[1,1024,768]{2,1,0:T(8,128)(2,1)S(1)} fusion(bf16[1024,1024]{1,0:T(8,128)(2,1)} %bitcast.16, bf16[1024,768]{1,0:T(8,128)(2,1)S(1)} %get-tuple-element.23), kind=kOutput, calls=%fused_computation.43 | convolution fusion | flops 1611399168 | bytes 5242880 | tf_op jit(solution)/shard_map/dot_general | solution.py:70
  193.9 2.4 pad_maximum_fusion
  197.7 4.5 %multiply_reduce_fusion = bf16[1024]{0:T(1024)(128)(2,1)S(1)} fusion(f32[1024,1024]{0,1:T(8,128)} %copy.52, bf16[1024,768]{1,0:T(8,128)(2,1)S(1)} %copy-done.6, bf16[1,3,1024,768]{3,2,1,0:T(8,128)(2,1)} %param.17), kind=kOutput, calls=%fused_computation.16 | convolution fusion | flops 1612708864 | bytes 7342080 | tf_op jit(solution)/shard_map/dot_general | solution.py:54
  202.8 3.5 %all-to-all-start.4 = ((bf16[1,8,128]{2,0,1:T(2,128)(2,1)}), bf16[1,8,128]{2,0,1:T(2,128)(2,1)S(1)}, u32[]{:S(2)}, u32[]{:S(2)}) async-start(bf16[1,8,128]{2,0,1:T(2,128)(2,1)} %copy.49), calls=%async_computation.4 | async-start | bytes 8192 | tf_op jit(solution)/shard_map/all_to_all | solution.py:150
  206.3 3.7 %fusion.5 = f32[1024,1024]{1,0:T(8,128)S(1)} fusion(bf16[1024,768]{1,0:T(8,128)(2,1)} %copy-done.4, bf16[1,3,1024,768]{3,2,1,0:T(8,128)(2,1)} %param.17), kind=kOutput, calls=%fused_computation.32 | convolution fusion | flops 1610612736 | bytes 7340032 | tf_op jit(solution)/shard_map/dot_general | solution.py:65
  210.0 3.2 %fusion.1 = bf16[1,1024,1024]{2,1,0:T(8,128)(2,1)S(1)} fusion(f32[1024,1024]{1,0:T(8,128)S(1)} %fusion.5, bf16[1024,768]{1,0:T(8,128)(2,1)S(1)} %get-tuple-element.24, bf16[1,3,1024,768]{3,2,1,0:T(8,128)(2,1)} %param.17), kind=kOutput, calls=%fused_computation.24 | convolution fusion | flops 1612709888 | bytes 9437184 | tf_op jit(solution)/shard_map/dot_general | solution.py:66
  213.3 5.3 %copy.58 = bf16[1,1024,1024]{2,0,1:T(2,128)(2,1)} copy(bf16[1,1024,1024]{2,1,0:T(8,128)(2,1)S(1)} %fusion.1) | data formatting | bytes 4194304 | tf_op jit(solution)/shard_map/stack | solution.py:145
  219.0 12.8 %reduce.6 = bf16[1024,1024]{1,0:T(8,128)(2,1)S(1)} reduce(bf16[1024,1,1024]{2,1,0:T(2,128)(2,1)} %bitcast.86, bf16[]{:T(256)} %broadcast.213), dimensions={1}, to_apply=%bitcast.81.reduce_sub_computation | reduce | bytes 4194306
  231.8 3.8 %reshape.416 = bf16[8,2,65536]{2,1,0:T(2,128)(2,1)} reshape(bf16[1024,1024]{1,0:T(8,128)(2,1)S(1)} %reduce.6) | data formatting | bytes 4194304
  235.7 5.1 %all-to-all-start.3 = ((bf16[8,2,65536]{2,1,0:T(2,128)(2,1)}), bf16[8,2,65536]{2,1,0:T(2,128)(2,1)S(1)}, u32[]{:S(2)}, u32[]{:S(2)}) async-start(bf16[8,2,65536]{2,1,0:T(2,128)(2,1)} %reshape.416), calls=%async_computation.3 | async-start | bytes 4194304 | tf_op jit(solution)/shard_map/all_to_all | solution.py:149
  246.1 43.7 %all-to-all-done.3 = bf16[8,2,65536]{2,1,0:T(2,128)(2,1)S(1)} async-done(((bf16[8,2,65536]{2,1,0:T(2,128)(2,1)}), bf16[8,2,65536]{2,1,0:T(2,128)(2,1)S(1)}, u32[]{:S(2)}, u32[]{:S(2)}) %all-to-all-start.3) | async-done | bytes 2097184 | tf_op jit(solution)/shard_map/all_to_all | solution.py:149
  289.8 4.4 %reshape.417 = bf16[1024,1,1024]{2,1,0:T(2,128)(2,1)} reshape(bf16[8,2,65536]{2,1,0:T(2,128)(2,1)S(1)} %all-to-all-done.3) | data formatting | bytes 4194304
  294.2 3.0 copy.53
  (108 shorter events, 34.5 us)
Async XLA Ops:
  7.2 25.0 %copy-start.2 = (bf16[256,1024]{1,0:T(8,128)(2,1)S(1)}, bf16[256,1024]{1,0:T(8,128)(2,1)}, u32[]{:S(2)}) copy-start(bf16[256,1024]{1,0:T(8,128)(2,1)} %param.14) | copy-start | bytes 1572868
  7.2 25.0 %copy-start.3 = (bf16[256,1024]{1,0:T(8,128)(2,1)S(1)}, bf16[256,1024]{1,0:T(8,128)(2,1)}, u32[]{:S(2)}) copy-start(bf16[256,1024]{1,0:T(8,128)(2,1)} %param.13) | copy-start | bytes 1572868
  25.8 21.7 %all-to-all-start = ((bf16[8,1,128]{2,1,0:T(2,128)(2,1)}), bf16[8,1,128]{2,1,0:T(2,128)(2,1)S(1)}, u32[]{:S(2)}, u32[]{:S(2)}) async-start(bf16[8,1,128]{2,1,0:T(2,128)(2,1)} %copy.43), calls=%async_computation | async-start | bytes 8192 | tf_op jit(solution)/shard_map/all_to_all | solution.py:128
  42.7 2.0 copy-start
  47.5 65.0 %all-to-all-start.2 = ((bf16[8,128,1024]{2,1,0:T(8,128)(2,1)}), bf16[8,128,1024]{2,1,0:T(8,128)(2,1)}, u32[]{:S(2)}, u32[]{:S(2)}) async-start(bf16[8,128,1024]{2,1,0:T(8,128)(2,1)} %pad_maximum_fusion.2), calls=%async_computation.2 | async-start | bytes 4194304 | tf_op jit(solution)/shard_map/all_to_all | solution.py:126
  112.5 53.4 %all-to-all-start.1 = ((bf16[8,128,1024]{1,2,0:T(8,128)(2,1)}), bf16[8,128,1024]{1,2,0:T(8,128)(2,1)}, u32[]{:S(2)}, u32[]{:S(2)}) async-start(bf16[8,128,1024]{1,2,0:T(8,128)(2,1)} %pad_maximum_fusion.1), calls=%async_computation.1 | async-start | bytes 4194304 | tf_op jit(solution)/shard_map/all_to_all | solution.py:127
  116.8 187.3 %reduce-scatter.2.cloned.1.call-start = ((), (), s32[]{:S(2)}) async-start(), calls=%async_computation.6 | async-start | bytes 5898240 | tf_op jit(solution)/shard_map/reduce_scatter | solution.py:141
  183.8 4.6 %copy-start.4 = (bf16[1024,768]{1,0:T(8,128)(2,1)}, bf16[1024,768]{1,0:T(8,128)(2,1)S(1)}, u32[]{:S(2)}) copy-start(bf16[1024,768]{1,0:T(8,128)(2,1)S(1)} %get-tuple-element.23) | copy-start | bytes 4718596
  183.8 8.3 %copy-start.5 = (bf16[1024,768]{1,0:T(8,128)(2,1)}, bf16[1024,768]{1,0:T(8,128)(2,1)S(1)}, u32[]{:S(2)}) copy-start(bf16[1024,768]{1,0:T(8,128)(2,1)S(1)} %get-tuple-element.22) | copy-start | bytes 4718596
  188.4 3.7 %copy-start.1 = (f32[1024,1024]{0,1:T(8,128)S(1)}, f32[1024,1024]{0,1:T(8,128)}, u32[]{:S(2)}) copy-start(f32[1024,1024]{0,1:T(8,128)} %copy.52) | copy-start | bytes 12582916
  196.3 1.4 copy-start.6
  202.8 32.8 %all-to-all-start.4 = ((bf16[1,8,128]{2,0,1:T(2,128)(2,1)}), bf16[1,8,128]{2,0,1:T(2,128)(2,1)S(1)}, u32[]{:S(2)}, u32[]{:S(2)}) async-start(bf16[1,8,128]{2,0,1:T(2,128)(2,1)} %copy.49), calls=%async_computation.4 | async-start | bytes 8192 | tf_op jit(solution)/shard_map/all_to_all | solution.py:150
  235.7 54.2 %all-to-all-start.3 = ((bf16[8,2,65536]{2,1,0:T(2,128)(2,1)}), bf16[8,2,65536]{2,1,0:T(2,128)(2,1)S(1)}, u32[]{:S(2)}, u32[]{:S(2)}) async-start(bf16[8,2,65536]{2,1,0:T(2,128)(2,1)} %reshape.416), calls=%async_computation.3 | async-start | bytes 4194304 | tf_op jit(solution)/shard_map/all_to_all | solution.py:149
Sparse Core Ops, SparseCore 0:
  196.4 55.9 reduce-scatter.1
where the time goes:
time: 315 us; the launch traced here: 311 us
  waiting for transfers between devices  128 us (41%)
  local copies, waits for them, and re-layouts  62.9 us (20%)
  matrix products  38.5 us (12%)
  starting transfers between devices  35.2 us (11%)
  other arithmetic  31.4 us (10%)
  between operations  15 us (5%)
    all_to_all x1, waiting for transfers between devices, on_device(): lax.all_to_all(stacked[0][0], 'expert', split_axis=1, concat_axis=0, tile...  43.7 us
    all_to_all x1, waiting for transfers between devices, on_device(): lax.all_to_all(joined[1], 'expert', split_axis=0, concat_axis=1, tiled=True)  43.5 us
    all_to_all x1, waiting for transfers between devices, on_device(): lax.all_to_all(joined[0], 'expert', split_axis=0, concat_axis=1, tiled=True)  41.2 us
    all_to_all x1, starting transfers between devices, on_device(): lax.all_to_all(joined[0], 'expert', split_axis=0, concat_axis=1, tiled=True)  15.8 us
    unnamed x19, local copies, waits for them, and re-layouts  13.2 us
    unnamed x1, other arithmetic  12.8 us
    gather x2, local copies, waits for them, and re-layouts, pack_rows(): jnp.take(gate_vals.reshape(-1), slot_route)  6.71 us
    dot_general x1, matrix products, expert_backward(): pre_up = jnp.dot(rows_in, w_up, preferred_element_type=jnp.float32)  6.63 us
  transfers between devices with their start and end apart: 6, of which 3 were waited for; matrix products, arithmetic and copies ran while one was open for 27% of the time, Pallas kernels for 0%

commit v1 on v0

v1 whole, which is shorter than its diff:
```python
import functools

import jax
import jax.numpy as jnp
from jax import lax
from jax.experimental import pallas as pl
from jax.experimental.pallas import tpu as pltpu
from jax.sharding import PartitionSpec as P

MICRO = 2
CORES = 2
META = 16
LAST = (((1,), (1,)), ((), ()))
FIRST = (((0,), (0,)), ((), ()))
F32 = jnp.float32
BF16 = jnp.bfloat16


def dot(lhs, rhs, dims=(((1,), (0,)), ((), ()))):
    return lax.dot_general(lhs, rhs, dims, preferred_element_type=F32)


def slot_kernel(choices, batch, capacity, middle, *refs):
    inputs = refs[: 4 * choices]
    w_hbm = refs[4 * choices]
    xr_out, q_out, h_out, da_out, db_out, dxa_out, dxb_out = refs[4 * choices + 1 : 4 * choices + 8]
    xbuf, cbuf, wbuf, sems = refs[4 * choices + 8 :]
    count = MICRO * batch
    me = lax.axis_index("expert")

    def copies(choice):
        xa, xb, ca, cb = inputs[4 * choice : 4 * choice + 4]
        return [
            pltpu.make_async_copy(xa, xbuf.at[0], sems.at[0]),
            pltpu.make_async_copy(xb, xbuf.at[1], sems.at[1]),
            pltpu.make_async_copy(ca, cbuf.at[0], sems.at[2]),
            pltpu.make_async_copy(cb, cbuf.at[1], sems.at[3]),
        ]

    if choices == 1:
        for copy in copies(0):
            copy.start()
    else:
        place = me // CORES
        inner = (place >= middle[0]) & (place <= middle[1])

        @pl.when(inner)
        def _():
            for copy in copies(0):
                copy.start()

        @pl.when(jnp.logical_not(inner))
        def _():
            for copy in copies(1):
                copy.start()

    weight_copies = [
        pltpu.make_async_copy(w_hbm.at[0, i], wbuf.at[i], sems.at[4 + i]) for i in range(3)
    ]
    for copy in weight_copies:
        copy.start()
    waits = copies(0)
    waits[0].wait()
    waits[1].wait()

    mine = (me + 1).astype(F32)
    upper = (
        lax.broadcasted_iota(jnp.int32, (batch, batch), 0)
        < lax.broadcasted_iota(jnp.int32, (batch, batch), 1)
    ).astype(BF16)
    slot_of = lax.broadcasted_iota(jnp.int32, (capacity, batch), 0).astype(F32)
    parts = []
    for half in range(CORES):
        for micro in range(MICRO):
            rows = slice(micro * batch, (micro + 1) * batch)
            meta = xbuf[half, count : count + META, rows].astype(F32)
            first = meta[0:1] == mine
            second = meta[1:2] == mine
            chosen = jnp.where(first | second, 1.0, 0.0)
            rank = dot(jnp.broadcast_to(chosen, (8, batch)).astype(BF16), upper)[0:1]
            onehot = jnp.where(rank == slot_of, chosen, 0.0)
            gate = jnp.sum(
                onehot * (jnp.where(first, meta[2:3], 0.0) + jnp.where(second, meta[3:4], 0.0)),
                axis=1,
                keepdims=True,
            )
            place_at = len(parts) * capacity
            xr_out[place_at : place_at + capacity, :] = dot(
                onehot.astype(BF16), xbuf[half, rows, :]
            ).astype(BF16)
            parts.append((half, rows, onehot, gate, first, second))
    xr = xr_out[...]
    for copy in weight_copies:
        copy.wait()
    pre_gate = dot(xr, wbuf[0])
    pre_up = dot(xr, wbuf[1])
    sig = jax.nn.sigmoid(pre_gate)
    activated = pre_gate * sig
    hidden = (activated * pre_up).astype(BF16)
    h_out[...] = hidden
    output = dot(hidden, wbuf[2], LAST)
    waits[2].wait()
    waits[3].wait()
    gate_grads = []
    for number, (half, rows, onehot, gate, first, second) in enumerate(parts):
        places = slice(number * capacity, (number + 1) * capacity)
        cot = dot(onehot.astype(BF16), cbuf[half, rows, :])
        q_out[places, :] = (gate * cot).astype(BF16)
        gate_grads.append(jnp.sum(output[places] * cot, axis=1, keepdims=True))
    hidden_grad = dot(q_out[...], wbuf[2])
    da = (hidden_grad * pre_up * sig * (1.0 + pre_gate * (1.0 - sig))).astype(BF16)
    db = (hidden_grad * activated).astype(BF16)
    da_out[...] = da
    db_out[...] = db
    dx = (dot(da, wbuf[0], LAST) + dot(db, wbuf[1], LAST)).astype(BF16)
    line = lax.broadcasted_iota(jnp.int32, (META, batch), 0)
    outs = (dxa_out, dxb_out)
    for out in outs:
        out[count : count + META, :] = jnp.zeros((META, out.shape[1]), BF16)
    for number, (half, rows, onehot, gate, first, second) in enumerate(parts):
        places = slice(number * capacity, (number + 1) * capacity)
        outs[half][rows, :] = dot(onehot.astype(BF16), dx[places], FIRST).astype(BF16)
        spread = jnp.sum(onehot * gate_grads[number], axis=0, keepdims=True)
        values = jnp.where(line == 0, jnp.where(first, spread, 0.0), 0.0) + jnp.where(
            line == 1, jnp.where(second, spread, 0.0), 0.0
        )
        outs[half][count : count + META, rows] = values.astype(BF16)


def run_slot(alternatives, weights, batch, capacity, middle):
    choices = len(alternatives)
    rows, width = alternatives[0][0].shape
    count = MICRO * batch
    hidden_width = weights.shape[-1]
    slots = CORES * MICRO * capacity
    operands = [array for group in alternatives for array in group]
    shape = jax.ShapeDtypeStruct
    return pl.pallas_call(
        functools.partial(slot_kernel, choices, batch, capacity, middle),
        out_shape=[
            shape((slots, width), BF16),
            shape((slots, width), BF16),
            shape((slots, hidden_width), BF16),
            shape((slots, hidden_width), BF16),
            shape((slots, hidden_width), BF16),
            shape((rows, width), BF16),
            shape((rows, width), BF16),
        ],
        in_specs=[pl.BlockSpec(memory_space=pl.ANY)] * (len(operands) + 1),
        out_specs=[pl.BlockSpec(memory_space=pltpu.VMEM)] * 7,
        scratch_shapes=[
            pltpu.VMEM((CORES, rows, width), BF16),
            pltpu.VMEM((CORES, count, width), BF16),
            pltpu.VMEM(weights.shape[1:], BF16),
            pltpu.SemaphoreType.DMA((7,)),
        ],
        compiler_params=pltpu.CompilerParams(vmem_limit_bytes=40 * 1024 * 1024),
        cost_estimate=pl.CostEstimate(
            flops=18 * slots * width * hidden_width,
            bytes_accessed=2 * (weights.size + 6 * rows * width),
            transcendentals=slots * hidden_width,
        ),
        name="expert_block",
    )(*operands, weights)


def weight_kernel(pieces, *refs):
    lefts = refs[:pieces]
    rights = refs[pieces : 2 * pieces]
    a_send, a_keep, b_send, b_keep = refs[2 * pieces :]
    here = lax.axis_index("dp")
    quarter = lefts[0].shape[1] // 4
    half = rights[0].shape[1] // 2

    def block(place):
        at = pl.multiple_of((here ^ place) * quarter, quarter)
        total = None
        for left, right in zip(lefts, rights):
            term = dot(left[:, pl.ds(at, quarter)], right[...], FIRST)
            total = term if total is None else total + term
        return total.astype(BF16)

    value = block(3)
    a_send[0] = value[:, :half]
    b_send[0] = value[:, half:]
    value = block(1)
    a_send[1] = value[:, :half]
    b_keep[0] = value[:, half:]
    value = block(2)
    a_keep[0] = value[:, :half]
    b_send[1] = value[:, half:]
    value = block(0)
    a_keep[1] = value[:, :half]
    b_keep[1] = value[:, half:]


def run_weight(lefts, rights):
    width = lefts[0].shape[1]
    hidden_width = rights[0].shape[1]
    rows = sum(left.shape[0] for left in lefts)
    piece = jax.ShapeDtypeStruct((2, width // 4, hidden_width // 2), BF16)
    return pl.pallas_call(
        functools.partial(weight_kernel, len(lefts)),
        out_shape=[piece] * 4,
        in_specs=[pl.BlockSpec(memory_space=pltpu.VMEM)] * (2 * len(lefts)),
        out_specs=[pl.BlockSpec(memory_space=pltpu.VMEM)] * 4,
        compiler_params=pltpu.CompilerParams(vmem_limit_bytes=40 * 1024 * 1024),
        cost_estimate=pl.CostEstimate(
            flops=2 * rows * width * hidden_width,
            bytes_accessed=2 * (rows * (width + hidden_width) + width * hidden_width),
            transcendentals=0,
        ),
        name="weight_block",
    )(*lefts, *rights)


def add(*values):
    total = values[0].astype(F32)
    for value in values[1:]:
        total = total + value.astype(F32)
    return total.astype(BF16)


def on_device(tokens, cotangent, gates, expert_ids, expert_weights):
    devices = lax.axis_size("expert")
    chips = devices // CORES
    count, width = tokens.shape
    batch = count // MICRO
    capacity = 4 * batch // devices
    routing = jnp.concatenate([(expert_ids + 1).astype(BF16).T, gates.T], axis=0)
    routing = jnp.pad(routing, ((0, META - 4), (0, width - count)))
    own = (jnp.concatenate([tokens, routing], axis=0), cotangent)

    def move(value, pairs):
        full = [(a * CORES + k, b * CORES + k) for a, b in pairs for k in range(CORES)]
        return lax.ppermute(value, "expert", full)

    def swap(value):
        return lax.ppermute(value, "expert", [(i, i ^ 1) for i in range(devices)])

    def send(pair, pairs):
        return tuple(move(value, pairs) for value in pair)

    def both(pair):
        return (pair[0], swap(pair[0]), pair[1], swap(pair[1]))

    def compute(*alternatives):
        result = run_slot(
            [both(pair) for pair in alternatives], expert_weights, batch, capacity, (1, chips - 2)
        )
        return result[:5], (result[5], result[6])

    def joined(grads):
        return (grads[0], swap(grads[1]))

    ahead = [(z, (z + 1) % chips) for z in range(chips)]
    behind = [(b, a) for a, b in ahead]
    if chips == 4:
        outer = [(0, 1), (1, 0), (2, 3), (3, 2)]
        inner = [(1, 2), (2, 1)]
        to_ends = [(1, 0), (2, 3)]
        from_ends = [(0, 1), (3, 2)]
        second = send(own, inner)
        first = send(own, outer)
        third = send(second, to_ends)
        fourth = send(first, inner)
        fifth = send(fourth, to_ends)
        kept = []
        rows, own_grads = compute(own)
        kept.append(rows)
        rows, grads = compute(first)
        kept.append(rows)
        first_sum = joined(grads)
        rows, grads = compute(second, third)
        kept.append(rows)
        third_sum = joined(grads)
        rows, grads = compute(fourth, fifth)
        kept.append(rows)
        fourth_sum = joined(grads)
        own_sum = joined(own_grads)
        third_back = add(*third_sum)
        third_back = add(*third_sum, move(third_back, from_ends))
        third_back = move(third_back, inner)
        back = add(*fourth_sum)
        back = add(*fourth_sum, move(back, from_ends))
        back = add(*first_sum, move(back, inner))
        back = move(back, outer)
        total = add(*own_sum, third_back, back)
    else:
        kept = []
        rows, own_grads = compute(own)
        kept.append(rows)
        total = [*joined(own_grads)]
        reach = chips // 2
        for forth, back, steps in ((ahead, behind, reach), (behind, ahead, chips - 1 - reach)):
            current, sums = own, []
            for _ in range(steps):
                current = send(current, forth)
                rows, grads = compute(current)
                kept.append(rows)
                sums.append(joined(grads))
            value = None
            for pair in reversed(sums):
                value = move(add(*pair) if value is None else add(*pair, value), back)
            if value is not None:
                total.append(value)
        total = add(*total)
    tokens_grad = total[:count]
    gates_grad = total[count : count + 2, :count].T

    xr, q, h, da, db = zip(*kept)
    if lax.axis_size("dp") == 4:

        def across(value, bit):
            return lax.ppermute(value, "dp", [(i, i ^ bit) for i in range(4)])

        pieces = []
        for lefts, rights in ((xr, da), (xr, db), (q, h)):
            a_send, a_keep, b_send, b_keep = run_weight(lefts, rights)
            pieces.append((a_keep, across(a_send, 1), b_keep, across(b_send, 2)))
        ends = []
        for a_keep, a_came, b_keep, b_came in pieces:
            a_came = (add(a_keep[1], a_came[1]), across(add(a_keep[0], a_came[0]), 2))
            b_came = (add(b_keep[1], b_came[1]), across(add(b_keep[0], b_came[0]), 1))
            ends.append(jnp.concatenate([add(*a_came), add(*b_came)], axis=1))
        weights_grad = jnp.stack(ends)[None]
    else:
        whole = [jnp.concatenate(value, axis=0) for value in (xr, q, h, da, db)]
        partial = jnp.stack(
            [
                dot(whole[0], whole[3], FIRST),
                dot(whole[0], whole[4], FIRST),
                dot(whole[1], whole[2], FIRST),
            ]
        ).astype(BF16)
        weights_grad = lax.psum_scatter(
            partial[None], "dp", scatter_dimension=2, tiled=True
        )
    return tokens_grad, gates_grad, weights_grad


def solution(mesh):
    placed = (
        P(("dp", "expert"), None),
        P(("dp", "expert"), None),
        P(("dp", "expert"), None),
        P(("dp", "expert"), None),
        P("expert", None, None, None),
    )
    return jax.shard_map(
        on_device,
        mesh=mesh,
        in_specs=placed,
        out_specs=(
            P(("dp", "expert"), None),
            P(("dp", "expert"), None),
            P("expert", None, "dp", None),
        ),
        check_vma=False,
    )
```

time: 315 us -> 186 us (0.59); the launches traced: 311 us -> 186 us
  local copies, waits for them, and re-layouts: 62.9 us -> 9.17 us
  waiting for transfers between devices: 128 us -> 82.2 us
  matrix products: 38.5 us -> 0 us
  Pallas kernels: 0 us -> 28.1 us
  other arithmetic: 31.4 us -> 9.26 us
  starting transfers between devices: 35.2 us -> 55.6 us
  between operations: 15 us -> 1.34 us
    all_to_all x5 -> x0, waiting for transfers between devices: 128 us -> none  [the longest x1 43.7 us: on_device(): lax.all_to_all(stacked[0][0], 'expert', split_axis=1, concat_axis=0, tile...]
    ppermute x0 -> x43, waiting for transfers between devices: none -> 82.2 us  [the longest x15 61.2 us: move(): return lax.ppermute(value, 'expert', full)]
    ppermute x0 -> x43, starting transfers between devices: none -> 55.6 us  [the longest x15 36.4 us: move(): return lax.ppermute(value, 'expert', full)]
    dot_general x9 -> x0, matrix products: 38.5 us -> none  [the longest x1 6.63 us: expert_backward(): pre_up = jnp.dot(rows_in, w_up, preferred_element_type=jnp.float32)]
    all_to_all x5 -> x0, starting transfers between devices: 35.1 us -> none  [the longest x1 15.8 us: on_device(): lax.all_to_all(joined[0], 'expert', split_axis=0, concat_axis=1, tiled=True)]
    pallas_call x0 -> x7, Pallas kernels: none -> 28.1 us  [the longest x4 22.5 us: run_slot(): pl.pallas_call(functools.partial(slot_kernel, choices, batch, capacity, m...]
    gather x10 -> x0, local copies, waits for them, and re-layouts: 23.3 us -> none  [the longest x2 6.71 us: pack_rows(): jnp.take(gate_vals.reshape(-1), slot_route)]
    unnamed x1, other arithmetic: 12.8 us -> 0.01 us
  transfers between devices with their start and end apart: 6 -> 43, of which waited for: 3 -> 14; matrix products, arithmetic and copies ran while one was open for 27% -> 5% of each run, Pallas kernels for 0% -> 15%
where the time goes in v1:
time: 186 us
  waiting for transfers between devices  82.2 us (44%)
  starting transfers between devices  55.6 us (30%)
  Pallas kernels  28.1 us (15%)
  other arithmetic  9.26 us (5%)
  local copies, waits for them, and re-layouts  9.17 us (5%)
    ppermute x15, waiting for transfers between devices, move(): return lax.ppermute(value, 'expert', full)  61.2 us
    ppermute x15, starting transfers between devices, move(): return lax.ppermute(value, 'expert', full)  36.4 us
    pallas_call x4, Pallas kernels, run_slot(): pl.pallas_call(functools.partial(slot_kernel, choices, batch, capacity, m...  22.5 us
    ppermute x12, waiting for transfers between devices, across(): return lax.ppermute(value, 'dp', [(i, i ^ bit) for i in range(4)])  21 us
    ppermute x12, starting transfers between devices, across(): return lax.ppermute(value, 'dp', [(i, i ^ bit) for i in range(4)])  15.7 us
    unnamed x60, local copies, waits for them, and re-layouts  7.78 us
    pallas_call x3, Pallas kernels, run_weight(): pl.pallas_call(functools.partial(weight_kernel, len(lefts)), out_shape=[p...  5.64 us
    convert_element_type x18, other arithmetic, add(): return total.astype(BF16)  5.57 us
  transfers between devices with their start and end apart: 43, of which 14 were waited for; matrix products, arithmetic and copies ran while one was open for 5% of the time, Pallas kernels for 15%

profile of v1, /device:TPU:0, one launch (start us, length us, event | category | flops | bytes accessed | tf_op | source)
XLA Modules:
  0.0 185.7 jit_solution(3799257829836114594)
XLA Ops:
  0.6 3.1 %collective-permute-start.16 = (bf16[256,1024]{1,0:T(8,128)(2,1)}, bf16[256,1024]{1,0:T(8,128)(2,1)S(1)}, u32[]{:S(2)}, u32[]{:S(2)}) collective-permute-start(bf16[256,1024]{1,0:T(8,128)(2,1)} %refs_2_.1), channel_id=1, source_target_pairs={{0,2},{1,3},{2,0},{3,1},{4,6},{5,7},{6,4},{7,5},{8,10},{9,11},{10,... | collective-permute-start | bytes 1572872 | tf_op jit(solution)/shard_map/ppermute | solution.py:236
  7.0 4.4 %collective-permute-start.14 = (bf16[272,1024]{1,0:T(8,128)(2,1)S(1)}, bf16[272,1024]{1,0:T(8,128)(2,1)S(1)}, u32[]{:S(2)}, u32[]{:S(2)}) collective-permute-start(bf16[272,1024]{1,0:T(8,128)(2,1)S(1)} %pad_maximum_fusion.refs_0_), channel_id=1, source_target_pairs={{0,2},{1,3},{2,0},{3,1},{4,6},{5,7},{6,4},{7,5},{8,10},{9,11},{10,... | collective-permute-start | bytes 1671176 | tf_op jit(solution)/shard_map/ppermute | solution.py:236
  12.1 4.6 %collective-permute-done.16.refs_2_ = bf16[256,1024]{1,0:T(8,128)(2,1)S(1)} collective-permute-done((bf16[256,1024]{1,0:T(8,128)(2,1)}, bf16[256,1024]{1,0:T(8,128)(2,1)S(1)}, u32[]{:S(2)}, u32[]{:S(2)}) %collective-permute-start.16) | collective-permute-done | bytes 524320 | tf_op jit(solution)/shard_map/ppermute | solution.py:236
  18.0 9.8 %collective-permute-done.14.refs_0_ = bf16[272,1024]{1,0:T(8,128)(2,1)S(1)} collective-permute-done((bf16[272,1024]{1,0:T(8,128)(2,1)S(1)}, bf16[272,1024]{1,0:T(8,128)(2,1)S(1)}, u32[]{:S(2)}, u32[]{:S(2)}) %collective-permute-start.14) | collective-permute-done | bytes 557088 | tf_op jit(solution)/shard_map/ppermute | solution.py:236
  33.1 13.6 %collective-permute-done.7.refs_4_ = bf16[272,1024]{1,0:T(8,128)(2,1)S(1)} collective-permute-done((bf16[272,1024]{1,0:T(8,128)(2,1)S(1)}, bf16[272,1024]{1,0:T(8,128)(2,1)S(1)}, u32[]{:S(2)}, u32[]{:S(2)}) %collective-permute-start.7) | collective-permute-done | bytes 557088 | tf_op jit(solution)/shard_map/ppermute | solution.py:236
  47.9 9.2 %collective-permute-done.9.refs_6_ = bf16[256,1024]{1,0:T(8,128)(2,1)S(1)} collective-permute-done((bf16[256,1024]{1,0:T(8,128)(2,1)S(1)}, bf16[256,1024]{1,0:T(8,128)(2,1)S(1)}, u32[]{:S(2)}, u32[]{:S(2)}) %collective-permute-start.9) | collective-permute-done | bytes 524320 | tf_op jit(solution)/shard_map/ppermute | solution.py:236
  57.7 2.3 %copy-done = bf16[1,3,1024,768]{3,2,1,0:T(8,128)(2,1)S(1)} copy-done((bf16[1,3,1024,768]{3,2,1,0:T(8,128)(2,1)S(1)}, bf16[1,3,1024,768]{3,2,1,0:T(8,128)(2,1)}, u32[]{:S(2)}) %copy-start) | copy-done | bytes 4718616
  60.0 5.5 %expert_block.4 = (bf16[256,1024]{1,0:T(8,128)(2,1)S(1)}, bf16[256,1024]{1,0:T(8,128)(2,1)S(1)}, bf16[256,768]{1,0:T(8,128)(2,1)S(1)}, bf16[256,768]{1,0:T(8,128...) custom-call(bf16[272,1024]{1,0:T(8,128)(2,1)S(1)} %pad_maximum_fusion.refs_0_, ...), custom_call_target="tpu_custom_call" | custom-call | flops 3623878656 | bytes 8060928 | tf_op jit(solution)/shard_map/expert_block/pallas_call | solution.py:138
  67.0 13.2 %collective-permute-done.25.refs_6_ = bf16[256,1024]{1,0:T(8,128)(2,1)S(1)} collective-permute-done((bf16[256,1024]{1,0:T(8,128)(2,1)S(1)}, bf16[256,1024]{1,0:T(8,128)(2,1)S(1)}, u32[]{:S(2)}, u32[]{:S(2)}) %collective-permute-start.25) | collective-permute-done | bytes 524320 | tf_op jit(solution)/shard_map/ppermute | solution.py:236
  81.2 5.7 %expert_block.5 = (bf16[256,1024]{1,0:T(8,128)(2,1)S(1)}, bf16[256,1024]{1,0:T(8,128)(2,1)S(1)}, bf16[256,768]{1,0:T(8,128)(2,1)S(1)}, bf16[256,768]{1,0:T(8,128...) custom-call(bf16[272,1024]{1,0:T(8,128)(2,1)S(1)} %collective-permute-done.3., ...), custom_call_target="tpu_custom_call" | custom-call | flops 3623878656 | bytes 8060928 | tf_op jit(solution)/shard_map/expert_block/pallas_call | solution.py:138
  89.4 5.5 %expert_block.6 = (bf16[256,1024]{1,0:T(8,128)(2,1)S(1)}, bf16[256,1024]{1,0:T(8,128)(2,1)S(1)}, bf16[256,768]{1,0:T(8,128)(2,1)S(1)}, bf16[256,768]{1,0:T(8,128...) custom-call(bf16[272,1024]{1,0:T(8,128)(2,1)S(1)} %collective-permute-done.14, ...), custom_call_target="tpu_custom_call" | custom-call | flops 3623878656 | bytes 8060928 | tf_op jit(solution)/shard_map/expert_block/pallas_call | solution.py:138
  97.2 5.8 %expert_block.7 = (bf16[256,1024]{1,0:T(8,128)(2,1)S(1)}, bf16[256,1024]{1,0:T(8,128)(2,1)S(1)}, bf16[256,768]{1,0:T(8,128)(2,1)S(1)}, bf16[256,768]{1,0:T(8,128...) custom-call(bf16[272,1024]{1,0:T(8,128)(2,1)S(1)} %collective-permute-done.19, ...), custom_call_target="tpu_custom_call" | custom-call | flops 3623878656 | bytes 8060928 | tf_op jit(solution)/shard_map/expert_block/pallas_call | solution.py:138
  103.0 1.9 %weight_block.5 = (bf16[2,256,384]{2,1,0:T(8,128)(2,1)S(1)}, bf16[2,256,384]{2,1,0:T(8,128)(2,1)S(1)}, bf16[2,256,384]{2,1,0:T(8,128)(2,1)S(1)}, bf16[2,256,384]{2,1,0:T(8,128)(2,1)S(1)}) custom-call(bf16[256,1024]{1,0:T(8,128)(2,1)S(1)} %copy-done.5, bf16[256,1024]{1,0:T(8,128)(2,1)S(1)} %copy-done.13, bf16[256,1024]{1,0:T(8,128)(2,1)S(1)} %copy-done.11, ...), custom_call_target="tpu_custom_call" | custom-call | flops 1610612736 | bytes 5242880 | tf_op jit(solution)/shard_map/weight_block/pallas_call | solution.py:202
  105.0 1.6 collective-permute-start.41
  109.3 1.6 collective-permute-start.39
  110.9 1.9 %weight_block.4 = (bf16[2,256,384]{2,1,0:T(8,128)(2,1)S(1)}, bf16[2,256,384]{2,1,0:T(8,128)(2,1)S(1)}, bf16[2,256,384]{2,1,0:T(8,128)(2,1)S(1)}, bf16[2,256,384]{2,1,0:T(8,128)(2,1)S(1)}) custom-call(bf16[256,1024]{1,0:T(8,128)(2,1)S(1)} %copy-done.3, bf16[256,1024]{1,0:T(8,128)(2,1)S(1)} %copy-done.9, bf16[256,1024]{1,0:T(8,128)(2,1)S(1)} %copy-done.7, ...), custom_call_target="tpu_custom_call" | custom-call | flops 1610612736 | bytes 5242880 | tf_op jit(solution)/shard_map/weight_block/pallas_call | solution.py:202
  112.8 1.9 %weight_block.3 = (bf16[2,256,384]{2,1,0:T(8,128)(2,1)S(1)}, bf16[2,256,384]{2,1,0:T(8,128)(2,1)S(1)}, bf16[2,256,384]{2,1,0:T(8,128)(2,1)S(1)}, bf16[2,256,384]{2,1,0:T(8,128)(2,1)S(1)}) custom-call(bf16[256,1024]{1,0:T(8,128)(2,1)S(1)} %copy-done.3, bf16[256,1024]{1,0:T(8,128)(2,1)S(1)} %copy-done.9, bf16[256,1024]{1,0:T(8,128)(2,1)S(1)} %copy-done.7, ...), custom_call_target="tpu_custom_call" | custom-call | flops 1610612736 | bytes 5242880 | tf_op jit(solution)/shard_map/weight_block/pallas_call | solution.py:202
  114.7 1.8 collective-permute-done.41
  116.5 1.5 collective-permute-start.37
  118.1 2.3 %collective-permute-done.39 = bf16[2,256,384]{2,1,0:T(8,128)(2,1)S(1)} collective-permute-done((bf16[2,256,384]{2,1,0:T(8,128)(2,1)S(1)}, bf16[2,256,384]{2,1,0:T(8,128)(2,1)S(1)}, u32[]{:S(2)}, u32[]{:S(2)}) %collective-permute-start.39) | collective-permute-done | bytes 393248 | tf_op jit(solution)/shard_map/ppermute | solution.py:315
  121.9 5.2 %collective-permute-done.37 = bf16[2,256,384]{2,1,0:T(8,128)(2,1)S(1)} collective-permute-done((bf16[2,256,384]{2,1,0:T(8,128)(2,1)S(1)}, bf16[2,256,384]{2,1,0:T(8,128)(2,1)S(1)}, u32[]{:S(2)}, u32[]{:S(2)}) %collective-permute-start.37) | collective-permute-done | bytes 393248 | tf_op jit(solution)/shard_map/ppermute | solution.py:315
  127.2 1.5 collective-permute-start.33
  128.7 1.8 collective-permute-done.35
  130.5 1.5 collective-permute-start.31
  132.1 4.8 %collective-permute-done.33 = bf16[2,256,384]{2,1,0:T(8,128)(2,1)S(1)} collective-permute-done((bf16[2,256,384]{2,1,0:T(8,128)(2,1)S(1)}, bf16[2,256,384]{2,1,0:T(8,128)(2,1)S(1)}, u32[]{:S(2)}, u32[]{:S(2)}) %collective-permute-start.33) | collective-permute-done | bytes 393248 | tf_op jit(solution)/shard_map/ppermute | solution.py:315
  137.0 2.8 %collective-permute-done.31 = bf16[2,256,384]{2,1,0:T(8,128)(2,1)S(1)} collective-permute-done((bf16[2,256,384]{2,1,0:T(8,128)(2,1)S(1)}, bf16[2,256,384]{2,1,0:T(8,128)(2,1)S(1)}, u32[]{:S(2)}, u32[]{:S(2)}) %collective-permute-start.31) | collective-permute-done | bytes 393248 | tf_op jit(solution)/shard_map/ppermute | solution.py:315
  139.8 1.5 collective-permute-start.42
  144.5 2.2 %collective-permute-done.42 = bf16[256,384]{1,0:T(8,128)(2,1)S(1)} collective-permute-done((bf16[256,384]{1,0:T(8,128)(2,1)S(1)}, bf16[256,384]{1,0:T(8,128)(2,1)S(1)}, u32[]{:S(2)}, u32[]{:S(2)}) %collective-permute-start.42) | collective-permute-done | bytes 196640 | tf_op jit(solution)/shard_map/ppermute | solution.py:315
  146.7 2.2 %collective-permute-start.28 = (bf16[272,1024]{1,0:T(8,128)(2,1)S(1)}, bf16[272,1024]{1,0:T(8,128)(2,1)S(1)}, u32[]{:S(2)}, u32[]{:S(2)}) collective-permute-start(bf16[272,1024]{1,0:T(8,128)(2,1)S(1)} %fusion.1), channel_id=1, source_target_pairs={{0,2},{1,3},{6,4},{7,5},{8,10},{9,11},{14,12},{15,13},{16,18},{17,... | collective-permute-start | bytes 1671176 | tf_op jit(solution)/shard_map/ppermute | solution.py:236
  151.4 4.6 %collective-permute-done.28 = bf16[272,1024]{1,0:T(8,128)(2,1)S(1)} collective-permute-done((bf16[272,1024]{1,0:T(8,128)(2,1)S(1)}, bf16[272,1024]{1,0:T(8,128)(2,1)S(1)}, u32[]{:S(2)}, u32[]{:S(2)}) %collective-permute-start.28) | collective-permute-done | bytes 557088 | tf_op jit(solution)/shard_map/ppermute | solution.py:236
  160.6 15.9 %collective-permute-start.30 = (bf16[272,1024]{1,0:T(8,128)(2,1)S(1)}, bf16[272,1024]{1,0:T(8,128)(2,1)S(1)}, u32[]{:S(2)}, u32[]{:S(2)}) collective-permute-start(bf16[272,1024]{1,0:T(8,128)(2,1)S(1)} %add_convert_fusion.1), channel_id=1, source_target_pairs={{0,2},{1,3},{2,0},{3,1},{4,6},{5,7},{6,4},{7,5},{8,10},{9,11},{10,... | collective-permute-start | bytes 1671176 | tf_op jit(solution)/shard_map/ppermute | solution.py:236
  177.8 6.2 %collective-permute-done.30 = bf16[272,1024]{1,0:T(8,128)(2,1)S(1)} collective-permute-done((bf16[272,1024]{1,0:T(8,128)(2,1)S(1)}, bf16[272,1024]{1,0:T(8,128)(2,1)S(1)}, u32[]{:S(2)}, u32[]{:S(2)}) %collective-permute-start.30) | collective-permute-done | bytes 557088 | tf_op jit(solution)/shard_map/ppermute | solution.py:236
  (149 shorter events, 37.0 us)
Async XLA Ops:
  0.6 16.1 %collective-permute-start.16 = (bf16[256,1024]{1,0:T(8,128)(2,1)}, bf16[256,1024]{1,0:T(8,128)(2,1)S(1)}, u32[]{:S(2)}, u32[]{:S(2)}) collective-permute-start(bf16[256,1024]{1,0:T(8,128)(2,1)} %refs_2_.1), channel_id=1, source_target_pairs={{0,2},{1,3},{2,0},{3,1},{4,6},{5,7},{6,4},{7,5},{8,10},{9,11},{10,... | collective-permute-start | bytes 1572872 | tf_op jit(solution)/shard_map/ppermute | solution.py:236
  3.7 13.0 %collective-permute-start.5 = (bf16[256,1024]{1,0:T(8,128)(2,1)}, bf16[256,1024]{1,0:T(8,128)(2,1)S(1)}, u32[]{:S(2)}, u32[]{:S(2)}) collective-permute-start(bf16[256,1024]{1,0:T(8,128)(2,1)} %refs_2_.1), channel_id=1, source_target_pairs={{2,4},{3,5},{4,2},{5,3},{10,12},{11,13},{12,10},{13,11},{18,20},{1... | collective-permute-start | bytes 1572872 | tf_op jit(solution)/shard_map/ppermute | solution.py:236
  4.4 13.0 %collective-permute-start.1 = (bf16[256,1024]{1,0:T(8,128)(2,1)}, bf16[256,1024]{1,0:T(8,128)(2,1)S(1)}, u32[]{:S(2)}, u32[]{:S(2)}) collective-permute-start(bf16[256,1024]{1,0:T(8,128)(2,1)} %refs_2_.1), channel_id=1, source_target_pairs={{0,1},{1,0},{2,3},{3,2},{4,5},{5,4},{6,7},{7,6},{8,9},{9,8},{10,11... | collective-permute-start | bytes 1572872 | tf_op jit(solution)/shard_map/ppermute | solution.py:239
  7.0 20.8 %collective-permute-start.14 = (bf16[272,1024]{1,0:T(8,128)(2,1)S(1)}, bf16[272,1024]{1,0:T(8,128)(2,1)S(1)}, u32[]{:S(2)}, u32[]{:S(2)}) collective-permute-start(bf16[272,1024]{1,0:T(8,128)(2,1)S(1)} %pad_maximum_fusion.refs_0_), channel_id=1, source_target_pairs={{0,2},{1,3},{2,0},{3,1},{4,6},{5,7},{6,4},{7,5},{8,10},{9,11},{10,... | collective-permute-start | bytes 1671176 | tf_op jit(solution)/shard_map/ppermute | solution.py:236
  11.4 17.1 %collective-permute-start.3 = (bf16[272,1024]{1,0:T(8,128)(2,1)S(1)}, bf16[272,1024]{1,0:T(8,128)(2,1)S(1)}, u32[]{:S(2)}, u32[]{:S(2)}) collective-permute-start(bf16[272,1024]{1,0:T(8,128)(2,1)S(1)} %pad_maximum_fusion.refs_0_), channel_id=1, source_target_pairs={{2,4},{3,5},{4,2},{5,3},{10,12},{11,13},{12,10},{13,11},{18,20},{1... | collective-permute-start | bytes 1671176 | tf_op jit(solution)/shard_map/ppermute | solution.py:236
  16.7 13.1 %collective-permute-start = (bf16[272,1024]{1,0:T(8,128)(2,1)S(1)}, bf16[272,1024]{1,0:T(8,128)(2,1)S(1)}, u32[]{:S(2)}, u32[]{:S(2)}) collective-permute-start(bf16[272,1024]{1,0:T(8,128)(2,1)S(1)} %pad_maximum_fusion.refs_0_), channel_id=1, source_target_pairs={{0,1},{1,0},{2,3},{3,2},{4,5},{5,4},{6,7},{7,6},{8,9},{9,8},{10,11... | collective-permute-start | bytes 1671176 | tf_op jit(solution)/shard_map/ppermute | solution.py:239
  16.7 13.2 %collective-permute-start.21 = (bf16[256,1024]{1,0:T(8,128)(2,1)S(1)}, bf16[256,1024]{1,0:T(8,128)(2,1)S(1)}, u32[]{:S(2)}, u32[]{:S(2)}) collective-permute-start(bf16[256,1024]{1,0:T(8,128)(2,1)S(1)} %collective-permute-done.16.refs_2_), channel_id=1, source_target_pairs={{2,4},{3,5},{4,2},{5,3},{10,12},{11,13},{12,10},{13,11},{18,20},{1... | collective-permute-start | bytes 1572872 | tf_op jit(solution)/shard_map/ppermute | solution.py:236
  17.4 13.8 %collective-permute-start.17 = (bf16[256,1024]{1,0:T(8,128)(2,1)S(1)}, bf16[256,1024]{1,0:T(8,128)(2,1)S(1)}, u32[]{:S(2)}, u32[]{:S(2)}) collective-permute-start(bf16[256,1024]{1,0:T(8,128)(2,1)S(1)} %collective-permute-done.16.refs_2_), channel_id=1, source_target_pairs={{0,1},{1,0},{2,3},{3,2},{4,5},{5,4},{6,7},{7,6},{8,9},{9,8},{10,11... | collective-permute-start | bytes 1572872 | tf_op jit(solution)/shard_map/ppermute | solution.py:239
  28.5 18.1 %collective-permute-start.7 = (bf16[272,1024]{1,0:T(8,128)(2,1)S(1)}, bf16[272,1024]{1,0:T(8,128)(2,1)S(1)}, u32[]{:S(2)}, u32[]{:S(2)}) collective-permute-start(bf16[272,1024]{1,0:T(8,128)(2,1)S(1)} %collective-permute-done.3.refs_0_), channel_id=1, source_target_pairs={{2,0},{3,1},{4,6},{5,7},{10,8},{11,9},{12,14},{13,15},{18,16},{19,... | collective-permute-start | bytes 1671176 | tf_op jit(solution)/shard_map/ppermute | solution.py:236
  29.8 16.8 %collective-permute-start.6 = (bf16[256,1024]{1,0:T(8,128)(2,1)S(1)}, bf16[256,1024]{1,0:T(8,128)(2,1)S(1)}, u32[]{:S(2)}, u32[]{:S(2)}) collective-permute-start(bf16[256,1024]{1,0:T(8,128)(2,1)S(1)} %collective-permute-done.5.refs_2_), channel_id=1, source_target_pairs={{0,1},{1,0},{2,3},{3,2},{4,5},{5,4},{6,7},{7,6},{8,9},{9,8},{10,11... | collective-permute-start | bytes 1572872 | tf_op jit(solution)/shard_map/ppermute | solution.py:239
  29.9 27.2 %collective-permute-start.9 = (bf16[256,1024]{1,0:T(8,128)(2,1)S(1)}, bf16[256,1024]{1,0:T(8,128)(2,1)S(1)}, u32[]{:S(2)}, u32[]{:S(2)}) collective-permute-start(bf16[256,1024]{1,0:T(8,128)(2,1)S(1)} %collective-permute-done.5.refs_2_), channel_id=1, source_target_pairs={{2,0},{3,1},{4,6},{5,7},{10,8},{11,9},{12,14},{13,15},{18,16},{19,... | collective-permute-start | bytes 1572872 | tf_op jit(solution)/shard_map/ppermute | solution.py:236
  31.2 25.9 %collective-permute-start.4 = (bf16[272,1024]{1,0:T(8,128)(2,1)S(1)}, bf16[272,1024]{1,0:T(8,128)(2,1)S(1)}, u32[]{:S(2)}, u32[]{:S(2)}) collective-permute-start(bf16[272,1024]{1,0:T(8,128)(2,1)S(1)} %collective-permute-done.3.refs_0_), channel_id=1, source_target_pairs={{0,1},{1,0},{2,3},{3,2},{4,5},{5,4},{6,7},{7,6},{8,9},{9,8},{10,11... | collective-permute-start | bytes 1671176 | tf_op jit(solution)/shard_map/ppermute | solution.py:239
  31.8 48.9 %collective-permute-start.23 = (bf16[272,1024]{1,0:T(8,128)(2,1)S(1)}, bf16[272,1024]{1,0:T(8,128)(2,1)S(1)}, u32[]{:S(2)}, u32[]{:S(2)}) collective-permute-start(bf16[272,1024]{1,0:T(8,128)(2,1)S(1)} %collective-permute-done.19.refs_0_), channel_id=1, source_target_pairs={{2,0},{3,1},{4,6},{5,7},{10,8},{11,9},{12,14},{13,15},{18,16},{19,... | collective-permute-start | bytes 1671176 | tf_op jit(solution)/shard_map/ppermute | solution.py:236
  46.6 34.2 %collective-permute-start.8 = (bf16[272,1024]{1,0:T(8,128)(2,1)S(1)}, bf16[272,1024]{1,0:T(8,128)(2,1)S(1)}, u32[]{:S(2)}, u32[]{:S(2)}) collective-permute-start(bf16[272,1024]{1,0:T(8,128)(2,1)S(1)} %collective-permute-done.7.refs_4_), channel_id=1, source_target_pairs={{0,1},{1,0},{2,3},{3,2},{4,5},{5,4},{6,7},{7,6},{8,9},{9,8},{10,11... | collective-permute-start | bytes 1671176 | tf_op jit(solution)/shard_map/ppermute | solution.py:239
  46.6 33.6 %collective-permute-start.25 = (bf16[256,1024]{1,0:T(8,128)(2,1)S(1)}, bf16[256,1024]{1,0:T(8,128)(2,1)S(1)}, u32[]{:S(2)}, u32[]{:S(2)}) collective-permute-start(bf16[256,1024]{1,0:T(8,128)(2,1)S(1)} %collective-permute-done.21.refs_2_), channel_id=1, source_target_pairs={{2,0},{3,1},{4,6},{5,7},{10,8},{11,9},{12,14},{13,15},{18,16},{19,... | collective-permute-start | bytes 1572872 | tf_op jit(solution)/shard_map/ppermute | solution.py:236
  57.1 23.0 %collective-permute-start.10 = (bf16[256,1024]{1,0:T(8,128)(2,1)S(1)}, bf16[256,1024]{1,0:T(8,128)(2,1)S(1)}, u32[]{:S(2)}, u32[]{:S(2)}) collective-permute-start(bf16[256,1024]{1,0:T(8,128)(2,1)S(1)} %collective-permute-done.9.refs_6_), channel_id=1, source_target_pairs={{0,1},{1,0},{2,3},{3,2},{4,5},{5,4},{6,7},{7,6},{8,9},{9,8},{10,11... | collective-permute-start | bytes 1572872 | tf_op jit(solution)/shard_map/ppermute | solution.py:239
  57.2 32.1 %collective-permute-start.15 = (bf16[272,1024]{1,0:T(8,128)(2,1)S(1)}, bf16[272,1024]{1,0:T(8,128)(2,1)S(1)}, u32[]{:S(2)}, u32[]{:S(2)}) collective-permute-start(bf16[272,1024]{1,0:T(8,128)(2,1)S(1)} %collective-permute-done.14.refs_0_), channel_id=1, source_target_pairs={{0,1},{1,0},{2,3},{3,2},{4,5},{5,4},{6,7},{7,6},{8,9},{9,8},{10,11... | collective-permute-start | bytes 1671176 | tf_op jit(solution)/shard_map/ppermute | solution.py:239
  80.2 16.3 %collective-permute-start.22 = (bf16[256,1024]{1,0:T(8,128)(2,1)S(1)}, bf16[256,1024]{1,0:T(8,128)(2,1)S(1)}, u32[]{:S(2)}, u32[]{:S(2)}) collective-permute-start(bf16[256,1024]{1,0:T(8,128)(2,1)S(1)} %collective-permute-done.21.refs_2_), channel_id=1, source_target_pairs={{0,1},{1,0},{2,3},{3,2},{4,5},{5,4},{6,7},{7,6},{8,9},{9,8},{10,11... | collective-permute-start | bytes 1572872 | tf_op jit(solution)/shard_map/ppermute | solution.py:239
  80.2 16.8 %collective-permute-start.20 = (bf16[272,1024]{1,0:T(8,128)(2,1)S(1)}, bf16[272,1024]{1,0:T(8,128)(2,1)S(1)}, u32[]{:S(2)}, u32[]{:S(2)}) collective-permute-start(bf16[272,1024]{1,0:T(8,128)(2,1)S(1)} %collective-permute-done.19.refs_0_), channel_id=1, source_target_pairs={{0,1},{1,0},{2,3},{3,2},{4,5},{5,4},{6,7},{7,6},{8,9},{9,8},{10,11... | collective-permute-start | bytes 1671176 | tf_op jit(solution)/shard_map/ppermute | solution.py:239
  80.7 16.4 %collective-permute-start.26 = (bf16[256,1024]{1,0:T(8,128)(2,1)S(1)}, bf16[256,1024]{1,0:T(8,128)(2,1)S(1)}, u32[]{:S(2)}, u32[]{:S(2)}) collective-permute-start(bf16[256,1024]{1,0:T(8,128)(2,1)S(1)} %collective-permute-done.25.refs_6_), channel_id=1, source_target_pairs={{0,1},{1,0},{2,3},{3,2},{4,5},{5,4},{6,7},{7,6},{8,9},{9,8},{10,11... | collective-permute-start | bytes 1572872 | tf_op jit(solution)/shard_map/ppermute | solution.py:239
  80.8 16.4 %collective-permute-start.24 = (bf16[272,1024]{1,0:T(8,128)(2,1)S(1)}, bf16[272,1024]{1,0:T(8,128)(2,1)S(1)}, u32[]{:S(2)}, u32[]{:S(2)}) collective-permute-start(bf16[272,1024]{1,0:T(8,128)(2,1)S(1)} %collective-permute-done.23.refs_4_), channel_id=1, source_target_pairs={{0,1},{1,0},{2,3},{3,2},{4,5},{5,4},{6,7},{7,6},{8,9},{9,8},{10,11... | collective-permute-start | bytes 1671176 | tf_op jit(solution)/shard_map/ppermute | solution.py:239
  89.3 17.2 %collective-permute-start.11 = (bf16[272,1024]{1,0:T(8,128)(2,1)S(1)}, bf16[272,1024]{1,0:T(8,128)(2,1)}, u32[]{:S(2)}, u32[]{:S(2)}) collective-permute-start(bf16[272,1024]{1,0:T(8,128)(2,1)S(1)} %get-tuple-element.46), channel_id=1, source_target_pairs={{0,1},{1,0},{2,3},{3,2},{4,5},{5,4},{6,7},{7,6},{8,9},{9,8},{10,11... | collective-permute-start | bytes 1671176 | tf_op jit(solution)/shard_map/ppermute | solution.py:239
  96.5 81.2 %collective-permute-start.2 = (bf16[272,1024]{1,0:T(8,128)(2,1)S(1)}, bf16[272,1024]{1,0:T(8,128)(2,1)S(1)}, u32[]{:S(2)}, u32[]{:S(2)}) collective-permute-start(bf16[272,1024]{1,0:T(8,128)(2,1)S(1)} %get-tuple-element.44), channel_id=1, source_target_pairs={{0,1},{1,0},{2,3},{3,2},{4,5},{5,4},{6,7},{7,6},{8,9},{9,8},{10,11... | collective-permute-start | bytes 1671176 | tf_op jit(solution)/shard_map/ppermute | solution.py:239
  97.0 62.2 %collective-permute-start.18 = (bf16[272,1024]{1,0:T(8,128)(2,1)S(1)}, bf16[272,1024]{1,0:T(8,128)(2,1)}, u32[]{:S(2)}, u32[]{:S(2)}) collective-permute-start(bf16[272,1024]{1,0:T(8,128)(2,1)S(1)} %get-tuple-element.48), channel_id=1, source_target_pairs={{0,1},{1,0},{2,3},{3,2},{4,5},{5,4},{6,7},{7,6},{8,9},{9,8},{10,11... | collective-permute-start | bytes 1671176 | tf_op jit(solution)/shard_map/ppermute | solution.py:239
  105.0 11.5 %collective-permute-start.41 = (bf16[2,256,384]{2,1,0:T(8,128)(2,1)S(1)}, bf16[2,256,384]{2,1,0:T(8,128)(2,1)S(1)}, u32[]{:S(2)}, u32[]{:S(2)}) collective-permute-start(bf16[2,256,384]{2,1,0:T(8,128)(2,1)S(1)} %get-tuple-element.82), channel_id=1, source_target_pairs={{0,16},{8,24},{16,0},{24,8},{1,17},{9,25},{17,1},{25,9},{2,18},{10... | collective-permute-start | bytes 1179656 | tf_op jit(solution)/shard_map/ppermute | solution.py:315
  107.8 33.6 %collective-permute-start.12 = (bf16[272,1024]{1,0:T(8,128)(2,1)S(1)}, bf16[272,1024]{1,0:T(8,128)(2,1)S(1)}, u32[]{:S(2)}, u32[]{:S(2)}) collective-permute-start(bf16[272,1024]{1,0:T(8,128)(2,1)S(1)} %fusion), channel_id=1, source_target_pairs={{0,2},{1,3},{6,4},{7,5},{8,10},{9,11},{14,12},{15,13},{16,18},{17,... | collective-permute-start | bytes 1671176 | tf_op jit(solution)/shard_map/ppermute | solution.py:236
  109.3 11.1 %collective-permute-start.39 = (bf16[2,256,384]{2,1,0:T(8,128)(2,1)S(1)}, bf16[2,256,384]{2,1,0:T(8,128)(2,1)S(1)}, u32[]{:S(2)}, u32[]{:S(2)}) collective-permute-start(bf16[2,256,384]{2,1,0:T(8,128)(2,1)S(1)} %get-tuple-element.80), channel_id=1, source_target_pairs={{0,8},{8,0},{16,24},{24,16},{1,9},{9,1},{17,25},{25,17},{2,10},{10... | collective-permute-start | bytes 1179656 | tf_op jit(solution)/shard_map/ppermute | solution.py:315
  116.5 10.7 %collective-permute-start.37 = (bf16[2,256,384]{2,1,0:T(8,128)(2,1)S(1)}, bf16[2,256,384]{2,1,0:T(8,128)(2,1)S(1)}, u32[]{:S(2)}, u32[]{:S(2)}) collective-permute-start(bf16[2,256,384]{2,1,0:T(8,128)(2,1)S(1)} %get-tuple-element.70), channel_id=1, source_target_pairs={{0,16},{8,24},{16,0},{24,8},{1,17},{9,25},{17,1},{25,9},{2,18},{10... | collective-permute-start | bytes 1179656 | tf_op jit(solution)/shard_map/ppermute | solution.py:315
  120.4 10.2 %collective-permute-start.35 = (bf16[2,256,384]{2,1,0:T(8,128)(2,1)S(1)}, bf16[2,256,384]{2,1,0:T(8,128)(2,1)S(1)}, u32[]{:S(2)}, u32[]{:S(2)}) collective-permute-start(bf16[2,256,384]{2,1,0:T(8,128)(2,1)S(1)} %get-tuple-element.68), channel_id=1, source_target_pairs={{0,8},{8,0},{16,24},{24,16},{1,9},{9,1},{17,25},{25,17},{2,10},{10... | collective-permute-start | bytes 1179656 | tf_op jit(solution)/shard_map/ppermute | solution.py:315
  157.0 19.5 %collective-permute-start.32 = (bf16[256,384]{1,0:T(8,128)(2,1)S(1)}, bf16[256,384]{1,0:T(8,128)(2,1)S(1)}, u32[]{:S(2)}, u32[]{:S(2)}) collective-permute-start(bf16[256,384]{1,0:T(8,128)(2,1)S(1)} %fusion.9), channel_id=1, source_target_pairs={{0,16},{8,24},{16,0},{24,8},{1,17},{9,25},{17,1},{25,9},{2,18},{10... | collective-permute-start | bytes 589832 | tf_op jit(solution)/shard_map/ppermute | solution.py:315
  158.4 19.3 %collective-permute-start.13 = (bf16[272,1024]{1,0:T(8,128)(2,1)S(1)}, bf16[272,1024]{1,0:T(8,128)(2,1)S(1)}, u32[]{:S(2)}, u32[]{:S(2)}) collective-permute-start(bf16[272,1024]{1,0:T(8,128)(2,1)S(1)} %add_convert_fusion.3), channel_id=1, source_target_pairs={{2,4},{3,5},{4,2},{5,3},{10,12},{11,13},{12,10},{13,11},{18,20},{1... | collective-permute-start | bytes 1671176 | tf_op jit(solution)/shard_map/ppermute | solution.py:236
  160.6 23.4 %collective-permute-start.30 = (bf16[272,1024]{1,0:T(8,128)(2,1)S(1)}, bf16[272,1024]{1,0:T(8,128)(2,1)S(1)}, u32[]{:S(2)}, u32[]{:S(2)}) collective-permute-start(bf16[272,1024]{1,0:T(8,128)(2,1)S(1)} %add_convert_fusion.1), channel_id=1, source_target_pairs={{0,2},{1,3},{2,0},{3,1},{4,6},{5,7},{6,4},{7,5},{8,10},{9,11},{10,... | collective-permute-start | bytes 1671176 | tf_op jit(solution)/shard_map/ppermute | solution.py:236
  (41 other events, 299.0 us)

commit v2 on v1

v2 whole, which is shorter than its diff:
```python
import functools

import jax
import jax.numpy as jnp
from jax import lax
from jax.experimental import pallas as pl
from jax.experimental.pallas import tpu as pltpu
from jax.sharding import PartitionSpec as P

MICRO = 2
CORES = 2
META = 16
LAST = (((1,), (1,)), ((), ()))
FIRST = (((0,), (0,)), ((), ()))
F32 = jnp.float32
BF16 = jnp.bfloat16


def dot(lhs, rhs, dims=(((1,), (0,)), ((), ()))):
    return lax.dot_general(lhs, rhs, dims, preferred_element_type=F32)


def slot_kernel(choices, batch, capacity, middle, *refs):
    inputs = refs[: 2 * choices]
    weights = refs[2 * choices]
    xr_out, q_out, h_out, da_out, db_out, dxa_out, dxb_out = refs[2 * choices + 1 : 2 * choices + 8]
    meta_buf, cot_buf = refs[2 * choices + 8 :]
    count = MICRO * batch
    me = lax.axis_index("expert")
    inner = (me // CORES >= middle[0]) & (me // CORES <= middle[1])

    def chosen_input(task):
        if choices == 1:
            task(inputs[:2])
        else:
            pl.when(inner)(lambda: task(inputs[:2]))
            pl.when(jnp.logical_not(inner))(lambda: task(inputs[2:]))

    def take_meta(pair):
        for half in range(CORES):
            meta_buf[half] = pair[half][count : count + META, :count]

    chosen_input(take_meta)
    mine = (me + 1).astype(F32)
    upper = (
        lax.broadcasted_iota(jnp.int32, (batch, batch), 0)
        < lax.broadcasted_iota(jnp.int32, (batch, batch), 1)
    ).astype(BF16)
    slot_of = lax.broadcasted_iota(jnp.int32, (capacity, batch), 0).astype(F32)
    parts = []
    for half in range(CORES):
        for micro in range(MICRO):
            rows = slice(micro * batch, (micro + 1) * batch)
            meta = meta_buf[half, :, rows].astype(F32)
            first = meta[0:1] == mine
            second = meta[1:2] == mine
            chosen = jnp.where(first | second, 1.0, 0.0)
            rank = dot(jnp.broadcast_to(chosen, (8, batch)).astype(BF16), upper)[0:1]
            onehot = jnp.where(rank == slot_of, chosen, 0.0)
            gate = jnp.sum(
                onehot * (jnp.where(first, meta[2:3], 0.0) + jnp.where(second, meta[3:4], 0.0)),
                axis=1,
                keepdims=True,
            )
            parts.append((half, rows, onehot, gate, first, second))

    def pack(pair):
        for number, (half, rows, onehot, gate, first, second) in enumerate(parts):
            places = slice(number * capacity, (number + 1) * capacity)
            pick = onehot.astype(BF16)
            xr_out[places, :] = dot(pick, pair[half][rows, :]).astype(BF16)
            cot = dot(pick, pair[half][count + META + rows.start : count + META + rows.stop, :])
            cot_buf[places, :] = cot
            q_out[places, :] = (gate * cot).astype(BF16)

    chosen_input(pack)
    xr = xr_out[...]
    pre_gate = dot(xr, weights[0, 0])
    pre_up = dot(xr, weights[0, 1])
    sig = jax.nn.sigmoid(pre_gate)
    activated = pre_gate * sig
    hidden = (activated * pre_up).astype(BF16)
    h_out[...] = hidden
    output = dot(hidden, weights[0, 2], LAST)
    gate_grad = jnp.sum(output * cot_buf[...], axis=1, keepdims=True)
    hidden_grad = dot(q_out[...], weights[0, 2])
    da = (hidden_grad * pre_up * sig * (1.0 + pre_gate * (1.0 - sig))).astype(BF16)
    db = (hidden_grad * activated).astype(BF16)
    da_out[...] = da
    db_out[...] = db
    dx = (dot(da, weights[0, 0], LAST) + dot(db, weights[0, 1], LAST)).astype(BF16)
    line = lax.broadcasted_iota(jnp.int32, (META, batch), 0)
    outs = (dxa_out, dxb_out)
    for out in outs:
        out[count : count + META, :] = jnp.zeros((META, out.shape[1]), BF16)
    for number, (half, rows, onehot, gate, first, second) in enumerate(parts):
        places = slice(number * capacity, (number + 1) * capacity)
        outs[half][rows, :] = dot(onehot.astype(BF16), dx[places], FIRST).astype(BF16)
        spread = jnp.sum(onehot * gate_grad[places], axis=0, keepdims=True)
        values = jnp.where(line == 0, jnp.where(first, spread, 0.0), 0.0) + jnp.where(
            line == 1, jnp.where(second, spread, 0.0), 0.0
        )
        outs[half][count : count + META, rows] = values.astype(BF16)


def run_slot(alternatives, weights, batch, capacity, middle):
    choices = len(alternatives)
    width = weights.shape[2]
    rows = MICRO * batch + META
    hidden_width = weights.shape[-1]
    slots = CORES * MICRO * capacity
    operands = [array for group in alternatives for array in group]
    shape = jax.ShapeDtypeStruct
    return pl.pallas_call(
        functools.partial(slot_kernel, choices, batch, capacity, middle),
        out_shape=[
            shape((slots, width), BF16),
            shape((slots, width), BF16),
            shape((slots, hidden_width), BF16),
            shape((slots, hidden_width), BF16),
            shape((slots, hidden_width), BF16),
            shape((rows, width), BF16),
            shape((rows, width), BF16),
        ],
        in_specs=[pl.BlockSpec(memory_space=pltpu.VMEM)] * (len(operands) + 1),
        out_specs=[pl.BlockSpec(memory_space=pltpu.VMEM)] * 7,
        scratch_shapes=[
            pltpu.VMEM((CORES, META, MICRO * batch), BF16),
            pltpu.VMEM((slots, width), F32),
        ],
        compiler_params=pltpu.CompilerParams(vmem_limit_bytes=24 * 1024 * 1024),
        cost_estimate=pl.CostEstimate(flops=1, bytes_accessed=1, transcendentals=0),
        name="expert_block",
    )(*operands, weights)


def weight_kernel(products, pieces, *refs):
    a_send, a_keep, b_send, b_keep = refs[2 * pieces * products :]
    here = lax.axis_index("dp")
    quarter = refs[0].shape[1] // 4
    half = refs[pieces].shape[1] // 2
    places = (
        (3, a_send, 0, b_send, 0),
        (1, a_send, 1, b_keep, 0),
        (2, a_keep, 0, b_send, 1),
        (0, a_keep, 1, b_keep, 1),
    )
    for place, a_out, a_at, b_out, b_at in places:
        at = pl.multiple_of((here ^ place) * quarter, quarter)
        for product in range(products):
            group = refs[2 * pieces * product : 2 * pieces * (product + 1)]
            total = None
            for left, right in zip(group[:pieces], group[pieces:]):
                term = dot(left[:, pl.ds(at, quarter)], right[...], FIRST)
                total = term if total is None else total + term
            value = total.astype(BF16)
            a_out[a_at, product] = value[:, :half]
            b_out[b_at, product] = value[:, half:]


def run_weight(*products):
    lefts, rights = products[0]
    width = lefts[0].shape[1]
    hidden_width = rights[0].shape[1]
    piece = jax.ShapeDtypeStruct((2, len(products), width // 4, hidden_width // 2), BF16)
    operands = [array for pair in products for group in pair for array in group]
    return pl.pallas_call(
        functools.partial(weight_kernel, len(products), len(lefts)),
        out_shape=[piece] * 4,
        in_specs=[pl.BlockSpec(memory_space=pltpu.VMEM)] * len(operands),
        out_specs=[pl.BlockSpec(memory_space=pltpu.VMEM)] * 4,
        compiler_params=pltpu.CompilerParams(vmem_limit_bytes=24 * 1024 * 1024),
        cost_estimate=pl.CostEstimate(flops=1, bytes_accessed=1, transcendentals=0),
        name="weight_block",
    )(*operands)


def add(*values):
    total = values[0].astype(F32)
    for value in values[1:]:
        total = total + value.astype(F32)
    return total.astype(BF16)


def after(value, *earlier):
    return lax.optimization_barrier((value, earlier))[0]


def on_device(tokens, cotangent, gates, expert_ids, expert_weights):
    devices = lax.axis_size("expert")
    chips = devices // CORES
    count, width = tokens.shape
    batch = count // MICRO
    capacity = 4 * batch // devices
    routing = jnp.concatenate([(expert_ids + 1).astype(BF16).T, gates.T], axis=0)
    routing = jnp.pad(routing, ((0, META - 4), (0, width - count)))
    own = jnp.concatenate([tokens, routing, cotangent], axis=0)

    def move(value, pairs):
        full = [(a * CORES + k, b * CORES + k) for a, b in pairs for k in range(CORES)]
        return lax.ppermute(value, "expert", full)

    def swap(value):
        return lax.ppermute(value, "expert", [(i, i ^ 1) for i in range(devices)])

    def compute(*alternatives):
        result = run_slot(alternatives, expert_weights, batch, capacity, (1, chips - 2))
        return result[:5], (result[5], result[6])

    def joined(grads):
        return (grads[0], swap(grads[1]))

    ahead = [(z, (z + 1) % chips) for z in range(chips)]
    behind = [(b, a) for a, b in ahead]
    if chips == 4:
        outer = [(0, 1), (1, 0), (2, 3), (3, 2)]
        inner = [(1, 2), (2, 1)]
        to_ends = [(1, 0), (2, 3)]
        from_ends = [(0, 1), (3, 2)]
        second = move(own, inner)
        first = move(own, outer)
        rows, grads = compute((own, swap(own)))
        kept = [rows]
        own_sum = joined(grads)
        second, first = after((second, first), own_sum[1])
        third = move(second, to_ends)
        fourth = move(first, inner)
        rows, grads = compute((first, swap(first)))
        kept.append(rows)
        first_sum = joined(grads)
        fourth, third = after((fourth, third), first_sum[1])
        fifth = move(fourth, to_ends)
        rows, grads = compute((second, swap(second)), (third, swap(third)))
        kept.append(rows)
        third_sum = joined(grads)
        came = move(add(*third_sum), from_ends)
        fifth = after(fifth, third_sum[1])
        third_back = move(add(*third_sum, came), inner)
        rows, grads = compute((fourth, swap(fourth)), (fifth, swap(fifth)))
        kept.append(rows)
        fourth_sum = joined(grads)
        back = sent = add(*fourth_sum)
        back = add(*fourth_sum, move(back, from_ends))
        back = add(*first_sum, move(back, inner))
        back = move(back, outer)
        total = add(*own_sum, third_back, back)
    else:
        rows, grads = compute((own, swap(own)))
        kept = [rows]
        sent = grads[0]
        total = [*joined(grads)]
        reach = chips // 2
        for forth, back, steps in ((ahead, behind, reach), (behind, ahead, chips - 1 - reach)):
            current, sums = own, []
            for _ in range(steps):
                current = move(current, forth)
                rows, grads = compute((current, swap(current)))
                kept.append(rows)
                sums.append(joined(grads))
            value = None
            for pair in reversed(sums):
                value = move(add(*pair) if value is None else add(*pair, value), back)
            if value is not None:
                total.append(value)
        total = add(*total)
    tokens_grad = total[:count]
    gates_grad = total[count : count + 2, :count].T

    xr, q, h, da, db = zip(*kept)
    if lax.axis_size("dp") == 4:

        def across(value, bit):
            return lax.ppermute(value, "dp", [(i, i ^ bit) for i in range(4)])

        ends = []
        for group in ([(q, h)], after([(xr, da), (xr, db)], sent)):
            a_send, a_keep, b_send, b_keep = run_weight(*group)
            a_came = across(a_send, 1)
            b_came = across(b_send, 2)
            a_last = across(add(a_keep[0], a_came[0]), 2)
            b_last = across(add(b_keep[0], b_came[0]), 1)
            ends.append(
                jnp.concatenate(
                    [add(a_keep[1], a_came[1], a_last), add(b_keep[1], b_came[1], b_last)], axis=-1
                )
            )
        weights_grad = jnp.concatenate([ends[1], ends[0]], axis=0)[None]
    else:
        whole = [jnp.concatenate(value, axis=0) for value in (xr, q, h, da, db)]
        partial = jnp.stack(
            [
                dot(whole[0], whole[3], FIRST),
                dot(whole[0], whole[4], FIRST),
                dot(whole[1], whole[2], FIRST),
            ]
        ).astype(BF16)
        weights_grad = lax.psum_scatter(
            partial[None], "dp", scatter_dimension=2, tiled=True
        )
    return tokens_grad, gates_grad, weights_grad


def solution(mesh):
    placed = (
        P(("dp", "expert"), None),
        P(("dp", "expert"), None),
        P(("dp", "expert"), None),
        P(("dp", "expert"), None),
        P("expert", None, None, None),
    )
    return jax.shard_map(
        on_device,
        mesh=mesh,
        in_specs=placed,
        out_specs=(
            P(("dp", "expert"), None),
            P(("dp", "expert"), None),
            P("expert", None, "dp", None),
        ),
        check_vma=False,
    )
```

time: 186 us -> 160 us (0.86)
  starting transfers between devices: 55.6 us -> 32 us
  waiting for transfers between devices: 82.2 us -> 94 us
  local copies, waits for them, and re-layouts: 9.17 us -> 3.74 us
  Pallas kernels: 28.1 us -> 22.9 us
  other arithmetic: 9.26 us -> 6.15 us
    ppermute x15 -> x10, starting transfers between devices: 36.4 us -> 19.3 us  [move(): return lax.ppermute(value, 'expert', full)]
    ppermute x15 -> x10, waiting for transfers between devices: 61.2 us -> 72 us  [move(): return lax.ppermute(value, 'expert', full)]
    unnamed x60 -> x6, local copies, waits for them, and re-layouts: 7.78 us -> 2.34 us
    ppermute x12 -> x8, starting transfers between devices: 15.7 us -> 10.5 us  [across(): return lax.ppermute(value, 'dp', [(i, i ^ bit) for i in range(4)])]
    pallas_call x4, Pallas kernels: 22.5 us -> 17.4 us  [run_slot(): pl.pallas_call(functools.partial(slot_kernel, choices, batch, capacity, m...]
    convert_element_type x18 -> x14, other arithmetic: 5.57 us -> 2.4 us  [add(): return total.astype(BF16)]
    ppermute x16 -> x10, waiting for transfers between devices: 0.04 us -> 3.06 us  [swap(): return lax.ppermute(value, 'expert', [(i, i ^ 1) for i in range(devices)])]
    ppermute x12 -> x8, waiting for transfers between devices: 21 us -> 19 us  [across(): return lax.ppermute(value, 'dp', [(i, i ^ bit) for i in range(4)])]
  transfers between devices with their start and end apart: 43 -> 28, of which waited for: 14 -> 12; matrix products, arithmetic and copies ran while one was open for 5% -> 2% of each run, Pallas kernels for 15% -> 14%
where the time goes in v2:
time: 160 us
  waiting for transfers between devices  94 us (59%)
  starting transfers between devices  32 us (20%)
  Pallas kernels  22.9 us (14%)
  other arithmetic  6.15 us (4%)
  local copies, waits for them, and re-layouts  3.74 us (2%)
    ppermute x10, waiting for transfers between devices, move(): return lax.ppermute(value, 'expert', full)  72 us
    ppermute x10, starting transfers between devices, move(): return lax.ppermute(value, 'expert', full)  19.3 us
    ppermute x8, waiting for transfers between devices, across(): return lax.ppermute(value, 'dp', [(i, i ^ bit) for i in range(4)])  19 us
    pallas_call x4, Pallas kernels, run_slot(): pl.pallas_call(functools.partial(slot_kernel, choices, batch, capacity, m...  17.4 us
    ppermute x8, starting transfers between devices, across(): return lax.ppermute(value, 'dp', [(i, i ^ bit) for i in range(4)])  10.5 us
    pallas_call x2, Pallas kernels, run_weight(): pl.pallas_call(functools.partial(weight_kernel, len(products), len(lefts)...  5.46 us
  transfers between devices with their start and end apart: 28, of which 12 were waited for; matrix products, arithmetic and copies ran while one was open for 2% of the time, Pallas kernels for 14%

profile of v2, /device:TPU:0, one launch (start us, length us, event | category | flops | bytes accessed | tf_op | source)
XLA Modules:
  0.0 159.7 jit_solution(17531683794313583543)
XLA Ops:
  2.0 1.3 pad_maximum_fusion.refs_0_
  3.8 2.6 %collective-permute-start.3 = (bf16[528,1024]{1,0:T(8,128)(2,1)S(1)}, bf16[528,1024]{1,0:T(8,128)(2,1)S(1)}, u32[]{:S(2)}, u32[]{:S(2)}) collective-permute-start(bf16[528,1024]{1,0:T(8,128)(2,1)S(1)} %pad_maximum_fusion.refs_0_), channel_id=1, source_target_pairs={{0,2},{1,3},{2,0},{3,1},{4,6},{5,7},{6,4},{7,5},{8,10},{9,11},{10,... | collective-permute-start | bytes 3244040 | tf_op jit(solution)/shard_map/ppermute | solution.py:201
  7.2 2.3 %copy-done = bf16[1,3,1024,768]{3,2,1,0:T(8,128)(2,1)S(1)} copy-done((bf16[1,3,1024,768]{3,2,1,0:T(8,128)(2,1)S(1)}, bf16[1,3,1024,768]{3,2,1,0:T(8,128)(2,1)}, u32[]{:S(2)}) %copy-start) | copy-done | bytes 4718616
  9.5 4.2 %expert_block.4 = (bf16[256,1024]{1,0:T(8,128)(2,1)S(1)}, bf16[256,1024]{1,0:T(8,128)(2,1)S(1)}, bf16[256,768]{1,0:T(8,128)(2,1)S(1)}, bf16[256,768]{1,0:T(8,128...) custom-call(bf16[528,1024]{1,0:T(8,128)(2,1)S(1)} %pad_maximum_fusion.refs_0_, ...), custom_call_target="tpu_custom_call" | custom-call | flops 1 | bytes 1 | tf_op jit(solution)/shard_map/expert_block/pallas_call | solution.py:114
  13.9 17.0 %collective-permute-done.3.refs_0_ = bf16[528,1024]{1,0:T(8,128)(2,1)S(1)} collective-permute-done((bf16[528,1024]{1,0:T(8,128)(2,1)S(1)}, bf16[528,1024]{1,0:T(8,128)(2,1)S(1)}, u32[]{:S(2)}, u32[]{:S(2)}) %collective-permute-start.3) | collective-permute-done | bytes 1081376 | tf_op jit(solution)/shard_map/ppermute | solution.py:201
  30.9 1.3 collective-permute-start.6
  33.6 4.2 %expert_block.5 = (bf16[256,1024]{1,0:T(8,128)(2,1)S(1)}, bf16[256,1024]{1,0:T(8,128)(2,1)S(1)}, bf16[256,768]{1,0:T(8,128)(2,1)S(1)}, bf16[256,768]{1,0:T(8,128...) custom-call(bf16[528,1024]{1,0:T(8,128)(2,1)S(1)} %collective-permute-done.3., ...), custom_call_target="tpu_custom_call" | custom-call | flops 1 | bytes 1 | tf_op jit(solution)/shard_map/expert_block/pallas_call | solution.py:114
  38.4 23.1 %collective-permute-done.6.refs_2_ = bf16[528,1024]{1,0:T(8,128)(2,1)S(1)} collective-permute-done((bf16[528,1024]{1,0:T(8,128)(2,1)S(1)}, bf16[528,1024]{1,0:T(8,128)(2,1)S(1)}, u32[]{:S(2)}, u32[]{:S(2)}) %collective-permute-start.6) | collective-permute-done | bytes 1081376 | tf_op jit(solution)/shard_map/ppermute | solution.py:201
  61.5 1.3 collective-permute-start.14
  62.8 1.4 collective-permute-done.9.refs_3_
  64.2 4.6 %expert_block.6 = (bf16[256,1024]{1,0:T(8,128)(2,1)S(1)}, bf16[256,1024]{1,0:T(8,128)(2,1)S(1)}, bf16[256,768]{1,0:T(8,128)(2,1)S(1)}, bf16[256,768]{1,0:T(8,128...) custom-call(bf16[528,1024]{1,0:T(8,128)(2,1)S(1)} %collective-permute-done.2., ...), custom_call_target="tpu_custom_call" | custom-call | flops 1 | bytes 1 | tf_op jit(solution)/shard_map/expert_block/pallas_call | solution.py:114
  69.4 21.6 %collective-permute-done.14.refs_2_ = bf16[528,1024]{1,0:T(8,128)(2,1)S(1)} collective-permute-done((bf16[528,1024]{1,0:T(8,128)(2,1)S(1)}, bf16[528,1024]{1,0:T(8,128)(2,1)S(1)}, u32[]{:S(2)}, u32[]{:S(2)}) %collective-permute-start.14) | collective-permute-done | bytes 1081376 | tf_op jit(solution)/shard_map/ppermute | solution.py:201
  91.2 1.5 collective-permute-start.11
  92.7 1.0 collective-permute-done.15.refs_3_
  93.7 4.4 %expert_block.7 = (bf16[256,1024]{1,0:T(8,128)(2,1)S(1)}, bf16[256,1024]{1,0:T(8,128)(2,1)S(1)}, bf16[256,768]{1,0:T(8,128)(2,1)S(1)}, bf16[256,768]{1,0:T(8,128...) custom-call(bf16[528,1024]{1,0:T(8,128)(2,1)S(1)} %collective-permute-done.5., ...), custom_call_target="tpu_custom_call" | custom-call | flops 1 | bytes 1 | tf_op jit(solution)/shard_map/expert_block/pallas_call | solution.py:114
  98.4 1.9 %weight_block.3 = (bf16[2,1,256,384]{3,2,1,0:T(8,128)(2,1)S(1)}, bf16[2,1,256,384]{3,2,1,0:T(8,128)(2,1)S(1)}, bf16[2,1,256,384]{3,2,1,0:T(8,128)(2,1)S(1)}, bf16[2,1,256,384]{3,2,1,0:T(8,128)(2,1)S(1)}) custom-call(bf16[256,1024]{1,0:T(8,128)(2,1)S(1)} %get-tuple-element.105.refs_0_, bf16[256,1024]{1,0:T(8,128)(2,1)S(1)} %get-tuple-element.106.refs_1_, ...), custom_call_target="tpu_custom_call" | custom-call | flops 1 | bytes 1 | tf_op jit(solution)/shard_map/weight_block/pallas_call | solution.py:167
  100.3 1.6 collective-permute-start.24
  101.8 3.5 %collective-permute-done.11 = bf16[272,1024]{1,0:T(8,128)(2,1)S(1)} collective-permute-done((bf16[272,1024]{1,0:T(8,128)(2,1)S(1)}, bf16[272,1024]{1,0:T(8,128)(2,1)S(1)}, u32[]{:S(2)}, u32[]{:S(2)}) %collective-permute-start.11) | collective-permute-done | bytes 557088 | tf_op jit(solution)/shard_map/ppermute | solution.py:201
  106.3 1.6 collective-permute-start.26
  108.1 7.6 %collective-permute-start.17 = (bf16[272,1024]{1,0:T(8,128)(2,1)S(1)}, bf16[272,1024]{1,0:T(8,128)(2,1)S(1)}, u32[]{:S(2)}, u32[]{:S(2)}) collective-permute-start(bf16[272,1024]{1,0:T(8,128)(2,1)S(1)} %fusion.1), channel_id=1, source_target_pairs={{0,2},{1,3},{6,4},{7,5},{8,10},{9,11},{14,12},{15,13},{16,18},{17,... | collective-permute-start | bytes 1671176 | tf_op jit(solution)/shard_map/ppermute | solution.py:201
  116.4 3.6 %weight_block.2 = (bf16[2,2,256,384]{3,2,1,0:T(8,128)(2,1)S(1)}, bf16[2,2,256,384]{3,2,1,0:T(8,128)(2,1)S(1)}, bf16[2,2,256,384]{3,2,1,0:T(8,128)(2,1)S(1)}, bf16[2,2,256,384]{3,2,1,0:T(8,128)(2,1)S(1)}) custom-call(bf16[256,1024]{1,0:T(8,128)(2,1)S(1)} %get-tuple-element.93.refs_0_.refs_8_, bf16[256,1024]{1,0:T(8,128)(2,1)S(1)} %get-tuple-element.94.refs_1_.refs_9_, ...), custom_call_target="tpu_custom_call" | custom-call | flops 1 | bytes 1 | tf_op jit(solution)/shard_map/weight_block/pallas_call | solution.py:167
  120.0 1.6 collective-permute-start.20
  122.2 1.5 collective-permute-start.22
  123.8 2.9 %collective-permute-done.17 = bf16[272,1024]{1,0:T(8,128)(2,1)S(1)} collective-permute-done((bf16[272,1024]{1,0:T(8,128)(2,1)S(1)}, bf16[272,1024]{1,0:T(8,128)(2,1)S(1)}, u32[]{:S(2)}, u32[]{:S(2)}) %collective-permute-start.17) | collective-permute-done | bytes 557088 | tf_op jit(solution)/shard_map/ppermute | solution.py:201
  127.7 14.6 %collective-permute-done.27 = bf16[1,256,384]{2,1,0:T(8,128)(2,1)S(1)} collective-permute-done((bf16[1,256,384]{2,1,0:T(8,128)(2,1)S(1)}, bf16[1,256,384]{2,1,0:T(8,128)(2,1)S(1)}, u32[]{:S(2)}, u32[]{:S(2)}) %collective-permute-start.27) | collective-permute-done | bytes 196640 | tf_op jit(solution)/shard_map/ppermute | solution.py:273
  142.5 1.6 collective-permute-start.21
  144.2 1.6 collective-permute-start.23
  146.1 2.2 %collective-permute-start.19 = (bf16[272,1024]{1,0:T(8,128)(2,1)S(1)}, bf16[272,1024]{1,0:T(8,128)(2,1)S(1)}, u32[]{:S(2)}, u32[]{:S(2)}) collective-permute-start(bf16[272,1024]{1,0:T(8,128)(2,1)S(1)} %add_convert_fusion.1), channel_id=1, source_target_pairs={{0,2},{1,3},{2,0},{3,1},{4,6},{5,7},{6,4},{7,5},{8,10},{9,11},{10,... | collective-permute-start | bytes 1671176 | tf_op jit(solution)/shard_map/ppermute | solution.py:201
  148.3 3.1 %collective-permute-done.21 = bf16[2,256,384]{2,1,0:T(8,128)(2,1)S(1)} collective-permute-done((bf16[2,256,384]{2,1,0:T(8,128)(2,1)S(1)}, bf16[2,256,384]{2,1,0:T(8,128)(2,1)S(1)}, u32[]{:S(2)}, u32[]{:S(2)}) %collective-permute-start.21) | collective-permute-done | bytes 393248 | tf_op jit(solution)/shard_map/ppermute | solution.py:273
  151.5 1.2 collective-permute-done.23
  152.9 1.1 maximum_bitcast_fusion
  154.0 3.8 %collective-permute-done.19 = bf16[272,1024]{1,0:T(8,128)(2,1)S(1)} collective-permute-done((bf16[272,1024]{1,0:T(8,128)(2,1)S(1)}, bf16[272,1024]{1,0:T(8,128)(2,1)S(1)}, u32[]{:S(2)}, u32[]{:S(2)}) %collective-permute-start.19) | collective-permute-done | bytes 557088 | tf_op jit(solution)/shard_map/ppermute | solution.py:201
  (57 shorter events, 12.0 us)
Async XLA Ops:
  3.3 3.9 %collective-permute-start = (bf16[528,1024]{1,0:T(8,128)(2,1)S(1)}, bf16[528,1024]{1,0:T(8,128)(2,1)S(1)}, u32[]{:S(2)}, u32[]{:S(2)}) collective-permute-start(bf16[528,1024]{1,0:T(8,128)(2,1)S(1)} %pad_maximum_fusion.refs_0_), channel_id=1, source_target_pairs={{0,1},{1,0},{2,3},{3,2},{4,5},{5,4},{6,7},{7,6},{8,9},{9,8},{10,11... | collective-permute-start | bytes 3244040 | tf_op jit(solution)/shard_map/ppermute | solution.py:204
  3.8 27.1 %collective-permute-start.3 = (bf16[528,1024]{1,0:T(8,128)(2,1)S(1)}, bf16[528,1024]{1,0:T(8,128)(2,1)S(1)}, u32[]{:S(2)}, u32[]{:S(2)}) collective-permute-start(bf16[528,1024]{1,0:T(8,128)(2,1)S(1)} %pad_maximum_fusion.refs_0_), channel_id=1, source_target_pairs={{0,2},{1,3},{2,0},{3,1},{4,6},{5,7},{6,4},{7,5},{8,10},{9,11},{10,... | collective-permute-start | bytes 3244040 | tf_op jit(solution)/shard_map/ppermute | solution.py:201
  6.5 24.5 %collective-permute-start.2 = (bf16[528,1024]{1,0:T(8,128)(2,1)S(1)}, bf16[528,1024]{1,0:T(8,128)(2,1)S(1)}, u32[]{:S(2)}, u32[]{:S(2)}) collective-permute-start(bf16[528,1024]{1,0:T(8,128)(2,1)S(1)} %pad_maximum_fusion.refs_0_), channel_id=1, source_target_pairs={{2,4},{3,5},{4,2},{5,3},{10,12},{11,13},{12,10},{13,11},{18,20},{1... | collective-permute-start | bytes 3244040 | tf_op jit(solution)/shard_map/ppermute | solution.py:201
  7.2 2.3 %copy-start = (bf16[1,3,1024,768]{3,2,1,0:T(8,128)(2,1)S(1)}, bf16[1,3,1024,768]{3,2,1,0:T(8,128)(2,1)}, u32[]{:S(2)}) copy-start(bf16[1,3,1024,768]{3,2,1,0:T(8,128)(2,1)} %refs_4_.3) | copy-start | bytes 14155780
  13.7 17.2 %collective-permute-start.1 = (bf16[272,1024]{1,0:T(8,128)(2,1)S(1)}, bf16[272,1024]{1,0:T(8,128)(2,1)S(1)}, u32[]{:S(2)}, u32[]{:S(2)}) collective-permute-start(bf16[272,1024]{1,0:T(8,128)(2,1)S(1)} %get-tuple-element.61), channel_id=1, source_target_pairs={{0,1},{1,0},{2,3},{3,2},{4,5},{5,4},{6,7},{7,6},{8,9},{9,8},{10,11... | collective-permute-start | bytes 1671176 | tf_op jit(solution)/shard_map/ppermute | solution.py:204
  30.9 2.7 %collective-permute-start.7 = (bf16[528,1024]{1,0:T(8,128)(2,1)S(1)}, bf16[528,1024]{1,0:T(8,128)(2,1)S(1)}, u32[]{:S(2)}, u32[]{:S(2)}) collective-permute-start(bf16[528,1024]{1,0:T(8,128)(2,1)S(1)} %collective-permute-done.3.refs_0_), channel_id=1, source_target_pairs={{0,1},{1,0},{2,3},{3,2},{4,5},{5,4},{6,7},{7,6},{8,9},{9,8},{10,11... | collective-permute-start | bytes 3244040 | tf_op jit(solution)/shard_map/ppermute | solution.py:204
  30.9 30.6 %collective-permute-start.6 = (bf16[528,1024]{1,0:T(8,128)(2,1)S(1)}, bf16[528,1024]{1,0:T(8,128)(2,1)S(1)}, u32[]{:S(2)}, u32[]{:S(2)}) collective-permute-start(bf16[528,1024]{1,0:T(8,128)(2,1)S(1)} %collective-permute-done.2.refs_0_), channel_id=1, source_target_pairs={{2,0},{3,1},{4,6},{5,7},{10,8},{11,9},{12,14},{13,15},{18,16},{19,... | collective-permute-start | bytes 3244040 | tf_op jit(solution)/shard_map/ppermute | solution.py:201
  32.2 29.3 %collective-permute-start.5 = (bf16[528,1024]{1,0:T(8,128)(2,1)S(1)}, bf16[528,1024]{1,0:T(8,128)(2,1)S(1)}, u32[]{:S(2)}, u32[]{:S(2)}) collective-permute-start(bf16[528,1024]{1,0:T(8,128)(2,1)S(1)} %collective-permute-done.3.refs_0_), channel_id=1, source_target_pairs={{2,4},{3,5},{4,2},{5,3},{10,12},{11,13},{12,10},{13,11},{18,20},{1... | collective-permute-start | bytes 3244040 | tf_op jit(solution)/shard_map/ppermute | solution.py:201
  37.8 56.0 %slice-start = ((s8[4718592]{0:T(1024)(128)(4,1)}), s8[4194304]{0:T(1024)(128)(4,1)S(1)}, s32[]{:S(2)}) async-start(s8[4718592]{0:T(1024)(128)(4,1)} %bitcast.31), calls=%async_computation | async-start | bytes 8388608
  37.8 55.9 %slice-start.1 = ((s8[4718592]{0:T(1024)(128)(4,1)}), s8[524288]{0:T(1024)(128)(4,1)S(1)}, s32[]{:S(2)}) async-start(s8[4718592]{0:T(1024)(128)(4,1)} %bitcast.31), calls=%async_computation.1 | async-start | bytes 1048576
  37.8 23.7 %collective-permute-start.8 = (bf16[272,1024]{1,0:T(8,128)(2,1)S(1)}, bf16[272,1024]{1,0:T(8,128)(2,1)S(1)}, u32[]{:S(2)}, u32[]{:S(2)}) collective-permute-start(bf16[272,1024]{1,0:T(8,128)(2,1)S(1)} %get-tuple-element.64), channel_id=1, source_target_pairs={{0,1},{1,0},{2,3},{3,2},{4,5},{5,4},{6,7},{7,6},{8,9},{9,8},{10,11... | collective-permute-start | bytes 1671176 | tf_op jit(solution)/shard_map/ppermute | solution.py:204
  38.0 24.8 %collective-permute-start.4 = (bf16[528,1024]{1,0:T(8,128)(2,1)S(1)}, bf16[528,1024]{1,0:T(8,128)(2,1)S(1)}, u32[]{:S(2)}, u32[]{:S(2)}) collective-permute-start(bf16[528,1024]{1,0:T(8,128)(2,1)S(1)} %collective-permute-done.2.refs_0_), channel_id=1, source_target_pairs={{0,1},{1,0},{2,3},{3,2},{4,5},{5,4},{6,7},{7,6},{8,9},{9,8},{10,11... | collective-permute-start | bytes 3244040 | tf_op jit(solution)/shard_map/ppermute | solution.py:204
  61.5 2.7 %collective-permute-start.9 = (bf16[528,1024]{1,0:T(8,128)(2,1)S(1)}, bf16[528,1024]{1,0:T(8,128)(2,1)S(1)}, u32[]{:S(2)}, u32[]{:S(2)}) collective-permute-start(bf16[528,1024]{1,0:T(8,128)(2,1)S(1)} %collective-permute-done.6.refs_2_), channel_id=1, source_target_pairs={{0,1},{1,0},{2,3},{3,2},{4,5},{5,4},{6,7},{7,6},{8,9},{9,8},{10,11... | collective-permute-start | bytes 3244040 | tf_op jit(solution)/shard_map/ppermute | solution.py:204
  61.5 29.5 %collective-permute-start.14 = (bf16[528,1024]{1,0:T(8,128)(2,1)S(1)}, bf16[528,1024]{1,0:T(8,128)(2,1)S(1)}, u32[]{:S(2)}, u32[]{:S(2)}) collective-permute-start(bf16[528,1024]{1,0:T(8,128)(2,1)S(1)} %collective-permute-done.5.refs_0_), channel_id=1, source_target_pairs={{2,0},{3,1},{4,6},{5,7},{10,8},{11,9},{12,14},{13,15},{18,16},{19,... | collective-permute-start | bytes 3244040 | tf_op jit(solution)/shard_map/ppermute | solution.py:201
  68.8 22.2 %collective-permute-start.10 = (bf16[272,1024]{1,0:T(8,128)(2,1)S(1)}, bf16[272,1024]{1,0:T(8,128)(2,1)S(1)}, u32[]{:S(2)}, u32[]{:S(2)}) collective-permute-start(bf16[272,1024]{1,0:T(8,128)(2,1)S(1)} %get-tuple-element.67), channel_id=1, source_target_pairs={{0,1},{1,0},{2,3},{3,2},{4,5},{5,4},{6,7},{7,6},{8,9},{9,8},{10,11... | collective-permute-start | bytes 1671176 | tf_op jit(solution)/shard_map/ppermute | solution.py:204
  69.0 23.7 %collective-permute-start.13 = (bf16[528,1024]{1,0:T(8,128)(2,1)S(1)}, bf16[528,1024]{1,0:T(8,128)(2,1)S(1)}, u32[]{:S(2)}, u32[]{:S(2)}) collective-permute-start(bf16[528,1024]{1,0:T(8,128)(2,1)S(1)} %collective-permute-done.5.refs_0_), channel_id=1, source_target_pairs={{0,1},{1,0},{2,3},{3,2},{4,5},{5,4},{6,7},{7,6},{8,9},{9,8},{10,11... | collective-permute-start | bytes 3244040 | tf_op jit(solution)/shard_map/ppermute | solution.py:204
  91.0 2.7 %collective-permute-start.15 = (bf16[528,1024]{1,0:T(8,128)(2,1)S(1)}, bf16[528,1024]{1,0:T(8,128)(2,1)S(1)}, u32[]{:S(2)}, u32[]{:S(2)}) collective-permute-start(bf16[528,1024]{1,0:T(8,128)(2,1)S(1)} %collective-permute-done.14.refs_2_), channel_id=1, source_target_pairs={{0,1},{1,0},{2,3},{3,2},{4,5},{5,4},{6,7},{7,6},{8,9},{9,8},{10,11... | collective-permute-start | bytes 3244040 | tf_op jit(solution)/shard_map/ppermute | solution.py:204
  91.2 14.1 %collective-permute-start.11 = (bf16[272,1024]{1,0:T(8,128)(2,1)S(1)}, bf16[272,1024]{1,0:T(8,128)(2,1)S(1)}, u32[]{:S(2)}, u32[]{:S(2)}) collective-permute-start(bf16[272,1024]{1,0:T(8,128)(2,1)S(1)} %fusion), channel_id=1, source_target_pairs={{0,2},{1,3},{6,4},{7,5},{8,10},{9,11},{14,12},{15,13},{16,18},{17,... | collective-permute-start | bytes 1671176 | tf_op jit(solution)/shard_map/ppermute | solution.py:201
  98.2 9.7 %collective-permute-start.16 = (bf16[272,1024]{1,0:T(8,128)(2,1)S(1)}, bf16[272,1024]{1,0:T(8,128)(2,1)S(1)}, u32[]{:S(2)}, u32[]{:S(2)}) collective-permute-start(bf16[272,1024]{1,0:T(8,128)(2,1)S(1)} %get-tuple-element.72), channel_id=1, source_target_pairs={{0,1},{1,0},{2,3},{3,2},{4,5},{5,4},{6,7},{7,6},{8,9},{9,8},{10,11... | collective-permute-start | bytes 1671176 | tf_op jit(solution)/shard_map/ppermute | solution.py:204
  100.3 15.5 %collective-permute-start.24 = (bf16[2,1,256,384]{3,2,1,0:T(8,128)(2,1)S(1)}, bf16[2,1,256,384]{3,2,1,0:T(8,128)(2,1)S(1)}, u32[]{:S(2)}, u32[]{:S(2)}) collective-permute-start(bf16[2,1,256,384]{3,2,1,0:T(8,128)(2,1)S(1)} %get-tuple-element.114), channel_id=1, source_target_pairs={{0,8},{8,0},{16,24},{24,16},{1,9},{9,1},{17,25},{25,17},{2,10},{10... | collective-permute-start | bytes 1179656 | tf_op jit(solution)/shard_map/ppermute | solution.py:273
  105.6 48.4 %collective-permute-start.12 = (bf16[272,1024]{1,0:T(8,128)(2,1)S(1)}, bf16[272,1024]{1,0:T(8,128)(2,1)S(1)}, u32[]{:S(2)}, u32[]{:S(2)}) collective-permute-start(bf16[272,1024]{1,0:T(8,128)(2,1)S(1)} %add_convert_fusion.3), channel_id=1, source_target_pairs={{2,4},{3,5},{4,2},{5,3},{10,12},{11,13},{12,10},{13,11},{18,20},{1... | collective-permute-start | bytes 1671176 | tf_op jit(solution)/shard_map/ppermute | solution.py:201
  106.3 15.2 %collective-permute-start.26 = (bf16[2,1,256,384]{3,2,1,0:T(8,128)(2,1)S(1)}, bf16[2,1,256,384]{3,2,1,0:T(8,128)(2,1)S(1)}, u32[]{:S(2)}, u32[]{:S(2)}) collective-permute-start(bf16[2,1,256,384]{3,2,1,0:T(8,128)(2,1)S(1)} %get-tuple-element.116), channel_id=1, source_target_pairs={{0,16},{8,24},{16,0},{24,8},{1,17},{9,25},{17,1},{25,9},{2,18},{10... | collective-permute-start | bytes 1179656 | tf_op jit(solution)/shard_map/ppermute | solution.py:273
  108.1 18.6 %collective-permute-start.17 = (bf16[272,1024]{1,0:T(8,128)(2,1)S(1)}, bf16[272,1024]{1,0:T(8,128)(2,1)S(1)}, u32[]{:S(2)}, u32[]{:S(2)}) collective-permute-start(bf16[272,1024]{1,0:T(8,128)(2,1)S(1)} %fusion.1), channel_id=1, source_target_pairs={{0,2},{1,3},{6,4},{7,5},{8,10},{9,11},{14,12},{15,13},{16,18},{17,... | collective-permute-start | bytes 1671176 | tf_op jit(solution)/shard_map/ppermute | solution.py:201
  115.8 6.4 %collective-permute-start.25 = (bf16[1,256,384]{2,1,0:T(8,128)(2,1)S(1)}, bf16[1,256,384]{2,1,0:T(8,128)(2,1)S(1)}, u32[]{:S(2)}, u32[]{:S(2)}) collective-permute-start(bf16[1,256,384]{2,1,0:T(8,128)(2,1)S(1)} %fusion.8), channel_id=1, source_target_pairs={{0,16},{8,24},{16,0},{24,8},{1,17},{9,25},{17,1},{25,9},{2,18},{10... | collective-permute-start | bytes 589832 | tf_op jit(solution)/shard_map/ppermute | solution.py:273
  120.0 22.5 %collective-permute-start.20 = (bf16[2,2,256,384]{3,2,1,0:T(8,128)(2,1)S(1)}, bf16[2,2,256,384]{3,2,1,0:T(8,128)(2,1)S(1)}, u32[]{:S(2)}, u32[]{:S(2)}) collective-permute-start(bf16[2,2,256,384]{3,2,1,0:T(8,128)(2,1)S(1)} %get-tuple-element.102), channel_id=1, source_target_pairs={{0,8},{8,0},{16,24},{24,16},{1,9},{9,1},{17,25},{25,17},{2,10},{10... | collective-permute-start | bytes 2359304 | tf_op jit(solution)/shard_map/ppermute | solution.py:273
  121.6 20.8 %collective-permute-start.27 = (bf16[1,256,384]{2,1,0:T(8,128)(2,1)S(1)}, bf16[1,256,384]{2,1,0:T(8,128)(2,1)S(1)}, u32[]{:S(2)}, u32[]{:S(2)}) collective-permute-start(bf16[1,256,384]{2,1,0:T(8,128)(2,1)S(1)} %fusion.9), channel_id=1, source_target_pairs={{0,8},{8,0},{16,24},{24,16},{1,9},{9,1},{17,25},{25,17},{2,10},{10... | collective-permute-start | bytes 589832 | tf_op jit(solution)/shard_map/ppermute | solution.py:273
  122.2 21.9 %collective-permute-start.22 = (bf16[2,2,256,384]{3,2,1,0:T(8,128)(2,1)S(1)}, bf16[2,2,256,384]{3,2,1,0:T(8,128)(2,1)S(1)}, u32[]{:S(2)}, u32[]{:S(2)}) collective-permute-start(bf16[2,2,256,384]{3,2,1,0:T(8,128)(2,1)S(1)} %get-tuple-element.104), channel_id=1, source_target_pairs={{0,16},{8,24},{16,0},{24,8},{1,17},{9,25},{17,1},{25,9},{2,18},{10... | collective-permute-start | bytes 2359304 | tf_op jit(solution)/shard_map/ppermute | solution.py:273
  127.0 18.8 %collective-permute-start.18 = (bf16[272,1024]{1,0:T(8,128)(2,1)S(1)}, bf16[272,1024]{1,0:T(8,128)(2,1)S(1)}, u32[]{:S(2)}, u32[]{:S(2)}) collective-permute-start(bf16[272,1024]{1,0:T(8,128)(2,1)S(1)} %add_convert_fusion.2), channel_id=1, source_target_pairs={{2,4},{3,5},{4,2},{5,3},{10,12},{11,13},{12,10},{13,11},{18,20},{1... | collective-permute-start | bytes 1671176 | tf_op jit(solution)/shard_map/ppermute | solution.py:201
  142.5 8.8 %collective-permute-start.21 = (bf16[2,256,384]{2,1,0:T(8,128)(2,1)S(1)}, bf16[2,256,384]{2,1,0:T(8,128)(2,1)S(1)}, u32[]{:S(2)}, u32[]{:S(2)}) collective-permute-start(bf16[2,256,384]{2,1,0:T(8,128)(2,1)S(1)} %fusion.4), channel_id=1, source_target_pairs={{0,16},{8,24},{16,0},{24,8},{1,17},{9,25},{17,1},{25,9},{2,18},{10... | collective-permute-start | bytes 1179656 | tf_op jit(solution)/shard_map/ppermute | solution.py:273
  144.2 8.5 %collective-permute-start.23 = (bf16[2,256,384]{2,1,0:T(8,128)(2,1)S(1)}, bf16[2,256,384]{2,1,0:T(8,128)(2,1)S(1)}, u32[]{:S(2)}, u32[]{:S(2)}) collective-permute-start(bf16[2,256,384]{2,1,0:T(8,128)(2,1)S(1)} %fusion.5), channel_id=1, source_target_pairs={{0,8},{8,0},{16,24},{24,16},{1,9},{9,1},{17,25},{25,17},{2,10},{10... | collective-permute-start | bytes 1179656 | tf_op jit(solution)/shard_map/ppermute | solution.py:273
  146.1 11.8 %collective-permute-start.19 = (bf16[272,1024]{1,0:T(8,128)(2,1)S(1)}, bf16[272,1024]{1,0:T(8,128)(2,1)S(1)}, u32[]{:S(2)}, u32[]{:S(2)}) collective-permute-start(bf16[272,1024]{1,0:T(8,128)(2,1)S(1)} %add_convert_fusion.1), channel_id=1, source_target_pairs={{0,2},{1,3},{2,0},{3,1},{4,6},{5,7},{6,4},{7,5},{8,10},{9,11},{10,... | collective-permute-start | bytes 1671176 | tf_op jit(solution)/shard_map/ppermute | solution.py:201

commit v3 on v2

--- a/solution.py
+++ b/solution.py
@@ -134,11 +134,42 @@
     )(*operands, weights)
 
 
-def weight_kernel(products, pieces, *refs):
-    a_send, a_keep, b_send, b_keep = refs[2 * pieces * products :]
+def partial_kernel(pieces, *refs):
+    operands, out = refs[:-1], refs[-1]
+    quarter = out.shape[1] // 4
+    for at in range(0, out.shape[1], quarter):
+        for product in range(out.shape[0]):
+            group = operands[2 * pieces * product : 2 * pieces * (product + 1)]
+            total = None
+            for left, right in zip(group[:pieces], group[pieces:]):
+                term = dot(left[:, at : at + quarter], right[...], FIRST)
+                total = term if total is None else total + term
+            out[product, at : at + quarter, :] = total
+
+
+def run_partial(products):
+    lefts, rights = products[0]
+    operands = [array for pair in products for group in pair for array in group]
+    whole = pl.BlockSpec(memory_space=pltpu.VMEM)
+    shape = (len(products), lefts[0].shape[1], rights[0].shape[1])
+    return pl.pallas_call(
+        functools.partial(partial_kernel, len(lefts)),
+        out_shape=jax.ShapeDtypeStruct(shape, F32),
+        in_specs=[whole] * len(operands),
+        out_specs=whole,
+        compiler_params=pltpu.CompilerParams(vmem_limit_bytes=24 * 1024 * 1024),
+        cost_estimate=pl.CostEstimate(flops=1, bytes_accessed=1, transcendentals=0),
+        name="partial_weights",
+    )(*operands)
+
+
+def weight_kernel(*refs):
+    operands = refs[:-5]
+    partial, a_send, a_keep, b_send, b_keep = refs[-5:]
     here = lax.axis_index("dp")
-    quarter = refs[0].shape[1] // 4
-    half = refs[pieces].shape[1] // 2
+    products, width, hidden_width = partial.shape
+    quarter = width // 4
+    half = hidden_width // 2
     places = (
         (3, a_send, 0, b_send, 0),
         (1, a_send, 1, b_keep, 0),
@@ -146,33 +177,28 @@
         (0, a_keep, 1, b_keep, 1),
     )
     for place, a_out, a_at, b_out, b_at in places:
-        at = pl.multiple_of((here ^ place) * quarter, quarter)
+        rows = pl.ds(pl.multiple_of((here ^ place) * quarter, quarter), quarter)
         for product in range(products):
-            group = refs[2 * pieces * product : 2 * pieces * (product + 1)]
-            total = None
-            for left, right in zip(group[:pieces], group[pieces:]):
-                term = dot(left[:, pl.ds(at, quarter)], right[...], FIRST)
-                total = term if total is None else total + term
-            value = total.astype(BF16)
+            left, right = operands[2 * product : 2 * product + 2]
+            value = (partial[product, rows, :] + dot(left[:, rows], right[...], FIRST)).astype(BF16)
             a_out[a_at, product] = value[:, :half]
             b_out[b_at, product] = value[:, half:]
 
 
-def run_weight(*products):
-    lefts, rights = products[0]
-    width = lefts[0].shape[1]
-    hidden_width = rights[0].shape[1]
-    piece = jax.ShapeDtypeStruct((2, len(products), width // 4, hidden_width // 2), BF16)
-    operands = [array for pair in products for group in pair for array in group]
+def run_weight(products, partial):
+    count, width, hidden_width = partial.shape
+    piece = jax.ShapeDtypeStruct((2, count, width // 4, hidden_width // 2), BF16)
+    operands = [array for pair in products for array in pair]
+    whole = pl.BlockSpec(memory_space=pltpu.VMEM)
     return pl.pallas_call(
-        functools.partial(weight_kernel, len(products), len(lefts)),
+        weight_kernel,
         out_shape=[piece] * 4,
-        in_specs=[pl.BlockSpec(memory_space=pltpu.VMEM)] * len(operands),
-        out_specs=[pl.BlockSpec(memory_space=pltpu.VMEM)] * 4,
+        in_specs=[whole] * (len(operands) + 1),
+        out_specs=[whole] * 4,
         compiler_params=pltpu.CompilerParams(vmem_limit_bytes=24 * 1024 * 1024),
         cost_estimate=pl.CostEstimate(flops=1, bytes_accessed=1, transcendentals=0),
         name="weight_block",
-    )(*operands)
+    )(*operands, partial)
 
 
 def add(*values):
@@ -182,8 +208,121 @@
     return total.astype(BF16)
 
 
+def final_kernel(a_keep, a_came, a_last, b_keep, b_came, b_last, out):
+    half = out.shape[2] // 2
+    out[:, :, :half] = (
+        a_keep[1].astype(F32) + a_came[1].astype(F32) + a_last[...].astype(F32)
+    ).astype(BF16)
+    out[:, :, half:] = (
+        b_keep[1].astype(F32) + b_came[1].astype(F32) + b_last[...].astype(F32)
+    ).astype(BF16)
+
+
+def run_final(*operands):
+    products, rows, half = operands[2].shape
+    whole = pl.BlockSpec(memory_space=pltpu.VMEM)
+    return pl.pallas_call(
+        final_kernel,
+        out_shape=jax.ShapeDtypeStruct((products, rows, 2 * half), BF16),
+        in_specs=[whole] * 6,
+        out_specs=whole,
+        compiler_params=pltpu.CompilerParams(vmem_limit_bytes=12 * 1024 * 1024),
+        cost_estimate=pl.CostEstimate(flops=1, bytes_accessed=1, transcendentals=0),
+        name="final_step",
+    )(*operands)
+
+
+def payload_kernel(tokens, cotangent, ids_hbm, gates_hbm, out, ids, gates, sems):
+    count = tokens.shape[0]
+    copies = [
+        pltpu.make_async_copy(ids_hbm, ids, sems.at[2]),
+        pltpu.make_async_copy(gates_hbm, gates, sems.at[3]),
+        pltpu.make_async_copy(tokens, out.at[:count], sems.at[0]),
+        pltpu.make_async_copy(cotangent, out.at[count + META :], sems.at[1]),
+    ]
+    for copy in copies:
+        copy.start()
+    copies[0].wait()
+    copies[1].wait()
+    line = lax.broadcasted_iota(jnp.int32, (META, count), 0)
+    routing = jnp.zeros((META, count), F32)
+    rows = (
+        ids[0:1, :].astype(F32) + 1.0,
+        ids[1:2, :].astype(F32) + 1.0,
+        gates[0:1, :].astype(F32),
+        gates[1:2, :].astype(F32),
+    )
+    for number, row in enumerate(rows):
+        routing = jnp.where(line == number, row, routing)
+    out[count : count + META, :] = jnp.zeros((META, out.shape[1]), BF16)
+    out[count : count + META, :count] = routing.astype(BF16)
+    copies[2].wait()
+    copies[3].wait()
+
+
+def make_payload(tokens, cotangent, gates, expert_ids):
+    count, width = tokens.shape
+    whole = pl.BlockSpec(memory_space=pltpu.VMEM)
+    return pl.pallas_call(
+        payload_kernel,
+        out_shape=jax.ShapeDtypeStruct((2 * count + META, width), BF16),
+        in_specs=[pl.BlockSpec(memory_space=pltpu.HBM)] * 4,
+        out_specs=whole,
+        scratch_shapes=[
+            pltpu.VMEM((2, count), jnp.int32),
+            pltpu.VMEM((2, count), BF16),
+            pltpu.SemaphoreType.DMA((4,)),
+        ],
+        compiler_params=pltpu.CompilerParams(vmem_limit_bytes=4 * 1024 * 1024),
+        cost_estimate=pl.CostEstimate(flops=1, bytes_accessed=1, transcendentals=0),
+        name="payload",
+    )(tokens, cotangent, expert_ids.T, gates.T)
+
+
+def total_kernel(parts, *refs):
+    values, (tokens_out, gates_out) = refs[:parts], refs[parts:]
+    count = tokens_out.shape[0]
+    total = values[0][...].astype(F32)
+    for value in values[1:]:
+        total = total + value[...].astype(F32)
+    tokens_out[...] = total[:count].astype(BF16)
+    gates_out[...] = total[count : count + META, :count].astype(BF16)[:2]
+
+
+def split_total(values, count):
+    width = values[0].shape[1]
+    whole = pl.BlockSpec(memory_space=pltpu.VMEM)
+    tokens_grad, gates_grad = pl.pallas_call(
+        functools.partial(total_kernel, len(values)),
+        out_shape=[
+            jax.ShapeDtypeStruct((count, width), BF16),
+            jax.ShapeDtypeStruct((2, count), BF16),
+        ],
+        in_specs=[whole] * len(values),
+        out_specs=[whole] * 2,
+        compiler_params=pltpu.CompilerParams(vmem_limit_bytes=8 * 1024 * 1024),
+        cost_estimate=pl.CostEstimate(flops=1, bytes_accessed=1, transcendentals=0),
+        name="total",
+    )(*values)
+    return tokens_grad, gates_grad.T
+
+
 def after(value, *earlier):
     return lax.optimization_barrier((value, earlier))[0]
+
+
+def products_of(rows):
+    xr, q, h, da, db = rows
+    return (xr, da), (xr, db), (q, h)
+
+
+def sum_early(kept):
+    return run_partial(
+        [
+            (tuple(pair[0] for pair in pairs), tuple(pair[1] for pair in pairs))
+            for pairs in zip(*[products_of(rows) for rows in kept])
+        ]
+    )
 
 
 def on_device(tokens, cotangent, gates, expert_ids, expert_weights):
@@ -192,9 +331,7 @@
     count, width = tokens.shape
     batch = count // MICRO
     capacity = 4 * batch // devices
-    routing = jnp.concatenate([(expert_ids + 1).astype(BF16).T, gates.T], axis=0)
-    routing = jnp.pad(routing, ((0, META - 4), (0, width - count)))
-    own = jnp.concatenate([tokens, routing, cotangent], axis=0)
+    own = make_payload(tokens, cotangent, gates, expert_ids)
 
     def move(value, pairs):
         full = [(a * CORES + k, b * CORES + k) for a, b in pairs for k in range(CORES)]
@@ -233,17 +370,18 @@
         rows, grads = compute((second, swap(second)), (third, swap(third)))
         kept.append(rows)
         third_sum = joined(grads)
-        came = move(add(*third_sum), from_ends)
-        fifth = after(fifth, third_sum[1])
-        third_back = move(add(*third_sum, came), inner)
+        partial = sum_early(kept)
+        fifth = after(fifth, third_sum[1], partial)
         rows, grads = compute((fourth, swap(fourth)), (fifth, swap(fifth)))
         kept.append(rows)
         fourth_sum = joined(grads)
-        back = sent = add(*fourth_sum)
-        back = add(*fourth_sum, move(back, from_ends))
-        back = add(*first_sum, move(back, inner))
-        back = move(back, outer)
-        total = add(*own_sum, third_back, back)
+        sent = add(*fourth_sum)
+        landed = move(sent, from_ends)
+        came = move(after(add(*third_sum), landed), from_ends)
+        landed = move(add(*fourth_sum, landed), inner)
+        third_back = move(after(add(*third_sum, came), landed), inner)
+        back = move(add(*first_sum, landed), outer)
+        total = [*own_sum, third_back, back]
     else:
         rows, grads = compute((own, swap(own)))
         kept = [rows]
@@ -262,31 +400,22 @@
                 value = move(add(*pair) if value is None else add(*pair, value), back)
             if value is not None:
                 total.append(value)
-        total = add(*total)
-    tokens_grad = total[:count]
-    gates_grad = total[count : count + 2, :count].T
-
-    xr, q, h, da, db = zip(*kept)
+        partial = sum_early(kept[:-1])
+    tokens_grad, gates_grad = split_total(total, count)
+
     if lax.axis_size("dp") == 4:
 
         def across(value, bit):
             return lax.ppermute(value, "dp", [(i, i ^ bit) for i in range(4)])
 
-        ends = []
-        for group in ([(q, h)], after([(xr, da), (xr, db)], sent)):
-            a_send, a_keep, b_send, b_keep = run_weight(*group)
-            a_came = across(a_send, 1)
-            b_came = across(b_send, 2)
-            a_last = across(add(a_keep[0], a_came[0]), 2)
-            b_last = across(add(b_keep[0], b_came[0]), 1)
-            ends.append(
-                jnp.concatenate(
-                    [add(a_keep[1], a_came[1], a_last), add(b_keep[1], b_came[1], b_last)], axis=-1
-                )
-            )
-        weights_grad = jnp.concatenate([ends[1], ends[0]], axis=0)[None]
+        a_send, a_keep, b_send, b_keep = run_weight(products_of(kept[-1]), partial)
+        a_came = across(a_send, 1)
+        b_came = across(b_send, 2)
+        a_last = across(add(a_keep[0], a_came[0]), 2)
+        b_last = across(add(b_keep[0], b_came[0]), 1)
+        weights_grad = run_final(a_keep, a_came, a_last, b_keep, b_came, b_last)[None]
     else:
-        whole = [jnp.concatenate(value, axis=0) for value in (xr, q, h, da, db)]
+        whole = [jnp.concatenate(value, axis=0) for value in zip(*kept)]
         partial = jnp.stack(
             [
                 dot(whole[0], whole[3], FIRST),

time: 160 us -> 153 us (0.956); the launches traced: 160 us -> 150 us
  waiting for transfers between devices: 94 us -> 87.8 us
  other arithmetic: 6.15 us -> 1.54 us
  starting transfers between devices: 32 us -> 28.6 us
  Pallas kernels: 22.9 us -> 25.6 us
  local copies, waits for them, and re-layouts: 3.74 us -> 5.78 us
    ppermute x8 -> x4, starting transfers between devices: 10.5 us -> 4.86 us  [across(): return lax.ppermute(value, 'dp', [(i, i ^ bit) for i in range(4)])]
    ppermute x8 -> x4, waiting for transfers between devices: 19 us -> 13.7 us  [across(): return lax.ppermute(value, 'dp', [(i, i ^ bit) for i in range(4)])]
    unnamed x6 -> x12, local copies, waits for them, and re-layouts: 2.34 us -> 5.78 us
    ppermute x10, waiting for transfers between devices: 72 us -> 69.3 us  [move(): return lax.ppermute(value, 'expert', full)]
    pallas_call x2 -> x5, Pallas kernels: 5.46 us -> 8.05 us  [the longest x1 3.89 us: run_partial(): pl.pallas_call(functools.partial(partial_kernel, len(lefts)), out_shape=j...]
    ppermute x10, starting transfers between devices: 19.3 us -> 21.7 us  [move(): return lax.ppermute(value, 'expert', full)]
    concatenate x2 -> x0, other arithmetic: 1.96 us -> none  [the longest x1 1.27 us: on_device(): own = jnp.concatenate([tokens, routing, cotangent], axis=0)]
    ppermute x10, waiting for transfers between devices: 3.06 us -> 4.8 us  [swap(): return lax.ppermute(value, 'expert', [(i, i ^ 1) for i in range(devices)])]
  transfers between devices with their start and end apart: 28 -> 24, of which waited for: 12 -> 12; matrix products, arithmetic and copies ran while one was open for 2% -> 1% of each run, Pallas kernels for 14% -> 13%
where the time goes in v3:
time: 153 us; the launch traced here: 150 us
  waiting for transfers between devices  87.8 us (57%)
  starting transfers between devices  28.6 us (19%)
  Pallas kernels  25.6 us (17%)
  local copies, waits for them, and re-layouts  5.78 us (4%)
  other arithmetic  1.54 us (1%)
    ppermute x10, waiting for transfers between devices, move(): return lax.ppermute(value, 'expert', full)  69.3 us
    ppermute x10, starting transfers between devices, move(): return lax.ppermute(value, 'expert', full)  21.7 us
    pallas_call x4, Pallas kernels, run_slot(): pl.pallas_call(functools.partial(slot_kernel, choices, batch, capacity, m...  17.6 us
    ppermute x4, waiting for transfers between devices, across(): return lax.ppermute(value, 'dp', [(i, i ^ bit) for i in range(4)])  13.7 us
    unnamed x12, local copies, waits for them, and re-layouts  5.78 us
    ppermute x4, starting transfers between devices, across(): return lax.ppermute(value, 'dp', [(i, i ^ bit) for i in range(4)])  4.86 us
    ppermute x10, waiting for transfers between devices, swap(): return lax.ppermute(value, 'expert', [(i, i ^ 1) for i in range(devices)])  4.8 us
    pallas_call x1, Pallas kernels, run_partial(): pl.pallas_call(functools.partial(partial_kernel, len(lefts)), out_shape=j...  3.89 us
  transfers between devices with their start and end apart: 24, of which 12 were waited for; matrix products, arithmetic and copies ran while one was open for 1% of the time, Pallas kernels for 13%

profile of v3, /device:TPU:0, one launch (start us, length us, event | category | flops | bytes accessed | tf_op | source)
XLA Modules:
  0.0 150.2 jit_solution(1788161453255260966)
XLA Ops:
  0.6 1.0 copy-done.2
  1.7 1.0 copy-done.3
  5.5 5.4 %collective-permute-start.3 = (bf16[528,1024]{1,0:T(8,128)(2,1)S(1)}, bf16[528,1024]{1,0:T(8,128)(2,1)S(1)}, u32[]{:S(2)}, u32[]{:S(2)}) collective-permute-start(bf16[528,1024]{1,0:T(8,128)(2,1)S(1)} %payload.1.refs_0_), channel_id=1, source_target_pairs={{0,2},{1,3},{2,0},{3,1},{4,6},{5,7},{6,4},{7,5},{8,10},{9,11},{10,... | collective-permute-start | bytes 3244040 | tf_op jit(solution)/shard_map/ppermute | solution.py:338
  10.9 2.3 %copy-done = bf16[1,3,1024,768]{3,2,1,0:T(8,128)(2,1)S(1)} copy-done((bf16[1,3,1024,768]{3,2,1,0:T(8,128)(2,1)S(1)}, bf16[1,3,1024,768]{3,2,1,0:T(8,128)(2,1)}, u32[]{:S(2)}) %copy-start) | copy-done | bytes 4718616
  13.2 4.2 %expert_block.4 = (bf16[256,1024]{1,0:T(8,128)(2,1)S(1)}, bf16[256,1024]{1,0:T(8,128)(2,1)S(1)}, bf16[256,768]{1,0:T(8,128)(2,1)S(1)}, bf16[256,768]{1,0:T(8,128...) custom-call(bf16[528,1024]{1,0:T(8,128)(2,1)S(1)} %payload.1.refs_0_, ...), custom_call_target="tpu_custom_call" | custom-call | flops 1 | bytes 1 | tf_op jit(solution)/shard_map/expert_block/pallas_call | solution.py:114
  17.5 17.6 %collective-permute-done.3.refs_0_ = bf16[528,1024]{1,0:T(8,128)(2,1)S(1)} collective-permute-done((bf16[528,1024]{1,0:T(8,128)(2,1)S(1)}, bf16[528,1024]{1,0:T(8,128)(2,1)S(1)}, u32[]{:S(2)}, u32[]{:S(2)}) %collective-permute-start.3) | collective-permute-done | bytes 1081376 | tf_op jit(solution)/shard_map/ppermute | solution.py:338
  35.1 0.7 collective-permute-start.5
  35.8 1.3 collective-permute-start.6
  37.8 4.2 %expert_block.5 = (bf16[256,1024]{1,0:T(8,128)(2,1)S(1)}, bf16[256,1024]{1,0:T(8,128)(2,1)S(1)}, bf16[256,768]{1,0:T(8,128)(2,1)S(1)}, bf16[256,768]{1,0:T(8,128...) custom-call(bf16[528,1024]{1,0:T(8,128)(2,1)S(1)} %collective-permute-done.3., ...), custom_call_target="tpu_custom_call" | custom-call | flops 1 | bytes 1 | tf_op jit(solution)/shard_map/expert_block/pallas_call | solution.py:114
  42.6 22.2 %collective-permute-done.6.refs_2_ = bf16[528,1024]{1,0:T(8,128)(2,1)S(1)} collective-permute-done((bf16[528,1024]{1,0:T(8,128)(2,1)S(1)}, bf16[528,1024]{1,0:T(8,128)(2,1)S(1)}, u32[]{:S(2)}, u32[]{:S(2)}) %collective-permute-start.6) | collective-permute-done | bytes 1081376 | tf_op jit(solution)/shard_map/ppermute | solution.py:338
  64.7 1.3 collective-permute-start.12
  66.0 1.4 collective-permute-done.9.refs_3_
  67.4 4.6 %expert_block.6 = (bf16[256,1024]{1,0:T(8,128)(2,1)S(1)}, bf16[256,1024]{1,0:T(8,128)(2,1)S(1)}, bf16[256,768]{1,0:T(8,128)(2,1)S(1)}, bf16[256,768]{1,0:T(8,128...) custom-call(bf16[528,1024]{1,0:T(8,128)(2,1)S(1)} %collective-permute-done.2., ...), custom_call_target="tpu_custom_call" | custom-call | flops 1 | bytes 1 | tf_op jit(solution)/shard_map/expert_block/pallas_call | solution.py:114
  72.7 3.9 %partial_weights.1.refs_6_ = f32[3,1024,768]{2,1,0:T(8,128)S(1)} custom-call(bf16[256,1024]{1,0:T(8,128)(2,1)S(1)} %get-tuple-element.53.refs_0_.refs_6_, bf16[256,1024]{1,0:T(8,128)(2,1)S(1)} %get-tuple-element.54.refs_1_.refs_7_, bf16[256,1024]{1,0:T(8,128)(2,1)S(1)} %get-tuple-element.55.refs_2_.refs_8_, bf16[256,768]{1,0:T(8,128)(2,1)S(1)} %get-tuple-element.56.refs_3_, ...), custom_call_target="tpu_custom_call" | custom-call | flops 1 | bytes 1 | tf_op jit(solution)/shard_map/partial_weights/pallas_call | solution.py:155
  76.5 16.3 %collective-permute-done.12.refs_2_ = bf16[528,1024]{1,0:T(8,128)(2,1)S(1)} collective-permute-done((bf16[528,1024]{1,0:T(8,128)(2,1)S(1)}, bf16[528,1024]{1,0:T(8,128)(2,1)S(1)}, u32[]{:S(2)}, u32[]{:S(2)}) %collective-permute-start.12) | collective-permute-done | bytes 1081376 | tf_op jit(solution)/shard_map/ppermute | solution.py:338
  92.9 2.7 %collective-permute-done.13.refs_3_ = bf16[528,1024]{1,0:T(8,128)(2,1)S(1)} collective-permute-done((bf16[528,1024]{1,0:T(8,128)(2,1)S(1)}, bf16[528,1024]{1,0:T(8,128)(2,1)S(1)}, u32[]{:S(2)}, u32[]{:S(2)}) %collective-permute-start.13) | collective-permute-done | bytes 1081376 | tf_op jit(solution)/shard_map/ppermute | solution.py:341
  95.6 4.7 %expert_block.7 = (bf16[256,1024]{1,0:T(8,128)(2,1)S(1)}, bf16[256,1024]{1,0:T(8,128)(2,1)S(1)}, bf16[256,768]{1,0:T(8,128)(2,1)S(1)}, bf16[256,768]{1,0:T(8,128...) custom-call(bf16[528,1024]{1,0:T(8,128)(2,1)S(1)} %collective-permute-done.5., ...), custom_call_target="tpu_custom_call" | custom-call | flops 1 | bytes 1 | tf_op jit(solution)/shard_map/expert_block/pallas_call | solution.py:114
  100.5 1.5 %weight_block.1 = (bf16[2,3,256,384]{3,2,1,0:T(8,128)(2,1)S(1)}, bf16[2,3,256,384]{3,2,1,0:T(8,128)(2,1)S(1)}, bf16[2,3,256,384]{3,2,1,0:T(8,128)(2,1)S(1)}, bf16[2,3,256,384]{3,2,1,0:T(8,128)(2,1)S(1)}) custom-call(bf16[256,1024]{1,0:T(8,128)(2,1)S(1)} %get-tuple-element.76.refs_0_.refs_2_, bf16[256,768]{1,0:T(8,128)(2,1)S(1)} %get-tuple-element.77.refs_1_, ...), custom_call_target="tpu_custom_call" | custom-call | flops 1 | bytes 1 | tf_op jit(solution)/shard_map/weight_block/pallas_call | solution.py:193
  102.0 1.6 %collective-permute-start.22 = (bf16[2,3,256,384]{3,2,1,0:T(8,128)(2,1)S(1)}, bf16[2,3,256,384]{3,2,1,0:T(8,128)(2,1)S(1)}, u32[]{:S(2)}, u32[]{:S(2)}) collective-permute-start(bf16[2,3,256,384]{3,2,1,0:T(8,128)(2,1)S(1)} %get-tuple-element.84), channel_id=1, source_target_pairs={{0,16},{8,24},{16,0},{24,8},{1,17},{9,25},{17,1},{25,9},{2,18},{10... | collective-permute-start | bytes 3538952 | tf_op jit(solution)/shard_map/ppermute | solution.py:409
  103.8 1.5 collective-permute-start.15
  105.3 1.5 %collective-permute-start.20 = (bf16[2,3,256,384]{3,2,1,0:T(8,128)(2,1)S(1)}, bf16[2,3,256,384]{3,2,1,0:T(8,128)(2,1)S(1)}, u32[]{:S(2)}, u32[]{:S(2)}) collective-permute-start(bf16[2,3,256,384]{3,2,1,0:T(8,128)(2,1)S(1)} %get-tuple-element.82), channel_id=1, source_target_pairs={{0,8},{8,0},{16,24},{24,16},{1,9},{9,1},{17,25},{25,17},{2,10},{10... | collective-permute-start | bytes 3538952 | tf_op jit(solution)/shard_map/ppermute | solution.py:409
  106.9 10.7 %collective-permute-done.15 = bf16[272,1024]{1,0:T(8,128)(2,1)S(1)} collective-permute-done((bf16[272,1024]{1,0:T(8,128)(2,1)S(1)}, bf16[272,1024]{1,0:T(8,128)(2,1)S(1)}, u32[]{:S(2)}, u32[]{:S(2)}) %collective-permute-start.15) | collective-permute-done | bytes 557088 | tf_op jit(solution)/shard_map/ppermute | solution.py:338
  118.7 7.2 %collective-permute-start.16 = (bf16[272,1024]{1,0:T(8,128)(2,1)S(1)}, bf16[272,1024]{1,0:T(8,128)(2,1)S(1)}, u32[]{:S(2)}, u32[]{:S(2)}) collective-permute-start(bf16[272,1024]{1,0:T(8,128)(2,1)S(1)} %fusion), channel_id=1, source_target_pairs={{0,2},{1,3},{6,4},{7,5},{8,10},{9,11},{14,12},{15,13},{16,18},{17,... | collective-permute-start | bytes 1671176 | tf_op jit(solution)/shard_map/ppermute | solution.py:338
  125.9 4.4 %collective-permute-done.22.b_came = bf16[2,3,256,384]{3,2,1,0:T(8,128)(2,1)S(1)} collective-permute-done((bf16[2,3,256,384]{3,2,1,0:T(8,128)(2,1)S(1)}, bf16[2,3,256,384]{3,2,1,0:T(8,128)(2,1)S(1)}, u32[]{:S(2)}, u32[]{:S(2)}) %collective-permute-start.22) | collective-permute-done | bytes 1179680 | tf_op jit(solution)/shard_map/ppermute | solution.py:409
  130.5 1.5 %collective-permute-start.23 = (bf16[3,256,384]{2,1,0:T(8,128)(2,1)S(1)}, bf16[3,256,384]{2,1,0:T(8,128)(2,1)S(1)}, u32[]{:S(2)}, u32[]{:S(2)}) collective-permute-start(bf16[3,256,384]{2,1,0:T(8,128)(2,1)S(1)} %fusion.3), channel_id=1, source_target_pairs={{0,8},{8,0},{16,24},{24,16},{1,9},{9,1},{17,25},{25,17},{2,10},{10... | collective-permute-start | bytes 1769480 | tf_op jit(solution)/shard_map/ppermute | solution.py:409
  132.0 1.6 %collective-permute-done.20.a_came = bf16[2,3,256,384]{3,2,1,0:T(8,128)(2,1)S(1)} collective-permute-done((bf16[2,3,256,384]{3,2,1,0:T(8,128)(2,1)S(1)}, bf16[2,3,256,384]{3,2,1,0:T(8,128)(2,1)S(1)}, u32[]{:S(2)}, u32[]{:S(2)}) %collective-permute-start.20) | collective-permute-done | bytes 1179680 | tf_op jit(solution)/shard_map/ppermute | solution.py:409
  134.2 2.2 %collective-permute-start.19 = (bf16[272,1024]{1,0:T(8,128)(2,1)S(1)}, bf16[272,1024]{1,0:T(8,128)(2,1)S(1)}, u32[]{:S(2)}, u32[]{:S(2)}) collective-permute-start(bf16[272,1024]{1,0:T(8,128)(2,1)S(1)} %add_convert_fusion.2), channel_id=1, source_target_pairs={{0,2},{1,3},{2,0},{3,1},{4,6},{5,7},{6,4},{7,5},{8,10},{9,11},{10,... | collective-permute-start | bytes 1671176 | tf_op jit(solution)/shard_map/ppermute | solution.py:338
  136.4 2.5 %collective-permute-done.16 = bf16[272,1024]{1,0:T(8,128)(2,1)S(1)} collective-permute-done((bf16[272,1024]{1,0:T(8,128)(2,1)S(1)}, bf16[272,1024]{1,0:T(8,128)(2,1)S(1)}, u32[]{:S(2)}, u32[]{:S(2)}) %collective-permute-start.16) | collective-permute-done | bytes 557088 | tf_op jit(solution)/shard_map/ppermute | solution.py:338
  140.0 5.9 %collective-permute-done.23.b_last = bf16[3,256,384]{2,1,0:T(8,128)(2,1)S(1)} collective-permute-done((bf16[3,256,384]{2,1,0:T(8,128)(2,1)S(1)}, bf16[3,256,384]{2,1,0:T(8,128)(2,1)S(1)}, u32[]{:S(2)}, u32[]{:S(2)}) %collective-permute-start.23) | collective-permute-done | bytes 589856 | tf_op jit(solution)/shard_map/ppermute | solution.py:409
  145.8 1.9 %collective-permute-done.21.a_last = bf16[3,256,384]{2,1,0:T(8,128)(2,1)S(1)} collective-permute-done((bf16[3,256,384]{2,1,0:T(8,128)(2,1)S(1)}, bf16[3,256,384]{2,1,0:T(8,128)(2,1)S(1)}, u32[]{:S(2)}, u32[]{:S(2)}) %collective-permute-start.21) | collective-permute-done | bytes 589856 | tf_op jit(solution)/shard_map/ppermute | solution.py:409
  147.7 1.4 final_step.1
  149.1 1.1 total.1
  (44 shorter events, 8.0 us)
Async XLA Ops:
  0.6 1.0 copy-start.2
  1.7 1.0 copy-start.3
  2.7 0.7 copy-start.4
  3.4 0.7 copy-start.5
  4.2 6.7 %collective-permute-start = (bf16[528,1024]{1,0:T(8,128)(2,1)S(1)}, bf16[528,1024]{1,0:T(8,128)(2,1)S(1)}, u32[]{:S(2)}, u32[]{:S(2)}) collective-permute-start(bf16[528,1024]{1,0:T(8,128)(2,1)S(1)} %payload.1.refs_0_), channel_id=1, source_target_pairs={{0,1},{1,0},{2,3},{3,2},{4,5},{5,4},{6,7},{7,6},{8,9},{9,8},{10,11... | collective-permute-start | bytes 3244040 | tf_op jit(solution)/shard_map/ppermute | solution.py:341
  4.7 12.7 %collective-permute-start.2 = (bf16[528,1024]{1,0:T(8,128)(2,1)S(1)}, bf16[528,1024]{1,0:T(8,128)(2,1)S(1)}, u32[]{:S(2)}, u32[]{:S(2)}) collective-permute-start(bf16[528,1024]{1,0:T(8,128)(2,1)S(1)} %payload.1.refs_0_), channel_id=1, source_target_pairs={{2,4},{3,5},{4,2},{5,3},{10,12},{11,13},{12,10},{13,11},{18,20},{1... | collective-permute-start | bytes 3244040 | tf_op jit(solution)/shard_map/ppermute | solution.py:338
  5.5 29.6 %collective-permute-start.3 = (bf16[528,1024]{1,0:T(8,128)(2,1)S(1)}, bf16[528,1024]{1,0:T(8,128)(2,1)S(1)}, u32[]{:S(2)}, u32[]{:S(2)}) collective-permute-start(bf16[528,1024]{1,0:T(8,128)(2,1)S(1)} %payload.1.refs_0_), channel_id=1, source_target_pairs={{0,2},{1,3},{2,0},{3,1},{4,6},{5,7},{6,4},{7,5},{8,10},{9,11},{10,... | collective-permute-start | bytes 3244040 | tf_op jit(solution)/shard_map/ppermute | solution.py:338
  10.9 2.3 %copy-start = (bf16[1,3,1024,768]{3,2,1,0:T(8,128)(2,1)S(1)}, bf16[1,3,1024,768]{3,2,1,0:T(8,128)(2,1)}, u32[]{:S(2)}) copy-start(bf16[1,3,1024,768]{3,2,1,0:T(8,128)(2,1)} %refs_4_.3) | copy-start | bytes 14155780
  13.2 24.6 %copy-start.1 = (bf16[1,3,1024,768]{3,2,1,0:T(8,128)(2,1)S(1)}, bf16[1,3,1024,768]{3,2,1,0:T(8,128)(2,1)}, u32[]{:S(2)}) copy-start(bf16[1,3,1024,768]{3,2,1,0:T(8,128)(2,1)} %refs_4_.3) | copy-start | bytes 14155780
  17.4 17.7 %collective-permute-start.1 = (bf16[272,1024]{1,0:T(8,128)(2,1)S(1)}, bf16[272,1024]{1,0:T(8,128)(2,1)S(1)}, u32[]{:S(2)}, u32[]{:S(2)}) collective-permute-start(bf16[272,1024]{1,0:T(8,128)(2,1)S(1)} %get-tuple-element.45), channel_id=1, source_target_pairs={{0,1},{1,0},{2,3},{3,2},{4,5},{5,4},{6,7},{7,6},{8,9},{9,8},{10,11... | collective-permute-start | bytes 1671176 | tf_op jit(solution)/shard_map/ppermute | solution.py:341
  35.1 2.7 %collective-permute-start.7 = (bf16[528,1024]{1,0:T(8,128)(2,1)S(1)}, bf16[528,1024]{1,0:T(8,128)(2,1)S(1)}, u32[]{:S(2)}, u32[]{:S(2)}) collective-permute-start(bf16[528,1024]{1,0:T(8,128)(2,1)S(1)} %collective-permute-done.3.refs_0_), channel_id=1, source_target_pairs={{0,1},{1,0},{2,3},{3,2},{4,5},{5,4},{6,7},{7,6},{8,9},{9,8},{10,11... | collective-permute-start | bytes 3244040 | tf_op jit(solution)/shard_map/ppermute | solution.py:341
  35.1 7.4 %collective-permute-start.5 = (bf16[528,1024]{1,0:T(8,128)(2,1)S(1)}, bf16[528,1024]{1,0:T(8,128)(2,1)S(1)}, u32[]{:S(2)}, u32[]{:S(2)}) collective-permute-start(bf16[528,1024]{1,0:T(8,128)(2,1)S(1)} %collective-permute-done.3.refs_0_), channel_id=1, source_target_pairs={{2,4},{3,5},{4,2},{5,3},{10,12},{11,13},{12,10},{13,11},{18,20},{1... | collective-permute-start | bytes 3244040 | tf_op jit(solution)/shard_map/ppermute | solution.py:338
  35.8 28.9 %collective-permute-start.6 = (bf16[528,1024]{1,0:T(8,128)(2,1)S(1)}, bf16[528,1024]{1,0:T(8,128)(2,1)S(1)}, u32[]{:S(2)}, u32[]{:S(2)}) collective-permute-start(bf16[528,1024]{1,0:T(8,128)(2,1)S(1)} %collective-permute-done.2.refs_0_), channel_id=1, source_target_pairs={{2,0},{3,1},{4,6},{5,7},{10,8},{11,9},{12,14},{13,15},{18,16},{19,... | collective-permute-start | bytes 3244040 | tf_op jit(solution)/shard_map/ppermute | solution.py:338
  42.0 22.8 %collective-permute-start.8 = (bf16[272,1024]{1,0:T(8,128)(2,1)S(1)}, bf16[272,1024]{1,0:T(8,128)(2,1)S(1)}, u32[]{:S(2)}, u32[]{:S(2)}) collective-permute-start(bf16[272,1024]{1,0:T(8,128)(2,1)S(1)} %get-tuple-element.48), channel_id=1, source_target_pairs={{0,1},{1,0},{2,3},{3,2},{4,5},{5,4},{6,7},{7,6},{8,9},{9,8},{10,11... | collective-permute-start | bytes 1671176 | tf_op jit(solution)/shard_map/ppermute | solution.py:341
  42.2 23.9 %collective-permute-start.4 = (bf16[528,1024]{1,0:T(8,128)(2,1)S(1)}, bf16[528,1024]{1,0:T(8,128)(2,1)S(1)}, u32[]{:S(2)}, u32[]{:S(2)}) collective-permute-start(bf16[528,1024]{1,0:T(8,128)(2,1)S(1)} %collective-permute-done.2.refs_0_), channel_id=1, source_target_pairs={{0,1},{1,0},{2,3},{3,2},{4,5},{5,4},{6,7},{7,6},{8,9},{9,8},{10,11... | collective-permute-start | bytes 3244040 | tf_op jit(solution)/shard_map/ppermute | solution.py:341
  64.7 2.7 %collective-permute-start.9 = (bf16[528,1024]{1,0:T(8,128)(2,1)S(1)}, bf16[528,1024]{1,0:T(8,128)(2,1)S(1)}, u32[]{:S(2)}, u32[]{:S(2)}) collective-permute-start(bf16[528,1024]{1,0:T(8,128)(2,1)S(1)} %collective-permute-done.6.refs_2_), channel_id=1, source_target_pairs={{0,1},{1,0},{2,3},{3,2},{4,5},{5,4},{6,7},{7,6},{8,9},{9,8},{10,11... | collective-permute-start | bytes 3244040 | tf_op jit(solution)/shard_map/ppermute | solution.py:341
  64.7 28.2 %collective-permute-start.12 = (bf16[528,1024]{1,0:T(8,128)(2,1)S(1)}, bf16[528,1024]{1,0:T(8,128)(2,1)S(1)}, u32[]{:S(2)}, u32[]{:S(2)}) collective-permute-start(bf16[528,1024]{1,0:T(8,128)(2,1)S(1)} %collective-permute-done.5.refs_0_), channel_id=1, source_target_pairs={{2,0},{3,1},{4,6},{5,7},{10,8},{11,9},{12,14},{13,15},{18,16},{19,... | collective-permute-start | bytes 3244040 | tf_op jit(solution)/shard_map/ppermute | solution.py:338
  72.1 20.8 %collective-permute-start.10 = (bf16[272,1024]{1,0:T(8,128)(2,1)S(1)}, bf16[272,1024]{1,0:T(8,128)(2,1)S(1)}, u32[]{:S(2)}, u32[]{:S(2)}) collective-permute-start(bf16[272,1024]{1,0:T(8,128)(2,1)S(1)} %get-tuple-element.51), channel_id=1, source_target_pairs={{0,1},{1,0},{2,3},{3,2},{4,5},{5,4},{6,7},{7,6},{8,9},{9,8},{10,11... | collective-permute-start | bytes 1671176 | tf_op jit(solution)/shard_map/ppermute | solution.py:341
  72.3 20.6 %collective-permute-start.11 = (bf16[528,1024]{1,0:T(8,128)(2,1)S(1)}, bf16[528,1024]{1,0:T(8,128)(2,1)S(1)}, u32[]{:S(2)}, u32[]{:S(2)}) collective-permute-start(bf16[528,1024]{1,0:T(8,128)(2,1)S(1)} %collective-permute-done.5.refs_0_), channel_id=1, source_target_pairs={{0,1},{1,0},{2,3},{3,2},{4,5},{5,4},{6,7},{7,6},{8,9},{9,8},{10,11... | collective-permute-start | bytes 3244040 | tf_op jit(solution)/shard_map/ppermute | solution.py:341
  92.9 2.7 %collective-permute-start.13 = (bf16[528,1024]{1,0:T(8,128)(2,1)S(1)}, bf16[528,1024]{1,0:T(8,128)(2,1)S(1)}, u32[]{:S(2)}, u32[]{:S(2)}) collective-permute-start(bf16[528,1024]{1,0:T(8,128)(2,1)S(1)} %collective-permute-done.12.refs_2_), channel_id=1, source_target_pairs={{0,1},{1,0},{2,3},{3,2},{4,5},{5,4},{6,7},{7,6},{8,9},{9,8},{10,11... | collective-permute-start | bytes 3244040 | tf_op jit(solution)/shard_map/ppermute | solution.py:341
  100.3 3.4 %collective-permute-start.14 = (bf16[272,1024]{1,0:T(8,128)(2,1)S(1)}, bf16[272,1024]{1,0:T(8,128)(2,1)S(1)}, u32[]{:S(2)}, u32[]{:S(2)}) collective-permute-start(bf16[272,1024]{1,0:T(8,128)(2,1)S(1)} %get-tuple-element.70), channel_id=1, source_target_pairs={{0,1},{1,0},{2,3},{3,2},{4,5},{5,4},{6,7},{7,6},{8,9},{9,8},{10,11... | collective-permute-start | bytes 1671176 | tf_op jit(solution)/shard_map/ppermute | solution.py:341
  102.0 28.3 %collective-permute-start.22 = (bf16[2,3,256,384]{3,2,1,0:T(8,128)(2,1)S(1)}, bf16[2,3,256,384]{3,2,1,0:T(8,128)(2,1)S(1)}, u32[]{:S(2)}, u32[]{:S(2)}) collective-permute-start(bf16[2,3,256,384]{3,2,1,0:T(8,128)(2,1)S(1)} %get-tuple-element.84), channel_id=1, source_target_pairs={{0,16},{8,24},{16,0},{24,8},{1,17},{9,25},{17,1},{25,9},{2,18},{10... | collective-permute-start | bytes 3538952 | tf_op jit(solution)/shard_map/ppermute | solution.py:409
  103.8 13.7 %collective-permute-start.15 = (bf16[272,1024]{1,0:T(8,128)(2,1)S(1)}, bf16[272,1024]{1,0:T(8,128)(2,1)S(1)}, u32[]{:S(2)}, u32[]{:S(2)}) collective-permute-start(bf16[272,1024]{1,0:T(8,128)(2,1)S(1)} %fusion.1), channel_id=1, source_target_pairs={{0,2},{1,3},{6,4},{7,5},{8,10},{9,11},{14,12},{15,13},{16,18},{17,... | collective-permute-start | bytes 1671176 | tf_op jit(solution)/shard_map/ppermute | solution.py:338
  105.3 28.3 %collective-permute-start.20 = (bf16[2,3,256,384]{3,2,1,0:T(8,128)(2,1)S(1)}, bf16[2,3,256,384]{3,2,1,0:T(8,128)(2,1)S(1)}, u32[]{:S(2)}, u32[]{:S(2)}) collective-permute-start(bf16[2,3,256,384]{3,2,1,0:T(8,128)(2,1)S(1)} %get-tuple-element.82), channel_id=1, source_target_pairs={{0,8},{8,0},{16,24},{24,16},{1,9},{9,1},{17,25},{25,17},{2,10},{10... | collective-permute-start | bytes 3538952 | tf_op jit(solution)/shard_map/ppermute | solution.py:409
  117.8 16.1 %collective-permute-start.17 = (bf16[272,1024]{1,0:T(8,128)(2,1)S(1)}, bf16[272,1024]{1,0:T(8,128)(2,1)S(1)}, u32[]{:S(2)}, u32[]{:S(2)}) collective-permute-start(bf16[272,1024]{1,0:T(8,128)(2,1)S(1)} %add_convert_fusion.3), channel_id=1, source_target_pairs={{2,4},{3,5},{4,2},{5,3},{10,12},{11,13},{12,10},{13,11},{18,20},{1... | collective-permute-start | bytes 1671176 | tf_op jit(solution)/shard_map/ppermute | solution.py:338
  118.7 20.2 %collective-permute-start.16 = (bf16[272,1024]{1,0:T(8,128)(2,1)S(1)}, bf16[272,1024]{1,0:T(8,128)(2,1)S(1)}, u32[]{:S(2)}, u32[]{:S(2)}) collective-permute-start(bf16[272,1024]{1,0:T(8,128)(2,1)S(1)} %fusion), channel_id=1, source_target_pairs={{0,2},{1,3},{6,4},{7,5},{8,10},{9,11},{14,12},{15,13},{16,18},{17,... | collective-permute-start | bytes 1671176 | tf_op jit(solution)/shard_map/ppermute | solution.py:338
  130.5 15.3 %collective-permute-start.23 = (bf16[3,256,384]{2,1,0:T(8,128)(2,1)S(1)}, bf16[3,256,384]{2,1,0:T(8,128)(2,1)S(1)}, u32[]{:S(2)}, u32[]{:S(2)}) collective-permute-start(bf16[3,256,384]{2,1,0:T(8,128)(2,1)S(1)} %fusion.3), channel_id=1, source_target_pairs={{0,8},{8,0},{16,24},{24,16},{1,9},{9,1},{17,25},{25,17},{2,10},{10... | collective-permute-start | bytes 1769480 | tf_op jit(solution)/shard_map/ppermute | solution.py:409
  133.7 13.9 %collective-permute-start.21 = (bf16[3,256,384]{2,1,0:T(8,128)(2,1)S(1)}, bf16[3,256,384]{2,1,0:T(8,128)(2,1)S(1)}, u32[]{:S(2)}, u32[]{:S(2)}) collective-permute-start(bf16[3,256,384]{2,1,0:T(8,128)(2,1)S(1)} %fusion.2), channel_id=1, source_target_pairs={{0,16},{8,24},{16,0},{24,8},{1,17},{9,25},{17,1},{25,9},{2,18},{10... | collective-permute-start | bytes 1769480 | tf_op jit(solution)/shard_map/ppermute | solution.py:409
  134.2 14.9 %collective-permute-start.19 = (bf16[272,1024]{1,0:T(8,128)(2,1)S(1)}, bf16[272,1024]{1,0:T(8,128)(2,1)S(1)}, u32[]{:S(2)}, u32[]{:S(2)}) collective-permute-start(bf16[272,1024]{1,0:T(8,128)(2,1)S(1)} %add_convert_fusion.2), channel_id=1, source_target_pairs={{0,2},{1,3},{2,0},{3,1},{4,6},{5,7},{6,4},{7,5},{8,10},{9,11},{10,... | collective-permute-start | bytes 1671176 | tf_op jit(solution)/shard_map/ppermute | solution.py:338
  139.3 9.9 %collective-permute-start.18 = (bf16[272,1024]{1,0:T(8,128)(2,1)S(1)}, bf16[272,1024]{1,0:T(8,128)(2,1)S(1)}, u32[]{:S(2)}, u32[]{:S(2)}) collective-permute-start(bf16[272,1024]{1,0:T(8,128)(2,1)S(1)} %add_convert_fusion.4), channel_id=1, source_target_pairs={{2,4},{3,5},{4,2},{5,3},{10,12},{11,13},{12,10},{13,11},{18,20},{1... | collective-permute-start | bytes 1671176 | tf_op jit(solution)/shard_map/ppermute | solution.py:338

commit v4 on v3

--- a/solution.py
+++ b/solution.py
@@ -273,7 +273,7 @@
             pltpu.VMEM((2, count), BF16),
             pltpu.SemaphoreType.DMA((4,)),
         ],
-        compiler_params=pltpu.CompilerParams(vmem_limit_bytes=4 * 1024 * 1024),
+        compiler_params=pltpu.CompilerParams(vmem_limit_bytes=60 * 1024 * 1024),
         cost_estimate=pl.CostEstimate(flops=1, bytes_accessed=1, transcendentals=0),
         name="payload",
     )(tokens, cotangent, expert_ids.T, gates.T)
@@ -354,34 +354,38 @@
         inner = [(1, 2), (2, 1)]
         to_ends = [(1, 0), (2, 3)]
         from_ends = [(0, 1), (3, 2)]
+        across_all = [(0, 3), (3, 0)]
+        first = move(own, outer)
         second = move(own, inner)
-        first = move(own, outer)
+        far = move(own, across_all)
         rows, grads = compute((own, swap(own)))
         kept = [rows]
         own_sum = joined(grads)
-        second, first = after((second, first), own_sum[1])
+        first, second, far = after((first, second, far), own_sum[1])
         third = move(second, to_ends)
         fourth = move(first, inner)
         rows, grads = compute((first, swap(first)))
         kept.append(rows)
         first_sum = joined(grads)
-        fourth, third = after((fourth, third), first_sum[1])
-        fifth = move(fourth, to_ends)
-        rows, grads = compute((second, swap(second)), (third, swap(third)))
+        rows, grads = compute((second, swap(second)), (far, swap(far)))
         kept.append(rows)
-        third_sum = joined(grads)
+        far_sum = joined(grads)
         partial = sum_early(kept)
-        fifth = after(fifth, third_sum[1], partial)
-        rows, grads = compute((fourth, swap(fourth)), (fifth, swap(fifth)))
+        third, fourth = after((third, fourth), first_sum[1], far_sum[1], partial)
+        last = add(fourth, third)
+        rows, grads = compute((last, swap(last)))
         kept.append(rows)
-        fourth_sum = joined(grads)
-        sent = add(*fourth_sum)
-        landed = move(sent, from_ends)
-        came = move(after(add(*third_sum), landed), from_ends)
-        landed = move(add(*fourth_sum, landed), inner)
-        third_back = move(after(add(*third_sum, came), landed), inner)
+        last_sum = joined(grads)
+        sent = add(*last_sum)
+        if lax.axis_size("dp") == 4:
+            pieces = run_weight(products_of(rows), partial)
+            far_sum = after(far_sum, pieces[1])
+        landed = move(sent, inner)
+        came = move(sent, from_ends)
+        far_back = move(add(*far_sum), across_all)
+        second_back = move(after(add(*far_sum, came), far_back), inner)
         back = move(add(*first_sum, landed), outer)
-        total = [*own_sum, third_back, back]
+        total = [*own_sum, second_back, back, far_back]
     else:
         rows, grads = compute((own, swap(own)))
         kept = [rows]
@@ -400,7 +404,8 @@
                 value = move(add(*pair) if value is None else add(*pair, value), back)
             if value is not None:
                 total.append(value)
-        partial = sum_early(kept[:-1])
+        if lax.axis_size("dp") == 4:
+            pieces = run_weight(products_of(rows), sum_early(kept[:-1]))
     tokens_grad, gates_grad = split_total(total, count)
 
     if lax.axis_size("dp") == 4:
@@ -408,7 +413,7 @@
         def across(value, bit):
             return lax.ppermute(value, "dp", [(i, i ^ bit) for i in range(4)])
 
-        a_send, a_keep, b_send, b_keep = run_weight(products_of(kept[-1]), partial)
+        a_send, a_keep, b_send, b_keep = pieces
         a_came = across(a_send, 1)
         b_came = across(b_send, 2)
         a_last = across(add(a_keep[0], a_came[0]), 2)

time: 153 us -> 148 us (0.967); the launches traced: 150 us -> 147 us
  waiting for transfers between devices: 87.8 us -> 80.7 us
  starting transfers between devices: 28.6 us -> 33 us
  local copies, waits for them, and re-layouts: 5.78 us -> 3.57 us
  Pallas kernels: 25.6 us -> 27.6 us
    ppermute x4, waiting for transfers between devices: 13.7 us -> 8.3 us  [across(): return lax.ppermute(value, 'dp', [(i, i ^ bit) for i in range(4)])]
    ppermute x10, starting transfers between devices: 21.7 us -> 24.5 us  [move(): return lax.ppermute(value, 'expert', full)]
    unnamed x12 -> x6, local copies, waits for them, and re-layouts: 5.78 us -> 3.57 us
    pallas_call x1, Pallas kernels: 0.12 us -> 2.25 us  [make_payload(): pl.pallas_call(payload_kernel, out_shape=jax.ShapeDtypeStruct((2 * count...]
    ppermute x10 -> x9, waiting for transfers between devices: 4.8 us -> 4.38 us  [swap(): return lax.ppermute(value, 'expert', [(i, i ^ 1) for i in range(devices)])]
  transfers between devices with their start and end apart: 24 -> 23, of which waited for: 12 -> 12; matrix products, arithmetic and copies ran while one was open for 1% -> 1% of each run, Pallas kernels for 13% -> 13%
where the time goes in v4:
time: 148 us; the launch traced here: 147 us
  waiting for transfers between devices  80.7 us (55%)
  starting transfers between devices  33 us (22%)
  Pallas kernels  27.6 us (19%)
  local copies, waits for them, and re-layouts  3.57 us (2%)
  other arithmetic  1.53 us (1%)
    ppermute x10, waiting for transfers between devices, move(): return lax.ppermute(value, 'expert', full)  68.1 us
    ppermute x10, starting transfers between devices, move(): return lax.ppermute(value, 'expert', full)  24.5 us
    pallas_call x4, Pallas kernels, run_slot(): pl.pallas_call(functools.partial(slot_kernel, choices, batch, capacity, m...  17.3 us
    ppermute x4, waiting for transfers between devices, across(): return lax.ppermute(value, 'dp', [(i, i ^ bit) for i in range(4)])  8.3 us
    ppermute x4, starting transfers between devices, across(): return lax.ppermute(value, 'dp', [(i, i ^ bit) for i in range(4)])  6.23 us
    ppermute x9, waiting for transfers between devices, swap(): return lax.ppermute(value, 'expert', [(i, i ^ 1) for i in range(devices)])  4.38 us
    pallas_call x1, Pallas kernels, run_partial(): pl.pallas_call(functools.partial(partial_kernel, len(lefts)), out_shape=j...  3.89 us
    unnamed x6, local copies, waits for them, and re-layouts  3.57 us
  transfers between devices with their start and end apart: 23, of which 12 were waited for; matrix products, arithmetic and copies ran while one was open for 1% of the time, Pallas kernels for 13%

profile of v4, /device:TPU:0, one launch (start us, length us, event | category | flops | bytes accessed | tf_op | source)
XLA Modules:
  0.0 147.3 jit_solution(8407950176797203747)
XLA Ops:
  0.6 2.2 %payload.1.refs_0_ = bf16[528,1024]{1,0:T(8,128)(2,1)} custom-call(bf16[256,1024]{1,0:T(8,128)(2,1)} %tokens.1, bf16[256,1024]{1,0:T(8,128)(2,1)} %cotangent.1, s32[2,256]{1,0:T(2,128)} %bitcast.9, bf16[2,256]{1,0:T(2,128)(2,1)} %bitcast.10), custom_call_target="tpu_custom_call" | custom-call | flops 1 | bytes 1 | tf_op jit(solution)/shard_map/payload/pallas_call | solution.py:266
  3.4 6.5 %collective-permute-start.4 = (bf16[528,1024]{1,0:T(8,128)(2,1)}, bf16[528,1024]{1,0:T(8,128)(2,1)S(1)}, u32[]{:S(2)}, u32[]{:S(2)}) collective-permute-start(bf16[528,1024]{1,0:T(8,128)(2,1)} %payload.1.refs_0_), channel_id=1, source_target_pairs={{0,6},{1,7},{6,0},{7,1},{8,14},{9,15},{14,8},{15,9},{16,22},{17,23... | collective-permute-start | bytes 3244040 | tf_op jit(solution)/shard_map/ppermute | solution.py:338
  9.9 0.7 collective-permute-start.3
  10.8 2.3 %copy-done = bf16[1,3,1024,768]{3,2,1,0:T(8,128)(2,1)S(1)} copy-done((bf16[1,3,1024,768]{3,2,1,0:T(8,128)(2,1)S(1)}, bf16[1,3,1024,768]{3,2,1,0:T(8,128)(2,1)}, u32[]{:S(2)}) %copy-start) | copy-done | bytes 4718616
  13.1 1.2 copy-done.2
  14.3 4.2 %expert_block.4 = (bf16[256,1024]{1,0:T(8,128)(2,1)S(1)}, bf16[256,1024]{1,0:T(8,128)(2,1)S(1)}, bf16[256,768]{1,0:T(8,128)(2,1)S(1)}, bf16[256,768]{1,0:T(8,128...) custom-call(bf16[528,1024]{1,0:T(8,128)(2,1)S(1)} %copy-done.2, ...), custom_call_target="tpu_custom_call" | custom-call | flops 1 | bytes 1 | tf_op jit(solution)/shard_map/expert_block/pallas_call | solution.py:114
  18.8 16.2 %collective-permute-done.4.refs_2_ = bf16[528,1024]{1,0:T(8,128)(2,1)S(1)} collective-permute-done((bf16[528,1024]{1,0:T(8,128)(2,1)}, bf16[528,1024]{1,0:T(8,128)(2,1)S(1)}, u32[]{:S(2)}, u32[]{:S(2)}) %collective-permute-start.4) | collective-permute-done | bytes 1081376 | tf_op jit(solution)/shard_map/ppermute | solution.py:338
  34.9 23.0 %collective-permute-done.2.refs_0_ = bf16[528,1024]{1,0:T(8,128)(2,1)S(1)} collective-permute-done((bf16[528,1024]{1,0:T(8,128)(2,1)}, bf16[528,1024]{1,0:T(8,128)(2,1)S(1)}, u32[]{:S(2)}, u32[]{:S(2)}) %collective-permute-start.2) | collective-permute-done | bytes 1081376 | tf_op jit(solution)/shard_map/ppermute | solution.py:338
  58.5 1.3 collective-permute-start.8
  60.6 1.5 %collective-permute-done.5.refs_1_ = bf16[528,1024]{1,0:T(8,128)(2,1)S(1)} collective-permute-done((bf16[528,1024]{1,0:T(8,128)(2,1)S(1)}, bf16[528,1024]{1,0:T(8,128)(2,1)S(1)}, u32[]{:S(2)}, u32[]{:S(2)}) %collective-permute-start.5) | collective-permute-done | bytes 1081376 | tf_op jit(solution)/shard_map/ppermute | solution.py:341
  62.2 4.6 %expert_block.5 = (bf16[256,1024]{1,0:T(8,128)(2,1)S(1)}, bf16[256,1024]{1,0:T(8,128)(2,1)S(1)}, bf16[256,768]{1,0:T(8,128)(2,1)S(1)}, bf16[256,768]{1,0:T(8,128...) custom-call(bf16[528,1024]{1,0:T(8,128)(2,1)S(1)} %collective-permute-done.3., ...), custom_call_target="tpu_custom_call" | custom-call | flops 1 | bytes 1 | tf_op jit(solution)/shard_map/expert_block/pallas_call | solution.py:114
  67.0 4.2 %expert_block.6 = (bf16[256,1024]{1,0:T(8,128)(2,1)S(1)}, bf16[256,1024]{1,0:T(8,128)(2,1)S(1)}, bf16[256,768]{1,0:T(8,128)(2,1)S(1)}, bf16[256,768]{1,0:T(8,128...) custom-call(bf16[528,1024]{1,0:T(8,128)(2,1)S(1)} %collective-permute-done.2., ...), custom_call_target="tpu_custom_call" | custom-call | flops 1 | bytes 1 | tf_op jit(solution)/shard_map/expert_block/pallas_call | solution.py:114
  71.6 3.9 %partial_weights.1.refs_6_ = f32[3,1024,768]{2,1,0:T(8,128)S(1)} custom-call(bf16[256,1024]{1,0:T(8,128)(2,1)S(1)} %get-tuple-element.53.refs_0_.refs_6_, bf16[256,1024]{1,0:T(8,128)(2,1)S(1)} %get-tuple-element.54.refs_1_.refs_7_, bf16[256,1024]{1,0:T(8,128)(2,1)S(1)} %get-tuple-element.55.refs_2_.refs_8_, bf16[256,768]{1,0:T(8,128)(2,1)S(1)} %get-tuple-element.56.refs_3_, ...), custom_call_target="tpu_custom_call" | custom-call | flops 1 | bytes 1 | tf_op jit(solution)/shard_map/partial_weights/pallas_call | solution.py:155
  75.5 11.1 %collective-permute-done.8 = bf16[528,1024]{1,0:T(8,128)(2,1)S(1)} collective-permute-done((bf16[528,1024]{1,0:T(8,128)(2,1)S(1)}, bf16[528,1024]{1,0:T(8,128)(2,1)S(1)}, u32[]{:S(2)}, u32[]{:S(2)}) %collective-permute-start.8) | collective-permute-done | bytes 1081376 | tf_op jit(solution)/shard_map/ppermute | solution.py:338
  87.1 2.7 %collective-permute-done.12.refs_1_ = bf16[528,1024]{1,0:T(8,128)(2,1)S(1)} collective-permute-done((bf16[528,1024]{1,0:T(8,128)(2,1)S(1)}, bf16[528,1024]{1,0:T(8,128)(2,1)S(1)}, u32[]{:S(2)}, u32[]{:S(2)}) %collective-permute-start.12) | collective-permute-done | bytes 1081376 | tf_op jit(solution)/shard_map/ppermute | solution.py:341
  89.8 4.4 %expert_block.7 = (bf16[256,1024]{1,0:T(8,128)(2,1)S(1)}, bf16[256,1024]{1,0:T(8,128)(2,1)S(1)}, bf16[256,768]{1,0:T(8,128)(2,1)S(1)}, bf16[256,768]{1,0:T(8,128...) custom-call(bf16[528,1024]{1,0:T(8,128)(2,1)S(1)} %add_convert_fusion.refs_0_, ...), custom_call_target="tpu_custom_call" | custom-call | flops 1 | bytes 1 | tf_op jit(solution)/shard_map/expert_block/pallas_call | solution.py:114
  94.4 1.5 %weight_block.1 = (bf16[2,3,256,384]{3,2,1,0:T(8,128)(2,1)S(1)}, bf16[2,3,256,384]{3,2,1,0:T(8,128)(2,1)S(1)}, bf16[2,3,256,384]{3,2,1,0:T(8,128)(2,1)S(1)}, bf16[2,3,256,384]{3,2,1,0:T(8,128)(2,1)S(1)}) custom-call(bf16[256,1024]{1,0:T(8,128)(2,1)S(1)} %get-tuple-element.70.refs_0_.refs_2_, bf16[256,768]{1,0:T(8,128)(2,1)S(1)} %get-tuple-element.71.refs_1_, ...), custom_call_target="tpu_custom_call" | custom-call | flops 1 | bytes 1 | tf_op jit(solution)/shard_map/weight_block/pallas_call | solution.py:193
  95.9 1.5 %collective-permute-start.19 = (bf16[2,3,256,384]{3,2,1,0:T(8,128)(2,1)S(1)}, bf16[2,3,256,384]{3,2,1,0:T(8,128)(2,1)S(1)}, u32[]{:S(2)}, u32[]{:S(2)}) collective-permute-start(bf16[2,3,256,384]{3,2,1,0:T(8,128)(2,1)S(1)} %get-tuple-element.84), channel_id=1, source_target_pairs={{0,8},{8,0},{16,24},{24,16},{1,9},{9,1},{17,25},{25,17},{2,10},{10... | collective-permute-start | bytes 3538952 | tf_op jit(solution)/shard_map/ppermute | solution.py:414
  97.5 1.5 %collective-permute-start.21 = (bf16[2,3,256,384]{3,2,1,0:T(8,128)(2,1)S(1)}, bf16[2,3,256,384]{3,2,1,0:T(8,128)(2,1)S(1)}, u32[]{:S(2)}, u32[]{:S(2)}) collective-permute-start(bf16[2,3,256,384]{3,2,1,0:T(8,128)(2,1)S(1)} %get-tuple-element.86), channel_id=1, source_target_pairs={{0,16},{8,24},{16,0},{24,8},{1,17},{9,25},{17,1},{25,9},{2,18},{10... | collective-permute-start | bytes 3538952 | tf_op jit(solution)/shard_map/ppermute | solution.py:414
  99.2 5.7 %collective-permute-start.14 = (bf16[272,1024]{1,0:T(8,128)(2,1)S(1)}, bf16[272,1024]{1,0:T(8,128)(2,1)S(1)}, u32[]{:S(2)}, u32[]{:S(2)}) collective-permute-start(bf16[272,1024]{1,0:T(8,128)(2,1)S(1)} %add_convert_fusion.5), channel_id=1, source_target_pairs={{0,2},{1,3},{6,4},{7,5},{8,10},{9,11},{14,12},{15,13},{16,18},{17,... | collective-permute-start | bytes 1671176 | tf_op jit(solution)/shard_map/ppermute | solution.py:338
  105.6 11.1 %collective-permute-done.14 = bf16[272,1024]{1,0:T(8,128)(2,1)S(1)} collective-permute-done((bf16[272,1024]{1,0:T(8,128)(2,1)S(1)}, bf16[272,1024]{1,0:T(8,128)(2,1)S(1)}, u32[]{:S(2)}, u32[]{:S(2)}) %collective-permute-start.14) | collective-permute-done | bytes 557088 | tf_op jit(solution)/shard_map/ppermute | solution.py:338
  117.1 4.4 %collective-permute-start.15 = (bf16[272,1024]{1,0:T(8,128)(2,1)S(1)}, bf16[272,1024]{1,0:T(8,128)(2,1)S(1)}, u32[]{:S(2)}, u32[]{:S(2)}) collective-permute-start(bf16[272,1024]{1,0:T(8,128)(2,1)S(1)} %get-tuple-element.87), channel_id=1, source_target_pairs={{0,6},{1,7},{6,0},{7,1},{8,14},{9,15},{14,8},{15,9},{16,22},{17,23... | collective-permute-start | bytes 1671176 | tf_op jit(solution)/shard_map/ppermute | solution.py:338
  121.4 2.8 %collective-permute-done.19.a_came = bf16[2,3,256,384]{3,2,1,0:T(8,128)(2,1)S(1)} collective-permute-done((bf16[2,3,256,384]{3,2,1,0:T(8,128)(2,1)S(1)}, bf16[2,3,256,384]{3,2,1,0:T(8,128)(2,1)S(1)}, u32[]{:S(2)}, u32[]{:S(2)}) %collective-permute-start.19) | collective-permute-done | bytes 1179680 | tf_op jit(solution)/shard_map/ppermute | solution.py:414
  124.4 1.6 %collective-permute-start.20 = (bf16[3,256,384]{2,1,0:T(8,128)(2,1)S(1)}, bf16[3,256,384]{2,1,0:T(8,128)(2,1)S(1)}, u32[]{:S(2)}, u32[]{:S(2)}) collective-permute-start(bf16[3,256,384]{2,1,0:T(8,128)(2,1)S(1)} %fusion.1), channel_id=1, source_target_pairs={{0,16},{8,24},{16,0},{24,8},{1,17},{9,25},{17,1},{25,9},{2,18},{10... | collective-permute-start | bytes 1769480 | tf_op jit(solution)/shard_map/ppermute | solution.py:414
  126.1 1.6 %collective-permute-start.22 = (bf16[3,256,384]{2,1,0:T(8,128)(2,1)S(1)}, bf16[3,256,384]{2,1,0:T(8,128)(2,1)S(1)}, u32[]{:S(2)}, u32[]{:S(2)}) collective-permute-start(bf16[3,256,384]{2,1,0:T(8,128)(2,1)S(1)} %fusion.2), channel_id=1, source_target_pairs={{0,8},{8,0},{16,24},{24,16},{1,9},{9,1},{17,25},{25,17},{2,10},{10... | collective-permute-start | bytes 1769480 | tf_op jit(solution)/shard_map/ppermute | solution.py:414
  128.0 3.8 %collective-permute-start.18 = (bf16[272,1024]{1,0:T(8,128)(2,1)S(1)}, bf16[272,1024]{1,0:T(8,128)(2,1)S(1)}, u32[]{:S(2)}, u32[]{:S(2)}) collective-permute-start(bf16[272,1024]{1,0:T(8,128)(2,1)S(1)} %add_convert_fusion.3), channel_id=1, source_target_pairs={{0,2},{1,3},{2,0},{3,1},{4,6},{5,7},{6,4},{7,5},{8,10},{9,11},{10,... | collective-permute-start | bytes 1671176 | tf_op jit(solution)/shard_map/ppermute | solution.py:338
  131.8 2.8 %collective-permute-done.15.refs_4_ = bf16[272,1024]{1,0:T(8,128)(2,1)S(1)} collective-permute-done((bf16[272,1024]{1,0:T(8,128)(2,1)S(1)}, bf16[272,1024]{1,0:T(8,128)(2,1)S(1)}, u32[]{:S(2)}, u32[]{:S(2)}) %collective-permute-start.15) | collective-permute-done | bytes 557088 | tf_op jit(solution)/shard_map/ppermute | solution.py:338
  135.2 4.0 %collective-permute-done.20.a_last = bf16[3,256,384]{2,1,0:T(8,128)(2,1)S(1)} collective-permute-done((bf16[3,256,384]{2,1,0:T(8,128)(2,1)S(1)}, bf16[3,256,384]{2,1,0:T(8,128)(2,1)S(1)}, u32[]{:S(2)}, u32[]{:S(2)}) %collective-permute-start.20) | collective-permute-done | bytes 589856 | tf_op jit(solution)/shard_map/ppermute | solution.py:414
  139.3 1.5 collective-permute-done.22.b_last
  140.7 1.4 final_step.1
  142.2 4.0 %collective-permute-done.18.refs_3_ = bf16[272,1024]{1,0:T(8,128)(2,1)S(1)} collective-permute-done((bf16[272,1024]{1,0:T(8,128)(2,1)S(1)}, bf16[272,1024]{1,0:T(8,128)(2,1)S(1)}, u32[]{:S(2)}, u32[]{:S(2)}) %collective-permute-start.18) | collective-permute-done | bytes 557088 | tf_op jit(solution)/shard_map/ppermute | solution.py:338
  146.1 1.1 total.1
  (35 shorter events, 6.1 us)
Async XLA Ops:
  2.9 7.9 %collective-permute-start = (bf16[528,1024]{1,0:T(8,128)(2,1)}, bf16[528,1024]{1,0:T(8,128)(2,1)S(1)}, u32[]{:S(2)}, u32[]{:S(2)}) collective-permute-start(bf16[528,1024]{1,0:T(8,128)(2,1)} %payload.1.refs_0_), channel_id=1, source_target_pairs={{0,1},{1,0},{2,3},{3,2},{4,5},{5,4},{6,7},{7,6},{8,9},{9,8},{10,11... | collective-permute-start | bytes 3244040 | tf_op jit(solution)/shard_map/ppermute | solution.py:341
  3.4 31.5 %collective-permute-start.4 = (bf16[528,1024]{1,0:T(8,128)(2,1)}, bf16[528,1024]{1,0:T(8,128)(2,1)S(1)}, u32[]{:S(2)}, u32[]{:S(2)}) collective-permute-start(bf16[528,1024]{1,0:T(8,128)(2,1)} %payload.1.refs_0_), channel_id=1, source_target_pairs={{0,6},{1,7},{6,0},{7,1},{8,14},{9,15},{14,8},{15,9},{16,22},{17,23... | collective-permute-start | bytes 3244040 | tf_op jit(solution)/shard_map/ppermute | solution.py:338
  9.9 25.0 %collective-permute-start.3 = (bf16[528,1024]{1,0:T(8,128)(2,1)}, bf16[528,1024]{1,0:T(8,128)(2,1)S(1)}, u32[]{:S(2)}, u32[]{:S(2)}) collective-permute-start(bf16[528,1024]{1,0:T(8,128)(2,1)} %payload.1.refs_0_), channel_id=1, source_target_pairs={{2,4},{3,5},{4,2},{5,3},{10,12},{11,13},{12,10},{13,11},{18,20},{1... | collective-permute-start | bytes 3244040 | tf_op jit(solution)/shard_map/ppermute | solution.py:338
  10.7 47.2 %collective-permute-start.2 = (bf16[528,1024]{1,0:T(8,128)(2,1)}, bf16[528,1024]{1,0:T(8,128)(2,1)S(1)}, u32[]{:S(2)}, u32[]{:S(2)}) collective-permute-start(bf16[528,1024]{1,0:T(8,128)(2,1)} %payload.1.refs_0_), channel_id=1, source_target_pairs={{0,2},{1,3},{2,0},{3,1},{4,6},{5,7},{6,4},{7,5},{8,10},{9,11},{10,... | collective-permute-start | bytes 3244040 | tf_op jit(solution)/shard_map/ppermute | solution.py:338
  10.8 2.3 %copy-start = (bf16[1,3,1024,768]{3,2,1,0:T(8,128)(2,1)S(1)}, bf16[1,3,1024,768]{3,2,1,0:T(8,128)(2,1)}, u32[]{:S(2)}) copy-start(bf16[1,3,1024,768]{3,2,1,0:T(8,128)(2,1)} %refs_2_.5) | copy-start | bytes 14155780
  13.1 1.2 copy-start.2
  14.3 47.8 %copy-start.1 = (bf16[1,3,1024,768]{3,2,1,0:T(8,128)(2,1)S(1)}, bf16[1,3,1024,768]{3,2,1,0:T(8,128)(2,1)}, u32[]{:S(2)}) copy-start(bf16[1,3,1024,768]{3,2,1,0:T(8,128)(2,1)} %refs_2_.5) | copy-start | bytes 14155780
  18.5 39.4 %collective-permute-start.1 = (bf16[272,1024]{1,0:T(8,128)(2,1)S(1)}, bf16[272,1024]{1,0:T(8,128)(2,1)S(1)}, u32[]{:S(2)}, u32[]{:S(2)}) collective-permute-start(bf16[272,1024]{1,0:T(8,128)(2,1)S(1)} %get-tuple-element.46), channel_id=1, source_target_pairs={{0,1},{1,0},{2,3},{3,2},{4,5},{5,4},{6,7},{7,6},{8,9},{9,8},{10,11... | collective-permute-start | bytes 1671176 | tf_op jit(solution)/shard_map/ppermute | solution.py:341
  57.9 2.7 %collective-permute-start.6 = (bf16[528,1024]{1,0:T(8,128)(2,1)S(1)}, bf16[528,1024]{1,0:T(8,128)(2,1)S(1)}, u32[]{:S(2)}, u32[]{:S(2)}) collective-permute-start(bf16[528,1024]{1,0:T(8,128)(2,1)S(1)} %collective-permute-done.4.refs_2_), channel_id=1, source_target_pairs={{0,1},{1,0},{2,3},{3,2},{4,5},{5,4},{6,7},{7,6},{8,9},{9,8},{10,11... | collective-permute-start | bytes 3244040 | tf_op jit(solution)/shard_map/ppermute | solution.py:341
  58.0 4.2 %collective-permute-start.5 = (bf16[528,1024]{1,0:T(8,128)(2,1)S(1)}, bf16[528,1024]{1,0:T(8,128)(2,1)S(1)}, u32[]{:S(2)}, u32[]{:S(2)}) collective-permute-start(bf16[528,1024]{1,0:T(8,128)(2,1)S(1)} %collective-permute-done.3.refs_0_), channel_id=1, source_target_pairs={{0,1},{1,0},{2,3},{3,2},{4,5},{5,4},{6,7},{7,6},{8,9},{9,8},{10,11... | collective-permute-start | bytes 3244040 | tf_op jit(solution)/shard_map/ppermute | solution.py:341
  58.4 8.6 %collective-permute-start.10 = (bf16[528,1024]{1,0:T(8,128)(2,1)S(1)}, bf16[528,1024]{1,0:T(8,128)(2,1)S(1)}, u32[]{:S(2)}, u32[]{:S(2)}) collective-permute-start(bf16[528,1024]{1,0:T(8,128)(2,1)S(1)} %collective-permute-done.2.refs_0_), channel_id=1, source_target_pairs={{0,1},{1,0},{2,3},{3,2},{4,5},{5,4},{6,7},{7,6},{8,9},{9,8},{10,11... | collective-permute-start | bytes 3244040 | tf_op jit(solution)/shard_map/ppermute | solution.py:341
  58.5 28.1 %collective-permute-start.8 = (bf16[528,1024]{1,0:T(8,128)(2,1)S(1)}, bf16[528,1024]{1,0:T(8,128)(2,1)S(1)}, u32[]{:S(2)}, u32[]{:S(2)}) collective-permute-start(bf16[528,1024]{1,0:T(8,128)(2,1)S(1)} %collective-permute-done.3.refs_0_), channel_id=1, source_target_pairs={{2,0},{3,1},{4,6},{5,7},{10,8},{11,9},{12,14},{13,15},{18,16},{19,... | collective-permute-start | bytes 3244040 | tf_op jit(solution)/shard_map/ppermute | solution.py:338
  59.8 26.8 %collective-permute-start.9 = (bf16[528,1024]{1,0:T(8,128)(2,1)S(1)}, bf16[528,1024]{1,0:T(8,128)(2,1)S(1)}, u32[]{:S(2)}, u32[]{:S(2)}) collective-permute-start(bf16[528,1024]{1,0:T(8,128)(2,1)S(1)} %collective-permute-done.2.refs_0_), channel_id=1, source_target_pairs={{2,4},{3,5},{4,2},{5,3},{10,12},{11,13},{12,10},{13,11},{18,20},{1... | collective-permute-start | bytes 3244040 | tf_op jit(solution)/shard_map/ppermute | solution.py:338
  66.8 19.8 %collective-permute-start.7 = (bf16[272,1024]{1,0:T(8,128)(2,1)S(1)}, bf16[272,1024]{1,0:T(8,128)(2,1)S(1)}, u32[]{:S(2)}, u32[]{:S(2)}) collective-permute-start(bf16[272,1024]{1,0:T(8,128)(2,1)S(1)} %get-tuple-element.50), channel_id=1, source_target_pairs={{0,1},{1,0},{2,3},{3,2},{4,5},{5,4},{6,7},{7,6},{8,9},{9,8},{10,11... | collective-permute-start | bytes 1671176 | tf_op jit(solution)/shard_map/ppermute | solution.py:341
  71.2 15.4 %collective-permute-start.11 = (bf16[272,1024]{1,0:T(8,128)(2,1)S(1)}, bf16[272,1024]{1,0:T(8,128)(2,1)S(1)}, u32[]{:S(2)}, u32[]{:S(2)}) collective-permute-start(bf16[272,1024]{1,0:T(8,128)(2,1)S(1)} %get-tuple-element.52), channel_id=1, source_target_pairs={{0,1},{1,0},{2,3},{3,2},{4,5},{5,4},{6,7},{7,6},{8,9},{9,8},{10,11... | collective-permute-start | bytes 1671176 | tf_op jit(solution)/shard_map/ppermute | solution.py:341
  87.0 2.8 %collective-permute-start.12 = (bf16[528,1024]{1,0:T(8,128)(2,1)S(1)}, bf16[528,1024]{1,0:T(8,128)(2,1)S(1)}, u32[]{:S(2)}, u32[]{:S(2)}) collective-permute-start(bf16[528,1024]{1,0:T(8,128)(2,1)S(1)} %add_convert_fusion.refs_0_), channel_id=1, source_target_pairs={{0,1},{1,0},{2,3},{3,2},{4,5},{5,4},{6,7},{7,6},{8,9},{9,8},{10,11... | collective-permute-start | bytes 3244040 | tf_op jit(solution)/shard_map/ppermute | solution.py:341
  94.2 4.8 %collective-permute-start.13 = (bf16[272,1024]{1,0:T(8,128)(2,1)S(1)}, bf16[272,1024]{1,0:T(8,128)(2,1)S(1)}, u32[]{:S(2)}, u32[]{:S(2)}) collective-permute-start(bf16[272,1024]{1,0:T(8,128)(2,1)S(1)} %get-tuple-element.79), channel_id=1, source_target_pairs={{0,1},{1,0},{2,3},{3,2},{4,5},{5,4},{6,7},{7,6},{8,9},{9,8},{10,11... | collective-permute-start | bytes 1671176 | tf_op jit(solution)/shard_map/ppermute | solution.py:341
  95.9 28.3 %collective-permute-start.19 = (bf16[2,3,256,384]{3,2,1,0:T(8,128)(2,1)S(1)}, bf16[2,3,256,384]{3,2,1,0:T(8,128)(2,1)S(1)}, u32[]{:S(2)}, u32[]{:S(2)}) collective-permute-start(bf16[2,3,256,384]{3,2,1,0:T(8,128)(2,1)S(1)} %get-tuple-element.84), channel_id=1, source_target_pairs={{0,8},{8,0},{16,24},{24,16},{1,9},{9,1},{17,25},{25,17},{2,10},{10... | collective-permute-start | bytes 3538952 | tf_op jit(solution)/shard_map/ppermute | solution.py:414
  97.5 28.5 %collective-permute-start.21 = (bf16[2,3,256,384]{3,2,1,0:T(8,128)(2,1)S(1)}, bf16[2,3,256,384]{3,2,1,0:T(8,128)(2,1)S(1)}, u32[]{:S(2)}, u32[]{:S(2)}) collective-permute-start(bf16[2,3,256,384]{3,2,1,0:T(8,128)(2,1)S(1)} %get-tuple-element.86), channel_id=1, source_target_pairs={{0,16},{8,24},{16,0},{24,8},{1,17},{9,25},{17,1},{25,9},{2,18},{10... | collective-permute-start | bytes 3538952 | tf_op jit(solution)/shard_map/ppermute | solution.py:414
  99.2 17.5 %collective-permute-start.14 = (bf16[272,1024]{1,0:T(8,128)(2,1)S(1)}, bf16[272,1024]{1,0:T(8,128)(2,1)S(1)}, u32[]{:S(2)}, u32[]{:S(2)}) collective-permute-start(bf16[272,1024]{1,0:T(8,128)(2,1)S(1)} %add_convert_fusion.5), channel_id=1, source_target_pairs={{0,2},{1,3},{6,4},{7,5},{8,10},{9,11},{14,12},{15,13},{16,18},{17,... | collective-permute-start | bytes 1671176 | tf_op jit(solution)/shard_map/ppermute | solution.py:338
  104.9 22.8 %collective-permute-start.17 = (bf16[272,1024]{1,0:T(8,128)(2,1)S(1)}, bf16[272,1024]{1,0:T(8,128)(2,1)S(1)}, u32[]{:S(2)}, u32[]{:S(2)}) collective-permute-start(bf16[272,1024]{1,0:T(8,128)(2,1)S(1)} %add_convert_fusion.5), channel_id=1, source_target_pairs={{2,4},{3,5},{4,2},{5,3},{10,12},{11,13},{12,10},{13,11},{18,20},{1... | collective-permute-start | bytes 1671176 | tf_op jit(solution)/shard_map/ppermute | solution.py:338
  117.1 17.5 %collective-permute-start.15 = (bf16[272,1024]{1,0:T(8,128)(2,1)S(1)}, bf16[272,1024]{1,0:T(8,128)(2,1)S(1)}, u32[]{:S(2)}, u32[]{:S(2)}) collective-permute-start(bf16[272,1024]{1,0:T(8,128)(2,1)S(1)} %get-tuple-element.87), channel_id=1, source_target_pairs={{0,6},{1,7},{6,0},{7,1},{8,14},{9,15},{14,8},{15,9},{16,22},{17,23... | collective-permute-start | bytes 1671176 | tf_op jit(solution)/shard_map/ppermute | solution.py:338
  124.4 14.9 %collective-permute-start.20 = (bf16[3,256,384]{2,1,0:T(8,128)(2,1)S(1)}, bf16[3,256,384]{2,1,0:T(8,128)(2,1)S(1)}, u32[]{:S(2)}, u32[]{:S(2)}) collective-permute-start(bf16[3,256,384]{2,1,0:T(8,128)(2,1)S(1)} %fusion.1), channel_id=1, source_target_pairs={{0,16},{8,24},{16,0},{24,8},{1,17},{9,25},{17,1},{25,9},{2,18},{10... | collective-permute-start | bytes 1769480 | tf_op jit(solution)/shard_map/ppermute | solution.py:414
  126.1 14.6 %collective-permute-start.22 = (bf16[3,256,384]{2,1,0:T(8,128)(2,1)S(1)}, bf16[3,256,384]{2,1,0:T(8,128)(2,1)S(1)}, u32[]{:S(2)}, u32[]{:S(2)}) collective-permute-start(bf16[3,256,384]{2,1,0:T(8,128)(2,1)S(1)} %fusion.2), channel_id=1, source_target_pairs={{0,8},{8,0},{16,24},{24,16},{1,9},{9,1},{17,25},{25,17},{2,10},{10... | collective-permute-start | bytes 1769480 | tf_op jit(solution)/shard_map/ppermute | solution.py:414
  128.0 18.2 %collective-permute-start.18 = (bf16[272,1024]{1,0:T(8,128)(2,1)S(1)}, bf16[272,1024]{1,0:T(8,128)(2,1)S(1)}, u32[]{:S(2)}, u32[]{:S(2)}) collective-permute-start(bf16[272,1024]{1,0:T(8,128)(2,1)S(1)} %add_convert_fusion.3), channel_id=1, source_target_pairs={{0,2},{1,3},{2,0},{3,1},{4,6},{5,7},{6,4},{7,5},{8,10},{9,11},{10,... | collective-permute-start | bytes 1671176 | tf_op jit(solution)/shard_map/ppermute | solution.py:338
  134.5 11.6 %collective-permute-start.16 = (bf16[272,1024]{1,0:T(8,128)(2,1)S(1)}, bf16[272,1024]{1,0:T(8,128)(2,1)S(1)}, u32[]{:S(2)}, u32[]{:S(2)}) collective-permute-start(bf16[272,1024]{1,0:T(8,128)(2,1)S(1)} %get-tuple-element.80), channel_id=1, source_target_pairs={{2,4},{3,5},{4,2},{5,3},{10,12},{11,13},{12,10},{13,11},{18,20},{1... | collective-permute-start | bytes 1671176 | tf_op jit(solution)/shard_map/ppermute | solution.py:338

commit v5 on v4

--- a/solution.py
+++ b/solution.py
@@ -232,20 +232,28 @@
     )(*operands)
 
 
-def payload_kernel(tokens, cotangent, ids_hbm, gates_hbm, out, ids, gates, sems):
+def payload_kernel(tokens, cotangent, ids_hbm, gates_hbm, out, ids, gates, held, sems):
     count = tokens.shape[0]
-    copies = [
-        pltpu.make_async_copy(ids_hbm, ids, sems.at[2]),
-        pltpu.make_async_copy(gates_hbm, gates, sems.at[3]),
-        pltpu.make_async_copy(tokens, out.at[:count], sems.at[0]),
-        pltpu.make_async_copy(cotangent, out.at[count + META :], sems.at[1]),
+    small = [
+        pltpu.make_async_copy(ids_hbm, ids, sems.at[0]),
+        pltpu.make_async_copy(gates_hbm, gates, sems.at[1]),
     ]
-    for copy in copies:
+    large = [
+        pltpu.make_async_copy(tokens, held.at[:count], sems.at[2]),
+        pltpu.make_async_copy(cotangent, held.at[count + META :], sems.at[3]),
+    ]
+    outward = [
+        pltpu.make_async_copy(held.at[part], out.at[part], sems.at[4 + number])
+        for number, part in enumerate(
+            (pl.ds(0, count), pl.ds(count + META, count), pl.ds(count, META))
+        )
+    ]
+    for copy in small + large:
         copy.start()
-    copies[0].wait()
-    copies[1].wait()
+    for copy in small:
+        copy.wait()
     line = lax.broadcasted_iota(jnp.int32, (META, count), 0)
-    routing = jnp.zeros((META, count), F32)
+    values = jnp.zeros((META, count), F32)
     rows = (
         ids[0:1, :].astype(F32) + 1.0,
         ids[1:2, :].astype(F32) + 1.0,
@@ -253,25 +261,29 @@
         gates[1:2, :].astype(F32),
     )
     for number, row in enumerate(rows):
-        routing = jnp.where(line == number, row, routing)
-    out[count : count + META, :] = jnp.zeros((META, out.shape[1]), BF16)
-    out[count : count + META, :count] = routing.astype(BF16)
-    copies[2].wait()
-    copies[3].wait()
+        values = jnp.where(line == number, row, values)
+    held[count : count + META, :] = jnp.zeros((META, held.shape[1]), BF16)
+    held[count : count + META, :count] = values.astype(BF16)
+    outward[2].start()
+    for came, sent in zip(large, outward):
+        came.wait()
+        sent.start()
+    for copy in outward:
+        copy.wait()
 
 
 def make_payload(tokens, cotangent, gates, expert_ids):
     count, width = tokens.shape
-    whole = pl.BlockSpec(memory_space=pltpu.VMEM)
     return pl.pallas_call(
         payload_kernel,
         out_shape=jax.ShapeDtypeStruct((2 * count + META, width), BF16),
         in_specs=[pl.BlockSpec(memory_space=pltpu.HBM)] * 4,
-        out_specs=whole,
+        out_specs=pl.BlockSpec(memory_space=pltpu.HBM),
         scratch_shapes=[
             pltpu.VMEM((2, count), jnp.int32),
             pltpu.VMEM((2, count), BF16),
-            pltpu.SemaphoreType.DMA((4,)),
+            pltpu.VMEM((2 * count + META, width), BF16),
+            pltpu.SemaphoreType.DMA((7,)),
         ],
         compiler_params=pltpu.CompilerParams(vmem_limit_bytes=60 * 1024 * 1024),
         cost_estimate=pl.CostEstimate(flops=1, bytes_accessed=1, transcendentals=0),
@@ -332,6 +344,16 @@
     batch = count // MICRO
     capacity = 4 * batch // devices
     own = make_payload(tokens, cotangent, gates, expert_ids)
+
+    def across(value, bit):
+        return lax.ppermute(value, "dp", [(i, i ^ bit) for i in range(4)])
+
+    def first_step(rows, partial):
+        a_send, a_keep, b_send, b_keep = run_weight(products_of(rows), partial)
+        a_came = across(a_send, 1)
+        b_came = across(b_send, 2)
+        next_pair = (add(a_keep[0], a_came[0]), add(b_keep[0], b_came[0]))
+        return (a_keep, a_came, b_keep, b_came), next_pair, a_keep
 
     def move(value, pairs):
         full = [(a * CORES + k, b * CORES + k) for a, b in pairs for k in range(CORES)]
@@ -378,13 +400,16 @@
         last_sum = joined(grads)
         sent = add(*last_sum)
         if lax.axis_size("dp") == 4:
-            pieces = run_weight(products_of(rows), partial)
-            far_sum = after(far_sum, pieces[1])
+            halves, next_pair, ready = first_step(rows, partial)
+            far_sum = after(far_sum, ready)
+        else:
+            next_pair = ()
         landed = move(sent, inner)
         came = move(sent, from_ends)
         far_back = move(add(*far_sum), across_all)
-        second_back = move(after(add(*far_sum, came), far_back), inner)
+        landed, came, far_back = after((landed, came, far_back), next_pair)
         back = move(add(*first_sum, landed), outer)
+        second_back = move(add(*far_sum, came), inner)
         total = [*own_sum, second_back, back, far_back]
     else:
         rows, grads = compute((own, swap(own)))
@@ -405,19 +430,12 @@
             if value is not None:
                 total.append(value)
         if lax.axis_size("dp") == 4:
-            pieces = run_weight(products_of(rows), sum_early(kept[:-1]))
-    tokens_grad, gates_grad = split_total(total, count)
+            halves, next_pair, _ = first_step(rows, sum_early(kept[:-1]))
 
     if lax.axis_size("dp") == 4:
-
-        def across(value, bit):
-            return lax.ppermute(value, "dp", [(i, i ^ bit) for i in range(4)])
-
-        a_send, a_keep, b_send, b_keep = pieces
-        a_came = across(a_send, 1)
-        b_came = across(b_send, 2)
-        a_last = across(add(a_keep[0], a_came[0]), 2)
-        b_last = across(add(b_keep[0], b_came[0]), 1)
+        a_keep, a_came, b_keep, b_came = halves
+        a_last = across(next_pair[0], 2)
+        b_last = across(next_pair[1], 1)
         weights_grad = run_final(a_keep, a_came, a_last, b_keep, b_came, b_last)[None]
     else:
         whole = [jnp.concatenate(value, axis=0) for value in zip(*kept)]
@@ -431,6 +449,8 @@
         weights_grad = lax.psum_scatter(
             partial[None], "dp", scatter_dimension=2, tiled=True
         )
+    total = after(total, weights_grad)
+    tokens_grad, gates_grad = split_total(total, count)
     return tokens_grad, gates_grad, weights_grad
 
 

time: 148 us -> 146 us (0.986)
  starting transfers between devices: 33 us -> 29.5 us
    ppermute x4, waiting for transfers between devices: 8.3 us -> 24.2 us  [across(): return lax.ppermute(value, 'dp', [(i, i ^ bit) for i in range(4)])]
    ppermute x10, waiting for transfers between devices: 68.1 us -> 53.2 us  [move(): return lax.ppermute(value, 'expert', full)]
    ppermute x10, starting transfers between devices: 24.5 us -> 21.2 us  [move(): return lax.ppermute(value, 'expert', full)]
  transfers between devices with their start and end apart: 23 -> 23, of which waited for: 12 -> 11; matrix products, arithmetic and copies ran while one was open for 1% -> 1% of each run, Pallas kernels for 13% -> 13%
where the time goes in v5:
time: 146 us; the launch traced here: 145 us
  waiting for transfers between devices  81.7 us (56%)
  starting transfers between devices  29.5 us (20%)
  Pallas kernels  27.4 us (19%)
  local copies, waits for them, and re-layouts  3.57 us (2%)
  other arithmetic  1.67 us (1%)
    ppermute x10, waiting for transfers between devices, move(): return lax.ppermute(value, 'expert', full)  53.2 us
    ppermute x4, waiting for transfers between devices, across(): return lax.ppermute(value, 'dp', [(i, i ^ bit) for i in range(4)])  24.2 us
    ppermute x10, starting transfers between devices, move(): return lax.ppermute(value, 'expert', full)  21.2 us
    pallas_call x4, Pallas kernels, run_slot(): pl.pallas_call(functools.partial(slot_kernel, choices, batch, capacity, m...  17.3 us
    ppermute x4, starting transfers between devices, across(): return lax.ppermute(value, 'dp', [(i, i ^ bit) for i in range(4)])  6.21 us
    ppermute x9, waiting for transfers between devices, swap(): return lax.ppermute(value, 'expert', [(i, i ^ 1) for i in range(devices)])  4.38 us
    pallas_call x1, Pallas kernels, run_partial(): pl.pallas_call(functools.partial(partial_kernel, len(lefts)), out_shape=j...  3.89 us
    unnamed x6, local copies, waits for them, and re-layouts  3.57 us
  transfers between devices with their start and end apart: 23, of which 11 were waited for; matrix products, arithmetic and copies ran while one was open for 1% of the time, Pallas kernels for 13%

profile of v5, /device:TPU:0, one launch (start us, length us, event | category | flops | bytes accessed | tf_op | source)
XLA Modules:
  0.0 144.7 jit_solution(7904377731247983810)
XLA Ops:
  0.6 2.1 %payload.1.refs_0_ = bf16[528,1024]{1,0:T(8,128)(2,1)} custom-call(bf16[256,1024]{1,0:T(8,128)(2,1)} %tokens.1, bf16[256,1024]{1,0:T(8,128)(2,1)} %cotangent.1, s32[2,256]{1,0:T(2,128)} %bitcast.9, bf16[2,256]{1,0:T(2,128)(2,1)} %bitcast.10), custom_call_target="tpu_custom_call" | custom-call | flops 1 | bytes 1 | tf_op jit(solution)/shard_map/payload/pallas_call | solution.py:277
  3.3 6.5 %collective-permute-start.4 = (bf16[528,1024]{1,0:T(8,128)(2,1)}, bf16[528,1024]{1,0:T(8,128)(2,1)S(1)}, u32[]{:S(2)}, u32[]{:S(2)}) collective-permute-start(bf16[528,1024]{1,0:T(8,128)(2,1)} %payload.1.refs_0_), channel_id=1, source_target_pairs={{0,6},{1,7},{6,0},{7,1},{8,14},{9,15},{14,8},{15,9},{16,22},{17,23... | collective-permute-start | bytes 3244040 | tf_op jit(solution)/shard_map/ppermute | solution.py:360
  9.8 0.7 collective-permute-start.3
  10.6 2.3 %copy-done = bf16[1,3,1024,768]{3,2,1,0:T(8,128)(2,1)S(1)} copy-done((bf16[1,3,1024,768]{3,2,1,0:T(8,128)(2,1)S(1)}, bf16[1,3,1024,768]{3,2,1,0:T(8,128)(2,1)}, u32[]{:S(2)}) %copy-start) | copy-done | bytes 4718616
  13.0 1.2 copy-done.2
  14.2 4.2 %expert_block.4 = (bf16[256,1024]{1,0:T(8,128)(2,1)S(1)}, bf16[256,1024]{1,0:T(8,128)(2,1)S(1)}, bf16[256,768]{1,0:T(8,128)(2,1)S(1)}, bf16[256,768]{1,0:T(8,128...) custom-call(bf16[528,1024]{1,0:T(8,128)(2,1)S(1)} %copy-done.2, ...), custom_call_target="tpu_custom_call" | custom-call | flops 1 | bytes 1 | tf_op jit(solution)/shard_map/expert_block/pallas_call | solution.py:114
  18.6 16.2 %collective-permute-done.4.refs_2_ = bf16[528,1024]{1,0:T(8,128)(2,1)S(1)} collective-permute-done((bf16[528,1024]{1,0:T(8,128)(2,1)}, bf16[528,1024]{1,0:T(8,128)(2,1)S(1)}, u32[]{:S(2)}, u32[]{:S(2)}) %collective-permute-start.4) | collective-permute-done | bytes 1081376 | tf_op jit(solution)/shard_map/ppermute | solution.py:360
  34.8 23.0 %collective-permute-done.2.refs_0_ = bf16[528,1024]{1,0:T(8,128)(2,1)S(1)} collective-permute-done((bf16[528,1024]{1,0:T(8,128)(2,1)}, bf16[528,1024]{1,0:T(8,128)(2,1)S(1)}, u32[]{:S(2)}, u32[]{:S(2)}) %collective-permute-start.2) | collective-permute-done | bytes 1081376 | tf_op jit(solution)/shard_map/ppermute | solution.py:360
  58.3 1.3 collective-permute-start.8
  59.6 0.7 collective-permute-start.9
  60.5 1.5 %collective-permute-done.5.refs_1_ = bf16[528,1024]{1,0:T(8,128)(2,1)S(1)} collective-permute-done((bf16[528,1024]{1,0:T(8,128)(2,1)S(1)}, bf16[528,1024]{1,0:T(8,128)(2,1)S(1)}, u32[]{:S(2)}, u32[]{:S(2)}) %collective-permute-start.5) | collective-permute-done | bytes 1081376 | tf_op jit(solution)/shard_map/ppermute | solution.py:363
  62.0 4.6 %expert_block.5 = (bf16[256,1024]{1,0:T(8,128)(2,1)S(1)}, bf16[256,1024]{1,0:T(8,128)(2,1)S(1)}, bf16[256,768]{1,0:T(8,128)(2,1)S(1)}, bf16[256,768]{1,0:T(8,128...) custom-call(bf16[528,1024]{1,0:T(8,128)(2,1)S(1)} %collective-permute-done.3., ...), custom_call_target="tpu_custom_call" | custom-call | flops 1 | bytes 1 | tf_op jit(solution)/shard_map/expert_block/pallas_call | solution.py:114
  66.9 4.2 %expert_block.6 = (bf16[256,1024]{1,0:T(8,128)(2,1)S(1)}, bf16[256,1024]{1,0:T(8,128)(2,1)S(1)}, bf16[256,768]{1,0:T(8,128)(2,1)S(1)}, bf16[256,768]{1,0:T(8,128...) custom-call(bf16[528,1024]{1,0:T(8,128)(2,1)S(1)} %collective-permute-done.2., ...), custom_call_target="tpu_custom_call" | custom-call | flops 1 | bytes 1 | tf_op jit(solution)/shard_map/expert_block/pallas_call | solution.py:114
  71.5 3.9 %partial_weights.1.refs_6_ = f32[3,1024,768]{2,1,0:T(8,128)S(1)} custom-call(bf16[256,1024]{1,0:T(8,128)(2,1)S(1)} %get-tuple-element.60.refs_0_.refs_6_, bf16[256,1024]{1,0:T(8,128)(2,1)S(1)} %get-tuple-element.61.refs_1_.refs_7_, bf16[256,1024]{1,0:T(8,128)(2,1)S(1)} %get-tuple-element.62.refs_2_.refs_8_, bf16[256,768]{1,0:T(8,128)(2,1)S(1)} %get-tuple-element.63.refs_3_, ...), custom_call_target="tpu_custom_call" | custom-call | flops 1 | bytes 1 | tf_op jit(solution)/shard_map/partial_weights/pallas_call | solution.py:155
  75.4 11.1 %collective-permute-done.8 = bf16[528,1024]{1,0:T(8,128)(2,1)S(1)} collective-permute-done((bf16[528,1024]{1,0:T(8,128)(2,1)S(1)}, bf16[528,1024]{1,0:T(8,128)(2,1)S(1)}, u32[]{:S(2)}, u32[]{:S(2)}) %collective-permute-start.8) | collective-permute-done | bytes 1081376 | tf_op jit(solution)/shard_map/ppermute | solution.py:360
  87.0 2.7 %collective-permute-done.12.refs_1_ = bf16[528,1024]{1,0:T(8,128)(2,1)S(1)} collective-permute-done((bf16[528,1024]{1,0:T(8,128)(2,1)S(1)}, bf16[528,1024]{1,0:T(8,128)(2,1)S(1)}, u32[]{:S(2)}, u32[]{:S(2)}) %collective-permute-start.12) | collective-permute-done | bytes 1081376 | tf_op jit(solution)/shard_map/ppermute | solution.py:363
  89.6 4.4 %expert_block.7 = (bf16[256,1024]{1,0:T(8,128)(2,1)S(1)}, bf16[256,1024]{1,0:T(8,128)(2,1)S(1)}, bf16[256,768]{1,0:T(8,128)(2,1)S(1)}, bf16[256,768]{1,0:T(8,128...) custom-call(bf16[528,1024]{1,0:T(8,128)(2,1)S(1)} %add_convert_fusion.refs_0_, ...), custom_call_target="tpu_custom_call" | custom-call | flops 1 | bytes 1 | tf_op jit(solution)/shard_map/expert_block/pallas_call | solution.py:114
  94.0 1.5 %weight_block.1 = (bf16[2,3,256,384]{3,2,1,0:T(8,128)(2,1)S(1)}, bf16[2,3,256,384]{3,2,1,0:T(8,128)(2,1)S(1)}, bf16[2,3,256,384]{3,2,1,0:T(8,128)(2,1)S(1)}, bf16[2,3,256,384]{3,2,1,0:T(8,128)(2,1)S(1)}) custom-call(bf16[256,1024]{1,0:T(8,128)(2,1)S(1)} %get-tuple-element.77.refs_0_.refs_2_, bf16[256,768]{1,0:T(8,128)(2,1)S(1)} %get-tuple-element.78.refs_1_, ...), custom_call_target="tpu_custom_call" | custom-call | flops 1 | bytes 1 | tf_op jit(solution)/shard_map/weight_block/pallas_call | solution.py:193
  95.6 1.5 %collective-permute-start.17 = (bf16[2,3,256,384]{3,2,1,0:T(8,128)(2,1)S(1)}, bf16[2,3,256,384]{3,2,1,0:T(8,128)(2,1)S(1)}, u32[]{:S(2)}, u32[]{:S(2)}) collective-permute-start(bf16[2,3,256,384]{3,2,1,0:T(8,128)(2,1)S(1)} %get-tuple-element.87), channel_id=1, source_target_pairs={{0,8},{8,0},{16,24},{24,16},{1,9},{9,1},{17,25},{25,17},{2,10},{10... | collective-permute-start | bytes 3538952 | tf_op jit(solution)/shard_map/ppermute | solution.py:349
  97.1 1.5 %collective-permute-start.18 = (bf16[2,3,256,384]{3,2,1,0:T(8,128)(2,1)S(1)}, bf16[2,3,256,384]{3,2,1,0:T(8,128)(2,1)S(1)}, u32[]{:S(2)}, u32[]{:S(2)}) collective-permute-start(bf16[2,3,256,384]{3,2,1,0:T(8,128)(2,1)S(1)} %get-tuple-element.89), channel_id=1, source_target_pairs={{0,16},{8,24},{16,0},{24,8},{1,17},{9,25},{17,1},{25,9},{2,18},{10... | collective-permute-start | bytes 3538952 | tf_op jit(solution)/shard_map/ppermute | solution.py:349
  98.9 4.4 %collective-permute-start.16 = (bf16[272,1024]{1,0:T(8,128)(2,1)S(1)}, bf16[272,1024]{1,0:T(8,128)(2,1)S(1)}, u32[]{:S(2)}, u32[]{:S(2)}) collective-permute-start(bf16[272,1024]{1,0:T(8,128)(2,1)S(1)} %fusion), channel_id=1, source_target_pairs={{0,6},{1,7},{6,0},{7,1},{8,14},{9,15},{14,8},{15,9},{16,22},{17,23... | collective-permute-start | bytes 1671176 | tf_op jit(solution)/shard_map/ppermute | solution.py:360
  103.5 3.0 %collective-permute-start.15 = (bf16[272,1024]{1,0:T(8,128)(2,1)S(1)}, bf16[272,1024]{1,0:T(8,128)(2,1)S(1)}, u32[]{:S(2)}, u32[]{:S(2)}) collective-permute-start(bf16[272,1024]{1,0:T(8,128)(2,1)S(1)} %add_convert_fusion.5), channel_id=1, source_target_pairs={{0,2},{1,3},{6,4},{7,5},{8,10},{9,11},{14,12},{15,13},{16,18},{17,... | collective-permute-start | bytes 1671176 | tf_op jit(solution)/shard_map/ppermute | solution.py:360
  106.5 0.7 collective-permute-start.14
  107.2 16.5 %collective-permute-done.17.a_came = bf16[2,3,256,384]{3,2,1,0:T(8,128)(2,1)S(1)} collective-permute-done((bf16[2,3,256,384]{3,2,1,0:T(8,128)(2,1)S(1)}, bf16[2,3,256,384]{3,2,1,0:T(8,128)(2,1)S(1)}, u32[]{:S(2)}, u32[]{:S(2)}) %collective-permute-start.17) | collective-permute-done | bytes 1179680 | tf_op jit(solution)/shard_map/ppermute | solution.py:349
  123.8 1.6 %collective-permute-start.21 = (bf16[3,256,384]{2,1,0:T(8,128)(2,1)S(1)}, bf16[3,256,384]{2,1,0:T(8,128)(2,1)S(1)}, u32[]{:S(2)}, u32[]{:S(2)}) collective-permute-start(bf16[3,256,384]{2,1,0:T(8,128)(2,1)S(1)} %fusion.1), channel_id=1, source_target_pairs={{0,16},{8,24},{16,0},{24,8},{1,17},{9,25},{17,1},{25,9},{2,18},{10... | collective-permute-start | bytes 1769480 | tf_op jit(solution)/shard_map/ppermute | solution.py:349
  125.6 1.5 %collective-permute-start.22 = (bf16[3,256,384]{2,1,0:T(8,128)(2,1)S(1)}, bf16[3,256,384]{2,1,0:T(8,128)(2,1)S(1)}, u32[]{:S(2)}, u32[]{:S(2)}) collective-permute-start(bf16[3,256,384]{2,1,0:T(8,128)(2,1)S(1)} %fusion.2), channel_id=1, source_target_pairs={{0,8},{8,0},{16,24},{24,16},{1,9},{9,1},{17,25},{25,17},{2,10},{10... | collective-permute-start | bytes 1769480 | tf_op jit(solution)/shard_map/ppermute | solution.py:349
  128.4 3.1 %collective-permute-start.20 = (bf16[272,1024]{1,0:T(8,128)(2,1)S(1)}, bf16[272,1024]{1,0:T(8,128)(2,1)S(1)}, u32[]{:S(2)}, u32[]{:S(2)}) collective-permute-start(bf16[272,1024]{1,0:T(8,128)(2,1)S(1)} %add_convert_fusion.3), channel_id=1, source_target_pairs={{0,2},{1,3},{2,0},{3,1},{4,6},{5,7},{6,4},{7,5},{8,10},{9,11},{10,... | collective-permute-start | bytes 1671176 | tf_op jit(solution)/shard_map/ppermute | solution.py:360
  132.2 6.3 %collective-permute-done.21.a_last = bf16[3,256,384]{2,1,0:T(8,128)(2,1)S(1)} collective-permute-done((bf16[3,256,384]{2,1,0:T(8,128)(2,1)S(1)}, bf16[3,256,384]{2,1,0:T(8,128)(2,1)S(1)}, u32[]{:S(2)}, u32[]{:S(2)}) %collective-permute-start.21) | collective-permute-done | bytes 589856 | tf_op jit(solution)/shard_map/ppermute | solution.py:349
  138.4 1.4 collective-permute-done.22.b_last
  139.9 1.4 final_step.1
  141.3 2.3 %collective-permute-done.20.refs_3_ = bf16[272,1024]{1,0:T(8,128)(2,1)S(1)} collective-permute-done((bf16[272,1024]{1,0:T(8,128)(2,1)S(1)}, bf16[272,1024]{1,0:T(8,128)(2,1)S(1)}, u32[]{:S(2)}, u32[]{:S(2)}) %collective-permute-start.20) | collective-permute-done | bytes 557088 | tf_op jit(solution)/shard_map/ppermute | solution.py:360
  143.6 1.1 total.1
  (36 shorter events, 5.3 us)
Async XLA Ops:
  2.7 7.9 %collective-permute-start = (bf16[528,1024]{1,0:T(8,128)(2,1)}, bf16[528,1024]{1,0:T(8,128)(2,1)S(1)}, u32[]{:S(2)}, u32[]{:S(2)}) collective-permute-start(bf16[528,1024]{1,0:T(8,128)(2,1)} %payload.1.refs_0_), channel_id=1, source_target_pairs={{0,1},{1,0},{2,3},{3,2},{4,5},{5,4},{6,7},{7,6},{8,9},{9,8},{10,11... | collective-permute-start | bytes 3244040 | tf_op jit(solution)/shard_map/ppermute | solution.py:363
  3.3 31.5 %collective-permute-start.4 = (bf16[528,1024]{1,0:T(8,128)(2,1)}, bf16[528,1024]{1,0:T(8,128)(2,1)S(1)}, u32[]{:S(2)}, u32[]{:S(2)}) collective-permute-start(bf16[528,1024]{1,0:T(8,128)(2,1)} %payload.1.refs_0_), channel_id=1, source_target_pairs={{0,6},{1,7},{6,0},{7,1},{8,14},{9,15},{14,8},{15,9},{16,22},{17,23... | collective-permute-start | bytes 3244040 | tf_op jit(solution)/shard_map/ppermute | solution.py:360
  9.8 25.0 %collective-permute-start.3 = (bf16[528,1024]{1,0:T(8,128)(2,1)}, bf16[528,1024]{1,0:T(8,128)(2,1)S(1)}, u32[]{:S(2)}, u32[]{:S(2)}) collective-permute-start(bf16[528,1024]{1,0:T(8,128)(2,1)} %payload.1.refs_0_), channel_id=1, source_target_pairs={{2,4},{3,5},{4,2},{5,3},{10,12},{11,13},{12,10},{13,11},{18,20},{1... | collective-permute-start | bytes 3244040 | tf_op jit(solution)/shard_map/ppermute | solution.py:360
  10.5 47.2 %collective-permute-start.2 = (bf16[528,1024]{1,0:T(8,128)(2,1)}, bf16[528,1024]{1,0:T(8,128)(2,1)S(1)}, u32[]{:S(2)}, u32[]{:S(2)}) collective-permute-start(bf16[528,1024]{1,0:T(8,128)(2,1)} %payload.1.refs_0_), channel_id=1, source_target_pairs={{0,2},{1,3},{2,0},{3,1},{4,6},{5,7},{6,4},{7,5},{8,10},{9,11},{10,... | collective-permute-start | bytes 3244040 | tf_op jit(solution)/shard_map/ppermute | solution.py:360
  10.6 2.3 %copy-start = (bf16[1,3,1024,768]{3,2,1,0:T(8,128)(2,1)S(1)}, bf16[1,3,1024,768]{3,2,1,0:T(8,128)(2,1)}, u32[]{:S(2)}) copy-start(bf16[1,3,1024,768]{3,2,1,0:T(8,128)(2,1)} %refs_2_.5) | copy-start | bytes 14155780
  12.9 1.2 copy-start.2
  14.2 47.8 %copy-start.1 = (bf16[1,3,1024,768]{3,2,1,0:T(8,128)(2,1)S(1)}, bf16[1,3,1024,768]{3,2,1,0:T(8,128)(2,1)}, u32[]{:S(2)}) copy-start(bf16[1,3,1024,768]{3,2,1,0:T(8,128)(2,1)} %refs_2_.5) | copy-start | bytes 14155780
  18.3 39.4 %collective-permute-start.1 = (bf16[272,1024]{1,0:T(8,128)(2,1)S(1)}, bf16[272,1024]{1,0:T(8,128)(2,1)S(1)}, u32[]{:S(2)}, u32[]{:S(2)}) collective-permute-start(bf16[272,1024]{1,0:T(8,128)(2,1)S(1)} %get-tuple-element.53), channel_id=1, source_target_pairs={{0,1},{1,0},{2,3},{3,2},{4,5},{5,4},{6,7},{7,6},{8,9},{9,8},{10,11... | collective-permute-start | bytes 1671176 | tf_op jit(solution)/shard_map/ppermute | solution.py:363
  57.8 2.7 %collective-permute-start.6 = (bf16[528,1024]{1,0:T(8,128)(2,1)S(1)}, bf16[528,1024]{1,0:T(8,128)(2,1)S(1)}, u32[]{:S(2)}, u32[]{:S(2)}) collective-permute-start(bf16[528,1024]{1,0:T(8,128)(2,1)S(1)} %collective-permute-done.4.refs_2_), channel_id=1, source_target_pairs={{0,1},{1,0},{2,3},{3,2},{4,5},{5,4},{6,7},{7,6},{8,9},{9,8},{10,11... | collective-permute-start | bytes 3244040 | tf_op jit(solution)/shard_map/ppermute | solution.py:363
  57.8 4.2 %collective-permute-start.5 = (bf16[528,1024]{1,0:T(8,128)(2,1)S(1)}, bf16[528,1024]{1,0:T(8,128)(2,1)S(1)}, u32[]{:S(2)}, u32[]{:S(2)}) collective-permute-start(bf16[528,1024]{1,0:T(8,128)(2,1)S(1)} %collective-permute-done.3.refs_0_), channel_id=1, source_target_pairs={{0,1},{1,0},{2,3},{3,2},{4,5},{5,4},{6,7},{7,6},{8,9},{9,8},{10,11... | collective-permute-start | bytes 3244040 | tf_op jit(solution)/shard_map/ppermute | solution.py:363
  58.3 8.6 %collective-permute-start.10 = (bf16[528,1024]{1,0:T(8,128)(2,1)S(1)}, bf16[528,1024]{1,0:T(8,128)(2,1)S(1)}, u32[]{:S(2)}, u32[]{:S(2)}) collective-permute-start(bf16[528,1024]{1,0:T(8,128)(2,1)S(1)} %collective-permute-done.2.refs_0_), channel_id=1, source_target_pairs={{0,1},{1,0},{2,3},{3,2},{4,5},{5,4},{6,7},{7,6},{8,9},{9,8},{10,11... | collective-permute-start | bytes 3244040 | tf_op jit(solution)/shard_map/ppermute | solution.py:363
  58.3 28.1 %collective-permute-start.8 = (bf16[528,1024]{1,0:T(8,128)(2,1)S(1)}, bf16[528,1024]{1,0:T(8,128)(2,1)S(1)}, u32[]{:S(2)}, u32[]{:S(2)}) collective-permute-start(bf16[528,1024]{1,0:T(8,128)(2,1)S(1)} %collective-permute-done.3.refs_0_), channel_id=1, source_target_pairs={{2,0},{3,1},{4,6},{5,7},{10,8},{11,9},{12,14},{13,15},{18,16},{19,... | collective-permute-start | bytes 3244040 | tf_op jit(solution)/shard_map/ppermute | solution.py:360
  59.6 26.8 %collective-permute-start.9 = (bf16[528,1024]{1,0:T(8,128)(2,1)S(1)}, bf16[528,1024]{1,0:T(8,128)(2,1)S(1)}, u32[]{:S(2)}, u32[]{:S(2)}) collective-permute-start(bf16[528,1024]{1,0:T(8,128)(2,1)S(1)} %collective-permute-done.2.refs_0_), channel_id=1, source_target_pairs={{2,4},{3,5},{4,2},{5,3},{10,12},{11,13},{12,10},{13,11},{18,20},{1... | collective-permute-start | bytes 3244040 | tf_op jit(solution)/shard_map/ppermute | solution.py:360
  66.7 19.8 %collective-permute-start.7 = (bf16[272,1024]{1,0:T(8,128)(2,1)S(1)}, bf16[272,1024]{1,0:T(8,128)(2,1)S(1)}, u32[]{:S(2)}, u32[]{:S(2)}) collective-permute-start(bf16[272,1024]{1,0:T(8,128)(2,1)S(1)} %get-tuple-element.57), channel_id=1, source_target_pairs={{0,1},{1,0},{2,3},{3,2},{4,5},{5,4},{6,7},{7,6},{8,9},{9,8},{10,11... | collective-permute-start | bytes 1671176 | tf_op jit(solution)/shard_map/ppermute | solution.py:363
  71.0 15.4 %collective-permute-start.11 = (bf16[272,1024]{1,0:T(8,128)(2,1)S(1)}, bf16[272,1024]{1,0:T(8,128)(2,1)S(1)}, u32[]{:S(2)}, u32[]{:S(2)}) collective-permute-start(bf16[272,1024]{1,0:T(8,128)(2,1)S(1)} %get-tuple-element.59), channel_id=1, source_target_pairs={{0,1},{1,0},{2,3},{3,2},{4,5},{5,4},{6,7},{7,6},{8,9},{9,8},{10,11... | collective-permute-start | bytes 1671176 | tf_op jit(solution)/shard_map/ppermute | solution.py:363
  86.9 2.8 %collective-permute-start.12 = (bf16[528,1024]{1,0:T(8,128)(2,1)S(1)}, bf16[528,1024]{1,0:T(8,128)(2,1)S(1)}, u32[]{:S(2)}, u32[]{:S(2)}) collective-permute-start(bf16[528,1024]{1,0:T(8,128)(2,1)S(1)} %add_convert_fusion.refs_0_), channel_id=1, source_target_pairs={{0,1},{1,0},{2,3},{3,2},{4,5},{5,4},{6,7},{7,6},{8,9},{9,8},{10,11... | collective-permute-start | bytes 3244040 | tf_op jit(solution)/shard_map/ppermute | solution.py:363
  95.6 28.1 %collective-permute-start.17 = (bf16[2,3,256,384]{3,2,1,0:T(8,128)(2,1)S(1)}, bf16[2,3,256,384]{3,2,1,0:T(8,128)(2,1)S(1)}, u32[]{:S(2)}, u32[]{:S(2)}) collective-permute-start(bf16[2,3,256,384]{3,2,1,0:T(8,128)(2,1)S(1)} %get-tuple-element.87), channel_id=1, source_target_pairs={{0,8},{8,0},{16,24},{24,16},{1,9},{9,1},{17,25},{25,17},{2,10},{10... | collective-permute-start | bytes 3538952 | tf_op jit(solution)/shard_map/ppermute | solution.py:349
  97.1 28.3 %collective-permute-start.18 = (bf16[2,3,256,384]{3,2,1,0:T(8,128)(2,1)S(1)}, bf16[2,3,256,384]{3,2,1,0:T(8,128)(2,1)S(1)}, u32[]{:S(2)}, u32[]{:S(2)}) collective-permute-start(bf16[2,3,256,384]{3,2,1,0:T(8,128)(2,1)S(1)} %get-tuple-element.89), channel_id=1, source_target_pairs={{0,16},{8,24},{16,0},{24,8},{1,17},{9,25},{17,1},{25,9},{2,18},{10... | collective-permute-start | bytes 3538952 | tf_op jit(solution)/shard_map/ppermute | solution.py:349
  98.7 4.6 %collective-permute-start.13 = (bf16[272,1024]{1,0:T(8,128)(2,1)S(1)}, bf16[272,1024]{1,0:T(8,128)(2,1)S(1)}, u32[]{:S(2)}, u32[]{:S(2)}) collective-permute-start(bf16[272,1024]{1,0:T(8,128)(2,1)S(1)} %get-tuple-element.86), channel_id=1, source_target_pairs={{0,1},{1,0},{2,3},{3,2},{4,5},{5,4},{6,7},{7,6},{8,9},{9,8},{10,11... | collective-permute-start | bytes 1671176 | tf_op jit(solution)/shard_map/ppermute | solution.py:363
  98.9 28.2 %collective-permute-start.16 = (bf16[272,1024]{1,0:T(8,128)(2,1)S(1)}, bf16[272,1024]{1,0:T(8,128)(2,1)S(1)}, u32[]{:S(2)}, u32[]{:S(2)}) collective-permute-start(bf16[272,1024]{1,0:T(8,128)(2,1)S(1)} %fusion), channel_id=1, source_target_pairs={{0,6},{1,7},{6,0},{7,1},{8,14},{9,15},{14,8},{15,9},{16,22},{17,23... | collective-permute-start | bytes 1671176 | tf_op jit(solution)/shard_map/ppermute | solution.py:360
  103.5 24.3 %collective-permute-start.15 = (bf16[272,1024]{1,0:T(8,128)(2,1)S(1)}, bf16[272,1024]{1,0:T(8,128)(2,1)S(1)}, u32[]{:S(2)}, u32[]{:S(2)}) collective-permute-start(bf16[272,1024]{1,0:T(8,128)(2,1)S(1)} %add_convert_fusion.5), channel_id=1, source_target_pairs={{0,2},{1,3},{6,4},{7,5},{8,10},{9,11},{14,12},{15,13},{16,18},{17,... | collective-permute-start | bytes 1671176 | tf_op jit(solution)/shard_map/ppermute | solution.py:360
  106.5 21.3 %collective-permute-start.14 = (bf16[272,1024]{1,0:T(8,128)(2,1)S(1)}, bf16[272,1024]{1,0:T(8,128)(2,1)S(1)}, u32[]{:S(2)}, u32[]{:S(2)}) collective-permute-start(bf16[272,1024]{1,0:T(8,128)(2,1)S(1)} %add_convert_fusion.5), channel_id=1, source_target_pairs={{2,4},{3,5},{4,2},{5,3},{10,12},{11,13},{12,10},{13,11},{18,20},{1... | collective-permute-start | bytes 1671176 | tf_op jit(solution)/shard_map/ppermute | solution.py:360
  123.8 14.6 %collective-permute-start.21 = (bf16[3,256,384]{2,1,0:T(8,128)(2,1)S(1)}, bf16[3,256,384]{2,1,0:T(8,128)(2,1)S(1)}, u32[]{:S(2)}, u32[]{:S(2)}) collective-permute-start(bf16[3,256,384]{2,1,0:T(8,128)(2,1)S(1)} %fusion.1), channel_id=1, source_target_pairs={{0,16},{8,24},{16,0},{24,8},{1,17},{9,25},{17,1},{25,9},{2,18},{10... | collective-permute-start | bytes 1769480 | tf_op jit(solution)/shard_map/ppermute | solution.py:349
  125.6 14.3 %collective-permute-start.22 = (bf16[3,256,384]{2,1,0:T(8,128)(2,1)S(1)}, bf16[3,256,384]{2,1,0:T(8,128)(2,1)S(1)}, u32[]{:S(2)}, u32[]{:S(2)}) collective-permute-start(bf16[3,256,384]{2,1,0:T(8,128)(2,1)S(1)} %fusion.2), channel_id=1, source_target_pairs={{0,8},{8,0},{16,24},{24,16},{1,9},{9,1},{17,25},{25,17},{2,10},{10... | collective-permute-start | bytes 1769480 | tf_op jit(solution)/shard_map/ppermute | solution.py:349
  128.4 15.2 %collective-permute-start.20 = (bf16[272,1024]{1,0:T(8,128)(2,1)S(1)}, bf16[272,1024]{1,0:T(8,128)(2,1)S(1)}, u32[]{:S(2)}, u32[]{:S(2)}) collective-permute-start(bf16[272,1024]{1,0:T(8,128)(2,1)S(1)} %add_convert_fusion.3), channel_id=1, source_target_pairs={{0,2},{1,3},{2,0},{3,1},{4,6},{5,7},{6,4},{7,5},{8,10},{9,11},{10,... | collective-permute-start | bytes 1671176 | tf_op jit(solution)/shard_map/ppermute | solution.py:360
  131.5 12.1 %collective-permute-start.19 = (bf16[272,1024]{1,0:T(8,128)(2,1)S(1)}, bf16[272,1024]{1,0:T(8,128)(2,1)S(1)}, u32[]{:S(2)}, u32[]{:S(2)}) collective-permute-start(bf16[272,1024]{1,0:T(8,128)(2,1)S(1)} %add_convert_fusion.4), channel_id=1, source_target_pairs={{2,4},{3,5},{4,2},{5,3},{10,12},{11,13},{12,10},{13,11},{18,20},{1... | collective-permute-start | bytes 1671176 | tf_op jit(solution)/shard_map/ppermute | solution.py:360

commit v6 on v5

--- a/solution.py
+++ b/solution.py
@@ -9,7 +9,7 @@
 
 MICRO = 2
 CORES = 2
-META = 16
+META = 8
 LAST = (((1,), (1,)), ((), ()))
 FIRST = (((0,), (0,)), ((), ()))
 F32 = jnp.float32
@@ -38,7 +38,7 @@
 
     def take_meta(pair):
         for half in range(CORES):
-            meta_buf[half] = pair[half][count : count + META, :count]
+            meta_buf[half] = pair[half][2 * count : 2 * count + META, :count]
 
     chosen_input(take_meta)
     mine = (me + 1).astype(F32)
@@ -69,7 +69,7 @@
             places = slice(number * capacity, (number + 1) * capacity)
             pick = onehot.astype(BF16)
             xr_out[places, :] = dot(pick, pair[half][rows, :]).astype(BF16)
-            cot = dot(pick, pair[half][count + META + rows.start : count + META + rows.stop, :])
+            cot = dot(pick, pair[half][count + rows.start : count + rows.stop, :])
             cot_buf[places, :] = cot
             q_out[places, :] = (gate * cot).astype(BF16)
 
@@ -208,23 +208,19 @@
     return total.astype(BF16)
 
 
-def final_kernel(a_keep, a_came, a_last, b_keep, b_came, b_last, out):
+def final_kernel(a_base, a_last, b_base, b_last, out):
     half = out.shape[2] // 2
-    out[:, :, :half] = (
-        a_keep[1].astype(F32) + a_came[1].astype(F32) + a_last[...].astype(F32)
-    ).astype(BF16)
-    out[:, :, half:] = (
-        b_keep[1].astype(F32) + b_came[1].astype(F32) + b_last[...].astype(F32)
-    ).astype(BF16)
+    out[:, :, :half] = (a_base[...] + a_last[...].astype(F32)).astype(BF16)
+    out[:, :, half:] = (b_base[...] + b_last[...].astype(F32)).astype(BF16)
 
 
 def run_final(*operands):
-    products, rows, half = operands[2].shape
+    products, rows, half = operands[1].shape
     whole = pl.BlockSpec(memory_space=pltpu.VMEM)
     return pl.pallas_call(
         final_kernel,
         out_shape=jax.ShapeDtypeStruct((products, rows, 2 * half), BF16),
-        in_specs=[whole] * 6,
+        in_specs=[whole] * 4,
         out_specs=whole,
         compiler_params=pltpu.CompilerParams(vmem_limit_bytes=12 * 1024 * 1024),
         cost_estimate=pl.CostEstimate(flops=1, bytes_accessed=1, transcendentals=0),
@@ -240,14 +236,9 @@
     ]
     large = [
         pltpu.make_async_copy(tokens, held.at[:count], sems.at[2]),
-        pltpu.make_async_copy(cotangent, held.at[count + META :], sems.at[3]),
+        pltpu.make_async_copy(cotangent, held.at[count : 2 * count], sems.at[3]),
     ]
-    outward = [
-        pltpu.make_async_copy(held.at[part], out.at[part], sems.at[4 + number])
-        for number, part in enumerate(
-            (pl.ds(0, count), pl.ds(count + META, count), pl.ds(count, META))
-        )
-    ]
+    outward = pltpu.make_async_copy(held, out, sems.at[4])
     for copy in small + large:
         copy.start()
     for copy in small:
@@ -262,14 +253,12 @@
     )
     for number, row in enumerate(rows):
         values = jnp.where(line == number, row, values)
-    held[count : count + META, :] = jnp.zeros((META, held.shape[1]), BF16)
-    held[count : count + META, :count] = values.astype(BF16)
-    outward[2].start()
-    for came, sent in zip(large, outward):
-        came.wait()
-        sent.start()
-    for copy in outward:
+    held[2 * count :, :] = jnp.zeros((META, held.shape[1]), BF16)
+    held[2 * count :, :count] = values.astype(BF16)
+    for copy in large:
         copy.wait()
+    outward.start()
+    outward.wait()
 
 
 def make_payload(tokens, cotangent, gates, expert_ids):
@@ -283,7 +272,7 @@
             pltpu.VMEM((2, count), jnp.int32),
             pltpu.VMEM((2, count), BF16),
             pltpu.VMEM((2 * count + META, width), BF16),
-            pltpu.SemaphoreType.DMA((7,)),
+            pltpu.SemaphoreType.DMA((5,)),
         ],
         compiler_params=pltpu.CompilerParams(vmem_limit_bytes=60 * 1024 * 1024),
         cost_estimate=pl.CostEstimate(flops=1, bytes_accessed=1, transcendentals=0),
@@ -353,7 +342,9 @@
         a_came = across(a_send, 1)
         b_came = across(b_send, 2)
         next_pair = (add(a_keep[0], a_came[0]), add(b_keep[0], b_came[0]))
-        return (a_keep, a_came, b_keep, b_came), next_pair, a_keep
+        a_base = a_keep[1].astype(F32) + a_came[1].astype(F32)
+        b_base = b_keep[1].astype(F32) + b_came[1].astype(F32)
+        return (a_base, b_base), next_pair, a_keep
 
     def move(value, pairs):
         full = [(a * CORES + k, b * CORES + k) for a, b in pairs for k in range(CORES)]
@@ -400,7 +391,7 @@
         last_sum = joined(grads)
         sent = add(*last_sum)
         if lax.axis_size("dp") == 4:
-            halves, next_pair, ready = first_step(rows, partial)
+            bases, next_pair, ready = first_step(rows, partial)
             far_sum = after(far_sum, ready)
         else:
             next_pair = ()
@@ -410,7 +401,7 @@
         landed, came, far_back = after((landed, came, far_back), next_pair)
         back = move(add(*first_sum, landed), outer)
         second_back = move(add(*far_sum, came), inner)
-        total = [*own_sum, second_back, back, far_back]
+        total = [add(*own_sum, far_back), back, second_back]
     else:
         rows, grads = compute((own, swap(own)))
         kept = [rows]
@@ -430,13 +421,13 @@
             if value is not None:
                 total.append(value)
         if lax.axis_size("dp") == 4:
-            halves, next_pair, _ = first_step(rows, sum_early(kept[:-1]))
+            bases, next_pair, _ = first_step(rows, sum_early(kept[:-1]))
 
     if lax.axis_size("dp") == 4:
-        a_keep, a_came, b_keep, b_came = halves
+        a_base, b_base = bases
         a_last = across(next_pair[0], 2)
         b_last = across(next_pair[1], 1)
-        weights_grad = run_final(a_keep, a_came, a_last, b_keep, b_came, b_last)[None]
+        weights_grad = run_final(a_base, a_last, b_base, b_last)[None]
     else:
         whole = [jnp.concatenate(value, axis=0) for value in zip(*kept)]
         partial = jnp.stack(

time: 146 us -> 144 us (0.986)
  waiting for transfers between devices: 81.7 us -> 79 us
    ppermute x10, waiting for transfers between devices: 53.2 us -> 50.8 us  [move(): return lax.ppermute(value, 'expert', full)]
  transfers between devices with their start and end apart: 23 -> 23, of which waited for: 11 -> 10; matrix products, arithmetic and copies ran while one was open for 1% -> 1% of each run, Pallas kernels for 13% -> 13%
where the time goes in v6:
time: 144 us; the launch traced here: 143 us
  waiting for transfers between devices  79 us (55%)
  starting transfers between devices  30.1 us (21%)
  Pallas kernels  27.2 us (19%)
  local copies, waits for them, and re-layouts  3.57 us (2%)
  other arithmetic  2.15 us (1%)
    ppermute x10, waiting for transfers between devices, move(): return lax.ppermute(value, 'expert', full)  50.8 us
    ppermute x4, waiting for transfers between devices, across(): return lax.ppermute(value, 'dp', [(i, i ^ bit) for i in range(4)])  23.9 us
    ppermute x10, starting transfers between devices, move(): return lax.ppermute(value, 'expert', full)  21.9 us
    pallas_call x4, Pallas kernels, run_slot(): pl.pallas_call(functools.partial(slot_kernel, choices, batch, capacity, m...  17.3 us
    ppermute x4, starting transfers between devices, across(): return lax.ppermute(value, 'dp', [(i, i ^ bit) for i in range(4)])  6.21 us
    ppermute x9, waiting for transfers between devices, swap(): return lax.ppermute(value, 'expert', [(i, i ^ 1) for i in range(devices)])  4.31 us
    pallas_call x1, Pallas kernels, run_partial(): pl.pallas_call(functools.partial(partial_kernel, len(lefts)), out_shape=j...  3.89 us
    unnamed x6, local copies, waits for them, and re-layouts  3.57 us
  transfers between devices with their start and end apart: 23, of which 10 were waited for; matrix products, arithmetic and copies ran while one was open for 1% of the time, Pallas kernels for 13%

profile of v6, /device:TPU:0, one launch (start us, length us, event | category | flops | bytes accessed | tf_op | source)
XLA Modules:
  0.0 142.9 jit_solution(2421161934528826717)
XLA Ops:
  0.6 2.2 %payload.1.refs_0_ = bf16[520,1024]{1,0:T(8,128)(2,1)} custom-call(bf16[256,1024]{1,0:T(8,128)(2,1)} %tokens.1, bf16[256,1024]{1,0:T(8,128)(2,1)} %cotangent.1, s32[2,256]{1,0:T(2,128)} %bitcast.13, bf16[2,256]{1,0:T(2,128)(2,1)} %bitcast.14), custom_call_target="tpu_custom_call" | custom-call | flops 1 | bytes 1 | tf_op jit(solution)/shard_map/payload/pallas_call | solution.py:266
  3.4 6.5 %collective-permute-start.4 = (bf16[520,1024]{1,0:T(8,128)(2,1)}, bf16[520,1024]{1,0:T(8,128)(2,1)S(1)}, u32[]{:S(2)}, u32[]{:S(2)}) collective-permute-start(bf16[520,1024]{1,0:T(8,128)(2,1)} %payload.1.refs_0_), channel_id=1, source_target_pairs={{0,6},{1,7},{6,0},{7,1},{8,14},{9,15},{14,8},{15,9},{16,22},{17,23... | collective-permute-start | bytes 3194888 | tf_op jit(solution)/shard_map/ppermute | solution.py:351
  9.9 0.7 collective-permute-start.3
  10.8 2.3 %copy-done = bf16[1,3,1024,768]{3,2,1,0:T(8,128)(2,1)S(1)} copy-done((bf16[1,3,1024,768]{3,2,1,0:T(8,128)(2,1)S(1)}, bf16[1,3,1024,768]{3,2,1,0:T(8,128)(2,1)}, u32[]{:S(2)}) %copy-start) | copy-done | bytes 4718616
  13.1 1.2 copy-done.2
  14.3 4.1 %expert_block.4 = (bf16[256,1024]{1,0:T(8,128)(2,1)S(1)}, bf16[256,1024]{1,0:T(8,128)(2,1)S(1)}, bf16[256,768]{1,0:T(8,128)(2,1)S(1)}, bf16[256,768]{1,0:T(8,128...) custom-call(bf16[520,1024]{1,0:T(8,128)(2,1)S(1)} %copy-done.2, ...), custom_call_target="tpu_custom_call" | custom-call | flops 1 | bytes 1 | tf_op jit(solution)/shard_map/expert_block/pallas_call | solution.py:114
  18.8 15.8 %collective-permute-done.4.refs_2_ = bf16[520,1024]{1,0:T(8,128)(2,1)S(1)} collective-permute-done((bf16[520,1024]{1,0:T(8,128)(2,1)}, bf16[520,1024]{1,0:T(8,128)(2,1)S(1)}, u32[]{:S(2)}, u32[]{:S(2)}) %collective-permute-start.4) | collective-permute-done | bytes 1064992 | tf_op jit(solution)/shard_map/ppermute | solution.py:351
  34.6 22.6 %collective-permute-done.2.refs_0_ = bf16[520,1024]{1,0:T(8,128)(2,1)S(1)} collective-permute-done((bf16[520,1024]{1,0:T(8,128)(2,1)}, bf16[520,1024]{1,0:T(8,128)(2,1)S(1)}, u32[]{:S(2)}, u32[]{:S(2)}) %collective-permute-start.2) | collective-permute-done | bytes 1064992 | tf_op jit(solution)/shard_map/ppermute | solution.py:351
  57.8 1.3 collective-permute-start.5
  59.1 0.7 collective-permute-start.6
  59.9 1.5 %collective-permute-done.9.refs_1_ = bf16[520,1024]{1,0:T(8,128)(2,1)S(1)} collective-permute-done((bf16[520,1024]{1,0:T(8,128)(2,1)S(1)}, bf16[520,1024]{1,0:T(8,128)(2,1)S(1)}, u32[]{:S(2)}, u32[]{:S(2)}) %collective-permute-start.9) | collective-permute-done | bytes 1064992 | tf_op jit(solution)/shard_map/ppermute | solution.py:354
  61.4 4.6 %expert_block.6 = (bf16[256,1024]{1,0:T(8,128)(2,1)S(1)}, bf16[256,1024]{1,0:T(8,128)(2,1)S(1)}, bf16[256,768]{1,0:T(8,128)(2,1)S(1)}, bf16[256,768]{1,0:T(8,128...) custom-call(bf16[520,1024]{1,0:T(8,128)(2,1)S(1)} %collective-permute-done.3., ...), custom_call_target="tpu_custom_call" | custom-call | flops 1 | bytes 1 | tf_op jit(solution)/shard_map/expert_block/pallas_call | solution.py:114
  66.3 4.1 %expert_block.5 = (bf16[256,1024]{1,0:T(8,128)(2,1)S(1)}, bf16[256,1024]{1,0:T(8,128)(2,1)S(1)}, bf16[256,768]{1,0:T(8,128)(2,1)S(1)}, bf16[256,768]{1,0:T(8,128...) custom-call(bf16[520,1024]{1,0:T(8,128)(2,1)S(1)} %collective-permute-done.2., ...), custom_call_target="tpu_custom_call" | custom-call | flops 1 | bytes 1 | tf_op jit(solution)/shard_map/expert_block/pallas_call | solution.py:114
  70.9 3.9 %partial_weights.1.refs_6_ = f32[3,1024,768]{2,1,0:T(8,128)S(1)} custom-call(bf16[256,1024]{1,0:T(8,128)(2,1)S(1)} %get-tuple-element.57.refs_0_.refs_6_, bf16[256,1024]{1,0:T(8,128)(2,1)S(1)} %get-tuple-element.58.refs_1_.refs_7_, bf16[256,1024]{1,0:T(8,128)(2,1)S(1)} %get-tuple-element.59.refs_2_.refs_8_, bf16[256,768]{1,0:T(8,128)(2,1)S(1)} %get-tuple-element.60.refs_3_, ...), custom_call_target="tpu_custom_call" | custom-call | flops 1 | bytes 1 | tf_op jit(solution)/shard_map/partial_weights/pallas_call | solution.py:155
  74.8 10.8 %collective-permute-done.5 = bf16[520,1024]{1,0:T(8,128)(2,1)S(1)} collective-permute-done((bf16[520,1024]{1,0:T(8,128)(2,1)S(1)}, bf16[520,1024]{1,0:T(8,128)(2,1)S(1)}, u32[]{:S(2)}, u32[]{:S(2)}) %collective-permute-start.5) | collective-permute-done | bytes 1064992 | tf_op jit(solution)/shard_map/ppermute | solution.py:351
  86.0 2.7 %collective-permute-done.12.refs_1_ = bf16[520,1024]{1,0:T(8,128)(2,1)S(1)} collective-permute-done((bf16[520,1024]{1,0:T(8,128)(2,1)S(1)}, bf16[520,1024]{1,0:T(8,128)(2,1)S(1)}, u32[]{:S(2)}, u32[]{:S(2)}) %collective-permute-start.12) | collective-permute-done | bytes 1064992 | tf_op jit(solution)/shard_map/ppermute | solution.py:354
  88.7 4.4 %expert_block.7 = (bf16[256,1024]{1,0:T(8,128)(2,1)S(1)}, bf16[256,1024]{1,0:T(8,128)(2,1)S(1)}, bf16[256,768]{1,0:T(8,128)(2,1)S(1)}, bf16[256,768]{1,0:T(8,128...) custom-call(bf16[520,1024]{1,0:T(8,128)(2,1)S(1)} %add_convert_fusion.refs_0_, ...), custom_call_target="tpu_custom_call" | custom-call | flops 1 | bytes 1 | tf_op jit(solution)/shard_map/expert_block/pallas_call | solution.py:114
  93.1 1.5 %weight_block.1 = (bf16[2,3,256,384]{3,2,1,0:T(8,128)(2,1)S(1)}, bf16[2,3,256,384]{3,2,1,0:T(8,128)(2,1)S(1)}, bf16[2,3,256,384]{3,2,1,0:T(8,128)(2,1)S(1)}, bf16[2,3,256,384]{3,2,1,0:T(8,128)(2,1)S(1)}) custom-call(bf16[256,1024]{1,0:T(8,128)(2,1)S(1)} %get-tuple-element.77.refs_0_.refs_2_, bf16[256,768]{1,0:T(8,128)(2,1)S(1)} %get-tuple-element.78.refs_1_, ...), custom_call_target="tpu_custom_call" | custom-call | flops 1 | bytes 1 | tf_op jit(solution)/shard_map/weight_block/pallas_call | solution.py:193
  94.7 1.5 %collective-permute-start.17 = (bf16[2,3,256,384]{3,2,1,0:T(8,128)(2,1)S(1)}, bf16[2,3,256,384]{3,2,1,0:T(8,128)(2,1)S(1)}, u32[]{:S(2)}, u32[]{:S(2)}) collective-permute-start(bf16[2,3,256,384]{3,2,1,0:T(8,128)(2,1)S(1)} %get-tuple-element.85), channel_id=1, source_target_pairs={{0,8},{8,0},{16,24},{24,16},{1,9},{9,1},{17,25},{25,17},{2,10},{10... | collective-permute-start | bytes 3538952 | tf_op jit(solution)/shard_map/ppermute | solution.py:338
  96.2 1.5 %collective-permute-start.18 = (bf16[2,3,256,384]{3,2,1,0:T(8,128)(2,1)S(1)}, bf16[2,3,256,384]{3,2,1,0:T(8,128)(2,1)S(1)}, u32[]{:S(2)}, u32[]{:S(2)}) collective-permute-start(bf16[2,3,256,384]{3,2,1,0:T(8,128)(2,1)S(1)} %get-tuple-element.87), channel_id=1, source_target_pairs={{0,16},{8,24},{16,0},{24,8},{1,17},{9,25},{17,1},{25,9},{2,18},{10... | collective-permute-start | bytes 3538952 | tf_op jit(solution)/shard_map/ppermute | solution.py:338
  97.9 4.4 %collective-permute-start.16 = (bf16[264,1024]{1,0:T(8,128)(2,1)S(1)}, bf16[264,1024]{1,0:T(8,128)(2,1)S(1)}, u32[]{:S(2)}, u32[]{:S(2)}) collective-permute-start(bf16[264,1024]{1,0:T(8,128)(2,1)S(1)} %fusion), channel_id=1, source_target_pairs={{0,6},{1,7},{6,0},{7,1},{8,14},{9,15},{14,8},{15,9},{16,22},{17,23... | collective-permute-start | bytes 1622024 | tf_op jit(solution)/shard_map/ppermute | solution.py:351
  102.5 3.0 %collective-permute-start.15 = (bf16[264,1024]{1,0:T(8,128)(2,1)S(1)}, bf16[264,1024]{1,0:T(8,128)(2,1)S(1)}, u32[]{:S(2)}, u32[]{:S(2)}) collective-permute-start(bf16[264,1024]{1,0:T(8,128)(2,1)S(1)} %add_convert_fusion.6), channel_id=1, source_target_pairs={{0,2},{1,3},{6,4},{7,5},{8,10},{9,11},{14,12},{15,13},{16,18},{17,... | collective-permute-start | bytes 1622024 | tf_op jit(solution)/shard_map/ppermute | solution.py:351
  105.5 0.7 collective-permute-start.14
  106.2 16.5 %collective-permute-done.17 = bf16[2,3,256,384]{3,2,1,0:T(8,128)(2,1)S(1)} collective-permute-done((bf16[2,3,256,384]{3,2,1,0:T(8,128)(2,1)S(1)}, bf16[2,3,256,384]{3,2,1,0:T(8,128)(2,1)S(1)}, u32[]{:S(2)}, u32[]{:S(2)}) %collective-permute-start.17) | collective-permute-done | bytes 1179680 | tf_op jit(solution)/shard_map/ppermute | solution.py:338
  123.0 1.6 %collective-permute-start.21 = (bf16[3,256,384]{2,1,0:T(8,128)(2,1)S(1)}, bf16[3,256,384]{2,1,0:T(8,128)(2,1)S(1)}, u32[]{:S(2)}, u32[]{:S(2)}) collective-permute-start(bf16[3,256,384]{2,1,0:T(8,128)(2,1)S(1)} %get-tuple-element.100), channel_id=1, source_target_pairs={{0,16},{8,24},{16,0},{24,8},{1,17},{9,25},{17,1},{25,9},{2,18},{10... | collective-permute-start | bytes 1769480 | tf_op jit(solution)/shard_map/ppermute | solution.py:338
  124.8 1.6 %collective-permute-start.22 = (bf16[3,256,384]{2,1,0:T(8,128)(2,1)S(1)}, bf16[3,256,384]{2,1,0:T(8,128)(2,1)S(1)}, u32[]{:S(2)}, u32[]{:S(2)}) collective-permute-start(bf16[3,256,384]{2,1,0:T(8,128)(2,1)S(1)} %get-tuple-element.98), channel_id=1, source_target_pairs={{0,8},{8,0},{16,24},{24,16},{1,9},{9,1},{17,25},{25,17},{2,10},{10... | collective-permute-start | bytes 1769480 | tf_op jit(solution)/shard_map/ppermute | solution.py:338
  127.0 3.8 %collective-permute-start.19 = (bf16[264,1024]{1,0:T(8,128)(2,1)S(1)}, bf16[264,1024]{1,0:T(8,128)(2,1)S(1)}, u32[]{:S(2)}, u32[]{:S(2)}) collective-permute-start(bf16[264,1024]{1,0:T(8,128)(2,1)S(1)} %add_convert_fusion.4), channel_id=1, source_target_pairs={{0,2},{1,3},{2,0},{3,1},{4,6},{5,7},{6,4},{7,5},{8,10},{9,11},{10,... | collective-permute-start | bytes 1622024 | tf_op jit(solution)/shard_map/ppermute | solution.py:351
  131.7 5.9 %collective-permute-done.21.a_last = bf16[3,256,384]{2,1,0:T(8,128)(2,1)S(1)} collective-permute-done((bf16[3,256,384]{2,1,0:T(8,128)(2,1)S(1)}, bf16[3,256,384]{2,1,0:T(8,128)(2,1)S(1)}, u32[]{:S(2)}, u32[]{:S(2)}) %collective-permute-start.21) | collective-permute-done | bytes 589856 | tf_op jit(solution)/shard_map/ppermute | solution.py:338
  137.6 1.5 %collective-permute-done.22.b_last = bf16[3,256,384]{2,1,0:T(8,128)(2,1)S(1)} collective-permute-done((bf16[3,256,384]{2,1,0:T(8,128)(2,1)S(1)}, bf16[3,256,384]{2,1,0:T(8,128)(2,1)S(1)}, u32[]{:S(2)}, u32[]{:S(2)}) %collective-permute-start.22) | collective-permute-done | bytes 589856 | tf_op jit(solution)/shard_map/ppermute | solution.py:338
  139.2 1.2 final_step.1
  140.4 1.6 %collective-permute-done.19.refs_1_ = bf16[264,1024]{1,0:T(8,128)(2,1)S(1)} collective-permute-done((bf16[264,1024]{1,0:T(8,128)(2,1)S(1)}, bf16[264,1024]{1,0:T(8,128)(2,1)S(1)}, u32[]{:S(2)}, u32[]{:S(2)}) %collective-permute-start.19) | collective-permute-done | bytes 540704 | tf_op jit(solution)/shard_map/ppermute | solution.py:351
  142.0 1.0 total.1
  (37 shorter events, 5.1 us)
Async XLA Ops:
  2.9 7.9 %collective-permute-start = (bf16[520,1024]{1,0:T(8,128)(2,1)}, bf16[520,1024]{1,0:T(8,128)(2,1)S(1)}, u32[]{:S(2)}, u32[]{:S(2)}) collective-permute-start(bf16[520,1024]{1,0:T(8,128)(2,1)} %payload.1.refs_0_), channel_id=1, source_target_pairs={{0,1},{1,0},{2,3},{3,2},{4,5},{5,4},{6,7},{7,6},{8,9},{9,8},{10,11... | collective-permute-start | bytes 3194888 | tf_op jit(solution)/shard_map/ppermute | solution.py:354
  3.4 31.2 %collective-permute-start.4 = (bf16[520,1024]{1,0:T(8,128)(2,1)}, bf16[520,1024]{1,0:T(8,128)(2,1)S(1)}, u32[]{:S(2)}, u32[]{:S(2)}) collective-permute-start(bf16[520,1024]{1,0:T(8,128)(2,1)} %payload.1.refs_0_), channel_id=1, source_target_pairs={{0,6},{1,7},{6,0},{7,1},{8,14},{9,15},{14,8},{15,9},{16,22},{17,23... | collective-permute-start | bytes 3194888 | tf_op jit(solution)/shard_map/ppermute | solution.py:351
  9.9 24.7 %collective-permute-start.3 = (bf16[520,1024]{1,0:T(8,128)(2,1)}, bf16[520,1024]{1,0:T(8,128)(2,1)S(1)}, u32[]{:S(2)}, u32[]{:S(2)}) collective-permute-start(bf16[520,1024]{1,0:T(8,128)(2,1)} %payload.1.refs_0_), channel_id=1, source_target_pairs={{2,4},{3,5},{4,2},{5,3},{10,12},{11,13},{12,10},{13,11},{18,20},{1... | collective-permute-start | bytes 3194888 | tf_op jit(solution)/shard_map/ppermute | solution.py:351
  10.7 46.5 %collective-permute-start.2 = (bf16[520,1024]{1,0:T(8,128)(2,1)}, bf16[520,1024]{1,0:T(8,128)(2,1)S(1)}, u32[]{:S(2)}, u32[]{:S(2)}) collective-permute-start(bf16[520,1024]{1,0:T(8,128)(2,1)} %payload.1.refs_0_), channel_id=1, source_target_pairs={{0,2},{1,3},{2,0},{3,1},{4,6},{5,7},{6,4},{7,5},{8,10},{9,11},{10,... | collective-permute-start | bytes 3194888 | tf_op jit(solution)/shard_map/ppermute | solution.py:351
  10.8 2.3 %copy-start = (bf16[1,3,1024,768]{3,2,1,0:T(8,128)(2,1)S(1)}, bf16[1,3,1024,768]{3,2,1,0:T(8,128)(2,1)}, u32[]{:S(2)}) copy-start(bf16[1,3,1024,768]{3,2,1,0:T(8,128)(2,1)} %refs_2_.5) | copy-start | bytes 14155780
  13.1 1.2 copy-start.2
  14.3 47.1 %copy-start.1 = (bf16[1,3,1024,768]{3,2,1,0:T(8,128)(2,1)S(1)}, bf16[1,3,1024,768]{3,2,1,0:T(8,128)(2,1)}, u32[]{:S(2)}) copy-start(bf16[1,3,1024,768]{3,2,1,0:T(8,128)(2,1)} %refs_2_.5) | copy-start | bytes 14155780
  18.5 38.7 %collective-permute-start.1 = (bf16[264,1024]{1,0:T(8,128)(2,1)S(1)}, bf16[264,1024]{1,0:T(8,128)(2,1)S(1)}, u32[]{:S(2)}, u32[]{:S(2)}) collective-permute-start(bf16[264,1024]{1,0:T(8,128)(2,1)S(1)} %get-tuple-element.51), channel_id=1, source_target_pairs={{0,1},{1,0},{2,3},{3,2},{4,5},{5,4},{6,7},{7,6},{8,9},{9,8},{10,11... | collective-permute-start | bytes 1622024 | tf_op jit(solution)/shard_map/ppermute | solution.py:354
  57.2 2.7 %collective-permute-start.10 = (bf16[520,1024]{1,0:T(8,128)(2,1)S(1)}, bf16[520,1024]{1,0:T(8,128)(2,1)S(1)}, u32[]{:S(2)}, u32[]{:S(2)}) collective-permute-start(bf16[520,1024]{1,0:T(8,128)(2,1)S(1)} %collective-permute-done.4.refs_2_), channel_id=1, source_target_pairs={{0,1},{1,0},{2,3},{3,2},{4,5},{5,4},{6,7},{7,6},{8,9},{9,8},{10,11... | collective-permute-start | bytes 3194888 | tf_op jit(solution)/shard_map/ppermute | solution.py:354
  57.3 4.2 %collective-permute-start.9 = (bf16[520,1024]{1,0:T(8,128)(2,1)S(1)}, bf16[520,1024]{1,0:T(8,128)(2,1)S(1)}, u32[]{:S(2)}, u32[]{:S(2)}) collective-permute-start(bf16[520,1024]{1,0:T(8,128)(2,1)S(1)} %collective-permute-done.3.refs_0_), channel_id=1, source_target_pairs={{0,1},{1,0},{2,3},{3,2},{4,5},{5,4},{6,7},{7,6},{8,9},{9,8},{10,11... | collective-permute-start | bytes 3194888 | tf_op jit(solution)/shard_map/ppermute | solution.py:354
  57.7 8.5 %collective-permute-start.7 = (bf16[520,1024]{1,0:T(8,128)(2,1)S(1)}, bf16[520,1024]{1,0:T(8,128)(2,1)S(1)}, u32[]{:S(2)}, u32[]{:S(2)}) collective-permute-start(bf16[520,1024]{1,0:T(8,128)(2,1)S(1)} %collective-permute-done.2.refs_0_), channel_id=1, source_target_pairs={{0,1},{1,0},{2,3},{3,2},{4,5},{5,4},{6,7},{7,6},{8,9},{9,8},{10,11... | collective-permute-start | bytes 3194888 | tf_op jit(solution)/shard_map/ppermute | solution.py:354
  57.8 27.8 %collective-permute-start.5 = (bf16[520,1024]{1,0:T(8,128)(2,1)S(1)}, bf16[520,1024]{1,0:T(8,128)(2,1)S(1)}, u32[]{:S(2)}, u32[]{:S(2)}) collective-permute-start(bf16[520,1024]{1,0:T(8,128)(2,1)S(1)} %collective-permute-done.3.refs_0_), channel_id=1, source_target_pairs={{2,0},{3,1},{4,6},{5,7},{10,8},{11,9},{12,14},{13,15},{18,16},{19,... | collective-permute-start | bytes 3194888 | tf_op jit(solution)/shard_map/ppermute | solution.py:351
  59.1 26.5 %collective-permute-start.6 = (bf16[520,1024]{1,0:T(8,128)(2,1)S(1)}, bf16[520,1024]{1,0:T(8,128)(2,1)S(1)}, u32[]{:S(2)}, u32[]{:S(2)}) collective-permute-start(bf16[520,1024]{1,0:T(8,128)(2,1)S(1)} %collective-permute-done.2.refs_0_), channel_id=1, source_target_pairs={{2,4},{3,5},{4,2},{5,3},{10,12},{11,13},{12,10},{13,11},{18,20},{1... | collective-permute-start | bytes 3194888 | tf_op jit(solution)/shard_map/ppermute | solution.py:351
  66.1 19.5 %collective-permute-start.11 = (bf16[264,1024]{1,0:T(8,128)(2,1)S(1)}, bf16[264,1024]{1,0:T(8,128)(2,1)S(1)}, u32[]{:S(2)}, u32[]{:S(2)}) collective-permute-start(bf16[264,1024]{1,0:T(8,128)(2,1)S(1)} %get-tuple-element.56), channel_id=1, source_target_pairs={{0,1},{1,0},{2,3},{3,2},{4,5},{5,4},{6,7},{7,6},{8,9},{9,8},{10,11... | collective-permute-start | bytes 1622024 | tf_op jit(solution)/shard_map/ppermute | solution.py:354
  70.4 15.1 %collective-permute-start.8 = (bf16[264,1024]{1,0:T(8,128)(2,1)S(1)}, bf16[264,1024]{1,0:T(8,128)(2,1)S(1)}, u32[]{:S(2)}, u32[]{:S(2)}) collective-permute-start(bf16[264,1024]{1,0:T(8,128)(2,1)S(1)} %get-tuple-element.54), channel_id=1, source_target_pairs={{0,1},{1,0},{2,3},{3,2},{4,5},{5,4},{6,7},{7,6},{8,9},{9,8},{10,11... | collective-permute-start | bytes 1622024 | tf_op jit(solution)/shard_map/ppermute | solution.py:354
  86.0 2.7 %collective-permute-start.12 = (bf16[520,1024]{1,0:T(8,128)(2,1)S(1)}, bf16[520,1024]{1,0:T(8,128)(2,1)S(1)}, u32[]{:S(2)}, u32[]{:S(2)}) collective-permute-start(bf16[520,1024]{1,0:T(8,128)(2,1)S(1)} %add_convert_fusion.refs_0_), channel_id=1, source_target_pairs={{0,1},{1,0},{2,3},{3,2},{4,5},{5,4},{6,7},{7,6},{8,9},{9,8},{10,11... | collective-permute-start | bytes 3194888 | tf_op jit(solution)/shard_map/ppermute | solution.py:354
  94.7 28.1 %collective-permute-start.17 = (bf16[2,3,256,384]{3,2,1,0:T(8,128)(2,1)S(1)}, bf16[2,3,256,384]{3,2,1,0:T(8,128)(2,1)S(1)}, u32[]{:S(2)}, u32[]{:S(2)}) collective-permute-start(bf16[2,3,256,384]{3,2,1,0:T(8,128)(2,1)S(1)} %get-tuple-element.85), channel_id=1, source_target_pairs={{0,8},{8,0},{16,24},{24,16},{1,9},{9,1},{17,25},{25,17},{2,10},{10... | collective-permute-start | bytes 3538952 | tf_op jit(solution)/shard_map/ppermute | solution.py:338
  96.2 28.4 %collective-permute-start.18 = (bf16[2,3,256,384]{3,2,1,0:T(8,128)(2,1)S(1)}, bf16[2,3,256,384]{3,2,1,0:T(8,128)(2,1)S(1)}, u32[]{:S(2)}, u32[]{:S(2)}) collective-permute-start(bf16[2,3,256,384]{3,2,1,0:T(8,128)(2,1)S(1)} %get-tuple-element.87), channel_id=1, source_target_pairs={{0,16},{8,24},{16,0},{24,8},{1,17},{9,25},{17,1},{25,9},{2,18},{10... | collective-permute-start | bytes 3538952 | tf_op jit(solution)/shard_map/ppermute | solution.py:338
  97.7 4.6 %collective-permute-start.13 = (bf16[264,1024]{1,0:T(8,128)(2,1)S(1)}, bf16[264,1024]{1,0:T(8,128)(2,1)S(1)}, u32[]{:S(2)}, u32[]{:S(2)}) collective-permute-start(bf16[264,1024]{1,0:T(8,128)(2,1)S(1)} %get-tuple-element.75), channel_id=1, source_target_pairs={{0,1},{1,0},{2,3},{3,2},{4,5},{5,4},{6,7},{7,6},{8,9},{9,8},{10,11... | collective-permute-start | bytes 1622024 | tf_op jit(solution)/shard_map/ppermute | solution.py:354
  97.9 28.5 %collective-permute-start.16 = (bf16[264,1024]{1,0:T(8,128)(2,1)S(1)}, bf16[264,1024]{1,0:T(8,128)(2,1)S(1)}, u32[]{:S(2)}, u32[]{:S(2)}) collective-permute-start(bf16[264,1024]{1,0:T(8,128)(2,1)S(1)} %fusion), channel_id=1, source_target_pairs={{0,6},{1,7},{6,0},{7,1},{8,14},{9,15},{14,8},{15,9},{16,22},{17,23... | collective-permute-start | bytes 1622024 | tf_op jit(solution)/shard_map/ppermute | solution.py:351
  102.5 23.9 %collective-permute-start.15 = (bf16[264,1024]{1,0:T(8,128)(2,1)S(1)}, bf16[264,1024]{1,0:T(8,128)(2,1)S(1)}, u32[]{:S(2)}, u32[]{:S(2)}) collective-permute-start(bf16[264,1024]{1,0:T(8,128)(2,1)S(1)} %add_convert_fusion.6), channel_id=1, source_target_pairs={{0,2},{1,3},{6,4},{7,5},{8,10},{9,11},{14,12},{15,13},{16,18},{17,... | collective-permute-start | bytes 1622024 | tf_op jit(solution)/shard_map/ppermute | solution.py:351
  105.5 20.9 %collective-permute-start.14 = (bf16[264,1024]{1,0:T(8,128)(2,1)S(1)}, bf16[264,1024]{1,0:T(8,128)(2,1)S(1)}, u32[]{:S(2)}, u32[]{:S(2)}) collective-permute-start(bf16[264,1024]{1,0:T(8,128)(2,1)S(1)} %add_convert_fusion.6), channel_id=1, source_target_pairs={{2,4},{3,5},{4,2},{5,3},{10,12},{11,13},{12,10},{13,11},{18,20},{1... | collective-permute-start | bytes 1622024 | tf_op jit(solution)/shard_map/ppermute | solution.py:351
  123.0 14.6 %collective-permute-start.21 = (bf16[3,256,384]{2,1,0:T(8,128)(2,1)S(1)}, bf16[3,256,384]{2,1,0:T(8,128)(2,1)S(1)}, u32[]{:S(2)}, u32[]{:S(2)}) collective-permute-start(bf16[3,256,384]{2,1,0:T(8,128)(2,1)S(1)} %get-tuple-element.100), channel_id=1, source_target_pairs={{0,16},{8,24},{16,0},{24,8},{1,17},{9,25},{17,1},{25,9},{2,18},{10... | collective-permute-start | bytes 1769480 | tf_op jit(solution)/shard_map/ppermute | solution.py:338
  124.8 14.3 %collective-permute-start.22 = (bf16[3,256,384]{2,1,0:T(8,128)(2,1)S(1)}, bf16[3,256,384]{2,1,0:T(8,128)(2,1)S(1)}, u32[]{:S(2)}, u32[]{:S(2)}) collective-permute-start(bf16[3,256,384]{2,1,0:T(8,128)(2,1)S(1)} %get-tuple-element.98), channel_id=1, source_target_pairs={{0,8},{8,0},{16,24},{24,16},{1,9},{9,1},{17,25},{25,17},{2,10},{10... | collective-permute-start | bytes 1769480 | tf_op jit(solution)/shard_map/ppermute | solution.py:338
  127.0 15.0 %collective-permute-start.19 = (bf16[264,1024]{1,0:T(8,128)(2,1)S(1)}, bf16[264,1024]{1,0:T(8,128)(2,1)S(1)}, u32[]{:S(2)}, u32[]{:S(2)}) collective-permute-start(bf16[264,1024]{1,0:T(8,128)(2,1)S(1)} %add_convert_fusion.4), channel_id=1, source_target_pairs={{0,2},{1,3},{2,0},{3,1},{4,6},{5,7},{6,4},{7,5},{8,10},{9,11},{10,... | collective-permute-start | bytes 1622024 | tf_op jit(solution)/shard_map/ppermute | solution.py:351
  130.8 11.2 %collective-permute-start.20 = (bf16[264,1024]{1,0:T(8,128)(2,1)S(1)}, bf16[264,1024]{1,0:T(8,128)(2,1)S(1)}, u32[]{:S(2)}, u32[]{:S(2)}) collective-permute-start(bf16[264,1024]{1,0:T(8,128)(2,1)S(1)} %add_convert_fusion.3), channel_id=1, source_target_pairs={{2,4},{3,5},{4,2},{5,3},{10,12},{11,13},{12,10},{13,11},{18,20},{1... | collective-permute-start | bytes 1622024 | tf_op jit(solution)/shard_map/ppermute | solution.py:351

commit v7 on v6

--- a/solution.py
+++ b/solution.py
@@ -20,11 +20,15 @@
     return lax.dot_general(lhs, rhs, dims, preferred_element_type=F32)
 
 
-def slot_kernel(choices, batch, capacity, middle, *refs):
-    inputs = refs[: 2 * choices]
-    weights = refs[2 * choices]
-    xr_out, q_out, h_out, da_out, db_out, dxa_out, dxb_out = refs[2 * choices + 1 : 2 * choices + 8]
-    meta_buf, cot_buf = refs[2 * choices + 8 :]
+def slot_kernel(choices, fused, batch, capacity, middle, *refs):
+    inputs, rest = refs[: 2 * choices], refs[2 * choices :]
+    weights, rest = rest[0], rest[1:]
+    if fused:
+        partial, pieces, rest = rest[0], rest[1:5], rest[5:]
+        dxa_out, dxb_out, xr_out, q_out, h_out, da_out, db_out = rest[:7]
+    else:
+        xr_out, q_out, h_out, da_out, db_out, dxa_out, dxb_out = rest[:7]
+    meta_buf, cot_buf = rest[7:]
     count = MICRO * batch
     me = lax.axis_index("expert")
     inner = (me // CORES >= middle[0]) & (me // CORES <= middle[1])
@@ -88,6 +92,8 @@
     db = (hidden_grad * activated).astype(BF16)
     da_out[...] = da
     db_out[...] = db
+    if fused:
+        weight_sums(((xr_out, da_out), (xr_out, db_out), (q_out, h_out)), partial, *pieces)
     dx = (dot(da, weights[0, 0], LAST) + dot(db, weights[0, 1], LAST)).astype(BF16)
     line = lax.broadcasted_iota(jnp.int32, (META, batch), 0)
     outs = (dxa_out, dxb_out)
@@ -103,35 +109,38 @@
         outs[half][count : count + META, rows] = values.astype(BF16)
 
 
-def run_slot(alternatives, weights, batch, capacity, middle):
+def run_slot(alternatives, weights, batch, capacity, middle, partial=None):
     choices = len(alternatives)
     width = weights.shape[2]
     rows = MICRO * batch + META
     hidden_width = weights.shape[-1]
     slots = CORES * MICRO * capacity
-    operands = [array for group in alternatives for array in group]
-    shape = jax.ShapeDtypeStruct
+    operands = [array for group in alternatives for array in group] + [weights]
+    wide, narrow = (slots, width), (slots, hidden_width)
+    packed = [wide, wide, narrow, narrow, narrow]
+    returned = [(rows, width)] * 2
+    scratch = [
+        pltpu.VMEM((CORES, META, MICRO * batch), BF16),
+        pltpu.VMEM(wide, F32),
+    ]
+    if partial is None:
+        shapes = packed + returned
+    else:
+        operands.append(partial)
+        shapes = [(2, partial.shape[0], width // 4, hidden_width // 2)] * 4 + returned
+        scratch = [pltpu.VMEM(shape, BF16) for shape in packed] + scratch
     return pl.pallas_call(
-        functools.partial(slot_kernel, choices, batch, capacity, middle),
-        out_shape=[
-            shape((slots, width), BF16),
-            shape((slots, width), BF16),
-            shape((slots, hidden_width), BF16),
-            shape((slots, hidden_width), BF16),
-            shape((slots, hidden_width), BF16),
-            shape((rows, width), BF16),
-            shape((rows, width), BF16),
-        ],
-        in_specs=[pl.BlockSpec(memory_space=pltpu.VMEM)] * (len(operands) + 1),
-        out_specs=[pl.BlockSpec(memory_space=pltpu.VMEM)] * 7,
-        scratch_shapes=[
-            pltpu.VMEM((CORES, META, MICRO * batch), BF16),
-            pltpu.VMEM((slots, width), F32),
-        ],
-        compiler_params=pltpu.CompilerParams(vmem_limit_bytes=24 * 1024 * 1024),
+        functools.partial(slot_kernel, choices, partial is not None, batch, capacity, middle),
+        out_shape=[jax.ShapeDtypeStruct(shape, BF16) for shape in shapes],
+        in_specs=[pl.BlockSpec(memory_space=pltpu.VMEM)] * len(operands),
+        out_specs=[pl.BlockSpec(memory_space=pltpu.VMEM)] * len(shapes),
+        scratch_shapes=scratch,
+        compiler_params=pltpu.CompilerParams(
+            vmem_limit_bytes=(24 if partial is None else 32) * 1024 * 1024
+        ),
         cost_estimate=pl.CostEstimate(flops=1, bytes_accessed=1, transcendentals=0),
         name="expert_block",
-    )(*operands, weights)
+    )(*operands)
 
 
 def partial_kernel(pieces, *refs):
@@ -163,11 +172,9 @@
     )(*operands)
 
 
-def weight_kernel(*refs):
-    operands = refs[:-5]
-    partial, a_send, a_keep, b_send, b_keep = refs[-5:]
+def weight_sums(products, partial, a_send, a_keep, b_send, b_keep):
     here = lax.axis_index("dp")
-    products, width, hidden_width = partial.shape
+    width, hidden_width = partial.shape[1:]
     quarter = width // 4
     half = hidden_width // 2
     places = (
@@ -178,27 +185,10 @@
     )
     for place, a_out, a_at, b_out, b_at in places:
         rows = pl.ds(pl.multiple_of((here ^ place) * quarter, quarter), quarter)
-        for product in range(products):
-            left, right = operands[2 * product : 2 * product + 2]
+        for product, (left, right) in enumerate(products):
             value = (partial[product, rows, :] + dot(left[:, rows], right[...], FIRST)).astype(BF16)
             a_out[a_at, product] = value[:, :half]
             b_out[b_at, product] = value[:, half:]
-
-
-def run_weight(products, partial):
-    count, width, hidden_width = partial.shape
-    piece = jax.ShapeDtypeStruct((2, count, width // 4, hidden_width // 2), BF16)
-    operands = [array for pair in products for array in pair]
-    whole = pl.BlockSpec(memory_space=pltpu.VMEM)
-    return pl.pallas_call(
-        weight_kernel,
-        out_shape=[piece] * 4,
-        in_specs=[whole] * (len(operands) + 1),
-        out_specs=[whole] * 4,
-        compiler_params=pltpu.CompilerParams(vmem_limit_bytes=24 * 1024 * 1024),
-        cost_estimate=pl.CostEstimate(flops=1, bytes_accessed=1, transcendentals=0),
-        name="weight_block",
-    )(*operands, partial)
 
 
 def add(*values):
@@ -337,8 +327,8 @@
     def across(value, bit):
         return lax.ppermute(value, "dp", [(i, i ^ bit) for i in range(4)])
 
-    def first_step(rows, partial):
-        a_send, a_keep, b_send, b_keep = run_weight(products_of(rows), partial)
+    def first_step(sums):
+        a_send, a_keep, b_send, b_keep = sums
         a_came = across(a_send, 1)
         b_came = across(b_send, 2)
         next_pair = (add(a_keep[0], a_came[0]), add(b_keep[0], b_came[0]))
@@ -353,16 +343,17 @@
     def swap(value):
         return lax.ppermute(value, "expert", [(i, i ^ 1) for i in range(devices)])
 
-    def compute(*alternatives):
-        result = run_slot(alternatives, expert_weights, batch, capacity, (1, chips - 2))
-        return result[:5], (result[5], result[6])
+    def compute(*alternatives, partial=None):
+        result = run_slot(alternatives, expert_weights, batch, capacity, (1, chips - 2), partial)
+        return result[:-2], (result[-2], result[-1])
 
     def joined(grads):
         return (grads[0], swap(grads[1]))
 
     ahead = [(z, (z + 1) % chips) for z in range(chips)]
     behind = [(b, a) for a, b in ahead]
-    if chips == 4:
+    tuned = chips == 4 and lax.axis_size("dp") == 4
+    if tuned:
         outer = [(0, 1), (1, 0), (2, 3), (3, 2)]
         inner = [(1, 2), (2, 1)]
         to_ends = [(1, 0), (2, 3)]
@@ -386,15 +377,11 @@
         partial = sum_early(kept)
         third, fourth = after((third, fourth), first_sum[1], far_sum[1], partial)
         last = add(fourth, third)
-        rows, grads = compute((last, swap(last)))
-        kept.append(rows)
+        sums, grads = compute((last, swap(last)), partial=partial)
         last_sum = joined(grads)
         sent = add(*last_sum)
-        if lax.axis_size("dp") == 4:
-            bases, next_pair, ready = first_step(rows, partial)
-            far_sum = after(far_sum, ready)
-        else:
-            next_pair = ()
+        bases, next_pair, ready = first_step(sums)
+        far_sum = after(far_sum, ready)
         landed = move(sent, inner)
         came = move(sent, from_ends)
         far_back = move(add(*far_sum), across_all)
@@ -405,7 +392,6 @@
     else:
         rows, grads = compute((own, swap(own)))
         kept = [rows]
-        sent = grads[0]
         total = [*joined(grads)]
         reach = chips // 2
         for forth, back, steps in ((ahead, behind, reach), (behind, ahead, chips - 1 - reach)):
@@ -420,10 +406,8 @@
                 value = move(add(*pair) if value is None else add(*pair, value), back)
             if value is not None:
                 total.append(value)
-        if lax.axis_size("dp") == 4:
-            bases, next_pair, _ = first_step(rows, sum_early(kept[:-1]))
-
-    if lax.axis_size("dp") == 4:
+
+    if tuned:
         a_base, b_base = bases
         a_last = across(next_pair[0], 2)
         b_last = across(next_pair[1], 1)

time: 144 us -> 143 us (level)
    pallas_call x5 -> x4, Pallas kernels: 18.9 us -> 18.3 us  [run_slot(): pl.pallas_call(functools.partial(slot_kernel, choices, partial is not Non...]
where the time goes in v7:
time: 143 us; the launch traced here: 142 us
  waiting for transfers between devices  79 us (55%)
  starting transfers between devices  30.1 us (21%)
  Pallas kernels  26.7 us (19%)
  local copies, waits for them, and re-layouts  3.57 us (2%)
  other arithmetic  2.18 us (2%)
    ppermute x10, waiting for transfers between devices, move(): return lax.ppermute(value, 'expert', full)  50.8 us
    ppermute x4, waiting for transfers between devices, across(): return lax.ppermute(value, 'dp', [(i, i ^ bit) for i in range(4)])  23.9 us
    ppermute x10, starting transfers between devices, move(): return lax.ppermute(value, 'expert', full)  21.9 us
    pallas_call x4, Pallas kernels, run_slot(): pl.pallas_call(functools.partial(slot_kernel, choices, partial is not Non...  18.3 us
    ppermute x4, starting transfers between devices, across(): return lax.ppermute(value, 'dp', [(i, i ^ bit) for i in range(4)])  6.19 us
    ppermute x9, waiting for transfers between devices, swap(): return lax.ppermute(value, 'expert', [(i, i ^ 1) for i in range(devices)])  4.31 us
    pallas_call x1, Pallas kernels, run_partial(): pl.pallas_call(functools.partial(partial_kernel, len(lefts)), out_shape=j...  3.89 us
    unnamed x6, local copies, waits for them, and re-layouts  3.57 us
  transfers between devices with their start and end apart: 23, of which 10 were waited for; matrix products, arithmetic and copies ran while one was open for 1% of the time, Pallas kernels for 13%

profile of v7, /device:TPU:0, one launch (start us, length us, event | category | flops | bytes accessed | tf_op | source)
XLA Modules:
  0.0 142.4 jit_solution(10017788103812365838)
XLA Ops:
  0.6 2.2 %payload.1.refs_0_ = bf16[520,1024]{1,0:T(8,128)(2,1)} custom-call(bf16[256,1024]{1,0:T(8,128)(2,1)} %tokens.1, bf16[256,1024]{1,0:T(8,128)(2,1)} %cotangent.1, s32[2,256]{1,0:T(2,128)} %bitcast.13, bf16[2,256]{1,0:T(2,128)(2,1)} %bitcast.14), custom_call_target="tpu_custom_call" | custom-call | flops 1 | bytes 1 | tf_op jit(solution)/shard_map/payload/pallas_call | solution.py:256
  3.4 6.5 %collective-permute-start.4 = (bf16[520,1024]{1,0:T(8,128)(2,1)}, bf16[520,1024]{1,0:T(8,128)(2,1)S(1)}, u32[]{:S(2)}, u32[]{:S(2)}) collective-permute-start(bf16[520,1024]{1,0:T(8,128)(2,1)} %payload.1.refs_0_), channel_id=1, source_target_pairs={{0,6},{1,7},{6,0},{7,1},{8,14},{9,15},{14,8},{15,9},{16,22},{17,23... | collective-permute-start | bytes 3194888 | tf_op jit(solution)/shard_map/ppermute | solution.py:341
  9.9 0.7 collective-permute-start.3
  10.8 2.3 %copy-done = bf16[1,3,1024,768]{3,2,1,0:T(8,128)(2,1)S(1)} copy-done((bf16[1,3,1024,768]{3,2,1,0:T(8,128)(2,1)S(1)}, bf16[1,3,1024,768]{3,2,1,0:T(8,128)(2,1)}, u32[]{:S(2)}) %copy-start) | copy-done | bytes 4718616
  13.1 1.2 copy-done.2
  14.3 4.1 %expert_block.4 = (bf16[256,1024]{1,0:T(8,128)(2,1)S(1)}, bf16[256,1024]{1,0:T(8,128)(2,1)S(1)}, bf16[256,768]{1,0:T(8,128)(2,1)S(1)}, bf16[256,768]{1,0:T(8,128...) custom-call(bf16[520,1024]{1,0:T(8,128)(2,1)S(1)} %copy-done.2, ...), custom_call_target="tpu_custom_call" | custom-call | flops 1 | bytes 1 | tf_op jit(solution)/shard_map/expert_block/pallas_call | solution.py:132
  18.8 15.8 %collective-permute-done.4.refs_2_ = bf16[520,1024]{1,0:T(8,128)(2,1)S(1)} collective-permute-done((bf16[520,1024]{1,0:T(8,128)(2,1)}, bf16[520,1024]{1,0:T(8,128)(2,1)S(1)}, u32[]{:S(2)}, u32[]{:S(2)}) %collective-permute-start.4) | collective-permute-done | bytes 1064992 | tf_op jit(solution)/shard_map/ppermute | solution.py:341
  34.6 22.6 %collective-permute-done.2.refs_0_ = bf16[520,1024]{1,0:T(8,128)(2,1)S(1)} collective-permute-done((bf16[520,1024]{1,0:T(8,128)(2,1)}, bf16[520,1024]{1,0:T(8,128)(2,1)S(1)}, u32[]{:S(2)}, u32[]{:S(2)}) %collective-permute-start.2) | collective-permute-done | bytes 1064992 | tf_op jit(solution)/shard_map/ppermute | solution.py:341
  57.8 1.3 collective-permute-start.5
  59.1 0.7 collective-permute-start.6
  59.9 1.5 %collective-permute-done.9.refs_1_ = bf16[520,1024]{1,0:T(8,128)(2,1)S(1)} collective-permute-done((bf16[520,1024]{1,0:T(8,128)(2,1)S(1)}, bf16[520,1024]{1,0:T(8,128)(2,1)S(1)}, u32[]{:S(2)}, u32[]{:S(2)}) %collective-permute-start.9) | collective-permute-done | bytes 1064992 | tf_op jit(solution)/shard_map/ppermute | solution.py:344
  61.4 4.6 %expert_block.6 = (bf16[256,1024]{1,0:T(8,128)(2,1)S(1)}, bf16[256,1024]{1,0:T(8,128)(2,1)S(1)}, bf16[256,768]{1,0:T(8,128)(2,1)S(1)}, bf16[256,768]{1,0:T(8,128...) custom-call(bf16[520,1024]{1,0:T(8,128)(2,1)S(1)} %collective-permute-done.3., ...), custom_call_target="tpu_custom_call" | custom-call | flops 1 | bytes 1 | tf_op jit(solution)/shard_map/expert_block/pallas_call | solution.py:132
  66.3 4.1 %expert_block.5 = (bf16[256,1024]{1,0:T(8,128)(2,1)S(1)}, bf16[256,1024]{1,0:T(8,128)(2,1)S(1)}, bf16[256,768]{1,0:T(8,128)(2,1)S(1)}, bf16[256,768]{1,0:T(8,128...) custom-call(bf16[520,1024]{1,0:T(8,128)(2,1)S(1)} %collective-permute-done.2., ...), custom_call_target="tpu_custom_call" | custom-call | flops 1 | bytes 1 | tf_op jit(solution)/shard_map/expert_block/pallas_call | solution.py:132
  70.9 3.9 %partial_weights.1.refs_3_ = f32[3,1024,768]{2,1,0:T(8,128)S(1)} custom-call(bf16[256,1024]{1,0:T(8,128)(2,1)S(1)} %get-tuple-element.52.refs_0_.refs_6_, bf16[256,1024]{1,0:T(8,128)(2,1)S(1)} %get-tuple-element.53.refs_1_.refs_7_, bf16[256,1024]{1,0:T(8,128)(2,1)S(1)} %get-tuple-element.54.refs_2_.refs_8_, bf16[256,768]{1,0:T(8,128)(2,1)S(1)} %get-tuple-element.55.refs_3_, ...), custom_call_target="tpu_custom_call" | custom-call | flops 1 | bytes 1 | tf_op jit(solution)/shard_map/partial_weights/pallas_call | solution.py:164
  74.8 10.8 %collective-permute-done.5 = bf16[520,1024]{1,0:T(8,128)(2,1)S(1)} collective-permute-done((bf16[520,1024]{1,0:T(8,128)(2,1)S(1)}, bf16[520,1024]{1,0:T(8,128)(2,1)S(1)}, u32[]{:S(2)}, u32[]{:S(2)}) %collective-permute-start.5) | collective-permute-done | bytes 1064992 | tf_op jit(solution)/shard_map/ppermute | solution.py:341
  86.0 2.7 %collective-permute-done.12.refs_1_ = bf16[520,1024]{1,0:T(8,128)(2,1)S(1)} collective-permute-done((bf16[520,1024]{1,0:T(8,128)(2,1)S(1)}, bf16[520,1024]{1,0:T(8,128)(2,1)S(1)}, u32[]{:S(2)}, u32[]{:S(2)}) %collective-permute-start.12) | collective-permute-done | bytes 1064992 | tf_op jit(solution)/shard_map/ppermute | solution.py:344
  88.7 5.4 %expert_block.7 = (bf16[2,3,256,384]{3,2,1,0:T(8,128)(2,1)S(1)}, bf16[2,3,256,384]{3,2,1,0:T(8,128)(2,1)S(1)}, bf16[2,3,256,384]{3,2,1,0:T(8,128)(2,1)S(1)}, bf1...) custom-call(bf16[520,1024]{1,0:T(8,128)(2,1)S(1)} %add_convert_fusion.refs_0_, ...), custom_call_target="tpu_custom_call" | custom-call | flops 1 | bytes 1 | tf_op jit(solution)/shard_map/expert_block/pallas_call | solution.py:132
  94.1 1.5 %collective-permute-start.17 = (bf16[2,3,256,384]{3,2,1,0:T(8,128)(2,1)S(1)}, bf16[2,3,256,384]{3,2,1,0:T(8,128)(2,1)S(1)}, u32[]{:S(2)}, u32[]{:S(2)}) collective-permute-start(bf16[2,3,256,384]{3,2,1,0:T(8,128)(2,1)S(1)} %get-tuple-element.75), channel_id=1, source_target_pairs={{0,8},{8,0},{16,24},{24,16},{1,9},{9,1},{17,25},{25,17},{2,10},{10... | collective-permute-start | bytes 3538952 | tf_op jit(solution)/shard_map/ppermute | solution.py:328
  95.6 1.5 %collective-permute-start.18 = (bf16[2,3,256,384]{3,2,1,0:T(8,128)(2,1)S(1)}, bf16[2,3,256,384]{3,2,1,0:T(8,128)(2,1)S(1)}, u32[]{:S(2)}, u32[]{:S(2)}) collective-permute-start(bf16[2,3,256,384]{3,2,1,0:T(8,128)(2,1)S(1)} %get-tuple-element.77), channel_id=1, source_target_pairs={{0,16},{8,24},{16,0},{24,8},{1,17},{9,25},{17,1},{25,9},{2,18},{10... | collective-permute-start | bytes 3538952 | tf_op jit(solution)/shard_map/ppermute | solution.py:328
  97.3 4.4 %collective-permute-start.16 = (bf16[264,1024]{1,0:T(8,128)(2,1)S(1)}, bf16[264,1024]{1,0:T(8,128)(2,1)S(1)}, u32[]{:S(2)}, u32[]{:S(2)}) collective-permute-start(bf16[264,1024]{1,0:T(8,128)(2,1)S(1)} %fusion), channel_id=1, source_target_pairs={{0,6},{1,7},{6,0},{7,1},{8,14},{9,15},{14,8},{15,9},{16,22},{17,23... | collective-permute-start | bytes 1622024 | tf_op jit(solution)/shard_map/ppermute | solution.py:341
  101.9 3.0 %collective-permute-start.15 = (bf16[264,1024]{1,0:T(8,128)(2,1)S(1)}, bf16[264,1024]{1,0:T(8,128)(2,1)S(1)}, u32[]{:S(2)}, u32[]{:S(2)}) collective-permute-start(bf16[264,1024]{1,0:T(8,128)(2,1)S(1)} %add_convert_fusion.6), channel_id=1, source_target_pairs={{0,2},{1,3},{6,4},{7,5},{8,10},{9,11},{14,12},{15,13},{16,18},{17,... | collective-permute-start | bytes 1622024 | tf_op jit(solution)/shard_map/ppermute | solution.py:341
  104.9 0.7 collective-permute-start.14
  105.6 16.5 %collective-permute-done.17 = bf16[2,3,256,384]{3,2,1,0:T(8,128)(2,1)S(1)} collective-permute-done((bf16[2,3,256,384]{3,2,1,0:T(8,128)(2,1)S(1)}, bf16[2,3,256,384]{3,2,1,0:T(8,128)(2,1)S(1)}, u32[]{:S(2)}, u32[]{:S(2)}) %collective-permute-start.17) | collective-permute-done | bytes 1179680 | tf_op jit(solution)/shard_map/ppermute | solution.py:328
  122.4 1.6 %collective-permute-start.21 = (bf16[3,256,384]{2,1,0:T(8,128)(2,1)S(1)}, bf16[3,256,384]{2,1,0:T(8,128)(2,1)S(1)}, u32[]{:S(2)}, u32[]{:S(2)}) collective-permute-start(bf16[3,256,384]{2,1,0:T(8,128)(2,1)S(1)} %get-tuple-element.90), channel_id=1, source_target_pairs={{0,16},{8,24},{16,0},{24,8},{1,17},{9,25},{17,1},{25,9},{2,18},{10... | collective-permute-start | bytes 1769480 | tf_op jit(solution)/shard_map/ppermute | solution.py:328
  124.3 1.6 %collective-permute-start.22 = (bf16[3,256,384]{2,1,0:T(8,128)(2,1)S(1)}, bf16[3,256,384]{2,1,0:T(8,128)(2,1)S(1)}, u32[]{:S(2)}, u32[]{:S(2)}) collective-permute-start(bf16[3,256,384]{2,1,0:T(8,128)(2,1)S(1)} %get-tuple-element.88), channel_id=1, source_target_pairs={{0,8},{8,0},{16,24},{24,16},{1,9},{9,1},{17,25},{25,17},{2,10},{10... | collective-permute-start | bytes 1769480 | tf_op jit(solution)/shard_map/ppermute | solution.py:328
  126.4 3.8 %collective-permute-start.19 = (bf16[264,1024]{1,0:T(8,128)(2,1)S(1)}, bf16[264,1024]{1,0:T(8,128)(2,1)S(1)}, u32[]{:S(2)}, u32[]{:S(2)}) collective-permute-start(bf16[264,1024]{1,0:T(8,128)(2,1)S(1)} %add_convert_fusion.4), channel_id=1, source_target_pairs={{0,2},{1,3},{2,0},{3,1},{4,6},{5,7},{6,4},{7,5},{8,10},{9,11},{10,... | collective-permute-start | bytes 1622024 | tf_op jit(solution)/shard_map/ppermute | solution.py:341
  130.2 0.7 collective-permute-start.20
  131.2 5.8 %collective-permute-done.21.a_last = bf16[3,256,384]{2,1,0:T(8,128)(2,1)S(1)} collective-permute-done((bf16[3,256,384]{2,1,0:T(8,128)(2,1)S(1)}, bf16[3,256,384]{2,1,0:T(8,128)(2,1)S(1)}, u32[]{:S(2)}, u32[]{:S(2)}) %collective-permute-start.21) | collective-permute-done | bytes 589856 | tf_op jit(solution)/shard_map/ppermute | solution.py:328
  137.0 1.6 %collective-permute-done.22.b_last = bf16[3,256,384]{2,1,0:T(8,128)(2,1)S(1)} collective-permute-done((bf16[3,256,384]{2,1,0:T(8,128)(2,1)S(1)}, bf16[3,256,384]{2,1,0:T(8,128)(2,1)S(1)}, u32[]{:S(2)}, u32[]{:S(2)}) %collective-permute-start.22) | collective-permute-done | bytes 589856 | tf_op jit(solution)/shard_map/ppermute | solution.py:328
  138.6 1.3 final_step.1
  139.9 1.5 %collective-permute-done.19.refs_1_ = bf16[264,1024]{1,0:T(8,128)(2,1)S(1)} collective-permute-done((bf16[264,1024]{1,0:T(8,128)(2,1)S(1)}, bf16[264,1024]{1,0:T(8,128)(2,1)S(1)}, u32[]{:S(2)}, u32[]{:S(2)}) %collective-permute-start.19) | collective-permute-done | bytes 540704 | tf_op jit(solution)/shard_map/ppermute | solution.py:341
  141.4 1.0 total.1
  (36 shorter events, 4.5 us)
Async XLA Ops:
  2.9 7.9 %collective-permute-start = (bf16[520,1024]{1,0:T(8,128)(2,1)}, bf16[520,1024]{1,0:T(8,128)(2,1)S(1)}, u32[]{:S(2)}, u32[]{:S(2)}) collective-permute-start(bf16[520,1024]{1,0:T(8,128)(2,1)} %payload.1.refs_0_), channel_id=1, source_target_pairs={{0,1},{1,0},{2,3},{3,2},{4,5},{5,4},{6,7},{7,6},{8,9},{9,8},{10,11... | collective-permute-start | bytes 3194888 | tf_op jit(solution)/shard_map/ppermute | solution.py:344
  3.4 31.2 %collective-permute-start.4 = (bf16[520,1024]{1,0:T(8,128)(2,1)}, bf16[520,1024]{1,0:T(8,128)(2,1)S(1)}, u32[]{:S(2)}, u32[]{:S(2)}) collective-permute-start(bf16[520,1024]{1,0:T(8,128)(2,1)} %payload.1.refs_0_), channel_id=1, source_target_pairs={{0,6},{1,7},{6,0},{7,1},{8,14},{9,15},{14,8},{15,9},{16,22},{17,23... | collective-permute-start | bytes 3194888 | tf_op jit(solution)/shard_map/ppermute | solution.py:341
  9.9 24.7 %collective-permute-start.3 = (bf16[520,1024]{1,0:T(8,128)(2,1)}, bf16[520,1024]{1,0:T(8,128)(2,1)S(1)}, u32[]{:S(2)}, u32[]{:S(2)}) collective-permute-start(bf16[520,1024]{1,0:T(8,128)(2,1)} %payload.1.refs_0_), channel_id=1, source_target_pairs={{2,4},{3,5},{4,2},{5,3},{10,12},{11,13},{12,10},{13,11},{18,20},{1... | collective-permute-start | bytes 3194888 | tf_op jit(solution)/shard_map/ppermute | solution.py:341
  10.7 46.5 %collective-permute-start.2 = (bf16[520,1024]{1,0:T(8,128)(2,1)}, bf16[520,1024]{1,0:T(8,128)(2,1)S(1)}, u32[]{:S(2)}, u32[]{:S(2)}) collective-permute-start(bf16[520,1024]{1,0:T(8,128)(2,1)} %payload.1.refs_0_), channel_id=1, source_target_pairs={{0,2},{1,3},{2,0},{3,1},{4,6},{5,7},{6,4},{7,5},{8,10},{9,11},{10,... | collective-permute-start | bytes 3194888 | tf_op jit(solution)/shard_map/ppermute | solution.py:341
  10.8 2.3 %copy-start = (bf16[1,3,1024,768]{3,2,1,0:T(8,128)(2,1)S(1)}, bf16[1,3,1024,768]{3,2,1,0:T(8,128)(2,1)}, u32[]{:S(2)}) copy-start(bf16[1,3,1024,768]{3,2,1,0:T(8,128)(2,1)} %refs_2_.5) | copy-start | bytes 14155780
  13.1 1.2 copy-start.2
  14.3 47.1 %copy-start.1 = (bf16[1,3,1024,768]{3,2,1,0:T(8,128)(2,1)S(1)}, bf16[1,3,1024,768]{3,2,1,0:T(8,128)(2,1)}, u32[]{:S(2)}) copy-start(bf16[1,3,1024,768]{3,2,1,0:T(8,128)(2,1)} %refs_2_.5) | copy-start | bytes 14155780
  18.5 38.7 %collective-permute-start.1 = (bf16[264,1024]{1,0:T(8,128)(2,1)S(1)}, bf16[264,1024]{1,0:T(8,128)(2,1)S(1)}, u32[]{:S(2)}, u32[]{:S(2)}) collective-permute-start(bf16[264,1024]{1,0:T(8,128)(2,1)S(1)} %get-tuple-element.46), channel_id=1, source_target_pairs={{0,1},{1,0},{2,3},{3,2},{4,5},{5,4},{6,7},{7,6},{8,9},{9,8},{10,11... | collective-permute-start | bytes 1622024 | tf_op jit(solution)/shard_map/ppermute | solution.py:344
  57.2 2.7 %collective-permute-start.10 = (bf16[520,1024]{1,0:T(8,128)(2,1)S(1)}, bf16[520,1024]{1,0:T(8,128)(2,1)S(1)}, u32[]{:S(2)}, u32[]{:S(2)}) collective-permute-start(bf16[520,1024]{1,0:T(8,128)(2,1)S(1)} %collective-permute-done.4.refs_2_), channel_id=1, source_target_pairs={{0,1},{1,0},{2,3},{3,2},{4,5},{5,4},{6,7},{7,6},{8,9},{9,8},{10,11... | collective-permute-start | bytes 3194888 | tf_op jit(solution)/shard_map/ppermute | solution.py:344
  57.3 4.2 %collective-permute-start.9 = (bf16[520,1024]{1,0:T(8,128)(2,1)S(1)}, bf16[520,1024]{1,0:T(8,128)(2,1)S(1)}, u32[]{:S(2)}, u32[]{:S(2)}) collective-permute-start(bf16[520,1024]{1,0:T(8,128)(2,1)S(1)} %collective-permute-done.3.refs_0_), channel_id=1, source_target_pairs={{0,1},{1,0},{2,3},{3,2},{4,5},{5,4},{6,7},{7,6},{8,9},{9,8},{10,11... | collective-permute-start | bytes 3194888 | tf_op jit(solution)/shard_map/ppermute | solution.py:344
  57.7 8.5 %collective-permute-start.7 = (bf16[520,1024]{1,0:T(8,128)(2,1)S(1)}, bf16[520,1024]{1,0:T(8,128)(2,1)S(1)}, u32[]{:S(2)}, u32[]{:S(2)}) collective-permute-start(bf16[520,1024]{1,0:T(8,128)(2,1)S(1)} %collective-permute-done.2.refs_0_), channel_id=1, source_target_pairs={{0,1},{1,0},{2,3},{3,2},{4,5},{5,4},{6,7},{7,6},{8,9},{9,8},{10,11... | collective-permute-start | bytes 3194888 | tf_op jit(solution)/shard_map/ppermute | solution.py:344
  57.8 27.8 %collective-permute-start.5 = (bf16[520,1024]{1,0:T(8,128)(2,1)S(1)}, bf16[520,1024]{1,0:T(8,128)(2,1)S(1)}, u32[]{:S(2)}, u32[]{:S(2)}) collective-permute-start(bf16[520,1024]{1,0:T(8,128)(2,1)S(1)} %collective-permute-done.3.refs_0_), channel_id=1, source_target_pairs={{2,0},{3,1},{4,6},{5,7},{10,8},{11,9},{12,14},{13,15},{18,16},{19,... | collective-permute-start | bytes 3194888 | tf_op jit(solution)/shard_map/ppermute | solution.py:341
  59.1 26.5 %collective-permute-start.6 = (bf16[520,1024]{1,0:T(8,128)(2,1)S(1)}, bf16[520,1024]{1,0:T(8,128)(2,1)S(1)}, u32[]{:S(2)}, u32[]{:S(2)}) collective-permute-start(bf16[520,1024]{1,0:T(8,128)(2,1)S(1)} %collective-permute-done.2.refs_0_), channel_id=1, source_target_pairs={{2,4},{3,5},{4,2},{5,3},{10,12},{11,13},{12,10},{13,11},{18,20},{1... | collective-permute-start | bytes 3194888 | tf_op jit(solution)/shard_map/ppermute | solution.py:341
  66.1 19.5 %collective-permute-start.11 = (bf16[264,1024]{1,0:T(8,128)(2,1)S(1)}, bf16[264,1024]{1,0:T(8,128)(2,1)S(1)}, u32[]{:S(2)}, u32[]{:S(2)}) collective-permute-start(bf16[264,1024]{1,0:T(8,128)(2,1)S(1)} %get-tuple-element.51), channel_id=1, source_target_pairs={{0,1},{1,0},{2,3},{3,2},{4,5},{5,4},{6,7},{7,6},{8,9},{9,8},{10,11... | collective-permute-start | bytes 1622024 | tf_op jit(solution)/shard_map/ppermute | solution.py:344
  70.4 15.1 %collective-permute-start.8 = (bf16[264,1024]{1,0:T(8,128)(2,1)S(1)}, bf16[264,1024]{1,0:T(8,128)(2,1)S(1)}, u32[]{:S(2)}, u32[]{:S(2)}) collective-permute-start(bf16[264,1024]{1,0:T(8,128)(2,1)S(1)} %get-tuple-element.49), channel_id=1, source_target_pairs={{0,1},{1,0},{2,3},{3,2},{4,5},{5,4},{6,7},{7,6},{8,9},{9,8},{10,11... | collective-permute-start | bytes 1622024 | tf_op jit(solution)/shard_map/ppermute | solution.py:344
  86.0 2.7 %collective-permute-start.12 = (bf16[520,1024]{1,0:T(8,128)(2,1)S(1)}, bf16[520,1024]{1,0:T(8,128)(2,1)S(1)}, u32[]{:S(2)}, u32[]{:S(2)}) collective-permute-start(bf16[520,1024]{1,0:T(8,128)(2,1)S(1)} %add_convert_fusion.refs_0_), channel_id=1, source_target_pairs={{0,1},{1,0},{2,3},{3,2},{4,5},{5,4},{6,7},{7,6},{8,9},{9,8},{10,11... | collective-permute-start | bytes 3194888 | tf_op jit(solution)/shard_map/ppermute | solution.py:344
  94.1 28.1 %collective-permute-start.17 = (bf16[2,3,256,384]{3,2,1,0:T(8,128)(2,1)S(1)}, bf16[2,3,256,384]{3,2,1,0:T(8,128)(2,1)S(1)}, u32[]{:S(2)}, u32[]{:S(2)}) collective-permute-start(bf16[2,3,256,384]{3,2,1,0:T(8,128)(2,1)S(1)} %get-tuple-element.75), channel_id=1, source_target_pairs={{0,8},{8,0},{16,24},{24,16},{1,9},{9,1},{17,25},{25,17},{2,10},{10... | collective-permute-start | bytes 3538952 | tf_op jit(solution)/shard_map/ppermute | solution.py:328
  95.6 28.4 %collective-permute-start.18 = (bf16[2,3,256,384]{3,2,1,0:T(8,128)(2,1)S(1)}, bf16[2,3,256,384]{3,2,1,0:T(8,128)(2,1)S(1)}, u32[]{:S(2)}, u32[]{:S(2)}) collective-permute-start(bf16[2,3,256,384]{3,2,1,0:T(8,128)(2,1)S(1)} %get-tuple-element.77), channel_id=1, source_target_pairs={{0,16},{8,24},{16,0},{24,8},{1,17},{9,25},{17,1},{25,9},{2,18},{10... | collective-permute-start | bytes 3538952 | tf_op jit(solution)/shard_map/ppermute | solution.py:328
  97.1 4.6 %collective-permute-start.13 = (bf16[264,1024]{1,0:T(8,128)(2,1)S(1)}, bf16[264,1024]{1,0:T(8,128)(2,1)S(1)}, u32[]{:S(2)}, u32[]{:S(2)}) collective-permute-start(bf16[264,1024]{1,0:T(8,128)(2,1)S(1)} %get-tuple-element.70), channel_id=1, source_target_pairs={{0,1},{1,0},{2,3},{3,2},{4,5},{5,4},{6,7},{7,6},{8,9},{9,8},{10,11... | collective-permute-start | bytes 1622024 | tf_op jit(solution)/shard_map/ppermute | solution.py:344
  97.3 28.5 %collective-permute-start.16 = (bf16[264,1024]{1,0:T(8,128)(2,1)S(1)}, bf16[264,1024]{1,0:T(8,128)(2,1)S(1)}, u32[]{:S(2)}, u32[]{:S(2)}) collective-permute-start(bf16[264,1024]{1,0:T(8,128)(2,1)S(1)} %fusion), channel_id=1, source_target_pairs={{0,6},{1,7},{6,0},{7,1},{8,14},{9,15},{14,8},{15,9},{16,22},{17,23... | collective-permute-start | bytes 1622024 | tf_op jit(solution)/shard_map/ppermute | solution.py:341
  101.9 23.9 %collective-permute-start.15 = (bf16[264,1024]{1,0:T(8,128)(2,1)S(1)}, bf16[264,1024]{1,0:T(8,128)(2,1)S(1)}, u32[]{:S(2)}, u32[]{:S(2)}) collective-permute-start(bf16[264,1024]{1,0:T(8,128)(2,1)S(1)} %add_convert_fusion.6), channel_id=1, source_target_pairs={{0,2},{1,3},{6,4},{7,5},{8,10},{9,11},{14,12},{15,13},{16,18},{17,... | collective-permute-start | bytes 1622024 | tf_op jit(solution)/shard_map/ppermute | solution.py:341
  104.9 20.9 %collective-permute-start.14 = (bf16[264,1024]{1,0:T(8,128)(2,1)S(1)}, bf16[264,1024]{1,0:T(8,128)(2,1)S(1)}, u32[]{:S(2)}, u32[]{:S(2)}) collective-permute-start(bf16[264,1024]{1,0:T(8,128)(2,1)S(1)} %add_convert_fusion.6), channel_id=1, source_target_pairs={{2,4},{3,5},{4,2},{5,3},{10,12},{11,13},{12,10},{13,11},{18,20},{1... | collective-permute-start | bytes 1622024 | tf_op jit(solution)/shard_map/ppermute | solution.py:341
  122.4 14.6 %collective-permute-start.21 = (bf16[3,256,384]{2,1,0:T(8,128)(2,1)S(1)}, bf16[3,256,384]{2,1,0:T(8,128)(2,1)S(1)}, u32[]{:S(2)}, u32[]{:S(2)}) collective-permute-start(bf16[3,256,384]{2,1,0:T(8,128)(2,1)S(1)} %get-tuple-element.90), channel_id=1, source_target_pairs={{0,16},{8,24},{16,0},{24,8},{1,17},{9,25},{17,1},{25,9},{2,18},{10... | collective-permute-start | bytes 1769480 | tf_op jit(solution)/shard_map/ppermute | solution.py:328
  124.3 14.3 %collective-permute-start.22 = (bf16[3,256,384]{2,1,0:T(8,128)(2,1)S(1)}, bf16[3,256,384]{2,1,0:T(8,128)(2,1)S(1)}, u32[]{:S(2)}, u32[]{:S(2)}) collective-permute-start(bf16[3,256,384]{2,1,0:T(8,128)(2,1)S(1)} %get-tuple-element.88), channel_id=1, source_target_pairs={{0,8},{8,0},{16,24},{24,16},{1,9},{9,1},{17,25},{25,17},{2,10},{10... | collective-permute-start | bytes 1769480 | tf_op jit(solution)/shard_map/ppermute | solution.py:328
  126.4 15.0 %collective-permute-start.19 = (bf16[264,1024]{1,0:T(8,128)(2,1)S(1)}, bf16[264,1024]{1,0:T(8,128)(2,1)S(1)}, u32[]{:S(2)}, u32[]{:S(2)}) collective-permute-start(bf16[264,1024]{1,0:T(8,128)(2,1)S(1)} %add_convert_fusion.4), channel_id=1, source_target_pairs={{0,2},{1,3},{2,0},{3,1},{4,6},{5,7},{6,4},{7,5},{8,10},{9,11},{10,... | collective-permute-start | bytes 1622024 | tf_op jit(solution)/shard_map/ppermute | solution.py:341
  130.2 11.2 %collective-permute-start.20 = (bf16[264,1024]{1,0:T(8,128)(2,1)S(1)}, bf16[264,1024]{1,0:T(8,128)(2,1)S(1)}, u32[]{:S(2)}, u32[]{:S(2)}) collective-permute-start(bf16[264,1024]{1,0:T(8,128)(2,1)S(1)} %add_convert_fusion.3), channel_id=1, source_target_pairs={{2,4},{3,5},{4,2},{5,3},{10,12},{11,13},{12,10},{13,11},{18,20},{1... | collective-permute-start | bytes 1622024 | tf_op jit(solution)/shard_map/ppermute | solution.py:341

commit v8 on v7

--- a/solution.py
+++ b/solution.py
@@ -365,7 +365,7 @@
         rows, grads = compute((own, swap(own)))
         kept = [rows]
         own_sum = joined(grads)
-        first, second, far = after((first, second, far), own_sum[1])
+        far, second, first = after((far, second, first), own_sum[1])
         third = move(second, to_ends)
         fourth = move(first, inner)
         rows, grads = compute((first, swap(first)))

time: 143 us -> 142 us (level)
  waiting for transfers between devices: 79 us -> 77.2 us
    ppermute x10, waiting for transfers between devices: 50.8 us -> 48.8 us  [move(): return lax.ppermute(value, 'expert', full)]
where the time goes in v8:
time: 142 us; the launch traced here: 141 us
  waiting for transfers between devices  77.2 us (54%)
  starting transfers between devices  30.3 us (21%)
  Pallas kernels  26.7 us (19%)
  local copies, waits for them, and re-layouts  3.57 us (3%)
  other arithmetic  2.18 us (2%)
    ppermute x10, waiting for transfers between devices, move(): return lax.ppermute(value, 'expert', full)  48.8 us
    ppermute x4, waiting for transfers between devices, across(): return lax.ppermute(value, 'dp', [(i, i ^ bit) for i in range(4)])  24 us
    ppermute x10, starting transfers between devices, move(): return lax.ppermute(value, 'expert', full)  22.3 us
    pallas_call x4, Pallas kernels, run_slot(): pl.pallas_call(functools.partial(slot_kernel, choices, partial is not Non...  18.3 us
    ppermute x4, starting transfers between devices, across(): return lax.ppermute(value, 'dp', [(i, i ^ bit) for i in range(4)])  6.2 us
    ppermute x9, waiting for transfers between devices, swap(): return lax.ppermute(value, 'expert', [(i, i ^ 1) for i in range(devices)])  4.35 us
    pallas_call x1, Pallas kernels, run_partial(): pl.pallas_call(functools.partial(partial_kernel, len(lefts)), out_shape=j...  3.89 us
    unnamed x6, local copies, waits for them, and re-layouts  3.57 us
  transfers between devices with their start and end apart: 23, of which 10 were waited for; matrix products, arithmetic and copies ran while one was open for 1% of the time, Pallas kernels for 13%

profile of v8, /device:TPU:0, one launch (start us, length us, event | category | flops | bytes accessed | tf_op | source)
XLA Modules:
  0.0 140.8 jit_solution(11172486220666815103)
XLA Ops:
  0.6 2.2 %payload.1.refs_0_ = bf16[520,1024]{1,0:T(8,128)(2,1)} custom-call(bf16[256,1024]{1,0:T(8,128)(2,1)} %tokens.1, bf16[256,1024]{1,0:T(8,128)(2,1)} %cotangent.1, s32[2,256]{1,0:T(2,128)} %bitcast.13, bf16[2,256]{1,0:T(2,128)(2,1)} %bitcast.14), custom_call_target="tpu_custom_call" | custom-call | flops 1 | bytes 1 | tf_op jit(solution)/shard_map/payload/pallas_call | solution.py:256
  3.4 2.6 %collective-permute-start.4 = (bf16[520,1024]{1,0:T(8,128)(2,1)}, bf16[520,1024]{1,0:T(8,128)(2,1)S(1)}, u32[]{:S(2)}, u32[]{:S(2)}) collective-permute-start(bf16[520,1024]{1,0:T(8,128)(2,1)} %payload.1.refs_0_), channel_id=1, source_target_pairs={{0,2},{1,3},{2,0},{3,1},{4,6},{5,7},{6,4},{7,5},{8,10},{9,11},{10,... | collective-permute-start | bytes 3194888 | tf_op jit(solution)/shard_map/ppermute | solution.py:341
  6.1 0.7 collective-permute-start.3
  6.8 4.4 %collective-permute-start.2 = (bf16[520,1024]{1,0:T(8,128)(2,1)}, bf16[520,1024]{1,0:T(8,128)(2,1)S(1)}, u32[]{:S(2)}, u32[]{:S(2)}) collective-permute-start(bf16[520,1024]{1,0:T(8,128)(2,1)} %payload.1.refs_0_), channel_id=1, source_target_pairs={{0,6},{1,7},{6,0},{7,1},{8,14},{9,15},{14,8},{15,9},{16,22},{17,23... | collective-permute-start | bytes 3194888 | tf_op jit(solution)/shard_map/ppermute | solution.py:341
  11.2 2.3 %copy-done = bf16[1,3,1024,768]{3,2,1,0:T(8,128)(2,1)S(1)} copy-done((bf16[1,3,1024,768]{3,2,1,0:T(8,128)(2,1)S(1)}, bf16[1,3,1024,768]{3,2,1,0:T(8,128)(2,1)}, u32[]{:S(2)}) %copy-start) | copy-done | bytes 4718616
  13.5 1.2 copy-done.2
  14.8 4.1 %expert_block.4 = (bf16[256,1024]{1,0:T(8,128)(2,1)S(1)}, bf16[256,1024]{1,0:T(8,128)(2,1)S(1)}, bf16[256,768]{1,0:T(8,128)(2,1)S(1)}, bf16[256,768]{1,0:T(8,128...) custom-call(bf16[520,1024]{1,0:T(8,128)(2,1)S(1)} %copy-done.2, ...), custom_call_target="tpu_custom_call" | custom-call | flops 1 | bytes 1 | tf_op jit(solution)/shard_map/expert_block/pallas_call | solution.py:132
  19.0 11.4 %collective-permute-done.4.refs_0_ = bf16[520,1024]{1,0:T(8,128)(2,1)S(1)} collective-permute-done((bf16[520,1024]{1,0:T(8,128)(2,1)}, bf16[520,1024]{1,0:T(8,128)(2,1)S(1)}, u32[]{:S(2)}, u32[]{:S(2)}) %collective-permute-start.4) | collective-permute-done | bytes 1064992 | tf_op jit(solution)/shard_map/ppermute | solution.py:341
  30.4 25.1 %collective-permute-done.2.refs_2_ = bf16[520,1024]{1,0:T(8,128)(2,1)S(1)} collective-permute-done((bf16[520,1024]{1,0:T(8,128)(2,1)}, bf16[520,1024]{1,0:T(8,128)(2,1)S(1)}, u32[]{:S(2)}, u32[]{:S(2)}) %collective-permute-start.2) | collective-permute-done | bytes 1064992 | tf_op jit(solution)/shard_map/ppermute | solution.py:341
  56.0 1.3 collective-permute-start.5
  57.3 0.7 collective-permute-start.6
  58.2 1.5 %collective-permute-done.9.refs_1_ = bf16[520,1024]{1,0:T(8,128)(2,1)S(1)} collective-permute-done((bf16[520,1024]{1,0:T(8,128)(2,1)S(1)}, bf16[520,1024]{1,0:T(8,128)(2,1)S(1)}, u32[]{:S(2)}, u32[]{:S(2)}) %collective-permute-start.9) | collective-permute-done | bytes 1064992 | tf_op jit(solution)/shard_map/ppermute | solution.py:344
  59.7 4.6 %expert_block.6 = (bf16[256,1024]{1,0:T(8,128)(2,1)S(1)}, bf16[256,1024]{1,0:T(8,128)(2,1)S(1)}, bf16[256,768]{1,0:T(8,128)(2,1)S(1)}, bf16[256,768]{1,0:T(8,128...) custom-call(bf16[520,1024]{1,0:T(8,128)(2,1)S(1)} %collective-permute-done.3., ...), custom_call_target="tpu_custom_call" | custom-call | flops 1 | bytes 1 | tf_op jit(solution)/shard_map/expert_block/pallas_call | solution.py:132
  64.6 4.2 %expert_block.5 = (bf16[256,1024]{1,0:T(8,128)(2,1)S(1)}, bf16[256,1024]{1,0:T(8,128)(2,1)S(1)}, bf16[256,768]{1,0:T(8,128)(2,1)S(1)}, bf16[256,768]{1,0:T(8,128...) custom-call(bf16[520,1024]{1,0:T(8,128)(2,1)S(1)} %collective-permute-done.4., ...), custom_call_target="tpu_custom_call" | custom-call | flops 1 | bytes 1 | tf_op jit(solution)/shard_map/expert_block/pallas_call | solution.py:132
  69.2 3.9 %partial_weights.1.refs_3_ = f32[3,1024,768]{2,1,0:T(8,128)S(1)} custom-call(bf16[256,1024]{1,0:T(8,128)(2,1)S(1)} %get-tuple-element.52.refs_0_.refs_6_, bf16[256,1024]{1,0:T(8,128)(2,1)S(1)} %get-tuple-element.53.refs_1_.refs_7_, bf16[256,1024]{1,0:T(8,128)(2,1)S(1)} %get-tuple-element.54.refs_2_.refs_8_, bf16[256,768]{1,0:T(8,128)(2,1)S(1)} %get-tuple-element.55.refs_3_, ...), custom_call_target="tpu_custom_call" | custom-call | flops 1 | bytes 1 | tf_op jit(solution)/shard_map/partial_weights/pallas_call | solution.py:164
  73.0 10.9 %collective-permute-done.5 = bf16[520,1024]{1,0:T(8,128)(2,1)S(1)} collective-permute-done((bf16[520,1024]{1,0:T(8,128)(2,1)S(1)}, bf16[520,1024]{1,0:T(8,128)(2,1)S(1)}, u32[]{:S(2)}, u32[]{:S(2)}) %collective-permute-start.5) | collective-permute-done | bytes 1064992 | tf_op jit(solution)/shard_map/ppermute | solution.py:341
  84.4 2.7 %collective-permute-done.12.refs_1_ = bf16[520,1024]{1,0:T(8,128)(2,1)S(1)} collective-permute-done((bf16[520,1024]{1,0:T(8,128)(2,1)S(1)}, bf16[520,1024]{1,0:T(8,128)(2,1)S(1)}, u32[]{:S(2)}, u32[]{:S(2)}) %collective-permute-start.12) | collective-permute-done | bytes 1064992 | tf_op jit(solution)/shard_map/ppermute | solution.py:344
  87.1 5.3 %expert_block.7 = (bf16[2,3,256,384]{3,2,1,0:T(8,128)(2,1)S(1)}, bf16[2,3,256,384]{3,2,1,0:T(8,128)(2,1)S(1)}, bf16[2,3,256,384]{3,2,1,0:T(8,128)(2,1)S(1)}, bf1...) custom-call(bf16[520,1024]{1,0:T(8,128)(2,1)S(1)} %add_convert_fusion.refs_0_, ...), custom_call_target="tpu_custom_call" | custom-call | flops 1 | bytes 1 | tf_op jit(solution)/shard_map/expert_block/pallas_call | solution.py:132
  92.5 1.6 %collective-permute-start.17 = (bf16[2,3,256,384]{3,2,1,0:T(8,128)(2,1)S(1)}, bf16[2,3,256,384]{3,2,1,0:T(8,128)(2,1)S(1)}, u32[]{:S(2)}, u32[]{:S(2)}) collective-permute-start(bf16[2,3,256,384]{3,2,1,0:T(8,128)(2,1)S(1)} %get-tuple-element.75), channel_id=1, source_target_pairs={{0,8},{8,0},{16,24},{24,16},{1,9},{9,1},{17,25},{25,17},{2,10},{10... | collective-permute-start | bytes 3538952 | tf_op jit(solution)/shard_map/ppermute | solution.py:328
  94.0 1.5 %collective-permute-start.18 = (bf16[2,3,256,384]{3,2,1,0:T(8,128)(2,1)S(1)}, bf16[2,3,256,384]{3,2,1,0:T(8,128)(2,1)S(1)}, u32[]{:S(2)}, u32[]{:S(2)}) collective-permute-start(bf16[2,3,256,384]{3,2,1,0:T(8,128)(2,1)S(1)} %get-tuple-element.77), channel_id=1, source_target_pairs={{0,16},{8,24},{16,0},{24,8},{1,17},{9,25},{17,1},{25,9},{2,18},{10... | collective-permute-start | bytes 3538952 | tf_op jit(solution)/shard_map/ppermute | solution.py:328
  95.7 4.6 %collective-permute-start.16 = (bf16[264,1024]{1,0:T(8,128)(2,1)S(1)}, bf16[264,1024]{1,0:T(8,128)(2,1)S(1)}, u32[]{:S(2)}, u32[]{:S(2)}) collective-permute-start(bf16[264,1024]{1,0:T(8,128)(2,1)S(1)} %fusion), channel_id=1, source_target_pairs={{0,6},{1,7},{6,0},{7,1},{8,14},{9,15},{14,8},{15,9},{16,22},{17,23... | collective-permute-start | bytes 1622024 | tf_op jit(solution)/shard_map/ppermute | solution.py:341
  100.5 2.8 %collective-permute-start.15 = (bf16[264,1024]{1,0:T(8,128)(2,1)S(1)}, bf16[264,1024]{1,0:T(8,128)(2,1)S(1)}, u32[]{:S(2)}, u32[]{:S(2)}) collective-permute-start(bf16[264,1024]{1,0:T(8,128)(2,1)S(1)} %add_convert_fusion.6), channel_id=1, source_target_pairs={{0,2},{1,3},{6,4},{7,5},{8,10},{9,11},{14,12},{15,13},{16,18},{17,... | collective-permute-start | bytes 1622024 | tf_op jit(solution)/shard_map/ppermute | solution.py:341
  103.3 0.7 collective-permute-start.14
  104.0 16.5 %collective-permute-done.17 = bf16[2,3,256,384]{3,2,1,0:T(8,128)(2,1)S(1)} collective-permute-done((bf16[2,3,256,384]{3,2,1,0:T(8,128)(2,1)S(1)}, bf16[2,3,256,384]{3,2,1,0:T(8,128)(2,1)S(1)}, u32[]{:S(2)}, u32[]{:S(2)}) %collective-permute-start.17) | collective-permute-done | bytes 1179680 | tf_op jit(solution)/shard_map/ppermute | solution.py:328
  120.8 1.6 %collective-permute-start.21 = (bf16[3,256,384]{2,1,0:T(8,128)(2,1)S(1)}, bf16[3,256,384]{2,1,0:T(8,128)(2,1)S(1)}, u32[]{:S(2)}, u32[]{:S(2)}) collective-permute-start(bf16[3,256,384]{2,1,0:T(8,128)(2,1)S(1)} %get-tuple-element.90), channel_id=1, source_target_pairs={{0,16},{8,24},{16,0},{24,8},{1,17},{9,25},{17,1},{25,9},{2,18},{10... | collective-permute-start | bytes 1769480 | tf_op jit(solution)/shard_map/ppermute | solution.py:328
  122.7 1.5 %collective-permute-start.22 = (bf16[3,256,384]{2,1,0:T(8,128)(2,1)S(1)}, bf16[3,256,384]{2,1,0:T(8,128)(2,1)S(1)}, u32[]{:S(2)}, u32[]{:S(2)}) collective-permute-start(bf16[3,256,384]{2,1,0:T(8,128)(2,1)S(1)} %get-tuple-element.88), channel_id=1, source_target_pairs={{0,8},{8,0},{16,24},{24,16},{1,9},{9,1},{17,25},{25,17},{2,10},{10... | collective-permute-start | bytes 1769480 | tf_op jit(solution)/shard_map/ppermute | solution.py:328
  124.8 3.8 %collective-permute-start.19 = (bf16[264,1024]{1,0:T(8,128)(2,1)S(1)}, bf16[264,1024]{1,0:T(8,128)(2,1)S(1)}, u32[]{:S(2)}, u32[]{:S(2)}) collective-permute-start(bf16[264,1024]{1,0:T(8,128)(2,1)S(1)} %add_convert_fusion.4), channel_id=1, source_target_pairs={{0,2},{1,3},{2,0},{3,1},{4,6},{5,7},{6,4},{7,5},{8,10},{9,11},{10,... | collective-permute-start | bytes 1622024 | tf_op jit(solution)/shard_map/ppermute | solution.py:341
  129.6 5.9 %collective-permute-done.21.a_last = bf16[3,256,384]{2,1,0:T(8,128)(2,1)S(1)} collective-permute-done((bf16[3,256,384]{2,1,0:T(8,128)(2,1)S(1)}, bf16[3,256,384]{2,1,0:T(8,128)(2,1)S(1)}, u32[]{:S(2)}, u32[]{:S(2)}) %collective-permute-start.21) | collective-permute-done | bytes 589856 | tf_op jit(solution)/shard_map/ppermute | solution.py:328
  135.4 1.7 %collective-permute-done.22.b_last = bf16[3,256,384]{2,1,0:T(8,128)(2,1)S(1)} collective-permute-done((bf16[3,256,384]{2,1,0:T(8,128)(2,1)S(1)}, bf16[3,256,384]{2,1,0:T(8,128)(2,1)S(1)}, u32[]{:S(2)}, u32[]{:S(2)}) %collective-permute-start.22) | collective-permute-done | bytes 589856 | tf_op jit(solution)/shard_map/ppermute | solution.py:328
  137.1 1.3 final_step.1
  138.4 1.4 %collective-permute-done.19.refs_1_ = bf16[264,1024]{1,0:T(8,128)(2,1)S(1)} collective-permute-done((bf16[264,1024]{1,0:T(8,128)(2,1)S(1)}, bf16[264,1024]{1,0:T(8,128)(2,1)S(1)}, u32[]{:S(2)}, u32[]{:S(2)}) %collective-permute-start.19) | collective-permute-done | bytes 540704 | tf_op jit(solution)/shard_map/ppermute | solution.py:341
  139.8 1.0 total.1
  (36 shorter events, 4.9 us)
Async XLA Ops:
  2.9 8.3 %collective-permute-start = (bf16[520,1024]{1,0:T(8,128)(2,1)}, bf16[520,1024]{1,0:T(8,128)(2,1)S(1)}, u32[]{:S(2)}, u32[]{:S(2)}) collective-permute-start(bf16[520,1024]{1,0:T(8,128)(2,1)} %payload.1.refs_0_), channel_id=1, source_target_pairs={{0,1},{1,0},{2,3},{3,2},{4,5},{5,4},{6,7},{7,6},{8,9},{9,8},{10,11... | collective-permute-start | bytes 3194888 | tf_op jit(solution)/shard_map/ppermute | solution.py:344
  3.4 27.0 %collective-permute-start.4 = (bf16[520,1024]{1,0:T(8,128)(2,1)}, bf16[520,1024]{1,0:T(8,128)(2,1)S(1)}, u32[]{:S(2)}, u32[]{:S(2)}) collective-permute-start(bf16[520,1024]{1,0:T(8,128)(2,1)} %payload.1.refs_0_), channel_id=1, source_target_pairs={{0,2},{1,3},{2,0},{3,1},{4,6},{5,7},{6,4},{7,5},{8,10},{9,11},{10,... | collective-permute-start | bytes 3194888 | tf_op jit(solution)/shard_map/ppermute | solution.py:341
  6.1 24.3 %collective-permute-start.3 = (bf16[520,1024]{1,0:T(8,128)(2,1)}, bf16[520,1024]{1,0:T(8,128)(2,1)S(1)}, u32[]{:S(2)}, u32[]{:S(2)}) collective-permute-start(bf16[520,1024]{1,0:T(8,128)(2,1)} %payload.1.refs_0_), channel_id=1, source_target_pairs={{2,4},{3,5},{4,2},{5,3},{10,12},{11,13},{12,10},{13,11},{18,20},{1... | collective-permute-start | bytes 3194888 | tf_op jit(solution)/shard_map/ppermute | solution.py:341
  6.8 48.7 %collective-permute-start.2 = (bf16[520,1024]{1,0:T(8,128)(2,1)}, bf16[520,1024]{1,0:T(8,128)(2,1)S(1)}, u32[]{:S(2)}, u32[]{:S(2)}) collective-permute-start(bf16[520,1024]{1,0:T(8,128)(2,1)} %payload.1.refs_0_), channel_id=1, source_target_pairs={{0,6},{1,7},{6,0},{7,1},{8,14},{9,15},{14,8},{15,9},{16,22},{17,23... | collective-permute-start | bytes 3194888 | tf_op jit(solution)/shard_map/ppermute | solution.py:341
  11.2 2.3 %copy-start = (bf16[1,3,1024,768]{3,2,1,0:T(8,128)(2,1)S(1)}, bf16[1,3,1024,768]{3,2,1,0:T(8,128)(2,1)}, u32[]{:S(2)}) copy-start(bf16[1,3,1024,768]{3,2,1,0:T(8,128)(2,1)} %refs_2_.5) | copy-start | bytes 14155780
  13.5 1.2 copy-start.2
  14.8 45.0 %copy-start.1 = (bf16[1,3,1024,768]{3,2,1,0:T(8,128)(2,1)S(1)}, bf16[1,3,1024,768]{3,2,1,0:T(8,128)(2,1)}, u32[]{:S(2)}) copy-start(bf16[1,3,1024,768]{3,2,1,0:T(8,128)(2,1)} %refs_2_.5) | copy-start | bytes 14155780
  18.9 36.6 %collective-permute-start.1 = (bf16[264,1024]{1,0:T(8,128)(2,1)S(1)}, bf16[264,1024]{1,0:T(8,128)(2,1)S(1)}, u32[]{:S(2)}, u32[]{:S(2)}) collective-permute-start(bf16[264,1024]{1,0:T(8,128)(2,1)S(1)} %get-tuple-element.46), channel_id=1, source_target_pairs={{0,1},{1,0},{2,3},{3,2},{4,5},{5,4},{6,7},{7,6},{8,9},{9,8},{10,11... | collective-permute-start | bytes 1622024 | tf_op jit(solution)/shard_map/ppermute | solution.py:344
  55.5 2.7 %collective-permute-start.10 = (bf16[520,1024]{1,0:T(8,128)(2,1)S(1)}, bf16[520,1024]{1,0:T(8,128)(2,1)S(1)}, u32[]{:S(2)}, u32[]{:S(2)}) collective-permute-start(bf16[520,1024]{1,0:T(8,128)(2,1)S(1)} %collective-permute-done.2.refs_2_), channel_id=1, source_target_pairs={{0,1},{1,0},{2,3},{3,2},{4,5},{5,4},{6,7},{7,6},{8,9},{9,8},{10,11... | collective-permute-start | bytes 3194888 | tf_op jit(solution)/shard_map/ppermute | solution.py:344
  55.5 4.2 %collective-permute-start.9 = (bf16[520,1024]{1,0:T(8,128)(2,1)S(1)}, bf16[520,1024]{1,0:T(8,128)(2,1)S(1)}, u32[]{:S(2)}, u32[]{:S(2)}) collective-permute-start(bf16[520,1024]{1,0:T(8,128)(2,1)S(1)} %collective-permute-done.3.refs_0_), channel_id=1, source_target_pairs={{0,1},{1,0},{2,3},{3,2},{4,5},{5,4},{6,7},{7,6},{8,9},{9,8},{10,11... | collective-permute-start | bytes 3194888 | tf_op jit(solution)/shard_map/ppermute | solution.py:344
  56.0 8.5 %collective-permute-start.7 = (bf16[520,1024]{1,0:T(8,128)(2,1)S(1)}, bf16[520,1024]{1,0:T(8,128)(2,1)S(1)}, u32[]{:S(2)}, u32[]{:S(2)}) collective-permute-start(bf16[520,1024]{1,0:T(8,128)(2,1)S(1)} %collective-permute-done.4.refs_0_), channel_id=1, source_target_pairs={{0,1},{1,0},{2,3},{3,2},{4,5},{5,4},{6,7},{7,6},{8,9},{9,8},{10,11... | collective-permute-start | bytes 3194888 | tf_op jit(solution)/shard_map/ppermute | solution.py:344
  56.0 27.9 %collective-permute-start.5 = (bf16[520,1024]{1,0:T(8,128)(2,1)S(1)}, bf16[520,1024]{1,0:T(8,128)(2,1)S(1)}, u32[]{:S(2)}, u32[]{:S(2)}) collective-permute-start(bf16[520,1024]{1,0:T(8,128)(2,1)S(1)} %collective-permute-done.3.refs_0_), channel_id=1, source_target_pairs={{2,0},{3,1},{4,6},{5,7},{10,8},{11,9},{12,14},{13,15},{18,16},{19,... | collective-permute-start | bytes 3194888 | tf_op jit(solution)/shard_map/ppermute | solution.py:341
  57.3 26.6 %collective-permute-start.6 = (bf16[520,1024]{1,0:T(8,128)(2,1)S(1)}, bf16[520,1024]{1,0:T(8,128)(2,1)S(1)}, u32[]{:S(2)}, u32[]{:S(2)}) collective-permute-start(bf16[520,1024]{1,0:T(8,128)(2,1)S(1)} %collective-permute-done.4.refs_0_), channel_id=1, source_target_pairs={{2,4},{3,5},{4,2},{5,3},{10,12},{11,13},{12,10},{13,11},{18,20},{1... | collective-permute-start | bytes 3194888 | tf_op jit(solution)/shard_map/ppermute | solution.py:341
  64.4 19.6 %collective-permute-start.11 = (bf16[264,1024]{1,0:T(8,128)(2,1)S(1)}, bf16[264,1024]{1,0:T(8,128)(2,1)S(1)}, u32[]{:S(2)}, u32[]{:S(2)}) collective-permute-start(bf16[264,1024]{1,0:T(8,128)(2,1)S(1)} %get-tuple-element.51), channel_id=1, source_target_pairs={{0,1},{1,0},{2,3},{3,2},{4,5},{5,4},{6,7},{7,6},{8,9},{9,8},{10,11... | collective-permute-start | bytes 1622024 | tf_op jit(solution)/shard_map/ppermute | solution.py:344
  68.7 15.2 %collective-permute-start.8 = (bf16[264,1024]{1,0:T(8,128)(2,1)S(1)}, bf16[264,1024]{1,0:T(8,128)(2,1)S(1)}, u32[]{:S(2)}, u32[]{:S(2)}) collective-permute-start(bf16[264,1024]{1,0:T(8,128)(2,1)S(1)} %get-tuple-element.49), channel_id=1, source_target_pairs={{0,1},{1,0},{2,3},{3,2},{4,5},{5,4},{6,7},{7,6},{8,9},{9,8},{10,11... | collective-permute-start | bytes 1622024 | tf_op jit(solution)/shard_map/ppermute | solution.py:344
  84.4 2.7 %collective-permute-start.12 = (bf16[520,1024]{1,0:T(8,128)(2,1)S(1)}, bf16[520,1024]{1,0:T(8,128)(2,1)S(1)}, u32[]{:S(2)}, u32[]{:S(2)}) collective-permute-start(bf16[520,1024]{1,0:T(8,128)(2,1)S(1)} %add_convert_fusion.refs_0_), channel_id=1, source_target_pairs={{0,1},{1,0},{2,3},{3,2},{4,5},{5,4},{6,7},{7,6},{8,9},{9,8},{10,11... | collective-permute-start | bytes 3194888 | tf_op jit(solution)/shard_map/ppermute | solution.py:344
  92.5 28.1 %collective-permute-start.17 = (bf16[2,3,256,384]{3,2,1,0:T(8,128)(2,1)S(1)}, bf16[2,3,256,384]{3,2,1,0:T(8,128)(2,1)S(1)}, u32[]{:S(2)}, u32[]{:S(2)}) collective-permute-start(bf16[2,3,256,384]{3,2,1,0:T(8,128)(2,1)S(1)} %get-tuple-element.75), channel_id=1, source_target_pairs={{0,8},{8,0},{16,24},{24,16},{1,9},{9,1},{17,25},{25,17},{2,10},{10... | collective-permute-start | bytes 3538952 | tf_op jit(solution)/shard_map/ppermute | solution.py:328
  94.0 28.4 %collective-permute-start.18 = (bf16[2,3,256,384]{3,2,1,0:T(8,128)(2,1)S(1)}, bf16[2,3,256,384]{3,2,1,0:T(8,128)(2,1)S(1)}, u32[]{:S(2)}, u32[]{:S(2)}) collective-permute-start(bf16[2,3,256,384]{3,2,1,0:T(8,128)(2,1)S(1)} %get-tuple-element.77), channel_id=1, source_target_pairs={{0,16},{8,24},{16,0},{24,8},{1,17},{9,25},{17,1},{25,9},{2,18},{10... | collective-permute-start | bytes 3538952 | tf_op jit(solution)/shard_map/ppermute | solution.py:328
  95.5 4.8 %collective-permute-start.13 = (bf16[264,1024]{1,0:T(8,128)(2,1)S(1)}, bf16[264,1024]{1,0:T(8,128)(2,1)S(1)}, u32[]{:S(2)}, u32[]{:S(2)}) collective-permute-start(bf16[264,1024]{1,0:T(8,128)(2,1)S(1)} %get-tuple-element.70), channel_id=1, source_target_pairs={{0,1},{1,0},{2,3},{3,2},{4,5},{5,4},{6,7},{7,6},{8,9},{9,8},{10,11... | collective-permute-start | bytes 1622024 | tf_op jit(solution)/shard_map/ppermute | solution.py:344
  95.7 28.5 %collective-permute-start.16 = (bf16[264,1024]{1,0:T(8,128)(2,1)S(1)}, bf16[264,1024]{1,0:T(8,128)(2,1)S(1)}, u32[]{:S(2)}, u32[]{:S(2)}) collective-permute-start(bf16[264,1024]{1,0:T(8,128)(2,1)S(1)} %fusion), channel_id=1, source_target_pairs={{0,6},{1,7},{6,0},{7,1},{8,14},{9,15},{14,8},{15,9},{16,22},{17,23... | collective-permute-start | bytes 1622024 | tf_op jit(solution)/shard_map/ppermute | solution.py:341
  100.5 23.8 %collective-permute-start.15 = (bf16[264,1024]{1,0:T(8,128)(2,1)S(1)}, bf16[264,1024]{1,0:T(8,128)(2,1)S(1)}, u32[]{:S(2)}, u32[]{:S(2)}) collective-permute-start(bf16[264,1024]{1,0:T(8,128)(2,1)S(1)} %add_convert_fusion.6), channel_id=1, source_target_pairs={{0,2},{1,3},{6,4},{7,5},{8,10},{9,11},{14,12},{15,13},{16,18},{17,... | collective-permute-start | bytes 1622024 | tf_op jit(solution)/shard_map/ppermute | solution.py:341
  103.3 20.9 %collective-permute-start.14 = (bf16[264,1024]{1,0:T(8,128)(2,1)S(1)}, bf16[264,1024]{1,0:T(8,128)(2,1)S(1)}, u32[]{:S(2)}, u32[]{:S(2)}) collective-permute-start(bf16[264,1024]{1,0:T(8,128)(2,1)S(1)} %add_convert_fusion.6), channel_id=1, source_target_pairs={{2,4},{3,5},{4,2},{5,3},{10,12},{11,13},{12,10},{13,11},{18,20},{1... | collective-permute-start | bytes 1622024 | tf_op jit(solution)/shard_map/ppermute | solution.py:341
  120.8 14.6 %collective-permute-start.21 = (bf16[3,256,384]{2,1,0:T(8,128)(2,1)S(1)}, bf16[3,256,384]{2,1,0:T(8,128)(2,1)S(1)}, u32[]{:S(2)}, u32[]{:S(2)}) collective-permute-start(bf16[3,256,384]{2,1,0:T(8,128)(2,1)S(1)} %get-tuple-element.90), channel_id=1, source_target_pairs={{0,16},{8,24},{16,0},{24,8},{1,17},{9,25},{17,1},{25,9},{2,18},{10... | collective-permute-start | bytes 1769480 | tf_op jit(solution)/shard_map/ppermute | solution.py:328
  122.7 14.4 %collective-permute-start.22 = (bf16[3,256,384]{2,1,0:T(8,128)(2,1)S(1)}, bf16[3,256,384]{2,1,0:T(8,128)(2,1)S(1)}, u32[]{:S(2)}, u32[]{:S(2)}) collective-permute-start(bf16[3,256,384]{2,1,0:T(8,128)(2,1)S(1)} %get-tuple-element.88), channel_id=1, source_target_pairs={{0,8},{8,0},{16,24},{24,16},{1,9},{9,1},{17,25},{25,17},{2,10},{10... | collective-permute-start | bytes 1769480 | tf_op jit(solution)/shard_map/ppermute | solution.py:328
  124.8 15.0 %collective-permute-start.19 = (bf16[264,1024]{1,0:T(8,128)(2,1)S(1)}, bf16[264,1024]{1,0:T(8,128)(2,1)S(1)}, u32[]{:S(2)}, u32[]{:S(2)}) collective-permute-start(bf16[264,1024]{1,0:T(8,128)(2,1)S(1)} %add_convert_fusion.4), channel_id=1, source_target_pairs={{0,2},{1,3},{2,0},{3,1},{4,6},{5,7},{6,4},{7,5},{8,10},{9,11},{10,... | collective-permute-start | bytes 1622024 | tf_op jit(solution)/shard_map/ppermute | solution.py:341
  128.6 11.2 %collective-permute-start.20 = (bf16[264,1024]{1,0:T(8,128)(2,1)S(1)}, bf16[264,1024]{1,0:T(8,128)(2,1)S(1)}, u32[]{:S(2)}, u32[]{:S(2)}) collective-permute-start(bf16[264,1024]{1,0:T(8,128)(2,1)S(1)} %add_convert_fusion.3), channel_id=1, source_target_pairs={{2,4},{3,5},{4,2},{5,3},{10,12},{11,13},{12,10},{13,11},{18,20},{1... | collective-permute-start | bytes 1622024 | tf_op jit(solution)/shard_map/ppermute | solution.py:341

commit v9 on v8

--- a/solution.py
+++ b/solution.py
@@ -385,7 +385,7 @@
         landed = move(sent, inner)
         came = move(sent, from_ends)
         far_back = move(add(*far_sum), across_all)
-        landed, came, far_back = after((landed, came, far_back), next_pair)
+        came, landed, far_back = after((came, landed, far_back), next_pair)
         back = move(add(*first_sum, landed), outer)
         second_back = move(add(*far_sum, came), inner)
         total = [add(*own_sum, far_back), back, second_back]

time: 142 us -> 142 us (level)
  waiting for transfers between devices: 77.2 us -> 74.3 us
  starting transfers between devices: 30.3 us -> 33.2 us
    ppermute x4, waiting for transfers between devices: 24 us -> 21.1 us  [across(): return lax.ppermute(value, 'dp', [(i, i ^ bit) for i in range(4)])]
    ppermute x10, starting transfers between devices: 22.3 us -> 25.2 us  [move(): return lax.ppermute(value, 'expert', full)]
where the time goes in v9:
time: 142 us; the launch traced here: 141 us
  waiting for transfers between devices  74.3 us (52%)
  starting transfers between devices  33.2 us (23%)
  Pallas kernels  26.7 us (19%)
  local copies, waits for them, and re-layouts  3.57 us (3%)
  other arithmetic  2.18 us (2%)
    ppermute x10, waiting for transfers between devices, move(): return lax.ppermute(value, 'expert', full)  48.8 us
    ppermute x10, starting transfers between devices, move(): return lax.ppermute(value, 'expert', full)  25.2 us
    ppermute x4, waiting for transfers between devices, across(): return lax.ppermute(value, 'dp', [(i, i ^ bit) for i in range(4)])  21.1 us
    pallas_call x4, Pallas kernels, run_slot(): pl.pallas_call(functools.partial(slot_kernel, choices, partial is not Non...  18.3 us
    ppermute x4, starting transfers between devices, across(): return lax.ppermute(value, 'dp', [(i, i ^ bit) for i in range(4)])  6.2 us
    ppermute x9, waiting for transfers between devices, swap(): return lax.ppermute(value, 'expert', [(i, i ^ 1) for i in range(devices)])  4.35 us
    pallas_call x1, Pallas kernels, run_partial(): pl.pallas_call(functools.partial(partial_kernel, len(lefts)), out_shape=j...  3.89 us
    unnamed x6, local copies, waits for them, and re-layouts  3.57 us
  transfers between devices with their start and end apart: 23, of which 10 were waited for; matrix products, arithmetic and copies ran while one was open for 1% of the time, Pallas kernels for 13%

profile of v9, /device:TPU:0, one launch (start us, length us, event | category | flops | bytes accessed | tf_op | source)
XLA Modules:
  0.0 140.8 jit_solution(14340470050548658806)
XLA Ops:
  0.6 2.2 %payload.1.refs_0_ = bf16[520,1024]{1,0:T(8,128)(2,1)} custom-call(bf16[256,1024]{1,0:T(8,128)(2,1)} %tokens.1, bf16[256,1024]{1,0:T(8,128)(2,1)} %cotangent.1, s32[2,256]{1,0:T(2,128)} %bitcast.13, bf16[2,256]{1,0:T(2,128)(2,1)} %bitcast.14), custom_call_target="tpu_custom_call" | custom-call | flops 1 | bytes 1 | tf_op jit(solution)/shard_map/payload/pallas_call | solution.py:256
  3.4 2.6 %collective-permute-start.4 = (bf16[520,1024]{1,0:T(8,128)(2,1)}, bf16[520,1024]{1,0:T(8,128)(2,1)S(1)}, u32[]{:S(2)}, u32[]{:S(2)}) collective-permute-start(bf16[520,1024]{1,0:T(8,128)(2,1)} %payload.1.refs_0_), channel_id=1, source_target_pairs={{0,2},{1,3},{2,0},{3,1},{4,6},{5,7},{6,4},{7,5},{8,10},{9,11},{10,... | collective-permute-start | bytes 3194888 | tf_op jit(solution)/shard_map/ppermute | solution.py:341
  6.1 0.7 collective-permute-start.3
  6.8 4.4 %collective-permute-start.2 = (bf16[520,1024]{1,0:T(8,128)(2,1)}, bf16[520,1024]{1,0:T(8,128)(2,1)S(1)}, u32[]{:S(2)}, u32[]{:S(2)}) collective-permute-start(bf16[520,1024]{1,0:T(8,128)(2,1)} %payload.1.refs_0_), channel_id=1, source_target_pairs={{0,6},{1,7},{6,0},{7,1},{8,14},{9,15},{14,8},{15,9},{16,22},{17,23... | collective-permute-start | bytes 3194888 | tf_op jit(solution)/shard_map/ppermute | solution.py:341
  11.2 2.3 %copy-done = bf16[1,3,1024,768]{3,2,1,0:T(8,128)(2,1)S(1)} copy-done((bf16[1,3,1024,768]{3,2,1,0:T(8,128)(2,1)S(1)}, bf16[1,3,1024,768]{3,2,1,0:T(8,128)(2,1)}, u32[]{:S(2)}) %copy-start) | copy-done | bytes 4718616
  13.5 1.2 copy-done.2
  14.8 4.1 %expert_block.4 = (bf16[256,1024]{1,0:T(8,128)(2,1)S(1)}, bf16[256,1024]{1,0:T(8,128)(2,1)S(1)}, bf16[256,768]{1,0:T(8,128)(2,1)S(1)}, bf16[256,768]{1,0:T(8,128...) custom-call(bf16[520,1024]{1,0:T(8,128)(2,1)S(1)} %copy-done.2, ...), custom_call_target="tpu_custom_call" | custom-call | flops 1 | bytes 1 | tf_op jit(solution)/shard_map/expert_block/pallas_call | solution.py:132
  19.0 11.4 %collective-permute-done.4.refs_0_ = bf16[520,1024]{1,0:T(8,128)(2,1)S(1)} collective-permute-done((bf16[520,1024]{1,0:T(8,128)(2,1)}, bf16[520,1024]{1,0:T(8,128)(2,1)S(1)}, u32[]{:S(2)}, u32[]{:S(2)}) %collective-permute-start.4) | collective-permute-done | bytes 1064992 | tf_op jit(solution)/shard_map/ppermute | solution.py:341
  30.4 25.1 %collective-permute-done.2.refs_2_ = bf16[520,1024]{1,0:T(8,128)(2,1)S(1)} collective-permute-done((bf16[520,1024]{1,0:T(8,128)(2,1)}, bf16[520,1024]{1,0:T(8,128)(2,1)S(1)}, u32[]{:S(2)}, u32[]{:S(2)}) %collective-permute-start.2) | collective-permute-done | bytes 1064992 | tf_op jit(solution)/shard_map/ppermute | solution.py:341
  56.0 1.3 collective-permute-start.5
  57.3 0.7 collective-permute-start.6
  58.2 1.5 %collective-permute-done.9.refs_1_ = bf16[520,1024]{1,0:T(8,128)(2,1)S(1)} collective-permute-done((bf16[520,1024]{1,0:T(8,128)(2,1)S(1)}, bf16[520,1024]{1,0:T(8,128)(2,1)S(1)}, u32[]{:S(2)}, u32[]{:S(2)}) %collective-permute-start.9) | collective-permute-done | bytes 1064992 | tf_op jit(solution)/shard_map/ppermute | solution.py:344
  59.7 4.6 %expert_block.6 = (bf16[256,1024]{1,0:T(8,128)(2,1)S(1)}, bf16[256,1024]{1,0:T(8,128)(2,1)S(1)}, bf16[256,768]{1,0:T(8,128)(2,1)S(1)}, bf16[256,768]{1,0:T(8,128...) custom-call(bf16[520,1024]{1,0:T(8,128)(2,1)S(1)} %collective-permute-done.3., ...), custom_call_target="tpu_custom_call" | custom-call | flops 1 | bytes 1 | tf_op jit(solution)/shard_map/expert_block/pallas_call | solution.py:132
  64.6 4.2 %expert_block.5 = (bf16[256,1024]{1,0:T(8,128)(2,1)S(1)}, bf16[256,1024]{1,0:T(8,128)(2,1)S(1)}, bf16[256,768]{1,0:T(8,128)(2,1)S(1)}, bf16[256,768]{1,0:T(8,128...) custom-call(bf16[520,1024]{1,0:T(8,128)(2,1)S(1)} %collective-permute-done.4., ...), custom_call_target="tpu_custom_call" | custom-call | flops 1 | bytes 1 | tf_op jit(solution)/shard_map/expert_block/pallas_call | solution.py:132
  69.2 3.9 %partial_weights.1.refs_3_ = f32[3,1024,768]{2,1,0:T(8,128)S(1)} custom-call(bf16[256,1024]{1,0:T(8,128)(2,1)S(1)} %get-tuple-element.52.refs_0_.refs_6_, bf16[256,1024]{1,0:T(8,128)(2,1)S(1)} %get-tuple-element.53.refs_1_.refs_7_, bf16[256,1024]{1,0:T(8,128)(2,1)S(1)} %get-tuple-element.54.refs_2_.refs_8_, bf16[256,768]{1,0:T(8,128)(2,1)S(1)} %get-tuple-element.55.refs_3_, ...), custom_call_target="tpu_custom_call" | custom-call | flops 1 | bytes 1 | tf_op jit(solution)/shard_map/partial_weights/pallas_call | solution.py:164
  73.0 10.9 %collective-permute-done.5 = bf16[520,1024]{1,0:T(8,128)(2,1)S(1)} collective-permute-done((bf16[520,1024]{1,0:T(8,128)(2,1)S(1)}, bf16[520,1024]{1,0:T(8,128)(2,1)S(1)}, u32[]{:S(2)}, u32[]{:S(2)}) %collective-permute-start.5) | collective-permute-done | bytes 1064992 | tf_op jit(solution)/shard_map/ppermute | solution.py:341
  84.4 2.7 %collective-permute-done.12.refs_1_ = bf16[520,1024]{1,0:T(8,128)(2,1)S(1)} collective-permute-done((bf16[520,1024]{1,0:T(8,128)(2,1)S(1)}, bf16[520,1024]{1,0:T(8,128)(2,1)S(1)}, u32[]{:S(2)}, u32[]{:S(2)}) %collective-permute-start.12) | collective-permute-done | bytes 1064992 | tf_op jit(solution)/shard_map/ppermute | solution.py:344
  87.1 5.3 %expert_block.7 = (bf16[2,3,256,384]{3,2,1,0:T(8,128)(2,1)S(1)}, bf16[2,3,256,384]{3,2,1,0:T(8,128)(2,1)S(1)}, bf16[2,3,256,384]{3,2,1,0:T(8,128)(2,1)S(1)}, bf1...) custom-call(bf16[520,1024]{1,0:T(8,128)(2,1)S(1)} %add_convert_fusion.refs_0_, ...), custom_call_target="tpu_custom_call" | custom-call | flops 1 | bytes 1 | tf_op jit(solution)/shard_map/expert_block/pallas_call | solution.py:132
  92.5 1.6 %collective-permute-start.17 = (bf16[2,3,256,384]{3,2,1,0:T(8,128)(2,1)S(1)}, bf16[2,3,256,384]{3,2,1,0:T(8,128)(2,1)S(1)}, u32[]{:S(2)}, u32[]{:S(2)}) collective-permute-start(bf16[2,3,256,384]{3,2,1,0:T(8,128)(2,1)S(1)} %get-tuple-element.75), channel_id=1, source_target_pairs={{0,8},{8,0},{16,24},{24,16},{1,9},{9,1},{17,25},{25,17},{2,10},{10... | collective-permute-start | bytes 3538952 | tf_op jit(solution)/shard_map/ppermute | solution.py:328
  94.0 1.5 %collective-permute-start.18 = (bf16[2,3,256,384]{3,2,1,0:T(8,128)(2,1)S(1)}, bf16[2,3,256,384]{3,2,1,0:T(8,128)(2,1)S(1)}, u32[]{:S(2)}, u32[]{:S(2)}) collective-permute-start(bf16[2,3,256,384]{3,2,1,0:T(8,128)(2,1)S(1)} %get-tuple-element.77), channel_id=1, source_target_pairs={{0,16},{8,24},{16,0},{24,8},{1,17},{9,25},{17,1},{25,9},{2,18},{10... | collective-permute-start | bytes 3538952 | tf_op jit(solution)/shard_map/ppermute | solution.py:328
  95.7 4.6 %collective-permute-start.16 = (bf16[264,1024]{1,0:T(8,128)(2,1)S(1)}, bf16[264,1024]{1,0:T(8,128)(2,1)S(1)}, u32[]{:S(2)}, u32[]{:S(2)}) collective-permute-start(bf16[264,1024]{1,0:T(8,128)(2,1)S(1)} %fusion), channel_id=1, source_target_pairs={{0,6},{1,7},{6,0},{7,1},{8,14},{9,15},{14,8},{15,9},{16,22},{17,23... | collective-permute-start | bytes 1622024 | tf_op jit(solution)/shard_map/ppermute | solution.py:341
  100.5 0.7 collective-permute-start.15
  101.2 5.8 %collective-permute-start.14 = (bf16[264,1024]{1,0:T(8,128)(2,1)S(1)}, bf16[264,1024]{1,0:T(8,128)(2,1)S(1)}, u32[]{:S(2)}, u32[]{:S(2)}) collective-permute-start(bf16[264,1024]{1,0:T(8,128)(2,1)S(1)} %add_convert_fusion.6), channel_id=1, source_target_pairs={{0,2},{1,3},{6,4},{7,5},{8,10},{9,11},{14,12},{15,13},{16,18},{17,... | collective-permute-start | bytes 1622024 | tf_op jit(solution)/shard_map/ppermute | solution.py:341
  107.0 13.6 %collective-permute-done.17 = bf16[2,3,256,384]{3,2,1,0:T(8,128)(2,1)S(1)} collective-permute-done((bf16[2,3,256,384]{3,2,1,0:T(8,128)(2,1)S(1)}, bf16[2,3,256,384]{3,2,1,0:T(8,128)(2,1)S(1)}, u32[]{:S(2)}, u32[]{:S(2)}) %collective-permute-start.17) | collective-permute-done | bytes 1179680 | tf_op jit(solution)/shard_map/ppermute | solution.py:328
  120.8 1.6 %collective-permute-start.21 = (bf16[3,256,384]{2,1,0:T(8,128)(2,1)S(1)}, bf16[3,256,384]{2,1,0:T(8,128)(2,1)S(1)}, u32[]{:S(2)}, u32[]{:S(2)}) collective-permute-start(bf16[3,256,384]{2,1,0:T(8,128)(2,1)S(1)} %get-tuple-element.90), channel_id=1, source_target_pairs={{0,16},{8,24},{16,0},{24,8},{1,17},{9,25},{17,1},{25,9},{2,18},{10... | collective-permute-start | bytes 1769480 | tf_op jit(solution)/shard_map/ppermute | solution.py:328
  122.7 1.5 %collective-permute-start.22 = (bf16[3,256,384]{2,1,0:T(8,128)(2,1)S(1)}, bf16[3,256,384]{2,1,0:T(8,128)(2,1)S(1)}, u32[]{:S(2)}, u32[]{:S(2)}) collective-permute-start(bf16[3,256,384]{2,1,0:T(8,128)(2,1)S(1)} %get-tuple-element.88), channel_id=1, source_target_pairs={{0,8},{8,0},{16,24},{24,16},{1,9},{9,1},{17,25},{25,17},{2,10},{10... | collective-permute-start | bytes 1769480 | tf_op jit(solution)/shard_map/ppermute | solution.py:328
  124.8 3.8 %collective-permute-start.19 = (bf16[264,1024]{1,0:T(8,128)(2,1)S(1)}, bf16[264,1024]{1,0:T(8,128)(2,1)S(1)}, u32[]{:S(2)}, u32[]{:S(2)}) collective-permute-start(bf16[264,1024]{1,0:T(8,128)(2,1)S(1)} %add_convert_fusion.4), channel_id=1, source_target_pairs={{0,2},{1,3},{2,0},{3,1},{4,6},{5,7},{6,4},{7,5},{8,10},{9,11},{10,... | collective-permute-start | bytes 1622024 | tf_op jit(solution)/shard_map/ppermute | solution.py:341
  129.6 5.9 %collective-permute-done.21.a_last = bf16[3,256,384]{2,1,0:T(8,128)(2,1)S(1)} collective-permute-done((bf16[3,256,384]{2,1,0:T(8,128)(2,1)S(1)}, bf16[3,256,384]{2,1,0:T(8,128)(2,1)S(1)}, u32[]{:S(2)}, u32[]{:S(2)}) %collective-permute-start.21) | collective-permute-done | bytes 589856 | tf_op jit(solution)/shard_map/ppermute | solution.py:328
  135.4 1.7 %collective-permute-done.22.b_last = bf16[3,256,384]{2,1,0:T(8,128)(2,1)S(1)} collective-permute-done((bf16[3,256,384]{2,1,0:T(8,128)(2,1)S(1)}, bf16[3,256,384]{2,1,0:T(8,128)(2,1)S(1)}, u32[]{:S(2)}, u32[]{:S(2)}) %collective-permute-start.22) | collective-permute-done | bytes 589856 | tf_op jit(solution)/shard_map/ppermute | solution.py:328
  137.1 1.3 final_step.1
  138.4 1.4 %collective-permute-done.19.refs_1_ = bf16[264,1024]{1,0:T(8,128)(2,1)S(1)} collective-permute-done((bf16[264,1024]{1,0:T(8,128)(2,1)S(1)}, bf16[264,1024]{1,0:T(8,128)(2,1)S(1)}, u32[]{:S(2)}, u32[]{:S(2)}) %collective-permute-start.19) | collective-permute-done | bytes 540704 | tf_op jit(solution)/shard_map/ppermute | solution.py:341
  139.8 1.0 total.1
  (36 shorter events, 4.9 us)
Async XLA Ops:
  2.9 8.3 %collective-permute-start = (bf16[520,1024]{1,0:T(8,128)(2,1)}, bf16[520,1024]{1,0:T(8,128)(2,1)S(1)}, u32[]{:S(2)}, u32[]{:S(2)}) collective-permute-start(bf16[520,1024]{1,0:T(8,128)(2,1)} %payload.1.refs_0_), channel_id=1, source_target_pairs={{0,1},{1,0},{2,3},{3,2},{4,5},{5,4},{6,7},{7,6},{8,9},{9,8},{10,11... | collective-permute-start | bytes 3194888 | tf_op jit(solution)/shard_map/ppermute | solution.py:344
  3.4 27.0 %collective-permute-start.4 = (bf16[520,1024]{1,0:T(8,128)(2,1)}, bf16[520,1024]{1,0:T(8,128)(2,1)S(1)}, u32[]{:S(2)}, u32[]{:S(2)}) collective-permute-start(bf16[520,1024]{1,0:T(8,128)(2,1)} %payload.1.refs_0_), channel_id=1, source_target_pairs={{0,2},{1,3},{2,0},{3,1},{4,6},{5,7},{6,4},{7,5},{8,10},{9,11},{10,... | collective-permute-start | bytes 3194888 | tf_op jit(solution)/shard_map/ppermute | solution.py:341
  6.1 24.3 %collective-permute-start.3 = (bf16[520,1024]{1,0:T(8,128)(2,1)}, bf16[520,1024]{1,0:T(8,128)(2,1)S(1)}, u32[]{:S(2)}, u32[]{:S(2)}) collective-permute-start(bf16[520,1024]{1,0:T(8,128)(2,1)} %payload.1.refs_0_), channel_id=1, source_target_pairs={{2,4},{3,5},{4,2},{5,3},{10,12},{11,13},{12,10},{13,11},{18,20},{1... | collective-permute-start | bytes 3194888 | tf_op jit(solution)/shard_map/ppermute | solution.py:341
  6.8 48.7 %collective-permute-start.2 = (bf16[520,1024]{1,0:T(8,128)(2,1)}, bf16[520,1024]{1,0:T(8,128)(2,1)S(1)}, u32[]{:S(2)}, u32[]{:S(2)}) collective-permute-start(bf16[520,1024]{1,0:T(8,128)(2,1)} %payload.1.refs_0_), channel_id=1, source_target_pairs={{0,6},{1,7},{6,0},{7,1},{8,14},{9,15},{14,8},{15,9},{16,22},{17,23... | collective-permute-start | bytes 3194888 | tf_op jit(solution)/shard_map/ppermute | solution.py:341
  11.2 2.3 %copy-start = (bf16[1,3,1024,768]{3,2,1,0:T(8,128)(2,1)S(1)}, bf16[1,3,1024,768]{3,2,1,0:T(8,128)(2,1)}, u32[]{:S(2)}) copy-start(bf16[1,3,1024,768]{3,2,1,0:T(8,128)(2,1)} %refs_2_.5) | copy-start | bytes 14155780
  13.5 1.2 copy-start.2
  14.8 45.0 %copy-start.1 = (bf16[1,3,1024,768]{3,2,1,0:T(8,128)(2,1)S(1)}, bf16[1,3,1024,768]{3,2,1,0:T(8,128)(2,1)}, u32[]{:S(2)}) copy-start(bf16[1,3,1024,768]{3,2,1,0:T(8,128)(2,1)} %refs_2_.5) | copy-start | bytes 14155780
  18.9 36.6 %collective-permute-start.1 = (bf16[264,1024]{1,0:T(8,128)(2,1)S(1)}, bf16[264,1024]{1,0:T(8,128)(2,1)S(1)}, u32[]{:S(2)}, u32[]{:S(2)}) collective-permute-start(bf16[264,1024]{1,0:T(8,128)(2,1)S(1)} %get-tuple-element.46), channel_id=1, source_target_pairs={{0,1},{1,0},{2,3},{3,2},{4,5},{5,4},{6,7},{7,6},{8,9},{9,8},{10,11... | collective-permute-start | bytes 1622024 | tf_op jit(solution)/shard_map/ppermute | solution.py:344
  55.5 2.7 %collective-permute-start.10 = (bf16[520,1024]{1,0:T(8,128)(2,1)S(1)}, bf16[520,1024]{1,0:T(8,128)(2,1)S(1)}, u32[]{:S(2)}, u32[]{:S(2)}) collective-permute-start(bf16[520,1024]{1,0:T(8,128)(2,1)S(1)} %collective-permute-done.2.refs_2_), channel_id=1, source_target_pairs={{0,1},{1,0},{2,3},{3,2},{4,5},{5,4},{6,7},{7,6},{8,9},{9,8},{10,11... | collective-permute-start | bytes 3194888 | tf_op jit(solution)/shard_map/ppermute | solution.py:344
  55.5 4.2 %collective-permute-start.9 = (bf16[520,1024]{1,0:T(8,128)(2,1)S(1)}, bf16[520,1024]{1,0:T(8,128)(2,1)S(1)}, u32[]{:S(2)}, u32[]{:S(2)}) collective-permute-start(bf16[520,1024]{1,0:T(8,128)(2,1)S(1)} %collective-permute-done.3.refs_0_), channel_id=1, source_target_pairs={{0,1},{1,0},{2,3},{3,2},{4,5},{5,4},{6,7},{7,6},{8,9},{9,8},{10,11... | collective-permute-start | bytes 3194888 | tf_op jit(solution)/shard_map/ppermute | solution.py:344
  56.0 8.5 %collective-permute-start.7 = (bf16[520,1024]{1,0:T(8,128)(2,1)S(1)}, bf16[520,1024]{1,0:T(8,128)(2,1)S(1)}, u32[]{:S(2)}, u32[]{:S(2)}) collective-permute-start(bf16[520,1024]{1,0:T(8,128)(2,1)S(1)} %collective-permute-done.4.refs_0_), channel_id=1, source_target_pairs={{0,1},{1,0},{2,3},{3,2},{4,5},{5,4},{6,7},{7,6},{8,9},{9,8},{10,11... | collective-permute-start | bytes 3194888 | tf_op jit(solution)/shard_map/ppermute | solution.py:344
  56.0 27.9 %collective-permute-start.5 = (bf16[520,1024]{1,0:T(8,128)(2,1)S(1)}, bf16[520,1024]{1,0:T(8,128)(2,1)S(1)}, u32[]{:S(2)}, u32[]{:S(2)}) collective-permute-start(bf16[520,1024]{1,0:T(8,128)(2,1)S(1)} %collective-permute-done.3.refs_0_), channel_id=1, source_target_pairs={{2,0},{3,1},{4,6},{5,7},{10,8},{11,9},{12,14},{13,15},{18,16},{19,... | collective-permute-start | bytes 3194888 | tf_op jit(solution)/shard_map/ppermute | solution.py:341
  57.3 26.6 %collective-permute-start.6 = (bf16[520,1024]{1,0:T(8,128)(2,1)S(1)}, bf16[520,1024]{1,0:T(8,128)(2,1)S(1)}, u32[]{:S(2)}, u32[]{:S(2)}) collective-permute-start(bf16[520,1024]{1,0:T(8,128)(2,1)S(1)} %collective-permute-done.4.refs_0_), channel_id=1, source_target_pairs={{2,4},{3,5},{4,2},{5,3},{10,12},{11,13},{12,10},{13,11},{18,20},{1... | collective-permute-start | bytes 3194888 | tf_op jit(solution)/shard_map/ppermute | solution.py:341
  64.4 19.6 %collective-permute-start.11 = (bf16[264,1024]{1,0:T(8,128)(2,1)S(1)}, bf16[264,1024]{1,0:T(8,128)(2,1)S(1)}, u32[]{:S(2)}, u32[]{:S(2)}) collective-permute-start(bf16[264,1024]{1,0:T(8,128)(2,1)S(1)} %get-tuple-element.51), channel_id=1, source_target_pairs={{0,1},{1,0},{2,3},{3,2},{4,5},{5,4},{6,7},{7,6},{8,9},{9,8},{10,11... | collective-permute-start | bytes 1622024 | tf_op jit(solution)/shard_map/ppermute | solution.py:344
  68.7 15.2 %collective-permute-start.8 = (bf16[264,1024]{1,0:T(8,128)(2,1)S(1)}, bf16[264,1024]{1,0:T(8,128)(2,1)S(1)}, u32[]{:S(2)}, u32[]{:S(2)}) collective-permute-start(bf16[264,1024]{1,0:T(8,128)(2,1)S(1)} %get-tuple-element.49), channel_id=1, source_target_pairs={{0,1},{1,0},{2,3},{3,2},{4,5},{5,4},{6,7},{7,6},{8,9},{9,8},{10,11... | collective-permute-start | bytes 1622024 | tf_op jit(solution)/shard_map/ppermute | solution.py:344
  84.4 2.7 %collective-permute-start.12 = (bf16[520,1024]{1,0:T(8,128)(2,1)S(1)}, bf16[520,1024]{1,0:T(8,128)(2,1)S(1)}, u32[]{:S(2)}, u32[]{:S(2)}) collective-permute-start(bf16[520,1024]{1,0:T(8,128)(2,1)S(1)} %add_convert_fusion.refs_0_), channel_id=1, source_target_pairs={{0,1},{1,0},{2,3},{3,2},{4,5},{5,4},{6,7},{7,6},{8,9},{9,8},{10,11... | collective-permute-start | bytes 3194888 | tf_op jit(solution)/shard_map/ppermute | solution.py:344
  92.5 28.1 %collective-permute-start.17 = (bf16[2,3,256,384]{3,2,1,0:T(8,128)(2,1)S(1)}, bf16[2,3,256,384]{3,2,1,0:T(8,128)(2,1)S(1)}, u32[]{:S(2)}, u32[]{:S(2)}) collective-permute-start(bf16[2,3,256,384]{3,2,1,0:T(8,128)(2,1)S(1)} %get-tuple-element.75), channel_id=1, source_target_pairs={{0,8},{8,0},{16,24},{24,16},{1,9},{9,1},{17,25},{25,17},{2,10},{10... | collective-permute-start | bytes 3538952 | tf_op jit(solution)/shard_map/ppermute | solution.py:328
  94.0 28.4 %collective-permute-start.18 = (bf16[2,3,256,384]{3,2,1,0:T(8,128)(2,1)S(1)}, bf16[2,3,256,384]{3,2,1,0:T(8,128)(2,1)S(1)}, u32[]{:S(2)}, u32[]{:S(2)}) collective-permute-start(bf16[2,3,256,384]{3,2,1,0:T(8,128)(2,1)S(1)} %get-tuple-element.77), channel_id=1, source_target_pairs={{0,16},{8,24},{16,0},{24,8},{1,17},{9,25},{17,1},{25,9},{2,18},{10... | collective-permute-start | bytes 3538952 | tf_op jit(solution)/shard_map/ppermute | solution.py:328
  95.5 4.8 %collective-permute-start.13 = (bf16[264,1024]{1,0:T(8,128)(2,1)S(1)}, bf16[264,1024]{1,0:T(8,128)(2,1)S(1)}, u32[]{:S(2)}, u32[]{:S(2)}) collective-permute-start(bf16[264,1024]{1,0:T(8,128)(2,1)S(1)} %get-tuple-element.70), channel_id=1, source_target_pairs={{0,1},{1,0},{2,3},{3,2},{4,5},{5,4},{6,7},{7,6},{8,9},{9,8},{10,11... | collective-permute-start | bytes 1622024 | tf_op jit(solution)/shard_map/ppermute | solution.py:344
  95.7 28.5 %collective-permute-start.16 = (bf16[264,1024]{1,0:T(8,128)(2,1)S(1)}, bf16[264,1024]{1,0:T(8,128)(2,1)S(1)}, u32[]{:S(2)}, u32[]{:S(2)}) collective-permute-start(bf16[264,1024]{1,0:T(8,128)(2,1)S(1)} %fusion), channel_id=1, source_target_pairs={{0,6},{1,7},{6,0},{7,1},{8,14},{9,15},{14,8},{15,9},{16,22},{17,23... | collective-permute-start | bytes 1622024 | tf_op jit(solution)/shard_map/ppermute | solution.py:341
  100.5 23.8 %collective-permute-start.15 = (bf16[264,1024]{1,0:T(8,128)(2,1)S(1)}, bf16[264,1024]{1,0:T(8,128)(2,1)S(1)}, u32[]{:S(2)}, u32[]{:S(2)}) collective-permute-start(bf16[264,1024]{1,0:T(8,128)(2,1)S(1)} %add_convert_fusion.6), channel_id=1, source_target_pairs={{2,4},{3,5},{4,2},{5,3},{10,12},{11,13},{12,10},{13,11},{18,20},{1... | collective-permute-start | bytes 1622024 | tf_op jit(solution)/shard_map/ppermute | solution.py:341
  101.2 23.1 %collective-permute-start.14 = (bf16[264,1024]{1,0:T(8,128)(2,1)S(1)}, bf16[264,1024]{1,0:T(8,128)(2,1)S(1)}, u32[]{:S(2)}, u32[]{:S(2)}) collective-permute-start(bf16[264,1024]{1,0:T(8,128)(2,1)S(1)} %add_convert_fusion.6), channel_id=1, source_target_pairs={{0,2},{1,3},{6,4},{7,5},{8,10},{9,11},{14,12},{15,13},{16,18},{17,... | collective-permute-start | bytes 1622024 | tf_op jit(solution)/shard_map/ppermute | solution.py:341
  120.8 14.6 %collective-permute-start.21 = (bf16[3,256,384]{2,1,0:T(8,128)(2,1)S(1)}, bf16[3,256,384]{2,1,0:T(8,128)(2,1)S(1)}, u32[]{:S(2)}, u32[]{:S(2)}) collective-permute-start(bf16[3,256,384]{2,1,0:T(8,128)(2,1)S(1)} %get-tuple-element.90), channel_id=1, source_target_pairs={{0,16},{8,24},{16,0},{24,8},{1,17},{9,25},{17,1},{25,9},{2,18},{10... | collective-permute-start | bytes 1769480 | tf_op jit(solution)/shard_map/ppermute | solution.py:328
  122.7 14.4 %collective-permute-start.22 = (bf16[3,256,384]{2,1,0:T(8,128)(2,1)S(1)}, bf16[3,256,384]{2,1,0:T(8,128)(2,1)S(1)}, u32[]{:S(2)}, u32[]{:S(2)}) collective-permute-start(bf16[3,256,384]{2,1,0:T(8,128)(2,1)S(1)} %get-tuple-element.88), channel_id=1, source_target_pairs={{0,8},{8,0},{16,24},{24,16},{1,9},{9,1},{17,25},{25,17},{2,10},{10... | collective-permute-start | bytes 1769480 | tf_op jit(solution)/shard_map/ppermute | solution.py:328
  124.8 15.0 %collective-permute-start.19 = (bf16[264,1024]{1,0:T(8,128)(2,1)S(1)}, bf16[264,1024]{1,0:T(8,128)(2,1)S(1)}, u32[]{:S(2)}, u32[]{:S(2)}) collective-permute-start(bf16[264,1024]{1,0:T(8,128)(2,1)S(1)} %add_convert_fusion.4), channel_id=1, source_target_pairs={{0,2},{1,3},{2,0},{3,1},{4,6},{5,7},{6,4},{7,5},{8,10},{9,11},{10,... | collective-permute-start | bytes 1622024 | tf_op jit(solution)/shard_map/ppermute | solution.py:341
  128.6 11.2 %collective-permute-start.20 = (bf16[264,1024]{1,0:T(8,128)(2,1)S(1)}, bf16[264,1024]{1,0:T(8,128)(2,1)S(1)}, u32[]{:S(2)}, u32[]{:S(2)}) collective-permute-start(bf16[264,1024]{1,0:T(8,128)(2,1)S(1)} %add_convert_fusion.3), channel_id=1, source_target_pairs={{2,4},{3,5},{4,2},{5,3},{10,12},{11,13},{12,10},{13,11},{18,20},{1... | collective-permute-start | bytes 1622024 | tf_op jit(solution)/shard_map/ppermute | solution.py:341

commit v10 on v9

--- a/solution.py
+++ b/solution.py
@@ -93,7 +93,8 @@
     da_out[...] = da
     db_out[...] = db
     if fused:
-        weight_sums(((xr_out, da_out), (xr_out, db_out), (q_out, h_out)), partial, *pieces)
+        pair = jnp.concatenate([da, db], axis=1)
+        weight_sums(xr_out, q_out, h_out, pair, partial, *pieces)
     dx = (dot(da, weights[0, 0], LAST) + dot(db, weights[0, 1], LAST)).astype(BF16)
     line = lax.broadcasted_iota(jnp.int32, (META, batch), 0)
     outs = (dxa_out, dxb_out)
@@ -172,7 +173,7 @@
     )(*operands)
 
 
-def weight_sums(products, partial, a_send, a_keep, b_send, b_keep):
+def weight_sums(xr, q, h, pair, partial, a_send, a_keep, b_send, b_keep):
     here = lax.axis_index("dp")
     width, hidden_width = partial.shape[1:]
     quarter = width // 4
@@ -185,8 +186,10 @@
     )
     for place, a_out, a_at, b_out, b_at in places:
         rows = pl.ds(pl.multiple_of((here ^ place) * quarter, quarter), quarter)
-        for product, (left, right) in enumerate(products):
-            value = (partial[product, rows, :] + dot(left[:, rows], right[...], FIRST)).astype(BF16)
+        joint = dot(xr[:, rows], pair, FIRST)
+        sums = (joint[:, :hidden_width], joint[:, hidden_width:], dot(q[:, rows], h[...], FIRST))
+        for product, term in enumerate(sums):
+            value = (partial[product, rows, :] + term).astype(BF16)
             a_out[a_at, product] = value[:, :half]
             b_out[b_at, product] = value[:, half:]
 
@@ -376,7 +379,7 @@
         far_sum = joined(grads)
         partial = sum_early(kept)
         third, fourth = after((third, fourth), first_sum[1], far_sum[1], partial)
-        last = add(fourth, third)
+        last = fourth + third
         sums, grads = compute((last, swap(last)), partial=partial)
         last_sum = joined(grads)
         sent = add(*last_sum)

time: 142 us -> 142 us (level)
  no operation moved by 1% of the time
where the time goes in v10:
time: 142 us; the launch traced here: 141 us
  waiting for transfers between devices  74.3 us (52%)
  starting transfers between devices  33.3 us (23%)
  Pallas kernels  26.7 us (19%)
  local copies, waits for them, and re-layouts  3.57 us (3%)
  other arithmetic  2.18 us (2%)
    ppermute x10, waiting for transfers between devices, move(): return lax.ppermute(value, 'expert', full)  48.9 us
    ppermute x10, starting transfers between devices, move(): return lax.ppermute(value, 'expert', full)  25.2 us
    ppermute x4, waiting for transfers between devices, across(): return lax.ppermute(value, 'dp', [(i, i ^ bit) for i in range(4)])  21 us
    pallas_call x4, Pallas kernels, run_slot(): pl.pallas_call(functools.partial(slot_kernel, choices, partial is not Non...  18.3 us
    ppermute x4, starting transfers between devices, across(): return lax.ppermute(value, 'dp', [(i, i ^ bit) for i in range(4)])  6.24 us
    ppermute x9, waiting for transfers between devices, swap(): return lax.ppermute(value, 'expert', [(i, i ^ 1) for i in range(devices)])  4.35 us
    pallas_call x1, Pallas kernels, run_partial(): pl.pallas_call(functools.partial(partial_kernel, len(lefts)), out_shape=j...  3.89 us
    unnamed x6, local copies, waits for them, and re-layouts  3.57 us
  transfers between devices with their start and end apart: 23, of which 10 were waited for; matrix products, arithmetic and copies ran while one was open for 1% of the time, Pallas kernels for 13%

profile of v10, /device:TPU:0, one launch (start us, length us, event | category | flops | bytes accessed | tf_op | source)
XLA Modules:
  0.0 140.8 jit_solution(11874470666672101699)
XLA Ops:
  0.6 2.2 %payload.1.refs_0_ = bf16[520,1024]{1,0:T(8,128)(2,1)} custom-call(bf16[256,1024]{1,0:T(8,128)(2,1)} %tokens.1, bf16[256,1024]{1,0:T(8,128)(2,1)} %cotangent.1, s32[2,256]{1,0:T(2,128)} %bitcast.13, bf16[2,256]{1,0:T(2,128)(2,1)} %bitcast.14), custom_call_target="tpu_custom_call" | custom-call | flops 1 | bytes 1 | tf_op jit(solution)/shard_map/payload/pallas_call | solution.py:259
  3.4 2.6 %collective-permute-start.4 = (bf16[520,1024]{1,0:T(8,128)(2,1)}, bf16[520,1024]{1,0:T(8,128)(2,1)S(1)}, u32[]{:S(2)}, u32[]{:S(2)}) collective-permute-start(bf16[520,1024]{1,0:T(8,128)(2,1)} %payload.1.refs_0_), channel_id=1, source_target_pairs={{0,2},{1,3},{2,0},{3,1},{4,6},{5,7},{6,4},{7,5},{8,10},{9,11},{10,... | collective-permute-start | bytes 3194888 | tf_op jit(solution)/shard_map/ppermute | solution.py:344
  6.1 0.7 collective-permute-start.3
  6.8 4.4 %collective-permute-start.2 = (bf16[520,1024]{1,0:T(8,128)(2,1)}, bf16[520,1024]{1,0:T(8,128)(2,1)S(1)}, u32[]{:S(2)}, u32[]{:S(2)}) collective-permute-start(bf16[520,1024]{1,0:T(8,128)(2,1)} %payload.1.refs_0_), channel_id=1, source_target_pairs={{0,6},{1,7},{6,0},{7,1},{8,14},{9,15},{14,8},{15,9},{16,22},{17,23... | collective-permute-start | bytes 3194888 | tf_op jit(solution)/shard_map/ppermute | solution.py:344
  11.2 2.3 %copy-done = bf16[1,3,1024,768]{3,2,1,0:T(8,128)(2,1)S(1)} copy-done((bf16[1,3,1024,768]{3,2,1,0:T(8,128)(2,1)S(1)}, bf16[1,3,1024,768]{3,2,1,0:T(8,128)(2,1)}, u32[]{:S(2)}) %copy-start) | copy-done | bytes 4718616
  13.5 1.2 copy-done.2
  14.8 4.1 %expert_block.4 = (bf16[256,1024]{1,0:T(8,128)(2,1)S(1)}, bf16[256,1024]{1,0:T(8,128)(2,1)S(1)}, bf16[256,768]{1,0:T(8,128)(2,1)S(1)}, bf16[256,768]{1,0:T(8,128...) custom-call(bf16[520,1024]{1,0:T(8,128)(2,1)S(1)} %copy-done.2, ...), custom_call_target="tpu_custom_call" | custom-call | flops 1 | bytes 1 | tf_op jit(solution)/shard_map/expert_block/pallas_call | solution.py:133
  19.0 11.4 %collective-permute-done.4.refs_0_ = bf16[520,1024]{1,0:T(8,128)(2,1)S(1)} collective-permute-done((bf16[520,1024]{1,0:T(8,128)(2,1)}, bf16[520,1024]{1,0:T(8,128)(2,1)S(1)}, u32[]{:S(2)}, u32[]{:S(2)}) %collective-permute-start.4) | collective-permute-done | bytes 1064992 | tf_op jit(solution)/shard_map/ppermute | solution.py:344
  30.4 25.1 %collective-permute-done.2.refs_2_ = bf16[520,1024]{1,0:T(8,128)(2,1)S(1)} collective-permute-done((bf16[520,1024]{1,0:T(8,128)(2,1)}, bf16[520,1024]{1,0:T(8,128)(2,1)S(1)}, u32[]{:S(2)}, u32[]{:S(2)}) %collective-permute-start.2) | collective-permute-done | bytes 1064992 | tf_op jit(solution)/shard_map/ppermute | solution.py:344
  56.0 1.3 collective-permute-start.5
  57.3 0.7 collective-permute-start.6
  58.2 1.5 %collective-permute-done.9.refs_1_ = bf16[520,1024]{1,0:T(8,128)(2,1)S(1)} collective-permute-done((bf16[520,1024]{1,0:T(8,128)(2,1)S(1)}, bf16[520,1024]{1,0:T(8,128)(2,1)S(1)}, u32[]{:S(2)}, u32[]{:S(2)}) %collective-permute-start.9) | collective-permute-done | bytes 1064992 | tf_op jit(solution)/shard_map/ppermute | solution.py:347
  59.7 4.6 %expert_block.6 = (bf16[256,1024]{1,0:T(8,128)(2,1)S(1)}, bf16[256,1024]{1,0:T(8,128)(2,1)S(1)}, bf16[256,768]{1,0:T(8,128)(2,1)S(1)}, bf16[256,768]{1,0:T(8,128...) custom-call(bf16[520,1024]{1,0:T(8,128)(2,1)S(1)} %collective-permute-done.3., ...), custom_call_target="tpu_custom_call" | custom-call | flops 1 | bytes 1 | tf_op jit(solution)/shard_map/expert_block/pallas_call | solution.py:133
  64.6 4.2 %expert_block.5 = (bf16[256,1024]{1,0:T(8,128)(2,1)S(1)}, bf16[256,1024]{1,0:T(8,128)(2,1)S(1)}, bf16[256,768]{1,0:T(8,128)(2,1)S(1)}, bf16[256,768]{1,0:T(8,128...) custom-call(bf16[520,1024]{1,0:T(8,128)(2,1)S(1)} %collective-permute-done.4., ...), custom_call_target="tpu_custom_call" | custom-call | flops 1 | bytes 1 | tf_op jit(solution)/shard_map/expert_block/pallas_call | solution.py:133
  69.2 3.9 %partial_weights.1.refs_3_ = f32[3,1024,768]{2,1,0:T(8,128)S(1)} custom-call(bf16[256,1024]{1,0:T(8,128)(2,1)S(1)} %get-tuple-element.52.refs_0_.refs_6_, bf16[256,1024]{1,0:T(8,128)(2,1)S(1)} %get-tuple-element.53.refs_1_.refs_7_, bf16[256,1024]{1,0:T(8,128)(2,1)S(1)} %get-tuple-element.54.refs_2_.refs_8_, bf16[256,768]{1,0:T(8,128)(2,1)S(1)} %get-tuple-element.55.refs_3_, ...), custom_call_target="tpu_custom_call" | custom-call | flops 1 | bytes 1 | tf_op jit(solution)/shard_map/partial_weights/pallas_call | solution.py:165
  73.0 10.9 %collective-permute-done.5 = bf16[520,1024]{1,0:T(8,128)(2,1)S(1)} collective-permute-done((bf16[520,1024]{1,0:T(8,128)(2,1)S(1)}, bf16[520,1024]{1,0:T(8,128)(2,1)S(1)}, u32[]{:S(2)}, u32[]{:S(2)}) %collective-permute-start.5) | collective-permute-done | bytes 1064992 | tf_op jit(solution)/shard_map/ppermute | solution.py:344
  84.4 2.7 %collective-permute-done.12.refs_1_ = bf16[520,1024]{1,0:T(8,128)(2,1)S(1)} collective-permute-done((bf16[520,1024]{1,0:T(8,128)(2,1)S(1)}, bf16[520,1024]{1,0:T(8,128)(2,1)S(1)}, u32[]{:S(2)}, u32[]{:S(2)}) %collective-permute-start.12) | collective-permute-done | bytes 1064992 | tf_op jit(solution)/shard_map/ppermute | solution.py:347
  87.1 5.3 %expert_block.7 = (bf16[2,3,256,384]{3,2,1,0:T(8,128)(2,1)S(1)}, bf16[2,3,256,384]{3,2,1,0:T(8,128)(2,1)S(1)}, bf16[2,3,256,384]{3,2,1,0:T(8,128)(2,1)S(1)}, bf1...) custom-call(bf16[520,1024]{1,0:T(8,128)(2,1)S(1)} %add.44.refs_0_, ...), custom_call_target="tpu_custom_call" | custom-call | flops 1 | bytes 1 | tf_op jit(solution)/shard_map/expert_block/pallas_call | solution.py:133
  92.4 1.6 %collective-permute-start.17 = (bf16[2,3,256,384]{3,2,1,0:T(8,128)(2,1)S(1)}, bf16[2,3,256,384]{3,2,1,0:T(8,128)(2,1)S(1)}, u32[]{:S(2)}, u32[]{:S(2)}) collective-permute-start(bf16[2,3,256,384]{3,2,1,0:T(8,128)(2,1)S(1)} %get-tuple-element.75), channel_id=1, source_target_pairs={{0,8},{8,0},{16,24},{24,16},{1,9},{9,1},{17,25},{25,17},{2,10},{10... | collective-permute-start | bytes 3538952 | tf_op jit(solution)/shard_map/ppermute | solution.py:331
  94.0 1.5 %collective-permute-start.18 = (bf16[2,3,256,384]{3,2,1,0:T(8,128)(2,1)S(1)}, bf16[2,3,256,384]{3,2,1,0:T(8,128)(2,1)S(1)}, u32[]{:S(2)}, u32[]{:S(2)}) collective-permute-start(bf16[2,3,256,384]{3,2,1,0:T(8,128)(2,1)S(1)} %get-tuple-element.77), channel_id=1, source_target_pairs={{0,16},{8,24},{16,0},{24,8},{1,17},{9,25},{17,1},{25,9},{2,18},{10... | collective-permute-start | bytes 3538952 | tf_op jit(solution)/shard_map/ppermute | solution.py:331
  95.7 4.5 %collective-permute-start.16 = (bf16[264,1024]{1,0:T(8,128)(2,1)S(1)}, bf16[264,1024]{1,0:T(8,128)(2,1)S(1)}, u32[]{:S(2)}, u32[]{:S(2)}) collective-permute-start(bf16[264,1024]{1,0:T(8,128)(2,1)S(1)} %fusion), channel_id=1, source_target_pairs={{0,6},{1,7},{6,0},{7,1},{8,14},{9,15},{14,8},{15,9},{16,22},{17,23... | collective-permute-start | bytes 1622024 | tf_op jit(solution)/shard_map/ppermute | solution.py:344
  100.5 0.7 collective-permute-start.15
  101.2 5.8 %collective-permute-start.14 = (bf16[264,1024]{1,0:T(8,128)(2,1)S(1)}, bf16[264,1024]{1,0:T(8,128)(2,1)S(1)}, u32[]{:S(2)}, u32[]{:S(2)}) collective-permute-start(bf16[264,1024]{1,0:T(8,128)(2,1)S(1)} %add_convert_fusion.5), channel_id=1, source_target_pairs={{0,2},{1,3},{6,4},{7,5},{8,10},{9,11},{14,12},{15,13},{16,18},{17,... | collective-permute-start | bytes 1622024 | tf_op jit(solution)/shard_map/ppermute | solution.py:344
  107.0 13.5 %collective-permute-done.17 = bf16[2,3,256,384]{3,2,1,0:T(8,128)(2,1)S(1)} collective-permute-done((bf16[2,3,256,384]{3,2,1,0:T(8,128)(2,1)S(1)}, bf16[2,3,256,384]{3,2,1,0:T(8,128)(2,1)S(1)}, u32[]{:S(2)}, u32[]{:S(2)}) %collective-permute-start.17) | collective-permute-done | bytes 1179680 | tf_op jit(solution)/shard_map/ppermute | solution.py:331
  120.8 1.6 %collective-permute-start.21 = (bf16[3,256,384]{2,1,0:T(8,128)(2,1)S(1)}, bf16[3,256,384]{2,1,0:T(8,128)(2,1)S(1)}, u32[]{:S(2)}, u32[]{:S(2)}) collective-permute-start(bf16[3,256,384]{2,1,0:T(8,128)(2,1)S(1)} %get-tuple-element.90), channel_id=1, source_target_pairs={{0,16},{8,24},{16,0},{24,8},{1,17},{9,25},{17,1},{25,9},{2,18},{10... | collective-permute-start | bytes 1769480 | tf_op jit(solution)/shard_map/ppermute | solution.py:331
  122.7 1.6 %collective-permute-start.22 = (bf16[3,256,384]{2,1,0:T(8,128)(2,1)S(1)}, bf16[3,256,384]{2,1,0:T(8,128)(2,1)S(1)}, u32[]{:S(2)}, u32[]{:S(2)}) collective-permute-start(bf16[3,256,384]{2,1,0:T(8,128)(2,1)S(1)} %get-tuple-element.88), channel_id=1, source_target_pairs={{0,8},{8,0},{16,24},{24,16},{1,9},{9,1},{17,25},{25,17},{2,10},{10... | collective-permute-start | bytes 1769480 | tf_op jit(solution)/shard_map/ppermute | solution.py:331
  124.8 3.8 %collective-permute-start.19 = (bf16[264,1024]{1,0:T(8,128)(2,1)S(1)}, bf16[264,1024]{1,0:T(8,128)(2,1)S(1)}, u32[]{:S(2)}, u32[]{:S(2)}) collective-permute-start(bf16[264,1024]{1,0:T(8,128)(2,1)S(1)} %add_convert_fusion.3), channel_id=1, source_target_pairs={{0,2},{1,3},{2,0},{3,1},{4,6},{5,7},{6,4},{7,5},{8,10},{9,11},{10,... | collective-permute-start | bytes 1622024 | tf_op jit(solution)/shard_map/ppermute | solution.py:344
  129.6 5.8 %collective-permute-done.21.a_last = bf16[3,256,384]{2,1,0:T(8,128)(2,1)S(1)} collective-permute-done((bf16[3,256,384]{2,1,0:T(8,128)(2,1)S(1)}, bf16[3,256,384]{2,1,0:T(8,128)(2,1)S(1)}, u32[]{:S(2)}, u32[]{:S(2)}) %collective-permute-start.21) | collective-permute-done | bytes 589856 | tf_op jit(solution)/shard_map/ppermute | solution.py:331
  135.4 1.6 %collective-permute-done.22.b_last = bf16[3,256,384]{2,1,0:T(8,128)(2,1)S(1)} collective-permute-done((bf16[3,256,384]{2,1,0:T(8,128)(2,1)S(1)}, bf16[3,256,384]{2,1,0:T(8,128)(2,1)S(1)}, u32[]{:S(2)}, u32[]{:S(2)}) %collective-permute-start.22) | collective-permute-done | bytes 589856 | tf_op jit(solution)/shard_map/ppermute | solution.py:331
  137.0 1.3 final_step.1
  138.3 1.5 %collective-permute-done.19.refs_1_ = bf16[264,1024]{1,0:T(8,128)(2,1)S(1)} collective-permute-done((bf16[264,1024]{1,0:T(8,128)(2,1)S(1)}, bf16[264,1024]{1,0:T(8,128)(2,1)S(1)}, u32[]{:S(2)}, u32[]{:S(2)}) %collective-permute-start.19) | collective-permute-done | bytes 540704 | tf_op jit(solution)/shard_map/ppermute | solution.py:344
  139.8 1.0 total.1
  (36 shorter events, 4.9 us)
Async XLA Ops:
  2.9 8.3 %collective-permute-start = (bf16[520,1024]{1,0:T(8,128)(2,1)}, bf16[520,1024]{1,0:T(8,128)(2,1)S(1)}, u32[]{:S(2)}, u32[]{:S(2)}) collective-permute-start(bf16[520,1024]{1,0:T(8,128)(2,1)} %payload.1.refs_0_), channel_id=1, source_target_pairs={{0,1},{1,0},{2,3},{3,2},{4,5},{5,4},{6,7},{7,6},{8,9},{9,8},{10,11... | collective-permute-start | bytes 3194888 | tf_op jit(solution)/shard_map/ppermute | solution.py:347
  3.4 27.0 %collective-permute-start.4 = (bf16[520,1024]{1,0:T(8,128)(2,1)}, bf16[520,1024]{1,0:T(8,128)(2,1)S(1)}, u32[]{:S(2)}, u32[]{:S(2)}) collective-permute-start(bf16[520,1024]{1,0:T(8,128)(2,1)} %payload.1.refs_0_), channel_id=1, source_target_pairs={{0,2},{1,3},{2,0},{3,1},{4,6},{5,7},{6,4},{7,5},{8,10},{9,11},{10,... | collective-permute-start | bytes 3194888 | tf_op jit(solution)/shard_map/ppermute | solution.py:344
  6.1 24.3 %collective-permute-start.3 = (bf16[520,1024]{1,0:T(8,128)(2,1)}, bf16[520,1024]{1,0:T(8,128)(2,1)S(1)}, u32[]{:S(2)}, u32[]{:S(2)}) collective-permute-start(bf16[520,1024]{1,0:T(8,128)(2,1)} %payload.1.refs_0_), channel_id=1, source_target_pairs={{2,4},{3,5},{4,2},{5,3},{10,12},{11,13},{12,10},{13,11},{18,20},{1... | collective-permute-start | bytes 3194888 | tf_op jit(solution)/shard_map/ppermute | solution.py:344
  6.8 48.7 %collective-permute-start.2 = (bf16[520,1024]{1,0:T(8,128)(2,1)}, bf16[520,1024]{1,0:T(8,128)(2,1)S(1)}, u32[]{:S(2)}, u32[]{:S(2)}) collective-permute-start(bf16[520,1024]{1,0:T(8,128)(2,1)} %payload.1.refs_0_), channel_id=1, source_target_pairs={{0,6},{1,7},{6,0},{7,1},{8,14},{9,15},{14,8},{15,9},{16,22},{17,23... | collective-permute-start | bytes 3194888 | tf_op jit(solution)/shard_map/ppermute | solution.py:344
  11.2 2.3 %copy-start = (bf16[1,3,1024,768]{3,2,1,0:T(8,128)(2,1)S(1)}, bf16[1,3,1024,768]{3,2,1,0:T(8,128)(2,1)}, u32[]{:S(2)}) copy-start(bf16[1,3,1024,768]{3,2,1,0:T(8,128)(2,1)} %refs_2_.5) | copy-start | bytes 14155780
  13.5 1.2 copy-start.2
  14.8 45.0 %copy-start.1 = (bf16[1,3,1024,768]{3,2,1,0:T(8,128)(2,1)S(1)}, bf16[1,3,1024,768]{3,2,1,0:T(8,128)(2,1)}, u32[]{:S(2)}) copy-start(bf16[1,3,1024,768]{3,2,1,0:T(8,128)(2,1)} %refs_2_.5) | copy-start | bytes 14155780
  18.9 36.6 %collective-permute-start.1 = (bf16[264,1024]{1,0:T(8,128)(2,1)S(1)}, bf16[264,1024]{1,0:T(8,128)(2,1)S(1)}, u32[]{:S(2)}, u32[]{:S(2)}) collective-permute-start(bf16[264,1024]{1,0:T(8,128)(2,1)S(1)} %get-tuple-element.46), channel_id=1, source_target_pairs={{0,1},{1,0},{2,3},{3,2},{4,5},{5,4},{6,7},{7,6},{8,9},{9,8},{10,11... | collective-permute-start | bytes 1622024 | tf_op jit(solution)/shard_map/ppermute | solution.py:347
  55.5 2.7 %collective-permute-start.10 = (bf16[520,1024]{1,0:T(8,128)(2,1)S(1)}, bf16[520,1024]{1,0:T(8,128)(2,1)S(1)}, u32[]{:S(2)}, u32[]{:S(2)}) collective-permute-start(bf16[520,1024]{1,0:T(8,128)(2,1)S(1)} %collective-permute-done.2.refs_2_), channel_id=1, source_target_pairs={{0,1},{1,0},{2,3},{3,2},{4,5},{5,4},{6,7},{7,6},{8,9},{9,8},{10,11... | collective-permute-start | bytes 3194888 | tf_op jit(solution)/shard_map/ppermute | solution.py:347
  55.5 4.2 %collective-permute-start.9 = (bf16[520,1024]{1,0:T(8,128)(2,1)S(1)}, bf16[520,1024]{1,0:T(8,128)(2,1)S(1)}, u32[]{:S(2)}, u32[]{:S(2)}) collective-permute-start(bf16[520,1024]{1,0:T(8,128)(2,1)S(1)} %collective-permute-done.3.refs_0_), channel_id=1, source_target_pairs={{0,1},{1,0},{2,3},{3,2},{4,5},{5,4},{6,7},{7,6},{8,9},{9,8},{10,11... | collective-permute-start | bytes 3194888 | tf_op jit(solution)/shard_map/ppermute | solution.py:347
  56.0 8.5 %collective-permute-start.7 = (bf16[520,1024]{1,0:T(8,128)(2,1)S(1)}, bf16[520,1024]{1,0:T(8,128)(2,1)S(1)}, u32[]{:S(2)}, u32[]{:S(2)}) collective-permute-start(bf16[520,1024]{1,0:T(8,128)(2,1)S(1)} %collective-permute-done.4.refs_0_), channel_id=1, source_target_pairs={{0,1},{1,0},{2,3},{3,2},{4,5},{5,4},{6,7},{7,6},{8,9},{9,8},{10,11... | collective-permute-start | bytes 3194888 | tf_op jit(solution)/shard_map/ppermute | solution.py:347
  56.0 27.9 %collective-permute-start.5 = (bf16[520,1024]{1,0:T(8,128)(2,1)S(1)}, bf16[520,1024]{1,0:T(8,128)(2,1)S(1)}, u32[]{:S(2)}, u32[]{:S(2)}) collective-permute-start(bf16[520,1024]{1,0:T(8,128)(2,1)S(1)} %collective-permute-done.3.refs_0_), channel_id=1, source_target_pairs={{2,0},{3,1},{4,6},{5,7},{10,8},{11,9},{12,14},{13,15},{18,16},{19,... | collective-permute-start | bytes 3194888 | tf_op jit(solution)/shard_map/ppermute | solution.py:344
  57.3 26.6 %collective-permute-start.6 = (bf16[520,1024]{1,0:T(8,128)(2,1)S(1)}, bf16[520,1024]{1,0:T(8,128)(2,1)S(1)}, u32[]{:S(2)}, u32[]{:S(2)}) collective-permute-start(bf16[520,1024]{1,0:T(8,128)(2,1)S(1)} %collective-permute-done.4.refs_0_), channel_id=1, source_target_pairs={{2,4},{3,5},{4,2},{5,3},{10,12},{11,13},{12,10},{13,11},{18,20},{1... | collective-permute-start | bytes 3194888 | tf_op jit(solution)/shard_map/ppermute | solution.py:344
  64.4 19.6 %collective-permute-start.11 = (bf16[264,1024]{1,0:T(8,128)(2,1)S(1)}, bf16[264,1024]{1,0:T(8,128)(2,1)S(1)}, u32[]{:S(2)}, u32[]{:S(2)}) collective-permute-start(bf16[264,1024]{1,0:T(8,128)(2,1)S(1)} %get-tuple-element.51), channel_id=1, source_target_pairs={{0,1},{1,0},{2,3},{3,2},{4,5},{5,4},{6,7},{7,6},{8,9},{9,8},{10,11... | collective-permute-start | bytes 1622024 | tf_op jit(solution)/shard_map/ppermute | solution.py:347
  68.7 15.2 %collective-permute-start.8 = (bf16[264,1024]{1,0:T(8,128)(2,1)S(1)}, bf16[264,1024]{1,0:T(8,128)(2,1)S(1)}, u32[]{:S(2)}, u32[]{:S(2)}) collective-permute-start(bf16[264,1024]{1,0:T(8,128)(2,1)S(1)} %get-tuple-element.49), channel_id=1, source_target_pairs={{0,1},{1,0},{2,3},{3,2},{4,5},{5,4},{6,7},{7,6},{8,9},{9,8},{10,11... | collective-permute-start | bytes 1622024 | tf_op jit(solution)/shard_map/ppermute | solution.py:347
  84.4 2.7 %collective-permute-start.12 = (bf16[520,1024]{1,0:T(8,128)(2,1)S(1)}, bf16[520,1024]{1,0:T(8,128)(2,1)S(1)}, u32[]{:S(2)}, u32[]{:S(2)}) collective-permute-start(bf16[520,1024]{1,0:T(8,128)(2,1)S(1)} %add.44.refs_0_), channel_id=1, source_target_pairs={{0,1},{1,0},{2,3},{3,2},{4,5},{5,4},{6,7},{7,6},{8,9},{9,8},{10,11... | collective-permute-start | bytes 3194888 | tf_op jit(solution)/shard_map/ppermute | solution.py:347
  92.4 28.1 %collective-permute-start.17 = (bf16[2,3,256,384]{3,2,1,0:T(8,128)(2,1)S(1)}, bf16[2,3,256,384]{3,2,1,0:T(8,128)(2,1)S(1)}, u32[]{:S(2)}, u32[]{:S(2)}) collective-permute-start(bf16[2,3,256,384]{3,2,1,0:T(8,128)(2,1)S(1)} %get-tuple-element.75), channel_id=1, source_target_pairs={{0,8},{8,0},{16,24},{24,16},{1,9},{9,1},{17,25},{25,17},{2,10},{10... | collective-permute-start | bytes 3538952 | tf_op jit(solution)/shard_map/ppermute | solution.py:331
  94.0 28.4 %collective-permute-start.18 = (bf16[2,3,256,384]{3,2,1,0:T(8,128)(2,1)S(1)}, bf16[2,3,256,384]{3,2,1,0:T(8,128)(2,1)S(1)}, u32[]{:S(2)}, u32[]{:S(2)}) collective-permute-start(bf16[2,3,256,384]{3,2,1,0:T(8,128)(2,1)S(1)} %get-tuple-element.77), channel_id=1, source_target_pairs={{0,16},{8,24},{16,0},{24,8},{1,17},{9,25},{17,1},{25,9},{2,18},{10... | collective-permute-start | bytes 3538952 | tf_op jit(solution)/shard_map/ppermute | solution.py:331
  95.5 4.8 %collective-permute-start.13 = (bf16[264,1024]{1,0:T(8,128)(2,1)S(1)}, bf16[264,1024]{1,0:T(8,128)(2,1)S(1)}, u32[]{:S(2)}, u32[]{:S(2)}) collective-permute-start(bf16[264,1024]{1,0:T(8,128)(2,1)S(1)} %get-tuple-element.70), channel_id=1, source_target_pairs={{0,1},{1,0},{2,3},{3,2},{4,5},{5,4},{6,7},{7,6},{8,9},{9,8},{10,11... | collective-permute-start | bytes 1622024 | tf_op jit(solution)/shard_map/ppermute | solution.py:347
  95.7 28.5 %collective-permute-start.16 = (bf16[264,1024]{1,0:T(8,128)(2,1)S(1)}, bf16[264,1024]{1,0:T(8,128)(2,1)S(1)}, u32[]{:S(2)}, u32[]{:S(2)}) collective-permute-start(bf16[264,1024]{1,0:T(8,128)(2,1)S(1)} %fusion), channel_id=1, source_target_pairs={{0,6},{1,7},{6,0},{7,1},{8,14},{9,15},{14,8},{15,9},{16,22},{17,23... | collective-permute-start | bytes 1622024 | tf_op jit(solution)/shard_map/ppermute | solution.py:344
  100.5 23.8 %collective-permute-start.15 = (bf16[264,1024]{1,0:T(8,128)(2,1)S(1)}, bf16[264,1024]{1,0:T(8,128)(2,1)S(1)}, u32[]{:S(2)}, u32[]{:S(2)}) collective-permute-start(bf16[264,1024]{1,0:T(8,128)(2,1)S(1)} %add_convert_fusion.5), channel_id=1, source_target_pairs={{2,4},{3,5},{4,2},{5,3},{10,12},{11,13},{12,10},{13,11},{18,20},{1... | collective-permute-start | bytes 1622024 | tf_op jit(solution)/shard_map/ppermute | solution.py:344
  101.2 23.1 %collective-permute-start.14 = (bf16[264,1024]{1,0:T(8,128)(2,1)S(1)}, bf16[264,1024]{1,0:T(8,128)(2,1)S(1)}, u32[]{:S(2)}, u32[]{:S(2)}) collective-permute-start(bf16[264,1024]{1,0:T(8,128)(2,1)S(1)} %add_convert_fusion.5), channel_id=1, source_target_pairs={{0,2},{1,3},{6,4},{7,5},{8,10},{9,11},{14,12},{15,13},{16,18},{17,... | collective-permute-start | bytes 1622024 | tf_op jit(solution)/shard_map/ppermute | solution.py:344
  120.8 14.6 %collective-permute-start.21 = (bf16[3,256,384]{2,1,0:T(8,128)(2,1)S(1)}, bf16[3,256,384]{2,1,0:T(8,128)(2,1)S(1)}, u32[]{:S(2)}, u32[]{:S(2)}) collective-permute-start(bf16[3,256,384]{2,1,0:T(8,128)(2,1)S(1)} %get-tuple-element.90), channel_id=1, source_target_pairs={{0,16},{8,24},{16,0},{24,8},{1,17},{9,25},{17,1},{25,9},{2,18},{10... | collective-permute-start | bytes 1769480 | tf_op jit(solution)/shard_map/ppermute | solution.py:331
  122.7 14.3 %collective-permute-start.22 = (bf16[3,256,384]{2,1,0:T(8,128)(2,1)S(1)}, bf16[3,256,384]{2,1,0:T(8,128)(2,1)S(1)}, u32[]{:S(2)}, u32[]{:S(2)}) collective-permute-start(bf16[3,256,384]{2,1,0:T(8,128)(2,1)S(1)} %get-tuple-element.88), channel_id=1, source_target_pairs={{0,8},{8,0},{16,24},{24,16},{1,9},{9,1},{17,25},{25,17},{2,10},{10... | collective-permute-start | bytes 1769480 | tf_op jit(solution)/shard_map/ppermute | solution.py:331
  124.8 15.0 %collective-permute-start.19 = (bf16[264,1024]{1,0:T(8,128)(2,1)S(1)}, bf16[264,1024]{1,0:T(8,128)(2,1)S(1)}, u32[]{:S(2)}, u32[]{:S(2)}) collective-permute-start(bf16[264,1024]{1,0:T(8,128)(2,1)S(1)} %add_convert_fusion.3), channel_id=1, source_target_pairs={{0,2},{1,3},{2,0},{3,1},{4,6},{5,7},{6,4},{7,5},{8,10},{9,11},{10,... | collective-permute-start | bytes 1622024 | tf_op jit(solution)/shard_map/ppermute | solution.py:344
  128.6 11.2 %collective-permute-start.20 = (bf16[264,1024]{1,0:T(8,128)(2,1)S(1)}, bf16[264,1024]{1,0:T(8,128)(2,1)S(1)}, u32[]{:S(2)}, u32[]{:S(2)}) collective-permute-start(bf16[264,1024]{1,0:T(8,128)(2,1)S(1)} %add_convert_fusion.2), channel_id=1, source_target_pairs={{2,4},{3,5},{4,2},{5,3},{10,12},{11,13},{12,10},{13,11},{18,20},{1... | collective-permute-start | bytes 1622024 | tf_op jit(solution)/shard_map/ppermute | solution.py:344

commit v11 on v9

--- a/solution.py
+++ b/solution.py
@@ -229,7 +229,7 @@
         pltpu.make_async_copy(cotangent, held.at[count : 2 * count], sems.at[3]),
     ]
     outward = pltpu.make_async_copy(held, out, sems.at[4])
-    for copy in small + large:
+    for copy in large + small:
         copy.start()
     for copy in small:
         copy.wait()

time: 142 us -> 142 us (level)
  no operation moved by 1% of the time
where the time goes in v11:
time: 142 us; the launch traced here: 141 us
  waiting for transfers between devices  74.2 us (52%)
  starting transfers between devices  33.3 us (23%)
  Pallas kernels  26.7 us (19%)
  local copies, waits for them, and re-layouts  3.57 us (3%)
  other arithmetic  2.18 us (2%)
    ppermute x10, waiting for transfers between devices, move(): return lax.ppermute(value, 'expert', full)  48.9 us
    ppermute x10, starting transfers between devices, move(): return lax.ppermute(value, 'expert', full)  25.2 us
    ppermute x4, waiting for transfers between devices, across(): return lax.ppermute(value, 'dp', [(i, i ^ bit) for i in range(4)])  21 us
    pallas_call x4, Pallas kernels, run_slot(): pl.pallas_call(functools.partial(slot_kernel, choices, partial is not Non...  18.3 us
    ppermute x4, starting transfers between devices, across(): return lax.ppermute(value, 'dp', [(i, i ^ bit) for i in range(4)])  6.22 us
    ppermute x9, waiting for transfers between devices, swap(): return lax.ppermute(value, 'expert', [(i, i ^ 1) for i in range(devices)])  4.35 us
    pallas_call x1, Pallas kernels, run_partial(): pl.pallas_call(functools.partial(partial_kernel, len(lefts)), out_shape=j...  3.9 us
    unnamed x6, local copies, waits for them, and re-layouts  3.57 us
  transfers between devices with their start and end apart: 23, of which 10 were waited for; matrix products, arithmetic and copies ran while one was open for 1% of the time, Pallas kernels for 13%

profile of v11, /device:TPU:0, one launch (start us, length us, event | category | flops | bytes accessed | tf_op | source)
XLA Modules:
  0.0 140.8 jit_solution(10103660370228628513)
XLA Ops:
  0.6 2.2 %payload.1.refs_0_ = bf16[520,1024]{1,0:T(8,128)(2,1)} custom-call(bf16[256,1024]{1,0:T(8,128)(2,1)} %tokens.1, bf16[256,1024]{1,0:T(8,128)(2,1)} %cotangent.1, s32[2,256]{1,0:T(2,128)} %bitcast.13, bf16[2,256]{1,0:T(2,128)(2,1)} %bitcast.14), custom_call_target="tpu_custom_call" | custom-call | flops 1 | bytes 1 | tf_op jit(solution)/shard_map/payload/pallas_call | solution.py:256
  3.4 2.6 %collective-permute-start.4 = (bf16[520,1024]{1,0:T(8,128)(2,1)}, bf16[520,1024]{1,0:T(8,128)(2,1)S(1)}, u32[]{:S(2)}, u32[]{:S(2)}) collective-permute-start(bf16[520,1024]{1,0:T(8,128)(2,1)} %payload.1.refs_0_), channel_id=1, source_target_pairs={{0,2},{1,3},{2,0},{3,1},{4,6},{5,7},{6,4},{7,5},{8,10},{9,11},{10,... | collective-permute-start | bytes 3194888 | tf_op jit(solution)/shard_map/ppermute | solution.py:341
  6.0 0.7 collective-permute-start.3
  6.7 4.4 %collective-permute-start.2 = (bf16[520,1024]{1,0:T(8,128)(2,1)}, bf16[520,1024]{1,0:T(8,128)(2,1)S(1)}, u32[]{:S(2)}, u32[]{:S(2)}) collective-permute-start(bf16[520,1024]{1,0:T(8,128)(2,1)} %payload.1.refs_0_), channel_id=1, source_target_pairs={{0,6},{1,7},{6,0},{7,1},{8,14},{9,15},{14,8},{15,9},{16,22},{17,23... | collective-permute-start | bytes 3194888 | tf_op jit(solution)/shard_map/ppermute | solution.py:341
  11.2 2.3 %copy-done = bf16[1,3,1024,768]{3,2,1,0:T(8,128)(2,1)S(1)} copy-done((bf16[1,3,1024,768]{3,2,1,0:T(8,128)(2,1)S(1)}, bf16[1,3,1024,768]{3,2,1,0:T(8,128)(2,1)}, u32[]{:S(2)}) %copy-start) | copy-done | bytes 4718616
  13.5 1.2 copy-done.2
  14.7 4.2 %expert_block.4 = (bf16[256,1024]{1,0:T(8,128)(2,1)S(1)}, bf16[256,1024]{1,0:T(8,128)(2,1)S(1)}, bf16[256,768]{1,0:T(8,128)(2,1)S(1)}, bf16[256,768]{1,0:T(8,128...) custom-call(bf16[520,1024]{1,0:T(8,128)(2,1)S(1)} %copy-done.2, ...), custom_call_target="tpu_custom_call" | custom-call | flops 1 | bytes 1 | tf_op jit(solution)/shard_map/expert_block/pallas_call | solution.py:132
  19.0 11.4 %collective-permute-done.4.refs_0_ = bf16[520,1024]{1,0:T(8,128)(2,1)S(1)} collective-permute-done((bf16[520,1024]{1,0:T(8,128)(2,1)}, bf16[520,1024]{1,0:T(8,128)(2,1)S(1)}, u32[]{:S(2)}, u32[]{:S(2)}) %collective-permute-start.4) | collective-permute-done | bytes 1064992 | tf_op jit(solution)/shard_map/ppermute | solution.py:341
  30.3 25.1 %collective-permute-done.2.refs_2_ = bf16[520,1024]{1,0:T(8,128)(2,1)S(1)} collective-permute-done((bf16[520,1024]{1,0:T(8,128)(2,1)}, bf16[520,1024]{1,0:T(8,128)(2,1)S(1)}, u32[]{:S(2)}, u32[]{:S(2)}) %collective-permute-start.2) | collective-permute-done | bytes 1064992 | tf_op jit(solution)/shard_map/ppermute | solution.py:341
  56.0 1.3 collective-permute-start.5
  57.3 0.7 collective-permute-start.6
  58.2 1.5 %collective-permute-done.9.refs_1_ = bf16[520,1024]{1,0:T(8,128)(2,1)S(1)} collective-permute-done((bf16[520,1024]{1,0:T(8,128)(2,1)S(1)}, bf16[520,1024]{1,0:T(8,128)(2,1)S(1)}, u32[]{:S(2)}, u32[]{:S(2)}) %collective-permute-start.9) | collective-permute-done | bytes 1064992 | tf_op jit(solution)/shard_map/ppermute | solution.py:344
  59.7 4.6 %expert_block.6 = (bf16[256,1024]{1,0:T(8,128)(2,1)S(1)}, bf16[256,1024]{1,0:T(8,128)(2,1)S(1)}, bf16[256,768]{1,0:T(8,128)(2,1)S(1)}, bf16[256,768]{1,0:T(8,128...) custom-call(bf16[520,1024]{1,0:T(8,128)(2,1)S(1)} %collective-permute-done.3., ...), custom_call_target="tpu_custom_call" | custom-call | flops 1 | bytes 1 | tf_op jit(solution)/shard_map/expert_block/pallas_call | solution.py:132
  64.5 4.1 %expert_block.5 = (bf16[256,1024]{1,0:T(8,128)(2,1)S(1)}, bf16[256,1024]{1,0:T(8,128)(2,1)S(1)}, bf16[256,768]{1,0:T(8,128)(2,1)S(1)}, bf16[256,768]{1,0:T(8,128...) custom-call(bf16[520,1024]{1,0:T(8,128)(2,1)S(1)} %collective-permute-done.4., ...), custom_call_target="tpu_custom_call" | custom-call | flops 1 | bytes 1 | tf_op jit(solution)/shard_map/expert_block/pallas_call | solution.py:132
  69.1 3.9 %partial_weights.1.refs_3_ = f32[3,1024,768]{2,1,0:T(8,128)S(1)} custom-call(bf16[256,1024]{1,0:T(8,128)(2,1)S(1)} %get-tuple-element.52.refs_0_.refs_6_, bf16[256,1024]{1,0:T(8,128)(2,1)S(1)} %get-tuple-element.53.refs_1_.refs_7_, bf16[256,1024]{1,0:T(8,128)(2,1)S(1)} %get-tuple-element.54.refs_2_.refs_8_, bf16[256,768]{1,0:T(8,128)(2,1)S(1)} %get-tuple-element.55.refs_3_, ...), custom_call_target="tpu_custom_call" | custom-call | flops 1 | bytes 1 | tf_op jit(solution)/shard_map/partial_weights/pallas_call | solution.py:164
  73.0 10.9 %collective-permute-done.5 = bf16[520,1024]{1,0:T(8,128)(2,1)S(1)} collective-permute-done((bf16[520,1024]{1,0:T(8,128)(2,1)S(1)}, bf16[520,1024]{1,0:T(8,128)(2,1)S(1)}, u32[]{:S(2)}, u32[]{:S(2)}) %collective-permute-start.5) | collective-permute-done | bytes 1064992 | tf_op jit(solution)/shard_map/ppermute | solution.py:341
  84.4 2.7 %collective-permute-done.12.refs_1_ = bf16[520,1024]{1,0:T(8,128)(2,1)S(1)} collective-permute-done((bf16[520,1024]{1,0:T(8,128)(2,1)S(1)}, bf16[520,1024]{1,0:T(8,128)(2,1)S(1)}, u32[]{:S(2)}, u32[]{:S(2)}) %collective-permute-start.12) | collective-permute-done | bytes 1064992 | tf_op jit(solution)/shard_map/ppermute | solution.py:344
  87.1 5.3 %expert_block.7 = (bf16[2,3,256,384]{3,2,1,0:T(8,128)(2,1)S(1)}, bf16[2,3,256,384]{3,2,1,0:T(8,128)(2,1)S(1)}, bf16[2,3,256,384]{3,2,1,0:T(8,128)(2,1)S(1)}, bf1...) custom-call(bf16[520,1024]{1,0:T(8,128)(2,1)S(1)} %add_convert_fusion.refs_0_, ...), custom_call_target="tpu_custom_call" | custom-call | flops 1 | bytes 1 | tf_op jit(solution)/shard_map/expert_block/pallas_call | solution.py:132
  92.4 1.6 %collective-permute-start.17 = (bf16[2,3,256,384]{3,2,1,0:T(8,128)(2,1)S(1)}, bf16[2,3,256,384]{3,2,1,0:T(8,128)(2,1)S(1)}, u32[]{:S(2)}, u32[]{:S(2)}) collective-permute-start(bf16[2,3,256,384]{3,2,1,0:T(8,128)(2,1)S(1)} %get-tuple-element.75), channel_id=1, source_target_pairs={{0,8},{8,0},{16,24},{24,16},{1,9},{9,1},{17,25},{25,17},{2,10},{10... | collective-permute-start | bytes 3538952 | tf_op jit(solution)/shard_map/ppermute | solution.py:328
  94.0 1.5 %collective-permute-start.18 = (bf16[2,3,256,384]{3,2,1,0:T(8,128)(2,1)S(1)}, bf16[2,3,256,384]{3,2,1,0:T(8,128)(2,1)S(1)}, u32[]{:S(2)}, u32[]{:S(2)}) collective-permute-start(bf16[2,3,256,384]{3,2,1,0:T(8,128)(2,1)S(1)} %get-tuple-element.77), channel_id=1, source_target_pairs={{0,16},{8,24},{16,0},{24,8},{1,17},{9,25},{17,1},{25,9},{2,18},{10... | collective-permute-start | bytes 3538952 | tf_op jit(solution)/shard_map/ppermute | solution.py:328
  95.7 4.5 %collective-permute-start.16 = (bf16[264,1024]{1,0:T(8,128)(2,1)S(1)}, bf16[264,1024]{1,0:T(8,128)(2,1)S(1)}, u32[]{:S(2)}, u32[]{:S(2)}) collective-permute-start(bf16[264,1024]{1,0:T(8,128)(2,1)S(1)} %fusion), channel_id=1, source_target_pairs={{0,6},{1,7},{6,0},{7,1},{8,14},{9,15},{14,8},{15,9},{16,22},{17,23... | collective-permute-start | bytes 1622024 | tf_op jit(solution)/shard_map/ppermute | solution.py:341
  100.5 0.7 collective-permute-start.15
  101.2 5.8 %collective-permute-start.14 = (bf16[264,1024]{1,0:T(8,128)(2,1)S(1)}, bf16[264,1024]{1,0:T(8,128)(2,1)S(1)}, u32[]{:S(2)}, u32[]{:S(2)}) collective-permute-start(bf16[264,1024]{1,0:T(8,128)(2,1)S(1)} %add_convert_fusion.6), channel_id=1, source_target_pairs={{0,2},{1,3},{6,4},{7,5},{8,10},{9,11},{14,12},{15,13},{16,18},{17,... | collective-permute-start | bytes 1622024 | tf_op jit(solution)/shard_map/ppermute | solution.py:341
  107.0 13.6 %collective-permute-done.17 = bf16[2,3,256,384]{3,2,1,0:T(8,128)(2,1)S(1)} collective-permute-done((bf16[2,3,256,384]{3,2,1,0:T(8,128)(2,1)S(1)}, bf16[2,3,256,384]{3,2,1,0:T(8,128)(2,1)S(1)}, u32[]{:S(2)}, u32[]{:S(2)}) %collective-permute-start.17) | collective-permute-done | bytes 1179680 | tf_op jit(solution)/shard_map/ppermute | solution.py:328
  120.8 1.6 %collective-permute-start.21 = (bf16[3,256,384]{2,1,0:T(8,128)(2,1)S(1)}, bf16[3,256,384]{2,1,0:T(8,128)(2,1)S(1)}, u32[]{:S(2)}, u32[]{:S(2)}) collective-permute-start(bf16[3,256,384]{2,1,0:T(8,128)(2,1)S(1)} %get-tuple-element.90), channel_id=1, source_target_pairs={{0,16},{8,24},{16,0},{24,8},{1,17},{9,25},{17,1},{25,9},{2,18},{10... | collective-permute-start | bytes 1769480 | tf_op jit(solution)/shard_map/ppermute | solution.py:328
  122.7 1.6 %collective-permute-start.22 = (bf16[3,256,384]{2,1,0:T(8,128)(2,1)S(1)}, bf16[3,256,384]{2,1,0:T(8,128)(2,1)S(1)}, u32[]{:S(2)}, u32[]{:S(2)}) collective-permute-start(bf16[3,256,384]{2,1,0:T(8,128)(2,1)S(1)} %get-tuple-element.88), channel_id=1, source_target_pairs={{0,8},{8,0},{16,24},{24,16},{1,9},{9,1},{17,25},{25,17},{2,10},{10... | collective-permute-start | bytes 1769480 | tf_op jit(solution)/shard_map/ppermute | solution.py:328
  124.8 3.8 %collective-permute-start.19 = (bf16[264,1024]{1,0:T(8,128)(2,1)S(1)}, bf16[264,1024]{1,0:T(8,128)(2,1)S(1)}, u32[]{:S(2)}, u32[]{:S(2)}) collective-permute-start(bf16[264,1024]{1,0:T(8,128)(2,1)S(1)} %add_convert_fusion.4), channel_id=1, source_target_pairs={{0,2},{1,3},{2,0},{3,1},{4,6},{5,7},{6,4},{7,5},{8,10},{9,11},{10,... | collective-permute-start | bytes 1622024 | tf_op jit(solution)/shard_map/ppermute | solution.py:341
  129.6 5.8 %collective-permute-done.21.a_last = bf16[3,256,384]{2,1,0:T(8,128)(2,1)S(1)} collective-permute-done((bf16[3,256,384]{2,1,0:T(8,128)(2,1)S(1)}, bf16[3,256,384]{2,1,0:T(8,128)(2,1)S(1)}, u32[]{:S(2)}, u32[]{:S(2)}) %collective-permute-start.21) | collective-permute-done | bytes 589856 | tf_op jit(solution)/shard_map/ppermute | solution.py:328
  135.4 1.6 %collective-permute-done.22.b_last = bf16[3,256,384]{2,1,0:T(8,128)(2,1)S(1)} collective-permute-done((bf16[3,256,384]{2,1,0:T(8,128)(2,1)S(1)}, bf16[3,256,384]{2,1,0:T(8,128)(2,1)S(1)}, u32[]{:S(2)}, u32[]{:S(2)}) %collective-permute-start.22) | collective-permute-done | bytes 589856 | tf_op jit(solution)/shard_map/ppermute | solution.py:328
  137.0 1.3 final_step.1
  138.3 1.5 %collective-permute-done.19.refs_1_ = bf16[264,1024]{1,0:T(8,128)(2,1)S(1)} collective-permute-done((bf16[264,1024]{1,0:T(8,128)(2,1)S(1)}, bf16[264,1024]{1,0:T(8,128)(2,1)S(1)}, u32[]{:S(2)}, u32[]{:S(2)}) %collective-permute-start.19) | collective-permute-done | bytes 540704 | tf_op jit(solution)/shard_map/ppermute | solution.py:341
  139.8 1.0 total.1
  (36 shorter events, 4.9 us)
Async XLA Ops:
  2.9 8.3 %collective-permute-start = (bf16[520,1024]{1,0:T(8,128)(2,1)}, bf16[520,1024]{1,0:T(8,128)(2,1)S(1)}, u32[]{:S(2)}, u32[]{:S(2)}) collective-permute-start(bf16[520,1024]{1,0:T(8,128)(2,1)} %payload.1.refs_0_), channel_id=1, source_target_pairs={{0,1},{1,0},{2,3},{3,2},{4,5},{5,4},{6,7},{7,6},{8,9},{9,8},{10,11... | collective-permute-start | bytes 3194888 | tf_op jit(solution)/shard_map/ppermute | solution.py:344
  3.4 27.0 %collective-permute-start.4 = (bf16[520,1024]{1,0:T(8,128)(2,1)}, bf16[520,1024]{1,0:T(8,128)(2,1)S(1)}, u32[]{:S(2)}, u32[]{:S(2)}) collective-permute-start(bf16[520,1024]{1,0:T(8,128)(2,1)} %payload.1.refs_0_), channel_id=1, source_target_pairs={{0,2},{1,3},{2,0},{3,1},{4,6},{5,7},{6,4},{7,5},{8,10},{9,11},{10,... | collective-permute-start | bytes 3194888 | tf_op jit(solution)/shard_map/ppermute | solution.py:341
  6.0 24.3 %collective-permute-start.3 = (bf16[520,1024]{1,0:T(8,128)(2,1)}, bf16[520,1024]{1,0:T(8,128)(2,1)S(1)}, u32[]{:S(2)}, u32[]{:S(2)}) collective-permute-start(bf16[520,1024]{1,0:T(8,128)(2,1)} %payload.1.refs_0_), channel_id=1, source_target_pairs={{2,4},{3,5},{4,2},{5,3},{10,12},{11,13},{12,10},{13,11},{18,20},{1... | collective-permute-start | bytes 3194888 | tf_op jit(solution)/shard_map/ppermute | solution.py:341
  6.7 48.7 %collective-permute-start.2 = (bf16[520,1024]{1,0:T(8,128)(2,1)}, bf16[520,1024]{1,0:T(8,128)(2,1)S(1)}, u32[]{:S(2)}, u32[]{:S(2)}) collective-permute-start(bf16[520,1024]{1,0:T(8,128)(2,1)} %payload.1.refs_0_), channel_id=1, source_target_pairs={{0,6},{1,7},{6,0},{7,1},{8,14},{9,15},{14,8},{15,9},{16,22},{17,23... | collective-permute-start | bytes 3194888 | tf_op jit(solution)/shard_map/ppermute | solution.py:341
  11.1 2.3 %copy-start = (bf16[1,3,1024,768]{3,2,1,0:T(8,128)(2,1)S(1)}, bf16[1,3,1024,768]{3,2,1,0:T(8,128)(2,1)}, u32[]{:S(2)}) copy-start(bf16[1,3,1024,768]{3,2,1,0:T(8,128)(2,1)} %refs_2_.5) | copy-start | bytes 14155780
  13.5 1.2 copy-start.2
  14.7 45.0 %copy-start.1 = (bf16[1,3,1024,768]{3,2,1,0:T(8,128)(2,1)S(1)}, bf16[1,3,1024,768]{3,2,1,0:T(8,128)(2,1)}, u32[]{:S(2)}) copy-start(bf16[1,3,1024,768]{3,2,1,0:T(8,128)(2,1)} %refs_2_.5) | copy-start | bytes 14155780
  18.9 36.6 %collective-permute-start.1 = (bf16[264,1024]{1,0:T(8,128)(2,1)S(1)}, bf16[264,1024]{1,0:T(8,128)(2,1)S(1)}, u32[]{:S(2)}, u32[]{:S(2)}) collective-permute-start(bf16[264,1024]{1,0:T(8,128)(2,1)S(1)} %get-tuple-element.46), channel_id=1, source_target_pairs={{0,1},{1,0},{2,3},{3,2},{4,5},{5,4},{6,7},{7,6},{8,9},{9,8},{10,11... | collective-permute-start | bytes 1622024 | tf_op jit(solution)/shard_map/ppermute | solution.py:344
  55.5 2.7 %collective-permute-start.10 = (bf16[520,1024]{1,0:T(8,128)(2,1)S(1)}, bf16[520,1024]{1,0:T(8,128)(2,1)S(1)}, u32[]{:S(2)}, u32[]{:S(2)}) collective-permute-start(bf16[520,1024]{1,0:T(8,128)(2,1)S(1)} %collective-permute-done.2.refs_2_), channel_id=1, source_target_pairs={{0,1},{1,0},{2,3},{3,2},{4,5},{5,4},{6,7},{7,6},{8,9},{9,8},{10,11... | collective-permute-start | bytes 3194888 | tf_op jit(solution)/shard_map/ppermute | solution.py:344
  55.5 4.2 %collective-permute-start.9 = (bf16[520,1024]{1,0:T(8,128)(2,1)S(1)}, bf16[520,1024]{1,0:T(8,128)(2,1)S(1)}, u32[]{:S(2)}, u32[]{:S(2)}) collective-permute-start(bf16[520,1024]{1,0:T(8,128)(2,1)S(1)} %collective-permute-done.3.refs_0_), channel_id=1, source_target_pairs={{0,1},{1,0},{2,3},{3,2},{4,5},{5,4},{6,7},{7,6},{8,9},{9,8},{10,11... | collective-permute-start | bytes 3194888 | tf_op jit(solution)/shard_map/ppermute | solution.py:344
  56.0 8.5 %collective-permute-start.7 = (bf16[520,1024]{1,0:T(8,128)(2,1)S(1)}, bf16[520,1024]{1,0:T(8,128)(2,1)S(1)}, u32[]{:S(2)}, u32[]{:S(2)}) collective-permute-start(bf16[520,1024]{1,0:T(8,128)(2,1)S(1)} %collective-permute-done.4.refs_0_), channel_id=1, source_target_pairs={{0,1},{1,0},{2,3},{3,2},{4,5},{5,4},{6,7},{7,6},{8,9},{9,8},{10,11... | collective-permute-start | bytes 3194888 | tf_op jit(solution)/shard_map/ppermute | solution.py:344
  56.0 27.9 %collective-permute-start.5 = (bf16[520,1024]{1,0:T(8,128)(2,1)S(1)}, bf16[520,1024]{1,0:T(8,128)(2,1)S(1)}, u32[]{:S(2)}, u32[]{:S(2)}) collective-permute-start(bf16[520,1024]{1,0:T(8,128)(2,1)S(1)} %collective-permute-done.3.refs_0_), channel_id=1, source_target_pairs={{2,0},{3,1},{4,6},{5,7},{10,8},{11,9},{12,14},{13,15},{18,16},{19,... | collective-permute-start | bytes 3194888 | tf_op jit(solution)/shard_map/ppermute | solution.py:341
  57.3 26.6 %collective-permute-start.6 = (bf16[520,1024]{1,0:T(8,128)(2,1)S(1)}, bf16[520,1024]{1,0:T(8,128)(2,1)S(1)}, u32[]{:S(2)}, u32[]{:S(2)}) collective-permute-start(bf16[520,1024]{1,0:T(8,128)(2,1)S(1)} %collective-permute-done.4.refs_0_), channel_id=1, source_target_pairs={{2,4},{3,5},{4,2},{5,3},{10,12},{11,13},{12,10},{13,11},{18,20},{1... | collective-permute-start | bytes 3194888 | tf_op jit(solution)/shard_map/ppermute | solution.py:341
  64.3 19.6 %collective-permute-start.11 = (bf16[264,1024]{1,0:T(8,128)(2,1)S(1)}, bf16[264,1024]{1,0:T(8,128)(2,1)S(1)}, u32[]{:S(2)}, u32[]{:S(2)}) collective-permute-start(bf16[264,1024]{1,0:T(8,128)(2,1)S(1)} %get-tuple-element.51), channel_id=1, source_target_pairs={{0,1},{1,0},{2,3},{3,2},{4,5},{5,4},{6,7},{7,6},{8,9},{9,8},{10,11... | collective-permute-start | bytes 1622024 | tf_op jit(solution)/shard_map/ppermute | solution.py:344
  68.7 15.2 %collective-permute-start.8 = (bf16[264,1024]{1,0:T(8,128)(2,1)S(1)}, bf16[264,1024]{1,0:T(8,128)(2,1)S(1)}, u32[]{:S(2)}, u32[]{:S(2)}) collective-permute-start(bf16[264,1024]{1,0:T(8,128)(2,1)S(1)} %get-tuple-element.49), channel_id=1, source_target_pairs={{0,1},{1,0},{2,3},{3,2},{4,5},{5,4},{6,7},{7,6},{8,9},{9,8},{10,11... | collective-permute-start | bytes 1622024 | tf_op jit(solution)/shard_map/ppermute | solution.py:344
  84.3 2.7 %collective-permute-start.12 = (bf16[520,1024]{1,0:T(8,128)(2,1)S(1)}, bf16[520,1024]{1,0:T(8,128)(2,1)S(1)}, u32[]{:S(2)}, u32[]{:S(2)}) collective-permute-start(bf16[520,1024]{1,0:T(8,128)(2,1)S(1)} %add_convert_fusion.refs_0_), channel_id=1, source_target_pairs={{0,1},{1,0},{2,3},{3,2},{4,5},{5,4},{6,7},{7,6},{8,9},{9,8},{10,11... | collective-permute-start | bytes 3194888 | tf_op jit(solution)/shard_map/ppermute | solution.py:344
  92.4 28.1 %collective-permute-start.17 = (bf16[2,3,256,384]{3,2,1,0:T(8,128)(2,1)S(1)}, bf16[2,3,256,384]{3,2,1,0:T(8,128)(2,1)S(1)}, u32[]{:S(2)}, u32[]{:S(2)}) collective-permute-start(bf16[2,3,256,384]{3,2,1,0:T(8,128)(2,1)S(1)} %get-tuple-element.75), channel_id=1, source_target_pairs={{0,8},{8,0},{16,24},{24,16},{1,9},{9,1},{17,25},{25,17},{2,10},{10... | collective-permute-start | bytes 3538952 | tf_op jit(solution)/shard_map/ppermute | solution.py:328
  94.0 28.4 %collective-permute-start.18 = (bf16[2,3,256,384]{3,2,1,0:T(8,128)(2,1)S(1)}, bf16[2,3,256,384]{3,2,1,0:T(8,128)(2,1)S(1)}, u32[]{:S(2)}, u32[]{:S(2)}) collective-permute-start(bf16[2,3,256,384]{3,2,1,0:T(8,128)(2,1)S(1)} %get-tuple-element.77), channel_id=1, source_target_pairs={{0,16},{8,24},{16,0},{24,8},{1,17},{9,25},{17,1},{25,9},{2,18},{10... | collective-permute-start | bytes 3538952 | tf_op jit(solution)/shard_map/ppermute | solution.py:328
  95.5 4.7 %collective-permute-start.13 = (bf16[264,1024]{1,0:T(8,128)(2,1)S(1)}, bf16[264,1024]{1,0:T(8,128)(2,1)S(1)}, u32[]{:S(2)}, u32[]{:S(2)}) collective-permute-start(bf16[264,1024]{1,0:T(8,128)(2,1)S(1)} %get-tuple-element.70), channel_id=1, source_target_pairs={{0,1},{1,0},{2,3},{3,2},{4,5},{5,4},{6,7},{7,6},{8,9},{9,8},{10,11... | collective-permute-start | bytes 1622024 | tf_op jit(solution)/shard_map/ppermute | solution.py:344
  95.7 28.5 %collective-permute-start.16 = (bf16[264,1024]{1,0:T(8,128)(2,1)S(1)}, bf16[264,1024]{1,0:T(8,128)(2,1)S(1)}, u32[]{:S(2)}, u32[]{:S(2)}) collective-permute-start(bf16[264,1024]{1,0:T(8,128)(2,1)S(1)} %fusion), channel_id=1, source_target_pairs={{0,6},{1,7},{6,0},{7,1},{8,14},{9,15},{14,8},{15,9},{16,22},{17,23... | collective-permute-start | bytes 1622024 | tf_op jit(solution)/shard_map/ppermute | solution.py:341
  100.5 23.8 %collective-permute-start.15 = (bf16[264,1024]{1,0:T(8,128)(2,1)S(1)}, bf16[264,1024]{1,0:T(8,128)(2,1)S(1)}, u32[]{:S(2)}, u32[]{:S(2)}) collective-permute-start(bf16[264,1024]{1,0:T(8,128)(2,1)S(1)} %add_convert_fusion.6), channel_id=1, source_target_pairs={{2,4},{3,5},{4,2},{5,3},{10,12},{11,13},{12,10},{13,11},{18,20},{1... | collective-permute-start | bytes 1622024 | tf_op jit(solution)/shard_map/ppermute | solution.py:341
  101.2 23.1 %collective-permute-start.14 = (bf16[264,1024]{1,0:T(8,128)(2,1)S(1)}, bf16[264,1024]{1,0:T(8,128)(2,1)S(1)}, u32[]{:S(2)}, u32[]{:S(2)}) collective-permute-start(bf16[264,1024]{1,0:T(8,128)(2,1)S(1)} %add_convert_fusion.6), channel_id=1, source_target_pairs={{0,2},{1,3},{6,4},{7,5},{8,10},{9,11},{14,12},{15,13},{16,18},{17,... | collective-permute-start | bytes 1622024 | tf_op jit(solution)/shard_map/ppermute | solution.py:341
  120.8 14.6 %collective-permute-start.21 = (bf16[3,256,384]{2,1,0:T(8,128)(2,1)S(1)}, bf16[3,256,384]{2,1,0:T(8,128)(2,1)S(1)}, u32[]{:S(2)}, u32[]{:S(2)}) collective-permute-start(bf16[3,256,384]{2,1,0:T(8,128)(2,1)S(1)} %get-tuple-element.90), channel_id=1, source_target_pairs={{0,16},{8,24},{16,0},{24,8},{1,17},{9,25},{17,1},{25,9},{2,18},{10... | collective-permute-start | bytes 1769480 | tf_op jit(solution)/shard_map/ppermute | solution.py:328
  122.7 14.3 %collective-permute-start.22 = (bf16[3,256,384]{2,1,0:T(8,128)(2,1)S(1)}, bf16[3,256,384]{2,1,0:T(8,128)(2,1)S(1)}, u32[]{:S(2)}, u32[]{:S(2)}) collective-permute-start(bf16[3,256,384]{2,1,0:T(8,128)(2,1)S(1)} %get-tuple-element.88), channel_id=1, source_target_pairs={{0,8},{8,0},{16,24},{24,16},{1,9},{9,1},{17,25},{25,17},{2,10},{10... | collective-permute-start | bytes 1769480 | tf_op jit(solution)/shard_map/ppermute | solution.py:328
  124.8 15.0 %collective-permute-start.19 = (bf16[264,1024]{1,0:T(8,128)(2,1)S(1)}, bf16[264,1024]{1,0:T(8,128)(2,1)S(1)}, u32[]{:S(2)}, u32[]{:S(2)}) collective-permute-start(bf16[264,1024]{1,0:T(8,128)(2,1)S(1)} %add_convert_fusion.4), channel_id=1, source_target_pairs={{0,2},{1,3},{2,0},{3,1},{4,6},{5,7},{6,4},{7,5},{8,10},{9,11},{10,... | collective-permute-start | bytes 1622024 | tf_op jit(solution)/shard_map/ppermute | solution.py:341
  128.6 11.2 %collective-permute-start.20 = (bf16[264,1024]{1,0:T(8,128)(2,1)S(1)}, bf16[264,1024]{1,0:T(8,128)(2,1)S(1)}, u32[]{:S(2)}, u32[]{:S(2)}) collective-permute-start(bf16[264,1024]{1,0:T(8,128)(2,1)S(1)} %add_convert_fusion.3), channel_id=1, source_target_pairs={{2,4},{3,5},{4,2},{5,3},{10,12},{11,13},{12,10},{13,11},{18,20},{1... | collective-permute-start | bytes 1622024 | tf_op jit(solution)/shard_map/ppermute | solution.py:341
